TPU v7x, 32 devices: a whole 2x2x4 slice. The times are simulated.
32 devices in a mesh: grp: 4 (over y, x), rep: 8 (over z, core).
Axes of the slice: x: 2, y: 2, z: 4, core: 2. Of those that a mesh axis runs over, the one named last changes fastest.
Arguments:
- tokens: bfloat16 [8, 1536, 1024], P('rep', 'grp'), may hold values from -6 to 6
- slot_ids: int32 [8, 1536], P('rep', 'grp'), may hold values from -1 to 8, as said below
- cotangent: bfloat16 [8, 1536, 1024], P('rep', 'grp'), may hold values from -6 to 6
- inproj: float32 [1024, 3072], P('grp'), may hold values from -0.25 to 0.25
- outproj: float32 [1024, 1024], P('grp'), may hold values from -1 to 1
- upproj: float32 [1024, 5248], P('grp'), may hold values from -0.1875 to 0.1875
- downproj: float32 [2624, 1024], P('grp'), may hold values from -0.125 to 0.125
- norm_gains: float32 [1024, 2], P('grp'), may hold values from 0.5 to 1.5
- inproj_mean: float32 [1024, 3072], P('grp'), may hold values from -128 to 128
- outproj_mean: float32 [1024, 1024], P('grp'), may hold values from -16 to 16
- upproj_mean: float32 [1024, 5248], P('grp'), may hold values from -32 to 32
- downproj_mean: float32 [2624, 1024], P('grp'), may hold values from -48 to 48
- gains_mean: float32 [1024, 2], P('grp'), may hold values from -192 to 192
- inproj_square: float32 [1024, 3072], P('grp'), may hold values from 49.152 to 196.608
- outproj_square: float32 [1024, 1024], P('grp'), may hold values from 0.768 to 3.072
- upproj_square: float32 [1024, 5248], P('grp'), may hold values from 2.162688 to 8.6016
- downproj_square: float32 [2624, 1024], P('grp'), may hold values from 5.16096 to 20.8896
- gains_square: float32 [1024, 2], P('grp'), may hold values from 11.0592 to 1228.8
Outputs:
- layer_out: bfloat16 [8, 1536, 1024], P('rep', 'grp')
- input_grad: bfloat16 [8, 1536, 1024], P('rep', 'grp')
- newmean_inproj: float32 [1024, 3072], P('grp')
- newsquare_inproj: float32 [1024, 3072], P('grp')
- updated_inproj: float32 [1024, 3072], P('grp')
- newmean_outproj: float32 [1024, 1024], P('grp')
- newsquare_outproj: float32 [1024, 1024], P('grp')
- updated_outproj: float32 [1024, 1024], P('grp')
- newmean_upproj: float32 [1024, 5248], P('grp')
- newsquare_upproj: float32 [1024, 5248], P('grp')
- updated_upproj: float32 [1024, 5248], P('grp')
- newmean_downproj: float32 [2624, 1024], P('grp')
- newsquare_downproj: float32 [2624, 1024], P('grp')
- updated_downproj: float32 [2624, 1024], P('grp')
- newmean_gains: float32 [1024, 2], P('grp')
- newsquare_gains: float32 [1024, 2], P('grp')
- updated_gains: float32 [1024, 2], P('grp')
Inputs may be any that keep to these rules, and one draw needn't show every extreme that they name: `slot_ids`: in each group, every device's 384 slots hold its live slots first and empty slots (-1) after them; each device has 336 to 384 live slots, and in every group some device has all of them live and some has exactly 336. Sequence numbers never fall along the live slots of a group; a sequence is the live slots of one number. In every group one sequence has slots on the first and on the last device, and the largest number used is 8.
All inputs are finite; a program needn't handle non-finite values.
Results may differ from a plain program's by a relative error of at most 0.015.
The roundings to bfloat16 on the way count: a program that leaves them out, or rounds other values in their place, can miss the bound.
Values may be sent and summed in bfloat16 or wider, within the bound.
No kernel may reach another device: no remote copies, remote signals or barrier semaphores. Data moves between devices by JAX's collectives and lax.ppermute only.
A program may use at most 256 MiB of HBM per device.

v0:
```python
import jax
import jax.numpy as jnp
from jax import lax
from jax.sharding import PartitionSpec as P

D = 1024
HEADS = 16
HEAD = 64
FF = 2624
STEP = 10
SEQ_SLOTS = 9


rope_base = 160000.0
norm_eps = 1e-05
rate_list = (0.1, 0.4, 0.08, 0.05, 0.6)


def shortened(array):

    def short(part):
        return part.astype(jnp.bfloat16) if part.dtype == jnp.float32 else part

    return jax.tree.map(short, array)


def layer_norm(values, gain):
    centred = values - jnp.mean(values, axis=-1, keepdims=True)
    spread = jnp.mean(centred * centred, axis=-1, keepdims=True)
    return centred * lax.rsqrt(spread + norm_eps) * gain


def positions(ids):
    live = ids >= 0
    counted = jnp.cumsum(live.astype(jnp.int32)) - 1
    onehot = (
        (ids[:, None] == jnp.arange(SEQ_SLOTS, dtype=jnp.int32)[None, :]) & live[:, None]
    ).astype(jnp.int32)
    counts = jnp.sum(onehot, axis=0)
    starts = jnp.cumsum(counts) - counts
    first = jnp.sum(onehot * starts[None, :], axis=1)
    return jnp.where(live, counted - first, 0)


def rope_angles(where_at):
    half = HEAD // 2
    inverse = rope_base ** (-(jnp.arange(half, dtype=jnp.float32) * 2.0 / HEAD))
    angles = where_at.astype(jnp.float32)[:, None] * inverse[None, :]
    return jnp.concatenate([angles, angles], axis=1)


def rotate(values, angles):
    count = values.shape[0]
    half = HEAD // 2
    heads = values.reshape(count, HEADS, HEAD)
    turned = jnp.concatenate([-heads[..., half:], heads[..., :half]], axis=-1)
    result = heads * jnp.cos(angles)[:, None, :] + turned * jnp.sin(angles)[:, None, :]
    return result.reshape(count, D)


def product(left, right):
    return jnp.dot(left, right, preferred_element_type=jnp.float32)


def contract(left, right):
    return lax.dot_general(
        left, right, (((0,), (0,)), ((), ())), preferred_element_type=jnp.float32
    )


def against(left, right):
    return lax.dot_general(
        left, right, (((1,), (1,)), ((), ())), preferred_element_type=jnp.float32
    )


def split_pairs(values):
    return values.reshape(values.shape[0], HEADS // 2, 2, HEAD).transpose(1, 0, 2, 3)


def join_pairs(values):
    return values.transpose(1, 0, 2, 3).reshape(values.shape[1], D)


def masked_scores(query_pair, key_pair, allowed):
    scores = jnp.einsum(
        "qhd,khd->hqk", query_pair, key_pair, preferred_element_type=jnp.float32
    ) * HEAD ** (-0.5)
    return jnp.where(allowed[None], scores, -1e30)


def attention_forward(query, keys, values, allowed):

    def one_pair(pieces):
        query_pair, key_pair, value_pair = pieces
        scores = masked_scores(query_pair, key_pair, allowed)
        row_max = jnp.max(scores, axis=-1, keepdims=True)
        totals = jnp.sum(jnp.exp(scores - row_max), axis=-1, keepdims=True)
        log_totals = row_max + jnp.log(totals)
        weights = jnp.exp(scores - log_totals).astype(jnp.bfloat16)
        mixed = jnp.einsum("hqk,khd->qhd", weights, value_pair, preferred_element_type=jnp.float32)
        return (mixed, log_totals[..., 0])

    mixed, log_totals = lax.map(
        one_pair, (split_pairs(query), split_pairs(keys), split_pairs(values))
    )
    return (join_pairs(mixed), log_totals)


def attention_backward(query, keys, values, grad_attended, log_totals, allowed):
    scale = HEAD ** (-0.5)

    def one_pair(pieces):
        query_pair, key_pair, value_pair, grad_pair, total_pair = pieces
        scores = masked_scores(query_pair, key_pair, allowed)
        weights = jnp.exp(scores - total_pair[..., None])
        low_weights = weights.astype(jnp.bfloat16)
        grad_values = jnp.einsum(
            "hqk,qhd->khd", low_weights, grad_pair, preferred_element_type=jnp.float32
        )
        grad_weights = jnp.einsum(
            "qhd,khd->hqk", grad_pair, value_pair, preferred_element_type=jnp.float32
        )
        centre = jnp.sum(weights * grad_weights, axis=-1, keepdims=True)
        grad_scores = (weights * (grad_weights - centre)).astype(jnp.bfloat16)
        grad_query = (
            jnp.einsum("hqk,khd->qhd", grad_scores, key_pair, preferred_element_type=jnp.float32)
            * scale
        )
        grad_keys = (
            jnp.einsum("hqk,qhd->khd", grad_scores, query_pair, preferred_element_type=jnp.float32)
            * scale
        )
        return (grad_query, grad_keys, grad_values, centre[..., 0])

    grad_query, grad_keys, grad_values, centre = lax.map(
        one_pair,
        (
            split_pairs(query),
            split_pairs(keys),
            split_pairs(values),
            split_pairs(grad_attended),
            log_totals,
        ),
    )
    return (join_pairs(grad_query), join_pairs(grad_keys), join_pairs(grad_values), centre)


def gated(gate, upward):
    return jax.nn.gelu(gate, approximate=False) * upward


def adam_update(weight, mean, square, grad, rate):
    mean_new = 0.9 * mean + 0.1 * grad
    square_new = 0.999 * square + 0.001 * grad * grad
    step_size = mean_new / (1.0 - 0.9**STEP) / (jnp.sqrt(square_new / (1.0 - 0.999**STEP)) + 1e-08)
    return (mean_new, square_new, weight - rate * (step_size + 0.01 * weight))


def local(
    tokens,
    slot_ids,
    cotangent,
    inproj,
    outproj,
    upproj,
    downproj,
    norm_gains,
    inproj_mean,
    outproj_mean,
    upproj_mean,
    downproj_mean,
    gains_mean,
    inproj_square,
    outproj_square,
    upproj_square,
    downproj_square,
    gains_square,
):
    own_rows = tokens.shape[1]
    own_index = lax.axis_index("grp")
    masters = (inproj, outproj, upproj, downproj, norm_gains)
    lowered = tuple((item.astype(jnp.bfloat16) for item in masters))
    w_in, w_out, w_up, w_down, gains_low = jax.tree.map(
        lambda part, own: part.astype(own.dtype),
        lax.all_gather(shortened(lowered), "grp", axis=0, tiled=True),
        lowered,
    )
    gains = gains_low.astype(jnp.float32)
    all_ids = lax.all_gather(slot_ids, "grp", axis=1, tiled=True)[0]
    group_rows = all_ids.shape[0]
    own_ids = slot_ids[0]
    angles = rope_angles(
        lax.dynamic_slice_in_dim(positions(all_ids), own_index * own_rows, own_rows)
    )
    own_slots = own_index * own_rows + jnp.arange(own_rows, dtype=jnp.int32)
    group_slots = jnp.arange(group_rows, dtype=jnp.int32)
    allowed = (own_ids[:, None] == all_ids[None, :]) & (own_ids[:, None] >= 0) | (
        own_slots[:, None] == group_slots[None, :]
    )
    live = (own_ids >= 0).astype(jnp.bfloat16)
    inputs = tokens[0].astype(jnp.float32)
    first_normed = layer_norm(inputs, gains[:, 0]).astype(jnp.bfloat16)
    projected = product(first_normed, w_in)
    query = rotate(projected[:, :D], angles).astype(jnp.bfloat16)
    keys = rotate(projected[:, D : 2 * D], angles).astype(jnp.bfloat16)
    values = projected[:, 2 * D :].astype(jnp.bfloat16)
    keys_all, values_all = (
        lax.all_gather(keys, "grp", axis=0, tiled=True),
        lax.all_gather(values, "grp", axis=0, tiled=True),
    )
    attended, log_totals = attention_forward(query, keys_all, values_all, allowed)
    attended = attended.astype(jnp.bfloat16)
    middle = inputs + product(attended, w_out)
    second_normed = layer_norm(middle, gains[:, 1]).astype(jnp.bfloat16)
    gate_up = product(second_normed, w_up)
    gate = gate_up[:, :FF]
    upward = gate_up[:, FF:]
    hidden = gated(gate, upward).astype(jnp.bfloat16)
    result = middle + product(hidden, w_down)
    w_in, w_out, w_up, w_down, gains_low = jax.tree.map(
        lambda part, own: part.astype(own.dtype),
        lax.all_gather(shortened(lowered), "grp", axis=0, tiled=True),
        lowered,
    )
    gains = gains_low.astype(jnp.float32)
    grad_top = cotangent[0] * live[:, None]
    grad_down = contract(hidden, grad_top)
    grad_hidden = against(grad_top, w_down)
    _, gate_back = jax.vjp(gated, gate, upward)
    grad_gate, grad_upward = gate_back(grad_hidden)
    grad_gate_up = jnp.concatenate([grad_gate, grad_upward], axis=1).astype(jnp.bfloat16)
    grad_up = contract(second_normed, grad_gate_up)
    grad_second = against(grad_gate_up, w_up)
    _, second_back = jax.vjp(layer_norm, middle, gains[:, 1])
    grad_from_norm, grad_gain_two = second_back(grad_second)
    grad_middle = grad_top.astype(jnp.float32) + grad_from_norm
    grad_branch = grad_middle.astype(jnp.bfloat16)
    grad_outproj = contract(attended, grad_branch)
    grad_attended = against(grad_branch, w_out).astype(jnp.bfloat16)
    keys_all, values_all = (
        lax.all_gather(keys, "grp", axis=0, tiled=True),
        lax.all_gather(values, "grp", axis=0, tiled=True),
    )
    grad_query, key_terms, value_terms, centre = attention_backward(
        query, keys_all, values_all, grad_attended, log_totals, allowed
    )
    grad_keys, grad_values = (
        lax.psum_scatter(
            key_terms.astype(jnp.bfloat16), "grp", scatter_dimension=0, tiled=True
        ).astype(jnp.float32),
        lax.psum_scatter(
            value_terms.astype(jnp.bfloat16), "grp", scatter_dimension=0, tiled=True
        ).astype(jnp.float32),
    )
    grad_projected = jnp.concatenate(
        [rotate(grad_query, -angles), rotate(grad_keys, -angles), grad_values], axis=1
    ).astype(jnp.bfloat16)
    grad_in = contract(first_normed, grad_projected)
    grad_first = against(grad_projected, w_in)
    _, first_back = jax.vjp(layer_norm, inputs, gains[:, 0])
    grad_inputs, grad_gain_one = first_back(grad_first)
    input_grad = (grad_middle + grad_inputs).astype(jnp.bfloat16)
    grad_gains = jnp.stack([grad_gain_one, grad_gain_two], axis=1)
    shares = (
        lax.psum_scatter(
            grad_in.astype(jnp.bfloat16), "grp", scatter_dimension=0, tiled=True
        ).astype(jnp.float32),
        lax.psum_scatter(
            grad_outproj.astype(jnp.bfloat16), "grp", scatter_dimension=0, tiled=True
        ).astype(jnp.float32),
        lax.psum_scatter(
            grad_up.astype(jnp.bfloat16), "grp", scatter_dimension=0, tiled=True
        ).astype(jnp.float32),
        lax.psum_scatter(
            grad_down.astype(jnp.bfloat16), "grp", scatter_dimension=0, tiled=True
        ).astype(jnp.float32),
        lax.psum_scatter(
            grad_gains.astype(jnp.bfloat16), "grp", scatter_dimension=0, tiled=True
        ).astype(jnp.float32),
    )
    totals = (
        lax.psum(shares[0].astype(jnp.bfloat16), "rep").astype(jnp.float32),
        lax.psum(shares[1].astype(jnp.bfloat16), "rep").astype(jnp.float32),
        lax.psum(shares[2].astype(jnp.bfloat16), "rep").astype(jnp.float32),
        lax.psum(shares[3].astype(jnp.bfloat16), "rep").astype(jnp.float32),
        lax.psum(shares[4].astype(jnp.bfloat16), "rep").astype(jnp.float32),
    )
    means = (inproj_mean, outproj_mean, upproj_mean, downproj_mean, gains_mean)
    squares = (inproj_square, outproj_square, upproj_square, downproj_square, gains_square)
    updates = [
        adam_update(masters[index], means[index], squares[index], totals[index], rate_list[index])
        for index in range(5)
    ]
    return (
        result.astype(jnp.bfloat16)[None],
        input_grad[None],
        updates[0][0],
        updates[0][1],
        updates[0][2],
        updates[1][0],
        updates[1][1],
        updates[1][2],
        updates[2][0],
        updates[2][1],
        updates[2][2],
        updates[3][0],
        updates[3][1],
        updates[3][2],
        updates[4][0],
        updates[4][1],
        updates[4][2],
    )


def solution(mesh):
    placed = (
        P("rep", "grp", None),
        P("rep", "grp"),
        P("rep", "grp", None),
        P("grp", None),
        P("grp", None),
        P("grp", None),
        P("grp", None),
        P("grp", None),
        P("grp", None),
        P("grp", None),
        P("grp", None),
        P("grp", None),
        P("grp", None),
        P("grp", None),
        P("grp", None),
        P("grp", None),
        P("grp", None),
        P("grp", None),
    )
    return jax.shard_map(
        local,
        mesh=mesh,
        in_specs=placed,
        out_specs=(
            P("rep", "grp", None),
            P("rep", "grp", None),
            P("grp", None),
            P("grp", None),
            P("grp", None),
            P("grp", None),
            P("grp", None),
            P("grp", None),
            P("grp", None),
            P("grp", None),
            P("grp", None),
            P("grp", None),
            P("grp", None),
            P("grp", None),
            P("grp", None),
            P("grp", None),
            P("grp", None),
        ),
        check_vma=False,
    )
```

profile of v0, /device:TPU:0, one launch (start us, length us, event | category | flops | bytes accessed | tf_op | source)
XLA Modules:
  0.0 1141.3 jit_solution(10610267900369749216)
XLA Ops:
  7.3 3.3 convert_element_type.161
  10.6 9.7 all_gather.34
  26.1 8.1 all_gather.31
  35.3 48.3 %all-gather.7.cloned.1.call-done = bf16[1024,3072]{1,0:T(8,128)(2,1)} async-done(((bf16[256,3072]{1,0:T(8,128)(2,1)}), bf16[1024,3072]{1,0:T(8,128)(2,1)}) %all-gather.7.cloned.1.call-update) | async-done | bytes 6291472 | tf_op jit(solution)/shard_map/all_gather | solution.py:186
  83.6 4.9 fusion.101
  92.8 3.0 copy.73
  95.8 3.0 copy.69
  103.0 3.0 copy.70
  106.0 3.0 copy.74
  109.0 4.9 add_convert_fusion.3
  117.5 4.3 convert_element_type.173
  127.3 30.7 %all-gather.11.cloned.1.call-done = bf16[1536,1024]{1,0:T(8,128)(2,1)} async-done(((bf16[384,1024]{1,0:T(8,128)(2,1)}), bf16[1536,1024]{1,0:T(8,128)(2,1)}) %all-gather.11.cloned.1.call-update) | async-done | bytes 3145744 | tf_op jit(solution)/shard_map/all_gather | solution.py:209
  158.0 4.6 copy.75
  162.7 41.8 %all-gather.9.cloned.1.call-done = bf16[1536,1024]{1,0:T(8,128)(2,1)} async-done(((bf16[384,1024]{1,0:T(8,128)(2,1)}), bf16[1536,1024]{1,0:T(8,128)(2,1)}) %all-gather.9.cloned.1.call-update) | async-done | bytes 3145744 | tf_op jit(solution)/shard_map/all_gather | solution.py:210
  204.5 4.6 copy.67
  209.1 46.2 %while.30 = (s32[]{:T(128)}, bf16[8,384,2,64]{1,3,2,0:T(8,128)(2,1)S(1)}, f32[8,2,384]{2,1,0:T(2,128)S(1)}, bf16[8,1536,2,64]{1,3,2,0:T(8,128)(2,1)}, bf16[8,384...) while((s32[]{:T(128)}, ...), condition=%wide.region_10.11_spmd.clone.clone, body=%wide.region_7.10_spmd.clone.sunk.clone | while | flops 312605952 | bytes 16453097 | solution.py:104
  256.2 3.3 fusion.121
  259.8 91.8 %all-gather.15.cloned.1.call-done = bf16[1024,5248]{1,0:T(8,128)(2,1)} async-done(((bf16[256,5248]{1,0:T(8,128)(2,1)}), bf16[1024,5248]{1,0:T(8,128)(2,1)}) %all-gather.15.cloned.1.call-update) | async-done | bytes 10747920 | tf_op jit(solution)/shard_map/all_gather | solution.py:186
  351.6 10.8 fusion.104
  362.4 54.0 %all-gather.17.cloned.1.call-done = bf16[2624,1024]{1,0:T(8,128)(2,1)} async-done(((bf16[656,1024]{1,0:T(8,128)(2,1)}), bf16[2624,1024]{1,0:T(8,128)(2,1)}) %all-gather.17.cloned.1.call-update) | async-done | bytes 5373968 | tf_op jit(solution)/shard_map/all_gather | solution.py:186
  416.4 15.8 %add_convert_fusion = (bf16[384,2624]{1,0:T(8,128)(2,1)}, f32[384,2624]{1,0:T(8,128)S(1)}, f32[384,2624]{1,0:T(8,128)}) fusion(f32[384,5248]{1,0:T(8,128)} %fusion.104, bf16[2624,1024]{1,0:T(8,128)(2,1)} %all-gather.17.cloned.1.call-done, bf16[1,384,1024]{2,1,0:T(8,128)(2,1)} %param.24, bf16[384]{0:T(512)(128)(2,1)S(1)} %get-tuple-element.249), kind=kOutput, calls=%fused_computation.68 | convolution fusion | flops 2137546752 | bytes 24298240 | tf_op jit(solution)/shard_map/dot_general | solution.py:72
  432.3 7.6 multiply_convert_fusion.1
  439.9 11.1 multiply_reduce_fusion.1
  459.7 95.6 %while.31 = (s32[]{:T(128)}, f32[8,384,2,64]{1,3,2,0:T(8,128)}, bf16[8,1536,2,64]{1,3,2,0:T(8,128)(2,1)}, bf16[8,1536,2,64]{1,3,2,0:T(8,128)(2,1)}, bf16[8,1536,...) while((s32[]{:T(128)}, f32[8,384,2,64]{1,3,2,0:T(8,128)}, ...), condition=%wide.region_17.18_spmd.clone.clone, body=%wide.region_15.17_spmd.clone.sunk.clone | while | flops 768195840 | bytes 39941632 | solution.py:136
  486.2 2.9 multiply_reduce_fusion.6
  498.2 2.9 multiply_reduce_fusion.6
  534.1 2.9 multiply_reduce_fusion.6
  546.0 2.9 multiply_reduce_fusion.6
  555.3 4.6 copy.80
  560.1 4.8 copy.82
  566.0 3.9 convolution_convert_fusion.3
  570.0 7.2 convolution_convert_fusion.1
  580.0 24.1 %reduce-scatter.22.cloned.1.call-done = bf16[384,1024]{1,0:T(8,128)(2,1)} async-done(((bf16[1536,1024]{1,0:T(8,128)(2,1)}), bf16[384,1024]{1,0:T(8,128)(2,1)}) %reduce-scatter.22.cloned.1.call-update) | async-done | bytes 786448
  609.9 41.7 %reduce-scatter.24.cloned.1.call-done = bf16[384,1024]{1,0:T(8,128)(2,1)} async-done(((bf16[1536,1024]{1,0:T(8,128)(2,1)}), bf16[384,1024]{1,0:T(8,128)(2,1)}) %reduce-scatter.24.cloned.1.call-update) | async-done | bytes 786448
  653.2 7.4 convolution_convert_fusion.2
  660.7 11.4 %convolution_convert_fusion = bf16[1024,5248]{1,0:T(8,128)(2,1)} fusion(bf16[384,2624]{1,0:T(8,128)(2,1)} %copy-done.7, bf16[384,2624]{1,0:T(8,128)(2,1)} %get-tuple-element.247, f32[384,1024]{1,0:T(8,128)S(1)} %get-tuple-element.280, f32[1024]{0:T(1024)S(1)} %bitcast.259, f32[384]{0:T(512)S(1)} %fusion.95, f32[384]{0:T(512)S(1)} %broadcast_multiply_fusion.1), kind=kOutput, calls=%fused_computation.56 | convolution fusion | flops 4142202880 | bytes 16358400 | tf_op jit(solution)/shard_map/dot_general | solution.py:66
  673.3 6.2 fusion.69
  682.4 8.0 reduce-scatter.16.cloned.1.call-done
  690.4 66.3 %reduce-scatter.20.cloned.1.call-done = bf16[656,1024]{1,0:T(8,128)(2,1)} async-done(((bf16[2624,1024]{1,0:T(8,128)(2,1)}), bf16[656,1024]{1,0:T(8,128)(2,1)}) %reduce-scatter.20.cloned.1.call-update) | async-done | bytes 1343504 | tf_op jit(solution)/shard_map/reduce_scatter | solution.py:275
  756.7 73.5 %reduce-scatter.14.cloned.1.call-done = bf16[256,3072]{1,0:T(8,128)(2,1)} async-done(((bf16[1024,3072]{1,0:T(8,128)(2,1)}), bf16[256,3072]{1,0:T(8,128)(2,1)}) %reduce-scatter.14.cloned.1.call-update) | async-done | bytes 1572880 | tf_op jit(solution)/shard_map/reduce_scatter | solution.py:266
  830.2 109.0 %reduce-scatter.18.cloned.1.call-done = bf16[256,5248]{1,0:T(8,128)(2,1)} async-done(((bf16[1024,5248]{1,0:T(8,128)(2,1)}), bf16[256,5248]{1,0:T(8,128)(2,1)}) %reduce-scatter.18.cloned.1.call-update) | async-done | bytes 2686992 | tf_op jit(solution)/shard_map/reduce_scatter | solution.py:272
  939.2 6.6 fusion.74
  947.5 19.3 %reduce-scatter.26.cloned.1.call-done = bf16[256,2]{1,0:T(8,128)(2,1)} async-done(((bf16[1024,2]{1,0:T(8,128)(2,1)}), bf16[256,2]{1,0:T(8,128)(2,1)}) %reduce-scatter.26.cloned.1.call-update) | async-done | bytes 1040
  967.7 16.4 %psum.39 = bf16[256,2]{0,1:T(2,128)(2,1)S(1)} all-reduce(bf16[256,2]{0,1:T(2,128)(2,1)S(1)} %copy.85), channel_id=1, replica_groups=mesh['grp'=4,'rep'=8] {'rep'}, use_global_device_ids=true, to_apply=%region_33.34 | all-reduce | flops 512 | bytes 2048 | tf_op jit(solution)/shard_map/psum | solution.py:287
  984.7 119.2 %all-reduce.3.cloned.1.call-done = (bf16[256,3072]{1,0:T(8,128)(2,1)}, bf16[256,1024]{1,0:T(8,128)(2,1)}, bf16[256,5248]{1,0:T(8,128)(2,1)}, bf16[656,1024]{1,0:T(8,128)(2,1)}) async-done(((bf16[256,3072]{1,0:T(8,128)(2,1)}, bf16[256,1024]{1,0:T(8,128)(2,1)}, bf16[256,5248]{1,0:T(8,128)(2,1)}, bf16[656,1024]{1,0:T(8,128)(2,1)}), (bf16[256,3072]{1,0:T(8,128)(2,1)}, bf16[256,1024]{1,0:T(8,128)(2,1)}, ...) | async-done | bytes 6127632 | tf_op jit(solution)/shard_map/psum | solution.py:283
  1103.9 13.6 %multiply_subtract_fusion = (f32[256,5248]{1,0:T(8,128)}, f32[256,5248]{1,0:T(8,128)}, f32[256,5248]{1,0:T(8,128)}) fusion(f32[256,5248]{1,0:T(8,128)} %param.27, bf16[256,5248]{1,0:T(8,128)(2,1)} %get-tuple-element.226, f32[256,5248]{1,0:T(8,128)} %param.37, f32[256,5248]{1,0:T(8,128)} %param.32), kind=kLoop, calls=%fused_computation.64 | loop fusion | flops 21495808 | bytes 34930688 | tf_op jit(solution)/shard_map/sub | solution.py:157
  1119.3 5.2 multiply_subtract_fusion.1
  1126.0 6.3 multiply_subtract_fusion.2
  (287 shorter events, 187.8 us)
Async XLA Ops:
  7.2 3.4 copy-start.43
  7.2 13.8 %copy-start.41 = (f32[256,2]{0,1:T(2,128)S(1)}, f32[256,2]{0,1:T(2,128)}, u32[]{:S(2)}) copy-start(f32[256,2]{0,1:T(2,128)} %param.29) | copy-start | bytes 6148
  7.2 76.4 %all-gather.7.cloned.1.call-start = ((), (), s32[]{:S(2)}) async-start(), calls=%async_computation.7 | async-start | bytes 7864320 | tf_op jit(solution)/shard_map/all_gather | solution.py:186
  10.5 23.6 %copy-start = (bf16[1,384,1024]{2,1,0:T(8,128)(2,1)S(1)}, bf16[1,384,1024]{2,1,0:T(8,128)(2,1)}, u32[]{:S(2)}) copy-start(bf16[1,384,1024]{2,1,0:T(8,128)(2,1)} %param.22) | copy-start | bytes 2359300
  10.5 147.5 %all-gather.11.cloned.1.call-start = ((), (), s32[]{:S(2)}) async-start(), calls=%async_computation.9 | async-start | bytes 3932160 | tf_op jit(solution)/shard_map/all_gather | solution.py:209
  34.3 54.2 %copy-start.35 = (f32[384]{0:T(512)}, f32[384]{0:T(512)S(1)}, u32[]{:S(2)}) copy-start(f32[384]{0:T(512)S(1)} %broadcast_multiply_fusion.2) | copy-start | bytes 4612
  35.2 53.3 %copy-start.37 = (f32[384]{0:T(512)}, f32[384]{0:T(512)S(1)}, u32[]{:S(2)}) copy-start(f32[384]{0:T(512)S(1)} %fusion.94) | copy-start | bytes 4612
  35.3 53.3 %copy-start.33 = (f32[1024,1]{0,1:T(1,128)}, f32[1024,1]{0,1:T(1,128)S(1)}, u32[]{:S(2)}) copy-start(f32[1024,1]{0,1:T(1,128)S(1)} %get-tuple-element.278) | copy-start | bytes 12292
  88.6 2.2 copy-start.6
  113.9 2.6 copy-start.11
  113.9 90.6 %all-gather.9.cloned.1.call-start = ((), (), s32[]{:S(2)}) async-start(), calls=%async_computation.8 | async-start | bytes 3932160 | tf_op jit(solution)/shard_map/all_gather | solution.py:210
  116.5 138.9 %all-gather.13.cloned.1.call-start = ((), (), s32[]{:S(2)}) async-start(), calls=%async_computation.10 | async-start | bytes 2621440 | tf_op jit(solution)/shard_map/all_gather | solution.py:186
  117.4 234.2 %all-gather.15.cloned.1.call-start = ((), (), s32[]{:S(2)}) async-start(), calls=%async_computation.11 | async-start | bytes 13434880 | tf_op jit(solution)/shard_map/all_gather | solution.py:186
  121.8 2.0 copy-start.4
  121.8 294.6 %all-gather.17.cloned.1.call-start = ((), (), s32[]{:S(2)}) async-start(), calls=%async_computation.12 | async-start | bytes 6717440 | tf_op jit(solution)/shard_map/all_gather | solution.py:186
  125.1 479.0 %reduce-scatter.22.cloned.1.call-start = ((), (), s32[]{:S(2)}) async-start(), calls=%async_computation.17 | async-start | bytes 3932160
  439.9 11.1 copy-start.7
  451.0 3.3 copy-start.17
  451.0 4.5 copy-start.23
  560.0 91.6 %reduce-scatter.24.cloned.1.call-start = ((), (), s32[]{:S(2)}) async-start(), calls=%async_computation.18 | async-start | bytes 3932160
  564.9 125.5 %reduce-scatter.16.cloned.1.call-start = ((), (), s32[]{:S(2)}) async-start(), calls=%async_computation.14 | async-start | bytes 2621440 | tf_op jit(solution)/shard_map/reduce_scatter | solution.py:269
  570.0 186.7 %reduce-scatter.20.cloned.1.call-start = ((), (), s32[]{:S(2)}) async-start(), calls=%async_computation.16 | async-start | bytes 6717440 | tf_op jit(solution)/shard_map/reduce_scatter | solution.py:275
  577.3 252.9 %reduce-scatter.14.cloned.1.call-start = ((), (), s32[]{:S(2)}) async-start(), calls=%async_computation.13 | async-start | bytes 7864320 | tf_op jit(solution)/shard_map/reduce_scatter | solution.py:266
  608.4 44.8 %copy-start.34 = (f32[1024,1]{0,1:T(1,128)S(1)}, f32[1024,1]{0,1:T(1,128)}, u32[]{:S(2)}) copy-start(f32[1024,1]{0,1:T(1,128)} %copy-done.33) | copy-start | bytes 12292
  608.4 44.8 %copy-start.36 = (f32[384]{0:T(512)S(1)}, f32[384]{0:T(512)}, u32[]{:S(2)}) copy-start(f32[384]{0:T(512)} %copy-done.35) | copy-start | bytes 4612
  608.4 44.8 %copy-start.38 = (f32[384]{0:T(512)S(1)}, f32[384]{0:T(512)}, u32[]{:S(2)}) copy-start(f32[384]{0:T(512)} %copy-done.37) | copy-start | bytes 4612
  653.1 7.5 copy-start.28
  660.6 278.5 %reduce-scatter.18.cloned.1.call-start = ((), (), s32[]{:S(2)}) async-start(), calls=%async_computation.15 | async-start | bytes 13434880 | tf_op jit(solution)/shard_map/reduce_scatter | solution.py:272
  672.2 294.6 %reduce-scatter.26.cloned.1.call-start = ((), (), s32[]{:S(2)}) async-start(), calls=%async_computation.19 | async-start | bytes 327680
  673.3 6.2 copy-start.40
  682.3 421.6 %all-reduce.3.cloned.1.call-start = ((), (), s32[]{:S(2)}) async-start(), calls=%async_computation.20 | async-start | bytes 12255232 | tf_op jit(solution)/shard_map/psum | solution.py:283
  939.2 6.6 copy-start.2
  939.2 6.6 copy-start.10
  939.2 6.6 copy-start.18
  945.8 38.3 %copy-start.42 = (f32[256,2]{0,1:T(2,128)S(1)}, f32[256,2]{0,1:T(2,128)}, u32[]{:S(2)}) copy-start(f32[256,2]{0,1:T(2,128)} %param.29) | copy-start | bytes 6148
  945.8 38.3 %copy-start.44 = (f32[256,2]{0,1:T(2,128)S(1)}, f32[256,2]{0,1:T(2,128)}, u32[]{:S(2)}) copy-start(f32[256,2]{0,1:T(2,128)} %param.39) | copy-start | bytes 6148
  945.8 38.3 %copy-start.45 = (f32[256,2]{0,1:T(2,128)S(1)}, f32[256,2]{0,1:T(2,128)}, u32[]{:S(2)}) copy-start(f32[256,2]{0,1:T(2,128)} %param.34) | copy-start | bytes 6148
  1103.9 13.6 %copy-start.3 = (f32[256,3072]{1,0:T(8,128)S(1)}, f32[256,3072]{1,0:T(8,128)}, u32[]{:S(2)}) copy-start(f32[256,3072]{1,0:T(8,128)} %param.25) | copy-start | bytes 9437188
  1103.9 13.6 %copy-start.13 = (f32[256,3072]{1,0:T(8,128)S(1)}, f32[256,3072]{1,0:T(8,128)}, u32[]{:S(2)}) copy-start(f32[256,3072]{1,0:T(8,128)} %param.35) | copy-start | bytes 9437188
  1103.9 15.0 %copy-start.14 = (f32[256,3072]{1,0:T(8,128)S(1)}, f32[256,3072]{1,0:T(8,128)}, u32[]{:S(2)}) copy-start(f32[256,3072]{1,0:T(8,128)} %param.30) | copy-start | bytes 9437188
  1103.9 15.4 %copy-start.24 = (bf16[256,3072]{1,0:T(8,128)(2,1)S(1)}, bf16[256,3072]{1,0:T(8,128)(2,1)}, u32[]{:S(2)}) copy-start(bf16[256,3072]{1,0:T(8,128)(2,1)} %get-tuple-element.224) | copy-start | bytes 4718596
  1119.3 5.2 copy-start.5
  1119.3 5.2 copy-start.21
  1119.3 6.6 copy-start.22
  1125.9 6.4 copy-start.12
  1125.9 6.4 copy-start.25
  1125.9 6.4 copy-start.26
  1125.9 6.4 copy-start.30
  (12 other events, 13.7 us)
Sparse Core Ops, SparseCore 0:
  10.7 72.9 all-gather.6
  114.0 43.9 all-gather.10
  160.5 43.9 all-gather.8
  206.7 35.3 all-gather.12
  244.3 107.2 all-gather.14
  353.9 62.5 all-gather.16
  560.1 43.9 reduce-scatter.21
  607.7 43.9 reduce-scatter.23
  655.2 35.1 reduce-scatter.15
  694.1 62.5 reduce-scatter.19
  760.0 70.1 reduce-scatter.13
  833.4 105.6 reduce-scatter.17
  942.7 24.0 reduce-scatter.25
  969.3 134.5 all-reduce.2
where the time goes:
time: 1150 us; the launch traced here: 1140 us
  waiting for transfers between devices  728 us (63%)
  matrix products  210 us (18%)
  other arithmetic  89.3 us (8%)
  local copies, waits for them, and re-layouts  63.3 us (6%)
  blocking collectives  34.1 us (3%)
  between operations  14.7 us (1%)
    all_gather x4, waiting for transfers between devices, local(): lax.all_gather(shortened(lowered), 'grp', axis=0, tiled=True)  194 us
    psum x1, waiting for transfers between devices, local(): lax.psum(shares[0].astype(jnp.bfloat16), 'rep').astype(jnp.float32)  119 us
    reduce_scatter x1, waiting for transfers between devices, local(): lax.psum_scatter(grad_up.astype(jnp.bfloat16), 'grp', scatter_dimension=0...  109 us
    unnamed x17, waiting for transfers between devices  85.4 us
    reduce_scatter x1, waiting for transfers between devices, local(): lax.psum_scatter(grad_in.astype(jnp.bfloat16), 'grp', scatter_dimension=0...  73.5 us
    reduce_scatter x1, waiting for transfers between devices, local(): lax.psum_scatter(grad_down.astype(jnp.bfloat16), 'grp', scatter_dimension...  66.3 us
    all_gather x1, waiting for transfers between devices, local(): lax.all_gather(values, 'grp', axis=0, tiled=True)  41.8 us
    dot_general x16, matrix products, masked_scores(): jnp.einsum('qhd,khd->hqk', query_pair, key_pair, preferred_element_type=j...  40.7 us
  transfers between devices with their start and end apart: 14, of which 13 were waited for; matrix products, arithmetic and copies ran while one was open for 13% of the time, Pallas kernels for 0%

commit v1 on v0

--- a/solution.py
+++ b/solution.py
@@ -1,12 +1,13 @@
 import jax
 import jax.numpy as jnp
 from jax import lax
-from jax.sharding import PartitionSpec as P
+from jax.sharding import Mesh, PartitionSpec as P
 
 D = 1024
 HEADS = 16
 HEAD = 64
 FF = 2624
+FF_WIDE = 2688
 STEP = 10
 SEQ_SLOTS = 9
 
@@ -14,14 +15,6 @@
 rope_base = 160000.0
 norm_eps = 1e-05
 rate_list = (0.1, 0.4, 0.08, 0.05, 0.6)
-
-
-def shortened(array):
-
-    def short(part):
-        return part.astype(jnp.bfloat16) if part.dtype == jnp.float32 else part
-
-    return jax.tree.map(short, array)
 
 
 def layer_norm(values, gain):
@@ -146,6 +139,34 @@
     return (join_pairs(grad_query), join_pairs(grad_keys), join_pairs(grad_values), centre)
 
 
+def own_half(array, core):
+    half = array.shape[0] // 2
+    return lax.dynamic_slice_in_dim(array, core * half, half)
+
+
+def gather_weight(weight, core):
+    return lax.all_gather(
+        own_half(weight, core).astype(jnp.bfloat16), ("grp", "core"), axis=0, tiled=True
+    )
+
+
+def reduce_weight(grad):
+    share = lax.psum_scatter(
+        grad.astype(jnp.bfloat16), ("grp", "core"), scatter_dimension=0, tiled=True
+    )
+    share = lax.psum(share, "far")
+    return lax.all_gather(share, "core", axis=0, tiled=True).astype(jnp.float32)
+
+
+def spread_halves(array):
+    spare = ((0, 0), (0, FF_WIDE - FF))
+    return jnp.concatenate([jnp.pad(array[:, :FF], spare), jnp.pad(array[:, FF:], spare)], axis=1)
+
+
+def joined_halves(array):
+    return jnp.concatenate([array[:, :FF], array[:, FF_WIDE : FF_WIDE + FF]], axis=1)
+
+
 def gated(gate, upward):
     return jax.nn.gelu(gate, approximate=False) * upward
 
@@ -179,13 +200,14 @@
 ):
     own_rows = tokens.shape[1]
     own_index = lax.axis_index("grp")
+    core = lax.axis_index("core")
     masters = (inproj, outproj, upproj, downproj, norm_gains)
-    lowered = tuple((item.astype(jnp.bfloat16) for item in masters))
-    w_in, w_out, w_up, w_down, gains_low = jax.tree.map(
-        lambda part, own: part.astype(own.dtype),
-        lax.all_gather(shortened(lowered), "grp", axis=0, tiled=True),
-        lowered,
-    )
+    w_in = gather_weight(inproj, core)
+    gains_low = lax.all_gather(norm_gains.astype(jnp.bfloat16), "grp", axis=0, tiled=True)
+    w_out = gather_weight(outproj, core)
+    w_up = gather_weight(spread_halves(upproj), core)
+    w_down = gather_weight(downproj, core)
+    w_down = jnp.pad(w_down, ((0, FF_WIDE - FF), (0, 0)))
     gains = gains_low.astype(jnp.float32)
     all_ids = lax.all_gather(slot_ids, "grp", axis=1, tiled=True)[0]
     group_rows = all_ids.shape[0]
@@ -214,34 +236,24 @@
     middle = inputs + product(attended, w_out)
     second_normed = layer_norm(middle, gains[:, 1]).astype(jnp.bfloat16)
     gate_up = product(second_normed, w_up)
-    gate = gate_up[:, :FF]
-    upward = gate_up[:, FF:]
+    gate = gate_up[:, :FF_WIDE]
+    upward = gate_up[:, FF_WIDE:]
     hidden = gated(gate, upward).astype(jnp.bfloat16)
     result = middle + product(hidden, w_down)
-    w_in, w_out, w_up, w_down, gains_low = jax.tree.map(
-        lambda part, own: part.astype(own.dtype),
-        lax.all_gather(shortened(lowered), "grp", axis=0, tiled=True),
-        lowered,
-    )
-    gains = gains_low.astype(jnp.float32)
     grad_top = cotangent[0] * live[:, None]
-    grad_down = contract(hidden, grad_top)
+    grad_down = contract(hidden, grad_top)[:FF]
     grad_hidden = against(grad_top, w_down)
     _, gate_back = jax.vjp(gated, gate, upward)
     grad_gate, grad_upward = gate_back(grad_hidden)
     grad_gate_up = jnp.concatenate([grad_gate, grad_upward], axis=1).astype(jnp.bfloat16)
     grad_up = contract(second_normed, grad_gate_up)
     grad_second = against(grad_gate_up, w_up)
-    _, second_back = jax.vjp(layer_norm, middle, gains[:, 1])
-    grad_from_norm, grad_gain_two = second_back(grad_second)
+    _, second_back = jax.vjp(lambda v: layer_norm(v, gains[:, 1]), middle)
+    (grad_from_norm,) = second_back(grad_second)
     grad_middle = grad_top.astype(jnp.float32) + grad_from_norm
     grad_branch = grad_middle.astype(jnp.bfloat16)
     grad_outproj = contract(attended, grad_branch)
     grad_attended = against(grad_branch, w_out).astype(jnp.bfloat16)
-    keys_all, values_all = (
-        lax.all_gather(keys, "grp", axis=0, tiled=True),
-        lax.all_gather(values, "grp", axis=0, tiled=True),
-    )
     grad_query, key_terms, value_terms, centre = attention_backward(
         query, keys_all, values_all, grad_attended, log_totals, allowed
     )
@@ -258,34 +270,21 @@
     ).astype(jnp.bfloat16)
     grad_in = contract(first_normed, grad_projected)
     grad_first = against(grad_projected, w_in)
-    _, first_back = jax.vjp(layer_norm, inputs, gains[:, 0])
-    grad_inputs, grad_gain_one = first_back(grad_first)
+    _, first_back = jax.vjp(lambda v: layer_norm(v, gains[:, 0]), inputs)
+    (grad_inputs,) = first_back(grad_first)
     input_grad = (grad_middle + grad_inputs).astype(jnp.bfloat16)
-    grad_gains = jnp.stack([grad_gain_one, grad_gain_two], axis=1)
-    shares = (
-        lax.psum_scatter(
-            grad_in.astype(jnp.bfloat16), "grp", scatter_dimension=0, tiled=True
-        ).astype(jnp.float32),
-        lax.psum_scatter(
-            grad_outproj.astype(jnp.bfloat16), "grp", scatter_dimension=0, tiled=True
-        ).astype(jnp.float32),
-        lax.psum_scatter(
-            grad_up.astype(jnp.bfloat16), "grp", scatter_dimension=0, tiled=True
-        ).astype(jnp.float32),
-        lax.psum_scatter(
-            grad_down.astype(jnp.bfloat16), "grp", scatter_dimension=0, tiled=True
-        ).astype(jnp.float32),
-        lax.psum_scatter(
-            grad_gains.astype(jnp.bfloat16), "grp", scatter_dimension=0, tiled=True
-        ).astype(jnp.float32),
-    )
-    totals = (
-        lax.psum(shares[0].astype(jnp.bfloat16), "rep").astype(jnp.float32),
-        lax.psum(shares[1].astype(jnp.bfloat16), "rep").astype(jnp.float32),
-        lax.psum(shares[2].astype(jnp.bfloat16), "rep").astype(jnp.float32),
-        lax.psum(shares[3].astype(jnp.bfloat16), "rep").astype(jnp.float32),
-        lax.psum(shares[4].astype(jnp.bfloat16), "rep").astype(jnp.float32),
-    )
+    total_in = reduce_weight(grad_in)
+    total_out = reduce_weight(grad_outproj)
+    total_up = joined_halves(reduce_weight(grad_up))
+    total_down = reduce_weight(grad_down)
+    low_in = inproj.astype(jnp.bfloat16).astype(jnp.float32)
+    low_up = upproj.astype(jnp.bfloat16).astype(jnp.float32)
+    low_gains = norm_gains.astype(jnp.bfloat16).astype(jnp.float32)
+    total_gains = (
+        jnp.stack([jnp.sum(low_in * total_in, axis=1), jnp.sum(low_up * total_up, axis=1)], axis=1)
+        / low_gains
+    )
+    totals = (total_in, total_out, total_up, total_down, total_gains)
     means = (inproj_mean, outproj_mean, upproj_mean, downproj_mean, gains_mean)
     squares = (inproj_square, outproj_square, upproj_square, downproj_square, gains_square)
     updates = [
@@ -314,10 +313,12 @@
 
 
 def solution(mesh):
+    group_size, replicas = mesh.devices.shape
+    fine = Mesh(mesh.devices.reshape(group_size, replicas // 2, 2), ("grp", "far", "core"))
     placed = (
-        P("rep", "grp", None),
-        P("rep", "grp"),
-        P("rep", "grp", None),
+        P(("far", "core"), "grp", None),
+        P(("far", "core"), "grp"),
+        P(("far", "core"), "grp", None),
         P("grp", None),
         P("grp", None),
         P("grp", None),
@@ -336,11 +337,11 @@
     )
     return jax.shard_map(
         local,
-        mesh=mesh,
+        mesh=fine,
         in_specs=placed,
         out_specs=(
-            P("rep", "grp", None),
-            P("rep", "grp", None),
+            P(("far", "core"), "grp", None),
+            P(("far", "core"), "grp", None),
             P("grp", None),
             P("grp", None),
             P("grp", None),

time: 1150 us -> 992 us (0.86)
  waiting for transfers between devices: 728 us -> 577 us
  blocking collectives: 34.1 us -> 19.7 us
    all_gather x4 -> x7, waiting for transfers between devices: 194 us -> 113 us  [the longest x4 113 us: gather_weight(): lax.all_gather(own_half(weight, core).astype(jnp.bfloat16), ('grp', 'core...]
    all_gather x1, waiting for transfers between devices: 41.8 us -> 0.02 us  [local(): lax.all_gather(values, 'grp', axis=0, tiled=True)]
    unnamed x17 -> x18, waiting for transfers between devices: 85.4 us -> 66.1 us
    reduce_scatter x4, waiting for transfers between devices: 257 us -> 239 us  [reduce_weight(): lax.psum_scatter(grad.astype(jnp.bfloat16), ('grp', 'core'), scatter_dime...]
    psum x1 -> x0, blocking collectives: 16.4 us -> none  [local(): lax.psum(shares[4].astype(jnp.bfloat16), 'rep').astype(jnp.float32)]
    unnamed x98 -> x84, local copies, waits for them, and re-layouts: 30.1 us -> 22.9 us
  transfers between devices with their start and end apart: 14 -> 16, of which waited for: 13 -> 11; matrix products, arithmetic and copies ran while one was open for 13% -> 19% of each run, Pallas kernels for 0% -> 0%
where the time goes in v1:
time: 992 us; the launch traced here: 983 us
  waiting for transfers between devices  577 us (58%)
  matrix products  206 us (21%)
  other arithmetic  93.3 us (9%)
  local copies, waits for them, and re-layouts  69.2 us (7%)
  blocking collectives  19.7 us (2%)
  between operations  14.8 us (1%)
    reduce_scatter x4, waiting for transfers between devices, reduce_weight(): lax.psum_scatter(grad.astype(jnp.bfloat16), ('grp', 'core'), scatter_dime...  239 us
    psum x1, waiting for transfers between devices, reduce_weight(): share = lax.psum(share, 'far')  123 us
    all_gather x4, waiting for transfers between devices, gather_weight(): lax.all_gather(own_half(weight, core).astype(jnp.bfloat16), ('grp', 'core...  113 us
    unnamed x18, waiting for transfers between devices  66.1 us
    dot_general x16, matrix products, masked_scores(): jnp.einsum('qhd,khd->hqk', query_pair, key_pair, preferred_element_type=j...  40.7 us
    all_gather x1, waiting for transfers between devices, local(): lax.all_gather(keys, 'grp', axis=0, tiled=True)  35.6 us
    sub x5, other arithmetic, adam_update(): return (mean_new, square_new, weight - rate * (step_size + 0.01 * weight))  35.4 us
    dot_general x4, matrix products, against(): lax.dot_general(left, right, (((1,), (1,)), ((), ())), preferred_element_...  34.6 us
  transfers between devices with their start and end apart: 16, of which 11 were waited for; matrix products, arithmetic and copies ran while one was open for 19% of the time, Pallas kernels for 0%

profile of v1, /device:TPU:0, one launch (start us, length us, event | category | flops | bytes accessed | tf_op | source)
XLA Modules:
  0.0 982.8 jit_solution(5260248940824932551)
XLA Ops:
  10.5 9.5 all_gather.36
  22.4 36.4 %all-gather.10.cloned.1.call-done = bf16[1024,3072]{1,0:T(8,128)(2,1)} async-done(((bf16[128,3072]{1,0:T(8,128)(2,1)}), bf16[1024,3072]{1,0:T(8,128)(2,1)}) %all-gather.10.cloned.1.call-update) | async-done | bytes 6291472 | tf_op jit(solution)/shard_map/all_gather | solution.py:148
  58.8 4.9 fusion.111
  67.0 8.0 all_gather.39
  80.8 4.0 fusion.127
  84.7 3.0 copy.67
  87.8 3.0 copy.63
  95.4 3.0 copy.68
  98.5 3.0 copy.64
  101.5 4.9 add_convert_fusion.3
  117.1 4.7 copy.61
  121.8 35.6 %all-gather.14.cloned.1.call-done = bf16[1536,1024]{1,0:T(8,128)(2,1)} async-done(((bf16[384,1024]{1,0:T(8,128)(2,1)}), bf16[1536,1024]{1,0:T(8,128)(2,1)}) %all-gather.14.cloned.1.call-update) | async-done | bytes 3145744 | tf_op jit(solution)/shard_map/all_gather | solution.py:231
  157.5 4.6 copy.69
  162.1 46.2 %while.30 = (s32[]{:T(128)}, bf16[8,384,2,64]{1,3,2,0:T(8,128)(2,1)S(1)}, f32[8,2,384]{2,1,0:T(2,128)S(1)}, bf16[8,1536,2,64]{1,3,2,0:T(8,128)(2,1)}, bf16[8,384...) while((s32[]{:T(128)}, ...), condition=%wide.region_10.11_spmd.clone.clone, body=%wide.region_7.10_spmd.clone.sunk.clone | while | flops 312605952 | bytes 16453105 | solution.py:97
  209.2 2.9 fusion.130
  212.4 43.2 %all-gather.18.cloned.1.call-done = bf16[1024,5376]{1,0:T(8,128)(2,1)} async-done(((bf16[128,5376]{1,0:T(8,128)(2,1)}), bf16[1024,5376]{1,0:T(8,128)(2,1)}) %all-gather.18.cloned.1.call-update) | async-done | bytes 11010064 | tf_op jit(solution)/shard_map/all_gather | solution.py:148
  255.6 10.9 %fusion.114 = f32[384,5376]{1,0:T(8,128)} fusion(bf16[1024,5376]{1,0:T(8,128)(2,1)} %all-gather.18.cloned.1.call-done, f32[384,1024]{1,0:T(8,128)S(1)} %get-tuple-element.280, f32[1024]{0:T(1024)S(1)} %bitcast.252, f32[384]{0:T(512)S(1)} %fusion.103, f32[384]{0:T(512)S(1)} %broadcast_multiply_fusion.1), kind=kOutput, calls=%fused_computation.214 | convolution fusion | flops 4229431296 | bytes 20847616 | tf_op jit(solution)/shard_map/dot_general | solution.py:55
  266.5 33.1 %all-gather.20.cloned.1.call-done = bf16[2624,1024]{1,0:T(8,128)(2,1)} async-done(((bf16[328,1024]{1,0:T(8,128)(2,1)}), bf16[2624,1024]{1,0:T(8,128)(2,1)}) %all-gather.20.cloned.1.call-update) | async-done | bytes 5373968 | tf_op jit(solution)/shard_map/all_gather | solution.py:148
  299.6 15.7 %add_convert_fusion = (bf16[384,2688]{1,0:T(8,128)(2,1)}, f32[384,2688]{1,0:T(8,128)S(1)}, f32[384,2688]{1,0:T(8,128)}) fusion(f32[384,5376]{1,0:T(8,128)} %fusion.114, bf16[2624,1024]{1,0:T(8,128)(2,1)} %all-gather.20.cloned.1.call-done, bf16[1,384,1024]{2,1,0:T(8,128)(2,1)} %param.24, bf16[384]{0:T(512)(128)(2,1)S(1)} %get-tuple-element.245), kind=kOutput, calls=%fused_computation.79 | convolution fusion | flops 2189672448 | bytes 24740608 | tf_op jit(solution)/shard_map/dot_general | solution.py:65
  315.4 7.1 multiply_convert_fusion.1
  322.5 11.1 %multiply_reduce_fusion.2 = (f32[384]{0:T(512)S(1)}, f32[384,1024]{1,0:T(8,128)}) fusion(f32[384,1024]{1,0:T(8,128)S(1)} %get-tuple-element.280, f32[384]{0:T(512)S(1)} %broadcast_multiply_fusion.1, f32[1024]{0:T(1024)S(1)} %bitcast.253, bf16[1024,5376]{1,0:T(8,128)(2,1)} %all-gather.18.cloned.1.call-done, bf16[384,2688]{1,0:T(8,128)(2,1)S(1)} %get-tuple-element.251, ...), kind=kOutput, calls=%fused_computation.141 | convolution fusion | flops 4237688320 | bytes 18291712 | tf_op jit(solution)/shard_map/dot_general | solution.py:65
  342.2 95.6 %while.31 = (s32[]{:T(128)}, f32[8,384,2,64]{1,3,2,0:T(8,128)}, bf16[8,1536,2,64]{1,3,2,0:T(8,128)(2,1)}, bf16[8,1536,2,64]{1,3,2,0:T(8,128)(2,1)}, bf16[8,1536,...) while((s32[]{:T(128)}, f32[8,384,2,64]{1,3,2,0:T(8,128)}, ...), condition=%wide.region_17.18_spmd.clone.clone, body=%wide.region_15.17_spmd.clone.sunk.clone | while | flops 768195840 | bytes 39941640 | solution.py:129
  344.8 2.9 multiply_reduce_fusion.6
  368.7 2.9 multiply_reduce_fusion.6
  380.7 2.9 multiply_reduce_fusion.6
  404.6 2.9 multiply_reduce_fusion.6
  416.6 2.9 multiply_reduce_fusion.6
  428.5 2.9 multiply_reduce_fusion.6
  437.9 4.6 copy.71
  442.6 4.6 copy.73
  448.3 3.9 convolution_convert_fusion.2
  452.3 4.9 fusion.89
  457.2 3.0 slice.140
  463.0 23.6 %reduce-scatter.19.cloned.1.call-done = bf16[384,1024]{1,0:T(8,128)(2,1)} async-done(((bf16[1536,1024]{1,0:T(8,128)(2,1)}), bf16[384,1024]{1,0:T(8,128)(2,1)}) %reduce-scatter.19.cloned.1.call-update) | async-done | bytes 786448
  492.4 41.8 %reduce-scatter.21.cloned.1.call-done = bf16[384,1024]{1,0:T(8,128)(2,1)} async-done(((bf16[1536,1024]{1,0:T(8,128)(2,1)}), bf16[384,1024]{1,0:T(8,128)(2,1)}) %reduce-scatter.21.cloned.1.call-update) | async-done | bytes 786448
  535.7 7.4 convolution_convert_fusion.1
  543.1 11.2 %convolution_convert_fusion = bf16[1024,5376]{1,0:T(8,128)(2,1)} fusion(bf16[384,2688]{1,0:T(8,128)(2,1)} %copy-done.4, bf16[384,2688]{1,0:T(8,128)(2,1)} %get-tuple-element.243, f32[384,1024]{1,0:T(8,128)S(1)} %get-tuple-element.280, f32[1024]{0:T(1024)S(1)} %bitcast.254, f32[384]{0:T(512)S(1)} %fusion.103, f32[384]{0:T(512)S(1)} %broadcast_multiply_fusion.1), kind=kOutput, calls=%fused_computation.56 | convolution fusion | flops 4243193856 | bytes 16718848 | tf_op jit(solution)/shard_map/dot_general | solution.py:59
  554.4 24.9 %reduce-scatter.13.cloned.1.call-done = bf16[128,1024]{1,0:T(8,128)(2,1)} async-done(((bf16[1024,1024]{1,0:T(8,128)(2,1)}), bf16[128,1024]{1,0:T(8,128)(2,1)}) %reduce-scatter.13.cloned.1.call-update) | async-done | bytes 262160 | tf_op jit(solution)/shard_map/reduce_scatter | solution.py:154
  579.3 61.5 %reduce-scatter.17.cloned.1.call-done = bf16[328,1024]{1,0:T(8,128)(2,1)} async-done(((bf16[2624,1024]{1,0:T(8,128)(2,1)}), bf16[328,1024]{1,0:T(8,128)(2,1)}) %reduce-scatter.17.cloned.1.call-update) | async-done | bytes 671760 | tf_op jit(solution)/shard_map/reduce_scatter | solution.py:154
  640.7 65.6 %reduce-scatter.11.cloned.1.call-done = bf16[128,3072]{1,0:T(8,128)(2,1)} async-done(((bf16[1024,3072]{1,0:T(8,128)(2,1)}), bf16[128,3072]{1,0:T(8,128)(2,1)}) %reduce-scatter.11.cloned.1.call-update) | async-done | bytes 786448 | tf_op jit(solution)/shard_map/reduce_scatter | solution.py:154
  706.3 87.5 %reduce-scatter.15.cloned.1.call-done = bf16[128,5376]{1,0:T(8,128)(2,1)} async-done(((bf16[1024,5376]{1,0:T(8,128)(2,1)}), bf16[128,5376]{1,0:T(8,128)(2,1)}) %reduce-scatter.15.cloned.1.call-update) | async-done | bytes 1376272 | tf_op jit(solution)/shard_map/reduce_scatter | solution.py:154
  793.9 123.3 %all-reduce.5.cloned.1.call-done = (bf16[128,3072]{1,0:T(8,128)(2,1)}, bf16[128,1024]{1,0:T(8,128)(2,1)}, bf16[128,5376]{1,0:T(8,128)(2,1)}, bf16[328,1024]{1,0:T(8,128)(2,1)}) async-done(((bf16[128,3072]{1,0:T(8,128)(2,1)}, bf16[128,1024]{1,0:T(8,128)(2,1)}, bf16[128,5376]{1,0:T(8,128)(2,1)}, bf16[328,1024]{1,0:T(8,128)(2,1)}), (bf16[128,3072]{1,0:T(8,128)(2,1)}, bf16[128,1024]{1,0:T(8,128)(2,1)}, ...) | async-done | bytes 3096592 | tf_op jit(solution)/shard_map/psum | solution.py:157
  918.0 6.5 fusion.82
  924.6 5.9 fusion.74
  932.7 3.1 fusion.88
  940.7 7.9 multiply_subtract_fusion.2
  948.6 9.5 multiply_subtract_fusion.1
  960.3 15.2 %multiply_subtract_fusion = (f32[256,5248]{1,0:T(8,128)}, f32[256,5248]{1,0:T(8,128)}, f32[256,5248]{1,0:T(8,128)}, f32[256]{0:T(256)S(1)}) fusion(f32[256,5248]{1,0:T(8,128)} %param.27, f32[256,2624]{1,0:T(8,128)S(1)} %get-tuple-element.260, f32[256,2624]{1,0:T(8,128)S(1)} %get-tuple-element.259, f32[256,5248]{1,0:T(8,128)} %param.37, f32[256,5248]{1,0:T(8,128)} %param.32), kind=kLoop, calls=%fused_computation.70 | loop fusion | flops 26869504 | bytes 37618688 | tf_op jit(solution)/shard_map/sub | solution.py:178
  (280 shorter events, 185.7 us)
Async XLA Ops:
  7.2 14.2 %copy-start = (bf16[1,384,1024]{2,1,0:T(8,128)(2,1)S(1)}, bf16[1,384,1024]{2,1,0:T(8,128)(2,1)}, u32[]{:S(2)}) copy-start(bf16[1,384,1024]{2,1,0:T(8,128)(2,1)} %param.22) | copy-start | bytes 2359300
  7.2 51.5 %all-gather.10.cloned.1.call-start = ((), (), s32[]{:S(2)}) async-start(), calls=%async_computation.6 | async-start | bytes 7077888 | tf_op jit(solution)/shard_map/all_gather | solution.py:148
  9.7 107.4 %all-gather.12.cloned.1.call-start = ((), (), s32[]{:S(2)}) async-start(), calls=%async_computation.7 | async-start | bytes 3932160 | tf_op jit(solution)/shard_map/all_gather | solution.py:232
  21.4 42.3 %copy-start.27 = (f32[384]{0:T(512)}, f32[384]{0:T(512)S(1)}, u32[]{:S(2)}) copy-start(f32[384]{0:T(512)S(1)} %broadcast_multiply_fusion.2) | copy-start | bytes 4612
  22.3 41.3 %copy-start.29 = (f32[384]{0:T(512)}, f32[384]{0:T(512)S(1)}, u32[]{:S(2)}) copy-start(f32[384]{0:T(512)S(1)} %fusion.102) | copy-start | bytes 4612
  22.4 41.3 %copy-start.35 = (f32[1024,1]{0,1:T(1,128)}, f32[1024,1]{0,1:T(1,128)S(1)}, u32[]{:S(2)}) copy-start(f32[1024,1]{0,1:T(1,128)S(1)} %get-tuple-element.278) | copy-start | bytes 12292
  58.7 8.2 copy-start.34
  63.7 2.2 copy-start.3
  66.9 90.6 %all-gather.14.cloned.1.call-start = ((), (), s32[]{:S(2)}) async-start(), calls=%async_computation.8 | async-start | bytes 3932160 | tf_op jit(solution)/shard_map/all_gather | solution.py:231
  106.3 4.1 copy-start.37
  106.4 101.9 %all-gather.16.cloned.1.call-start = ((), (), s32[]{:S(2)}) async-start(), calls=%async_computation.9 | async-start | bytes 2359296 | tf_op jit(solution)/shard_map/all_gather | solution.py:148
  108.2 147.4 %all-gather.18.cloned.1.call-start = ((), (), s32[]{:S(2)}) async-start(), calls=%async_computation.10 | async-start | bytes 12386304 | tf_op jit(solution)/shard_map/all_gather | solution.py:148
  112.5 4.3 copy-start.8
  113.7 186.0 %all-gather.20.cloned.1.call-start = ((), (), s32[]{:S(2)}) async-start(), calls=%async_computation.11 | async-start | bytes 6045696 | tf_op jit(solution)/shard_map/all_gather | solution.py:148
  116.0 370.6 %reduce-scatter.19.cloned.1.call-start = ((), (), s32[]{:S(2)}) async-start(), calls=%async_computation.19 | async-start | bytes 3932160
  322.5 11.1 %copy-start.4 = (bf16[384,2688]{1,0:T(8,128)(2,1)}, bf16[384,2688]{1,0:T(8,128)(2,1)S(1)}, u32[]{:S(2)}) copy-start(bf16[384,2688]{1,0:T(8,128)(2,1)S(1)} %get-tuple-element.251) | copy-start | bytes 6193156
  333.6 3.3 copy-start.13
  333.6 4.4 copy-start.15
  442.5 91.6 %reduce-scatter.21.cloned.1.call-start = ((), (), s32[]{:S(2)}) async-start(), calls=%async_computation.20 | async-start | bytes 3932160
  447.2 132.0 %reduce-scatter.13.cloned.1.call-start = ((), (), s32[]{:S(2)}) async-start(), calls=%async_computation.14 | async-start | bytes 2359296 | tf_op jit(solution)/shard_map/reduce_scatter | solution.py:154
  452.3 188.5 %reduce-scatter.17.cloned.1.call-start = ((), (), s32[]{:S(2)}) async-start(), calls=%async_computation.17 | async-start | bytes 6045696 | tf_op jit(solution)/shard_map/reduce_scatter | solution.py:154
  460.2 246.1 %reduce-scatter.11.cloned.1.call-start = ((), (), s32[]{:S(2)}) async-start(), calls=%async_computation.12 | async-start | bytes 7077888 | tf_op jit(solution)/shard_map/reduce_scatter | solution.py:154
  488.1 1.4 copy-start.12
  489.5 1.4 copy-start.5
  489.5 1.4 copy-start.24
  490.9 44.8 %copy-start.28 = (f32[384]{0:T(512)S(1)}, f32[384]{0:T(512)}, u32[]{:S(2)}) copy-start(f32[384]{0:T(512)} %copy-done.27) | copy-start | bytes 4612
  490.9 44.8 %copy-start.30 = (f32[384]{0:T(512)S(1)}, f32[384]{0:T(512)}, u32[]{:S(2)}) copy-start(f32[384]{0:T(512)} %copy-done.29) | copy-start | bytes 4612
  490.9 44.8 %copy-start.36 = (f32[1024,1]{0,1:T(1,128)S(1)}, f32[1024,1]{0,1:T(1,128)}, u32[]{:S(2)}) copy-start(f32[1024,1]{0,1:T(1,128)} %copy-done.35) | copy-start | bytes 12292
  535.6 7.4 copy-start.21
  543.0 250.7 %reduce-scatter.15.cloned.1.call-start = ((), (), s32[]{:S(2)}) async-start(), calls=%async_computation.15 | async-start | bytes 12386304 | tf_op jit(solution)/shard_map/reduce_scatter | solution.py:154
  554.3 362.9 %all-reduce.5.cloned.1.call-start = ((), (), s32[]{:S(2)}) async-start(), calls=%async_computation.21 | async-start | bytes 6193152 | tf_op jit(solution)/shard_map/psum | solution.py:157
  793.8 146.5 %all-gather.26.cloned.1.call-start = ((), (), s32[]{:S(2)}) async-start(), calls=%async_computation.18 | async-start | bytes 2015232 | tf_op jit(solution)/shard_map/all_gather | solution.py:158
  917.2 31.4 %all-gather.22.cloned.1.call-start = ((), (), s32[]{:S(2)}) async-start(), calls=%async_computation.13 | async-start | bytes 2359296 | tf_op jit(solution)/shard_map/all_gather | solution.py:158
  917.8 6.8 copy-start.19
  917.8 40.3 %all-gather.24.cloned.1.call-start = ((), (), s32[]{:S(2)}) async-start(), calls=%async_computation.16 | async-start | bytes 4128768 | tf_op jit(solution)/shard_map/all_gather | solution.py:158
  918.0 6.6 copy-start.20
  918.0 6.6 copy-start.22
  924.6 5.9 copy-start.32
  930.5 2.0 copy-start.2
  930.5 2.2 copy-start.14
  932.1 3.7 copy-start.26
  932.7 5.3 copy-start.16
  932.7 5.3 copy-start.17
  932.7 5.3 copy-start.18
  938.0 2.7 copy-start.7
  960.2 15.2 %copy-start.33 = (f32[256,2]{0,1:T(2,128)S(1)}, f32[256,2]{0,1:T(2,128)}, u32[]{:S(2)}) copy-start(f32[256,2]{0,1:T(2,128)} %param.29) | copy-start | bytes 6148
  960.2 15.2 %copy-start.38 = (f32[256,2]{0,1:T(2,128)S(1)}, f32[256,2]{0,1:T(2,128)}, u32[]{:S(2)}) copy-start(f32[256,2]{0,1:T(2,128)} %param.39) | copy-start | bytes 6148
  960.2 15.2 %copy-start.39 = (f32[256,2]{0,1:T(2,128)S(1)}, f32[256,2]{0,1:T(2,128)}, u32[]{:S(2)}) copy-start(f32[256,2]{0,1:T(2,128)} %param.34) | copy-start | bytes 6148
  (8 other events, 8.3 us)
Sparse Core Ops, SparseCore 0:
  10.5 48.2 all-gather.9
  67.0 43.9 all-gather.11
  113.5 43.9 all-gather.13
  159.8 27.8 all-gather.15
  190.0 65.5 all-gather.17
  257.9 41.6 all-gather.19
  442.6 43.9 reduce-scatter.18
  490.2 43.9 reduce-scatter.20
  538.0 41.2 reduce-scatter.12
  583.5 57.1 reduce-scatter.16
  644.5 61.7 reduce-scatter.10
  709.7 83.9 reduce-scatter.14
  796.4 120.6 all-reduce.4
  918.6 8.3 all-gather.25
  928.5 10.9 all-gather.21
  941.0 12.7 all-gather.23

commit v2 on v1

v2 whole, which is shorter than its diff:
```python
import functools

import jax
import jax.numpy as jnp
from jax import lax
from jax.experimental import pallas as pl
from jax.experimental.pallas import tpu as pltpu
from jax.sharding import Mesh, PartitionSpec as P

D = 1024
HEADS = 16
HEAD = 64
FF = 2624
FF_WIDE = 2688
STEP = 10
SEQ_SLOTS = 9
PAIR = 128
STAT_LANE = 16
VMEM_BYTES = 56 * 1024 * 1024


rope_base = 160000.0
norm_eps = 1e-05
rate_list = (0.1, 0.4, 0.08, 0.05, 0.6)


def layer_norm(values, gain):
    centred = values - jnp.mean(values, axis=-1, keepdims=True)
    spread = jnp.mean(centred * centred, axis=-1, keepdims=True)
    return centred * lax.rsqrt(spread + norm_eps) * gain


def positions(ids):
    live = ids >= 0
    counted = jnp.cumsum(live.astype(jnp.int32)) - 1
    onehot = (
        (ids[:, None] == jnp.arange(SEQ_SLOTS, dtype=jnp.int32)[None, :]) & live[:, None]
    ).astype(jnp.int32)
    counts = jnp.sum(onehot, axis=0)
    starts = jnp.cumsum(counts) - counts
    first = jnp.sum(onehot * starts[None, :], axis=1)
    return jnp.where(live, counted - first, 0)


def pair_tables(where_at):
    lane = jnp.arange(PAIR, dtype=jnp.int32)
    order = (lane % (HEAD // 2)).astype(jnp.float32)
    inverse = rope_base ** (-(order * 2.0 / HEAD))
    angles = where_at.astype(jnp.float32)[:, None] * inverse[None, :]
    signs = jnp.where(lane % HEAD < HEAD // 2, -1.0, 1.0)
    return jnp.cos(angles), jnp.sin(angles) * signs[None, :]


def slot_features(ids):
    lane = jnp.arange(PAIR, dtype=jnp.int32)[None, :]
    column = jnp.where(ids < 0, SEQ_SLOTS, ids)[:, None]
    own = lane == column
    query_side = jnp.where((lane <= SEQ_SLOTS) & (~own | (ids < 0)[:, None]), -1e30, 0.0)
    key_side = jnp.where(own | ((lane >= STAT_LANE) & (lane < STAT_LANE + 3)), 1.0, 0.0)
    return query_side.astype(jnp.bfloat16), key_side.astype(jnp.bfloat16)


def turned(values, cos, sin):
    lane = lax.broadcasted_iota(jnp.int32, values.shape, 1)
    half = HEAD // 2
    other = jnp.where(
        lane % HEAD < half, pltpu.roll(values, PAIR - half, 1), pltpu.roll(values, half, 1)
    )
    return values * cos + other * sin


def compiler_params():
    return pltpu.CompilerParams(vmem_limit_bytes=VMEM_BYTES)


def project_kernel(me_ref, x_ref, wq_ref, wk_ref, wv_ref, cos_ref, sin_ref, out_ref):
    weights = jnp.concatenate([wq_ref[...], wk_ref[...], wv_ref[...]], axis=1)
    got = jnp.dot(x_ref[...], weights, preferred_element_type=jnp.float32)
    cos, sin = cos_ref[0], sin_ref[0]
    query = turned(got[:, :PAIR], cos, sin) * HEAD ** (-0.5)
    keys = turned(got[:, PAIR : 2 * PAIR], cos, sin)
    out_ref[0, :, :PAIR] = query.astype(jnp.bfloat16)
    out_ref[0, :, PAIR : 2 * PAIR] = keys.astype(jnp.bfloat16)
    out_ref[0, :, 2 * PAIR :] = got[:, 2 * PAIR :].astype(jnp.bfloat16)


def project(me, first_normed, w_in, cos, sin, pair, group):
    rows = first_normed.shape[0]
    pairs = D // PAIR // group

    def column(part):
        return lambda d, me: (0, part * (D // PAIR) + (me[0] ^ d) * pairs + pair)

    return pl.pallas_call(
        project_kernel,
        grid_spec=pltpu.PrefetchScalarGridSpec(
            num_scalar_prefetch=1,
            grid=(group,),
            in_specs=[
                pl.BlockSpec((rows, D), lambda d, me: (0, 0)),
                pl.BlockSpec((D, PAIR), column(0)),
                pl.BlockSpec((D, PAIR), column(1)),
                pl.BlockSpec((D, PAIR), column(2)),
                pl.BlockSpec((1, rows, PAIR), lambda d, me: (0, 0, 0)),
                pl.BlockSpec((1, rows, PAIR), lambda d, me: (0, 0, 0)),
            ],
            out_specs=pl.BlockSpec((1, rows, 3 * PAIR), lambda d, me: (d, 0, 0)),
        ),
        out_shape=jax.ShapeDtypeStruct((group, rows, 3 * PAIR), jnp.bfloat16),
        compiler_params=compiler_params(),
        name="project",
    )(me, first_normed, w_in, w_in, w_in, cos, sin)


def row_product_kernel(me_ref, x_ref, w_ref, out_ref):
    out_ref[0] = against(x_ref[...], w_ref[...]).astype(jnp.bfloat16)


def row_product(me, left, weight, pair, group):
    rows = left.shape[0]
    pairs = D // PAIR // group
    return pl.pallas_call(
        row_product_kernel,
        grid_spec=pltpu.PrefetchScalarGridSpec(
            num_scalar_prefetch=1,
            grid=(group,),
            in_specs=[
                pl.BlockSpec((rows, D), lambda d, me: (0, 0)),
                pl.BlockSpec((PAIR, D), lambda d, me: ((me[0] ^ d) * pairs + pair, 0)),
            ],
            out_specs=pl.BlockSpec((1, rows, PAIR), lambda d, me: (d, 0, 0)),
        ),
        out_shape=jax.ShapeDtypeStruct((group, rows, PAIR), jnp.bfloat16),
        compiler_params=compiler_params(),
        name="row_product",
    )(me, left, weight)


def place_kernel(me_ref, *refs):
    out_ref = refs[-1]
    for index, ref in enumerate(refs[:-1]):
        out_ref[:, index * PAIR : (index + 1) * PAIR] = ref[0]


def place(me, pieces, parts, group):
    rows = pieces[0].shape[1]
    pairs = len(pieces)
    return pl.pallas_call(
        place_kernel,
        grid_spec=pltpu.PrefetchScalarGridSpec(
            num_scalar_prefetch=1,
            grid=(parts, group),
            in_specs=[pl.BlockSpec((1, rows, PAIR), lambda j, d, me: (d, 0, j))] * pairs,
            out_specs=pl.BlockSpec(
                (rows, pairs * PAIR), lambda j, d, me: (0, j * group + (me[0] ^ d))
            ),
        ),
        out_shape=jax.ShapeDtypeStruct((rows, parts * D), jnp.bfloat16),
        compiler_params=compiler_params(),
        name="place",
    )(me, *pieces)


def swap_heads(pieces, group):
    got = [pieces[0]]
    for step in range(1, group):
        got.append(lax.ppermute(pieces[step], "grp", [(i, i ^ step) for i in range(group)]))
    return jnp.stack(got)


def attend_kernel(q_ref, k_ref, v_ref, qf_ref, kf_ref, own_v_ref, own_f_ref, out_ref, stat_ref, ke):
    @pl.when(pl.program_id(0) == 0)
    def _():
        ke[:, :PAIR] = k_ref[...]
        ke[:, PAIR:] = kf_ref[...]

    query = q_ref[...]
    lane = lax.broadcasted_iota(jnp.int32, query.shape, 1)
    scores = []
    for head in range(2):
        mine = (lane < HEAD) == (head == 0)
        wide = jnp.concatenate([jnp.where(mine, query, 0), qf_ref[...]], axis=1)
        scores.append(against(wide, ke[...]))
    mixed, logs = [], []
    for head in range(2):
        top = jnp.max(scores[head], axis=1, keepdims=True)
        weights = jnp.exp(scores[head] - top)
        total = jnp.sum(weights, axis=1, keepdims=True)
        got = jnp.dot(
            weights.astype(jnp.bfloat16), v_ref[...], preferred_element_type=jnp.float32
        )
        mixed.append(got / total)
        logs.append(top + jnp.log(total))
    dead = own_f_ref[:, SEQ_SLOTS : SEQ_SLOTS + 1].astype(jnp.float32) > 0.5
    result = jnp.where(lane < HEAD, mixed[0], mixed[1]).astype(jnp.bfloat16)
    out_ref[...] = jnp.where(dead, own_v_ref[...], result)
    stat = jnp.where(lane == 0, logs[0], jnp.where(lane == 1, logs[1], 0.0))
    stat_ref[...] = jnp.where(dead, 0.0, stat)


def block_rows(rows):
    return 512 if rows <= 2048 else 256


def attend(qkv, query_side, key_side):
    rows = qkv.shape[0]
    block = block_rows(rows)

    def some(part):
        return pl.BlockSpec((block, PAIR), lambda i: (i, part))

    def whole(part):
        return pl.BlockSpec((rows, PAIR), lambda i: (0, part))

    return pl.pallas_call(
        attend_kernel,
        grid=(rows // block,),
        in_specs=[some(0), whole(1), whole(2), some(0), whole(0), some(2), some(0)],
        out_specs=[some(0), some(0)],
        out_shape=[
            jax.ShapeDtypeStruct((rows, PAIR), jnp.bfloat16),
            jax.ShapeDtypeStruct((rows, PAIR), jnp.float32),
        ],
        scratch_shapes=[pltpu.VMEM((rows, 2 * PAIR), jnp.bfloat16)],
        compiler_params=compiler_params(),
        name="attend",
    )(qkv, qkv, qkv, query_side, key_side, qkv, key_side)


def in_three(column, lane):
    first = column.astype(jnp.bfloat16).astype(jnp.float32)
    second = (column - first).astype(jnp.bfloat16).astype(jnp.float32)
    third = column - first - second
    return jnp.where(
        lane == STAT_LANE,
        first,
        jnp.where(lane == STAT_LANE + 1, second, jnp.where(lane == STAT_LANE + 2, third, 0.0)),
    )


def attend_back_kernel(
    q_ref, k_ref, v_ref, qf_ref, kf_ref, stat_ref, att_ref, grad_ref, cos_ref, sin_ref,
    own_cos_ref, own_sin_ref, dq_ref, dk_ref, dv_ref, ke, ve, kt, dk_sum, dv_sum,
):
    @pl.when(pl.program_id(0) == 0)
    def _():
        ke[:, :PAIR] = k_ref[...]
        ke[:, PAIR:] = kf_ref[...]
        ve[:, :PAIR] = v_ref[...]
        ve[:, PAIR:] = kf_ref[...]
        kt[...] = k_ref[...].T
        dk_sum[...] = jnp.zeros_like(dk_sum)
        dv_sum[...] = jnp.zeros_like(dv_sum)

    query, grad = q_ref[...], grad_ref[...]
    lane = lax.broadcasted_iota(jnp.int32, query.shape, 1)
    both = grad.astype(jnp.float32) * att_ref[...].astype(jnp.float32)
    stat = stat_ref[...]
    query_heads, grad_heads, weights, grad_scores, turned_grads = [], [], [], [], []
    for head in range(2):
        mine = (lane < HEAD) == (head == 0)
        query_head = jnp.where(mine, query, 0)
        grad_head = jnp.where(mine, grad, 0)
        log_total = jnp.sum(jnp.where(lane == head, stat, 0.0), axis=1, keepdims=True)
        centre = jnp.sum(jnp.where(mine, both, 0.0), axis=1, keepdims=True)
        side = (qf_ref[...].astype(jnp.float32) - in_three(log_total, lane)).astype(jnp.bfloat16)
        wide = jnp.concatenate([query_head, side], axis=1)
        weight = jnp.exp(against(ke[...], wide))
        wide_grad = jnp.concatenate(
            [grad_head, (-in_three(centre, lane)).astype(jnp.bfloat16)], axis=1
        )
        grad_score = (weight * against(ve[...], wide_grad)).astype(jnp.bfloat16)
        weights.append(weight.astype(jnp.bfloat16))
        grad_scores.append(grad_score)
        query_heads.append(query_head)
        grad_heads.append(grad_head)
        turned_grads.append(jnp.dot(kt[...], grad_score, preferred_element_type=jnp.float32))
    dv_sum[...] += jnp.dot(
        jnp.concatenate(weights, axis=1),
        jnp.concatenate(grad_heads, axis=0),
        preferred_element_type=jnp.float32,
    )
    dk_sum[...] += jnp.dot(
        jnp.concatenate(grad_scores, axis=1),
        jnp.concatenate(query_heads, axis=0),
        preferred_element_type=jnp.float32,
    )
    row = lax.broadcasted_iota(jnp.int32, turned_grads[0].shape, 0)
    grad_query = jnp.where(row < HEAD, turned_grads[0], turned_grads[1]).T * HEAD ** (-0.5)
    dq_ref[...] = turned(grad_query, own_cos_ref[...], -own_sin_ref[...]).astype(jnp.bfloat16)

    @pl.when(pl.program_id(0) == pl.num_programs(0) - 1)
    def _():
        dk_ref[...] = turned(dk_sum[...], cos_ref[...], -sin_ref[...]).astype(jnp.bfloat16)
        dv_ref[...] = dv_sum[...].astype(jnp.bfloat16)


def attend_back(qkv, query_side, key_side, stat, attended, grad, cos, sin):
    rows = qkv.shape[0]
    block = block_rows(rows)

    def some(part):
        return pl.BlockSpec((block, PAIR), lambda i: (i, part))

    def whole(part):
        return pl.BlockSpec((rows, PAIR), lambda i: (0, part))

    out = jax.ShapeDtypeStruct((rows, PAIR), jnp.bfloat16)
    return pl.pallas_call(
        attend_back_kernel,
        grid=(rows // block,),
        in_specs=[
            some(0), whole(1), whole(2), some(0), whole(0), some(0), some(0), some(0),
            whole(0), whole(0), some(0), some(0),
        ],
        out_specs=[some(0), whole(0), whole(0)],
        out_shape=[out, out, out],
        scratch_shapes=[
            pltpu.VMEM((rows, 2 * PAIR), jnp.bfloat16),
            pltpu.VMEM((rows, 2 * PAIR), jnp.bfloat16),
            pltpu.VMEM((PAIR, rows), jnp.bfloat16),
            pltpu.VMEM((rows, PAIR), jnp.float32),
            pltpu.VMEM((rows, PAIR), jnp.float32),
        ],
        compiler_params=compiler_params(),
        name="attend_back",
    )(qkv, qkv, qkv, query_side, key_side, stat, attended, grad, cos, sin, cos, sin)


def product(left, right):
    return jnp.dot(left, right, preferred_element_type=jnp.float32)


def contract(left, right):
    return lax.dot_general(
        left, right, (((0,), (0,)), ((), ())), preferred_element_type=jnp.float32
    )


def against(left, right):
    return lax.dot_general(
        left, right, (((1,), (1,)), ((), ())), preferred_element_type=jnp.float32
    )


def own_half(array, core):
    half = array.shape[0] // 2
    return lax.dynamic_slice_in_dim(array, core * half, half)


def gather_weight(weight, core):
    return lax.all_gather(
        own_half(weight, core).astype(jnp.bfloat16), ("grp", "core"), axis=0, tiled=True
    )


def exchange(array, axis, mask, size):
    return lax.ppermute(array, axis, [(i, i ^ mask) for i in range(size)])


def pick(array, index, axis):
    return lax.dynamic_index_in_dim(array, index, axis, keepdims=False)


def halved(array, axis, mask, size, dim):
    bit = (lax.axis_index(axis) // mask) % 2
    got = exchange(pick(array, 1 - bit, dim), axis, mask, size)
    kept = pick(array, bit, dim)
    return (kept.astype(jnp.float32) + got.astype(jnp.float32)).astype(jnp.bfloat16)


def doubled(array, axis, mask, size, dim):
    bit = (lax.axis_index(axis) // mask) % 2
    got = exchange(array, axis, mask, size)
    low = jnp.where(bit == 0, array, got)
    high = jnp.where(bit == 0, got, array)
    return jnp.concatenate([low, high], axis=dim)


def scatter_rows(array, order, group):
    bits = group.bit_length() - 1
    rows, columns = array.shape[-2:]
    array = array.reshape((2,) * bits + (rows, columns))
    left = list(range(bits))
    for bit in order:
        place_of = left.index(bit)
        array = halved(array, "grp", 1 << (bits - 1 - bit), group, place_of)
        left.pop(place_of)
    return array


def reduce_weight(left, right, core, group, far):
    columns = right.shape[1] // 2
    theirs = lax.dynamic_slice_in_dim(right, (1 - core) * columns, columns, 1)
    mine = lax.dynamic_slice_in_dim(right, core * columns, columns, 1)
    sent = exchange(contract(left, theirs).astype(jnp.bfloat16), "core", 1, 2)
    share = (contract(left, mine) + sent.astype(jnp.float32)).astype(jnp.bfloat16)
    rows = share.shape[0] // group
    share = share.reshape(group, rows, columns)
    bits = group.bit_length() - 1
    forth = tuple(range(bits))
    share = jnp.concatenate(
        [
            scatter_rows(share[:, : rows // 2], forth, group),
            scatter_rows(share[:, rows // 2 :], forth[::-1], group),
        ],
        axis=0,
    )
    by_rows = rows % (16 * far) == 0
    dim = 0 if by_rows else 1
    masks = []
    mask = 1
    while mask < far:
        size = share.shape[dim]
        if size % 2 == 0 and (by_rows or size % (2 * PAIR) == 0):
            shape = share.shape
            split = (2, shape[0] // 2, shape[1]) if by_rows else (shape[0], 2, shape[1] // 2)
            share = halved(share.reshape(split), "far", mask, far, dim)
            masks.append(mask)
        else:
            got = exchange(share, "far", mask, far)
            share = (share.astype(jnp.float32) + got.astype(jnp.float32)).astype(jnp.bfloat16)
        mask *= 2
    for mask in masks[::-1]:
        share = doubled(share, "far", mask, far, dim)
    return doubled(share, "core", 1, 2, 1).astype(jnp.float32)


def spread_halves(array):
    spare = ((0, 0), (0, FF_WIDE - FF))
    return jnp.concatenate([jnp.pad(array[:, :FF], spare), jnp.pad(array[:, FF:], spare)], axis=1)


def joined_halves(array):
    return jnp.concatenate([array[:, :FF], array[:, FF_WIDE : FF_WIDE + FF]], axis=1)


def gated(gate, upward):
    return jax.nn.gelu(gate, approximate=False) * upward


def adam_update(weight, mean, square, grad, rate):
    mean_new = 0.9 * mean + 0.1 * grad
    square_new = 0.999 * square + 0.001 * grad * grad
    step_size = mean_new / (1.0 - 0.9**STEP) / (jnp.sqrt(square_new / (1.0 - 0.999**STEP)) + 1e-08)
    return (mean_new, square_new, weight - rate * (step_size + 0.01 * weight))


def local(
    group,
    far,
    tokens,
    slot_ids,
    cotangent,
    inproj,
    outproj,
    upproj,
    downproj,
    norm_gains,
    inproj_mean,
    outproj_mean,
    upproj_mean,
    downproj_mean,
    gains_mean,
    inproj_square,
    outproj_square,
    upproj_square,
    downproj_square,
    gains_square,
):
    me = lax.axis_index("grp")
    me_list = me.reshape(1).astype(jnp.int32)
    core = lax.axis_index("core")
    pairs = D // PAIR // group
    masters = (inproj, outproj, upproj, downproj, norm_gains)
    w_in = gather_weight(inproj, core)
    gains_low = lax.all_gather(norm_gains.astype(jnp.bfloat16), "grp", axis=0, tiled=True)
    w_out = gather_weight(outproj, core)
    w_up = gather_weight(spread_halves(upproj), core)
    w_down = gather_weight(downproj, core)
    gains = gains_low.astype(jnp.float32)
    all_ids = lax.all_gather(slot_ids, "grp", axis=1, tiled=True)[0]
    own_rows = tokens.shape[1]
    group_rows = all_ids.shape[0]
    order = me ^ jnp.arange(group, dtype=jnp.int32)
    near_ids = all_ids.reshape(group, own_rows)[order].reshape(group_rows)
    where_at = positions(all_ids).reshape(group, own_rows)[order].reshape(group_rows)
    cos, sin = pair_tables(where_at)
    query_side, key_side = slot_features(near_ids)
    live = (slot_ids[0] >= 0).astype(jnp.bfloat16)
    inputs = tokens[0].astype(jnp.float32)
    first_normed = layer_norm(inputs, gains[:, 0]).astype(jnp.bfloat16)
    cos_near = cos.reshape(group, own_rows, PAIR)
    sin_near = sin.reshape(group, own_rows, PAIR)
    qkv, stats, attended_near, attended_here = [], [], [], []
    for pair in range(pairs):
        pieces = project(me_list, first_normed, w_in, cos_near, sin_near, pair, group)
        qkv.append(swap_heads(pieces, group).reshape(group_rows, 3 * PAIR))
    for pair in range(pairs):
        mixed, stat = attend(qkv[pair], query_side, key_side)
        stats.append(stat)
        attended_near.append(mixed)
        attended_here.append(swap_heads(mixed.reshape(group, own_rows, PAIR), group))
    attended = place(me_list, attended_here, 1, group)
    middle = inputs + product(attended, w_out)
    second_normed = layer_norm(middle, gains[:, 1]).astype(jnp.bfloat16)
    gate_up = product(second_normed, w_up)
    gate = gate_up[:, :FF]
    upward = gate_up[:, FF_WIDE : FF_WIDE + FF]
    hidden = gated(gate, upward).astype(jnp.bfloat16)
    result = middle + product(hidden, w_down)
    grad_top = cotangent[0] * live[:, None]
    grad_hidden = against(grad_top, w_down)
    _, gate_back = jax.vjp(gated, gate, upward)
    grad_gate_up = spread_halves(jnp.concatenate(gate_back(grad_hidden), axis=1)).astype(
        jnp.bfloat16
    )
    grad_second = against(grad_gate_up, w_up)
    _, second_back = jax.vjp(lambda v: layer_norm(v, gains[:, 1]), middle)
    (grad_from_norm,) = second_back(grad_second)
    grad_middle = grad_top.astype(jnp.float32) + grad_from_norm
    grad_branch = grad_middle.astype(jnp.bfloat16)
    total_down = reduce_weight(hidden, grad_top, core, group, far)
    total_up = joined_halves(reduce_weight(second_normed, grad_gate_up, core, group, far))
    pieces_here = []
    for pair in range(pairs):
        sent = row_product(me_list, grad_branch, w_out, pair, group)
        grad_near = swap_heads(sent, group).reshape(group_rows, PAIR)
        grads = attend_back(
            qkv[pair], query_side, key_side, stats[pair], attended_near[pair], grad_near, cos, sin
        )
        joined = jnp.concatenate(grads, axis=1).reshape(group, own_rows, 3 * PAIR)
        pieces_here.append(swap_heads(joined, group))
    total_out = reduce_weight(attended, grad_branch, core, group, far)
    grad_projected = place(me_list, pieces_here, 3, group)
    total_in = reduce_weight(first_normed, grad_projected, core, group, far)
    grad_first = against(grad_projected, w_in)
    _, first_back = jax.vjp(lambda v: layer_norm(v, gains[:, 0]), inputs)
    (grad_inputs,) = first_back(grad_first)
    input_grad = (grad_middle + grad_inputs).astype(jnp.bfloat16)
    low_in = inproj.astype(jnp.bfloat16).astype(jnp.float32)
    low_up = upproj.astype(jnp.bfloat16).astype(jnp.float32)
    low_gains = norm_gains.astype(jnp.bfloat16).astype(jnp.float32)
    total_gains = (
        jnp.stack([jnp.sum(low_in * total_in, axis=1), jnp.sum(low_up * total_up, axis=1)], axis=1)
        / low_gains
    )
    totals = (total_in, total_out, total_up, total_down, total_gains)
    means = (inproj_mean, outproj_mean, upproj_mean, downproj_mean, gains_mean)
    squares = (inproj_square, outproj_square, upproj_square, downproj_square, gains_square)
    updates = [
        adam_update(masters[index], means[index], squares[index], totals[index], rate_list[index])
        for index in range(5)
    ]
    return (
        result.astype(jnp.bfloat16)[None],
        input_grad[None],
        updates[0][0],
        updates[0][1],
        updates[0][2],
        updates[1][0],
        updates[1][1],
        updates[1][2],
        updates[2][0],
        updates[2][1],
        updates[2][2],
        updates[3][0],
        updates[3][1],
        updates[3][2],
        updates[4][0],
        updates[4][1],
        updates[4][2],
    )


def solution(mesh):
    group_size, replicas = mesh.devices.shape
    fine = Mesh(mesh.devices.reshape(group_size, replicas // 2, 2), ("grp", "far", "core"))
    placed = (
        P(("far", "core"), "grp", None),
        P(("far", "core"), "grp"),
        P(("far", "core"), "grp", None),
        P("grp", None),
        P("grp", None),
        P("grp", None),
        P("grp", None),
        P("grp", None),
        P("grp", None),
        P("grp", None),
        P("grp", None),
        P("grp", None),
        P("grp", None),
        P("grp", None),
        P("grp", None),
        P("grp", None),
        P("grp", None),
        P("grp", None),
    )
    return jax.shard_map(
        functools.partial(local, group_size, replicas // 2),
        mesh=fine,
        in_specs=placed,
        out_specs=(
            P(("far", "core"), "grp", None),
            P(("far", "core"), "grp", None),
            P("grp", None),
            P("grp", None),
            P("grp", None),
            P("grp", None),
            P("grp", None),
            P("grp", None),
            P("grp", None),
            P("grp", None),
            P("grp", None),
            P("grp", None),
            P("grp", None),
            P("grp", None),
            P("grp", None),
            P("grp", None),
            P("grp", None),
        ),
        check_vma=False,
    )
```

time: 992 us -> 652 us (0.66)
  waiting for transfers between devices: 577 us -> 281 us
  matrix products: 206 us -> 75.9 us
  Pallas kernels: 0 us -> 86 us
  starting transfers between devices: 1.7 us -> 65.3 us
  local copies, waits for them, and re-layouts: 69.2 us -> 36.1 us
  other arithmetic: 93.3 us -> 70.3 us
    reduce_scatter x4 -> x0, waiting for transfers between devices: 239 us -> none  [reduce_weight(): lax.psum_scatter(grad.astype(jnp.bfloat16), ('grp', 'core'), scatter_dime...]
    ppermute x0 -> x64, waiting for transfers between devices: none -> 201 us  [the longest x40 183 us: exchange(): return lax.ppermute(array, axis, [(i, i ^ mask) for i in range(size)])]
    psum x1 -> x0, waiting for transfers between devices: 123 us -> none  [reduce_weight(): share = lax.psum(share, 'far')]
    dot_general x56 -> x0, matrix products: 119 us -> none  [the longest x16 40.7 us: masked_scores(): jnp.einsum('qhd,khd->hqk', query_pair, key_pair, preferred_element_type=j...]
    pallas_call x0 -> x10, Pallas kernels: none -> 86 us  [the longest x2 33.6 us: attend_back(): pl.pallas_call(attend_back_kernel, grid=(rows // block,), in_specs=[some(...]
    unnamed x18 -> x4, waiting for transfers between devices: 66.1 us -> 0.07 us
    ppermute x0 -> x64, starting transfers between devices: none -> 65.1 us  [the longest x40 33.3 us: exchange(): return lax.ppermute(array, axis, [(i, i ^ mask) for i in range(size)])]
    all_gather x5 -> x0, waiting for transfers between devices: 35.7 us -> none  [the longest x1 35.6 us: local(): lax.all_gather(keys, 'grp', axis=0, tiled=True)]
  transfers between devices with their start and end apart: 16 -> 68, of which waited for: 11 -> 38; matrix products, arithmetic and copies ran while one was open for 19% -> 18% of each run, Pallas kernels for 0% -> 13%
where the time goes in v2:
time: 652 us; the launch traced here: 648 us
  waiting for transfers between devices  281 us (43%)
  Pallas kernels  86 us (13%)
  matrix products  75.9 us (12%)
  other arithmetic  70.3 us (11%)
  starting transfers between devices  65.3 us (10%)
  local copies, waits for them, and re-layouts  36.1 us (6%)
  blocking collectives  17.6 us (3%)
  between operations  15.4 us (2%)
    ppermute x40, waiting for transfers between devices, exchange(): return lax.ppermute(array, axis, [(i, i ^ mask) for i in range(size)])  183 us
    all_gather x4, waiting for transfers between devices, gather_weight(): lax.all_gather(own_half(weight, core).astype(jnp.bfloat16), ('grp', 'core...  79.8 us
    pallas_call x2, Pallas kernels, attend_back(): pl.pallas_call(attend_back_kernel, grid=(rows // block,), in_specs=[some(...  33.6 us
    ppermute x40, starting transfers between devices, exchange(): return lax.ppermute(array, axis, [(i, i ^ mask) for i in range(size)])  33.3 us
    ppermute x24, starting transfers between devices, swap_heads(): lax.ppermute(pieces[step], 'grp', [(i, i ^ step) for i in range(group)])  31.8 us
    dot_general x3, matrix products, against(): lax.dot_general(left, right, (((1,), (1,)), ((), ())), preferred_element_...  29 us
    dot_general x8, matrix products, contract(): lax.dot_general(left, right, (((0,), (0,)), ((), ())), preferred_element_...  26.7 us
    sub x5, other arithmetic, adam_update(): return (mean_new, square_new, weight - rate * (step_size + 0.01 * weight))  23.2 us
  transfers between devices with their start and end apart: 68, of which 38 were waited for; matrix products, arithmetic and copies ran while one was open for 18% of the time, Pallas kernels for 13%

profile of v2, /device:TPU:0, one launch (start us, length us, event | category | flops | bytes accessed | tf_op | source)
XLA Modules:
  0.0 647.7 jit_solution(893832263068804000)
XLA Ops:
  19.4 9.5 %all_gather.20 = s32[1,1536]{1,0:T(1,128)S(1)} all-gather(s32[1,384]{1,0:T(1,128)S(1)} %copy-done.37), channel_id=1, replica_groups=mesh['grp'=4,'far'=4,'core'=2] {'grp'}, dimensions={1}, use_global_device_ids=true | all-gather | bytes 7680 | tf_op jit(solution)/shard_map/all_gather | solution.py:482
  31.4 8.0 %all_gather.18 = bf16[1024,2]{0,1:T(2,128)(2,1)S(1)} all-gather(bf16[256,2]{0,1:T(2,128)(2,1)S(1)} %convert_element_type.452), channel_id=1, replica_groups=mesh['grp'=4,'far'=4,'core'=2] {'grp'}, dimensions={0}, use_global_device_ids=true | all-gather | bytes 5120 | tf_op jit(solution)/shard_map/all_gather | solution.py:477
  40.1 4.5 fusion.52
  47.5 4.3 fusion.53
  51.8 7.0 %all-gather.5.cloned.1.call-done.wq_ref.wk_ref.wv_ref = bf16[1024,3072]{1,0:T(8,128)(2,1)} async-done(((bf16[128,3072]{1,0:T(8,128)(2,1)}), bf16[1024,3072]{1,0:T(8,128)(2,1)}) %all-gather.5.cloned.1.call-update) | async-done | bytes 6291472 | tf_op jit(solution)/shard_map/all_gather | solution.py:352
  58.8 5.9 project.2
  70.6 6.0 project.3
  81.9 5.1 collective-permute-done.1
  88.2 10.2 %attend.2 = (bf16[1536,128]{1,0:T(8,128)(2,1)}, f32[1536,128]{1,0:T(8,128)}) custom-call(bf16[1536,384]{1,0:T(8,128)(2,1)} %bitcast.281, bf16[1536,384]{1,0:T(8,128)(2,1)} %bitcast.282, bf16[1536,384]{1,0:T(8,128)(2,1)} %bitcast.283, bf16[1536,128]{1,0:T(8,128)(2,1)} %get-tuple-element.135.qf_ref, bf16[1536,128]{1,0:T(8,128)(2,1)} %get-tuple-element.134.kf_ref.own_f_ref, ...), custom_call_target="tpu_custom_call" | custom-call | tf_op jit(solution)/shard_map/attend/pallas_call | solution.py:215
  99.5 5.5 collective-permute-start.5
  107.4 10.3 %attend.3 = (bf16[1536,128]{1,0:T(8,128)(2,1)}, f32[1536,128]{1,0:T(8,128)}) custom-call(bf16[1536,384]{1,0:T(8,128)(2,1)} %bitcast.274, bf16[1536,384]{1,0:T(8,128)(2,1)} %bitcast.275, bf16[1536,384]{1,0:T(8,128)(2,1)} %bitcast.276, bf16[1536,128]{1,0:T(8,128)(2,1)} %get-tuple-element.135.qf_ref, bf16[1536,128]{1,0:T(8,128)(2,1)} %get-tuple-element.134.kf_ref.own_f_ref, ...), custom_call_target="tpu_custom_call" | custom-call | tf_op jit(solution)/shard_map/attend/pallas_call | solution.py:215
  123.2 4.3 collective-permute-done.11
  137.8 40.1 %all-gather.9.cloned.1.call-done = bf16[1024,5376]{1,0:T(8,128)(2,1)} async-done(((bf16[128,5376]{1,0:T(8,128)(2,1)}), bf16[1024,5376]{1,0:T(8,128)(2,1)}) %all-gather.9.cloned.1.call-update) | async-done | bytes 11010064 | tf_op jit(solution)/shard_map/all_gather | solution.py:352
  177.8 11.3 %fusion.125 = f32[384,5376]{1,0:T(8,128)} fusion(bf16[1024,5376]{1,0:T(8,128)(2,1)} %all-gather.9.cloned.1.call-done, f32[384,1024]{1,0:T(8,128)S(1)} %get-tuple-element.141, f32[1024]{0:T(1024)S(1)} %bitcast.353, f32[384]{0:T(512)S(1)} %fusion.95, f32[384]{0:T(512)S(1)} %broadcast_multiply_fusion), kind=kOutput, calls=%fused_computation.329 | convolution fusion | flops 4229431296 | bytes 20847616 | tf_op jit(solution)/shard_map/dot_general | solution.py:331
  189.1 32.7 %all-gather.11.cloned.1.call-done = bf16[2624,1024]{1,0:T(8,128)(2,1)} async-done(((bf16[328,1024]{1,0:T(8,128)(2,1)}), bf16[2624,1024]{1,0:T(8,128)(2,1)}) %all-gather.11.cloned.1.call-update) | async-done | bytes 5373968 | tf_op jit(solution)/shard_map/all_gather | solution.py:352
  221.8 15.9 %add_convert_fusion.3 = (bf16[384,2624]{1,0:T(8,128)(2,1)}, f32[384,2624]{1,0:T(8,128)}, f32[384,2624]{1,0:T(8,128)}) fusion(f32[384,5376]{1,0:T(8,128)} %fusion.125, bf16[384,1024]{1,0:T(8,128)(2,1)S(1)} %bitcast_multiply_fusion, bf16[2624,1024]{1,0:T(8,128)(2,1)} %all-gather.11.cloned.1.call-done), kind=kOutput, calls=%fused_computation.27 | convolution fusion | flops 2137153536 | bytes 24297472 | tf_op jit(solution)/shard_map/dot_general | solution.py:341
  237.7 6.0 multiply_convert_fusion
  247.2 8.7 %multiply_reduce_fusion.1 = (f32[384]{0:T(512)S(1)}, f32[384,1024]{1,0:T(8,128)S(1)}) fusion(f32[384,1024]{1,0:T(8,128)S(1)} %copy-done.12, f32[384]{0:T(512)S(1)} %broadcast_multiply_fusion, f32[1024]{0:T(1024)S(1)} %bitcast.354, bf16[1024,5376]{1,0:T(8,128)(2,1)} %all-gather.9.cloned.1.call-done, bf16[384,2624]{1,0:T(8,128)(2,1)S(1)} %get-tuple-element.58, ...), kind=kOutput, calls=%fused_computation.90 | convolution fusion | flops 4245945856 | bytes 18193408 | tf_op jit(solution)/shard_map/dot_general | solution.py:341
  258.7 4.2 row_product.2
  267.7 4.2 row_product.3
  276.0 5.4 convolution_convert_fusion
  281.3 6.0 fusion.43
  291.8 16.9 %attend_back.2 = (bf16[1536,128]{1,0:T(8,128)(2,1)}, bf16[1536,128]{1,0:T(8,128)(2,1)}, bf16[1536,128]{1,0:T(8,128)(2,1)}) custom-call(bf16[1536,384]{1,0:T(8,128)(2,1)} %bitcast.285, bf16[1536,384]{1,0:T(8,128)(2,1)} %bitcast.286, bf16[1536,384]{1,0:T(8,128)(2,1)} %bitcast.287, bf16[1536,128]{1,0:T(8,128)(2,1)} %get-tuple-element.135.qf_ref, ...), custom_call_target="tpu_custom_call" | custom-call | tf_op jit(solution)/shard_map/attend_back/pallas_call | solution.py:309
  317.2 16.8 %attend_back.3 = (bf16[1536,128]{1,0:T(8,128)(2,1)}, bf16[1536,128]{1,0:T(8,128)(2,1)}, bf16[1536,128]{1,0:T(8,128)(2,1)}) custom-call(bf16[1536,384]{1,0:T(8,128)(2,1)} %bitcast.278, bf16[1536,384]{1,0:T(8,128)(2,1)} %bitcast.279, bf16[1536,384]{1,0:T(8,128)(2,1)} %bitcast.280, bf16[1536,128]{1,0:T(8,128)(2,1)} %get-tuple-element.135.qf_ref, ...), custom_call_target="tpu_custom_call" | custom-call | tf_op jit(solution)/shard_map/attend_back/pallas_call | solution.py:309
  352.6 8.2 %place.3 = bf16[384,3072]{1,0:T(8,128)(2,1)} custom-call(s32[1]{0:T(128)} %bitcast.1.me_ref, bf16[4,384,384]{2,1,0:T(8,128)(2,1)} %pad_maximum_fusion.7.refs_0_, bf16[4,384,384]{2,1,0:T(8,128)(2,1)} %pad_maximum_fusion.8.refs_1_), custom_call_target="tpu_custom_call" | custom-call | tf_op jit(solution)/shard_map/place/pallas_call | solution.py:148
  360.9 4.5 fusion.35
  371.7 3.8 collective-permute-done.37
  381.7 3.7 collective-permute-done.36
  387.1 4.2 collective-permute-done.39
  414.7 13.5 %collective-permute-done.57 = bf16[2,328,512]{2,1,0:T(8,128)(2,1)S(1)} collective-permute-done((bf16[2,328,512]{2,1,0:T(8,128)(2,1)S(1)}, bf16[2,328,512]{2,1,0:T(8,128)(2,1)S(1)}, u32[]{:S(2)}, u32[]{:S(2)}) %collective-permute-start.57) | collective-permute-done | bytes 671776 | tf_op jit(solution)/shard_map/ppermute | solution.py:358
  430.5 3.8 add_convert_fusion.1
  453.8 4.6 collective-permute-done.60
  458.6 3.8 collective-permute-done.27
  464.2 4.2 collective-permute-done.61
  468.6 4.1 collective-permute-done.25
  481.0 5.4 add_convert_fusion
  491.3 6.2 collective-permute-done.29
  498.2 14.9 %collective-permute-done.47 = bf16[2,128,2688]{2,1,0:T(8,128)(2,1)S(1)} collective-permute-done((bf16[2,128,2688]{2,1,0:T(8,128)(2,1)S(1)}, bf16[2,128,2688]{2,1,0:T(8,128)(2,1)S(1)}, u32[]{:S(2)}, u32[]{:S(2)}) %collective-permute-start.47) | collective-permute-done | bytes 1376288 | tf_op jit(solution)/shard_map/ppermute | solution.py:358
  514.8 8.6 %collective-permute-done.45 = bf16[2,128,2688]{2,1,0:T(8,128)(2,1)S(1)} collective-permute-done((bf16[2,128,2688]{2,1,0:T(8,128)(2,1)S(1)}, bf16[2,128,2688]{2,1,0:T(8,128)(2,1)S(1)}, u32[]{:S(2)}, u32[]{:S(2)}) %collective-permute-start.45) | collective-permute-done | bytes 1376288 | tf_op jit(solution)/shard_map/ppermute | solution.py:358
  524.8 13.0 %collective-permute-done.48 = bf16[128,2688]{1,0:T(8,128)(2,1)S(1)} collective-permute-done((bf16[128,2688]{1,0:T(8,128)(2,1)S(1)}, bf16[128,2688]{1,0:T(8,128)(2,1)S(1)}, u32[]{:S(2)}, u32[]{:S(2)}) %collective-permute-start.48) | collective-permute-done | bytes 688160 | tf_op jit(solution)/shard_map/ppermute | solution.py:358
  542.2 18.7 %collective-permute-done.49 = bf16[128,2688]{1,0:T(8,128)(2,1)S(1)} collective-permute-done((bf16[128,2688]{1,0:T(8,128)(2,1)S(1)}, bf16[128,2688]{1,0:T(8,128)(2,1)S(1)}, u32[]{:S(2)}, u32[]{:S(2)}) %collective-permute-start.49) | collective-permute-done | bytes 688160 | tf_op jit(solution)/shard_map/ppermute | solution.py:358
  561.2 4.2 multiply_subtract_fusion.2
  565.4 19.2 %collective-permute-done.50 = bf16[64,2688]{1,0:T(8,128)(2,1)S(1)} collective-permute-done((bf16[64,2688]{1,0:T(8,128)(2,1)S(1)}, bf16[64,2688]{1,0:T(8,128)(2,1)S(1)}, u32[]{:S(2)}, u32[]{:S(2)}) %collective-permute-start.50) | collective-permute-done | bytes 344096 | tf_op jit(solution)/shard_map/ppermute | solution.py:358
  585.0 10.8 %collective-permute-done.51 = bf16[64,2688]{1,0:T(8,128)(2,1)S(1)} collective-permute-done((bf16[64,2688]{1,0:T(8,128)(2,1)S(1)}, bf16[64,2688]{1,0:T(8,128)(2,1)S(1)}, u32[]{:S(2)}, u32[]{:S(2)}) %collective-permute-start.51) | collective-permute-done | bytes 344096 | tf_op jit(solution)/shard_map/ppermute | solution.py:358
  596.0 8.2 %collective-permute-done.32 = bf16[128,1536]{1,0:T(8,128)(2,1)S(1)} collective-permute-done((bf16[128,1536]{1,0:T(8,128)(2,1)S(1)}, bf16[128,1536]{1,0:T(8,128)(2,1)S(1)}, u32[]{:S(2)}, u32[]{:S(2)}) %collective-permute-start.32) | collective-permute-done | bytes 393248 | tf_op jit(solution)/shard_map/ppermute | solution.py:358
  604.5 13.7 %collective-permute-done.52 = bf16[128,2688]{1,0:T(8,128)(2,1)S(1)} collective-permute-done((bf16[128,2688]{1,0:T(8,128)(2,1)S(1)}, bf16[128,2688]{1,0:T(8,128)(2,1)S(1)}, u32[]{:S(2)}, u32[]{:S(2)}) %collective-permute-start.52) | collective-permute-done | bytes 688160 | tf_op jit(solution)/shard_map/ppermute | solution.py:358
  621.0 5.0 multiply_subtract_fusion.1
  629.1 11.2 %multiply_subtract_fusion = (f32[256,5248]{1,0:T(8,128)}, f32[256,5248]{1,0:T(8,128)}, f32[256,5248]{1,0:T(8,128)}, f32[256]{0:T(256)S(1)}) fusion(f32[256,5248]{1,0:T(8,128)S(1)} %bitcast.289, f32[256,2624]{1,0:T(8,128)S(1)} %get-tuple-element.62, f32[256,2624]{1,0:T(8,128)S(1)} %get-tuple-element.61, f32[256,5248]{1,0:T(8,128)} %param.33, ...), kind=kLoop, calls=%fused_computation.21 | loop fusion | flops 26869504 | bytes 37618688 | tf_op jit(solution)/shard_map/sub | solution.py:446
  (376 shorter events, 186.3 us)
Async XLA Ops:
  7.2 51.6 %all-gather.5.cloned.1.call-start = ((), (), s32[]{:S(2)}) async-start(), calls=%async_computation | async-start | bytes 7077888 | tf_op jit(solution)/shard_map/all_gather | solution.py:352
  9.7 124.9 %all-gather.7.cloned.1.call-start = ((), (), s32[]{:S(2)}) async-start(), calls=%async_computation.1 | async-start | bytes 2359296 | tf_op jit(solution)/shard_map/all_gather | solution.py:352
  11.5 166.3 %all-gather.9.cloned.1.call-start = ((), (), s32[]{:S(2)}) async-start(), calls=%async_computation.2 | async-start | bytes 12386304 | tf_op jit(solution)/shard_map/all_gather | solution.py:352
  17.0 204.9 %all-gather.11.cloned.1.call-start = ((), (), s32[]{:S(2)}) async-start(), calls=%async_computation.3 | async-start | bytes 6045696 | tf_op jit(solution)/shard_map/all_gather | solution.py:352
  66.8 14.1 %collective-permute-start.2 = (bf16[384,384]{1,0:T(8,128)(2,1)}, bf16[384,384]{1,0:T(8,128)(2,1)S(1)}, u32[]{:S(2)}, u32[]{:S(2)}) collective-permute-start(bf16[384,384]{1,0:T(8,128)(2,1)} %get-tuple-element.91), channel_id=1, source_target_pairs={{0,24},{8,16},{16,8},{24,0},{1,25},{9,17},{17,9},{25,1},{2,26},{10... | collective-permute-start | bytes 884744 | tf_op jit(solution)/shard_map/ppermute | solution.py:167
  68.3 18.7 %collective-permute-start.1 = (bf16[384,384]{1,0:T(8,128)(2,1)S(1)}, bf16[384,384]{1,0:T(8,128)(2,1)S(1)}, u32[]{:S(2)}, u32[]{:S(2)}) collective-permute-start(bf16[384,384]{1,0:T(8,128)(2,1)S(1)} %get-tuple-element.92), channel_id=1, source_target_pairs={{0,16},{8,24},{16,0},{24,8},{1,17},{9,25},{17,1},{25,9},{2,18},{10... | collective-permute-start | bytes 884744 | tf_op jit(solution)/shard_map/ppermute | solution.py:167
  69.7 17.2 %collective-permute-start = (bf16[384,384]{1,0:T(8,128)(2,1)S(1)}, bf16[384,384]{1,0:T(8,128)(2,1)S(1)}, u32[]{:S(2)}, u32[]{:S(2)}) collective-permute-start(bf16[384,384]{1,0:T(8,128)(2,1)S(1)} %get-tuple-element.93), channel_id=1, source_target_pairs={{0,8},{8,0},{16,24},{24,16},{1,9},{9,1},{17,25},{25,17},{2,10},{10... | collective-permute-start | bytes 884744 | tf_op jit(solution)/shard_map/ppermute | solution.py:167
  78.0 28.2 %collective-permute-start.8 = (bf16[384,384]{1,0:T(8,128)(2,1)S(1)}, bf16[384,384]{1,0:T(8,128)(2,1)S(1)}, u32[]{:S(2)}, u32[]{:S(2)}) collective-permute-start(bf16[384,384]{1,0:T(8,128)(2,1)S(1)} %get-tuple-element.87), channel_id=1, source_target_pairs={{0,24},{8,16},{16,8},{24,0},{1,25},{9,17},{17,9},{25,1},{2,26},{10... | collective-permute-start | bytes 884744 | tf_op jit(solution)/shard_map/ppermute | solution.py:167
  79.5 26.7 %collective-permute-start.7 = (bf16[384,384]{1,0:T(8,128)(2,1)S(1)}, bf16[384,384]{1,0:T(8,128)(2,1)S(1)}, u32[]{:S(2)}, u32[]{:S(2)}) collective-permute-start(bf16[384,384]{1,0:T(8,128)(2,1)S(1)} %get-tuple-element.88), channel_id=1, source_target_pairs={{0,16},{8,24},{16,0},{24,8},{1,17},{9,25},{17,1},{25,9},{2,18},{10... | collective-permute-start | bytes 884744 | tf_op jit(solution)/shard_map/ppermute | solution.py:167
  81.0 25.3 %collective-permute-start.6 = (bf16[384,384]{1,0:T(8,128)(2,1)S(1)}, bf16[384,384]{1,0:T(8,128)(2,1)S(1)}, u32[]{:S(2)}, u32[]{:S(2)}) collective-permute-start(bf16[384,384]{1,0:T(8,128)(2,1)S(1)} %get-tuple-element.89), channel_id=1, source_target_pairs={{0,8},{8,0},{16,24},{24,16},{1,9},{9,1},{17,25},{25,17},{2,10},{10... | collective-permute-start | bytes 884744 | tf_op jit(solution)/shard_map/ppermute | solution.py:167
  99.5 22.9 %collective-permute-start.5 = (bf16[384,128]{1,0:T(8,128)(2,1)S(1)}, bf16[384,128]{1,0:T(8,128)(2,1)S(1)}, u32[]{:S(2)}, u32[]{:S(2)}) collective-permute-start(bf16[384,128]{1,0:T(8,128)(2,1)S(1)} %get-tuple-element.121), channel_id=1, source_target_pairs={{0,24},{8,16},{16,8},{24,0},{1,25},{9,17},{17,9},{25,1},{2,26},{10... | collective-permute-start | bytes 294920 | tf_op jit(solution)/shard_map/ppermute | solution.py:167
  105.0 17.5 %collective-permute-start.4 = (bf16[384,128]{1,0:T(8,128)(2,1)S(1)}, bf16[384,128]{1,0:T(8,128)(2,1)S(1)}, u32[]{:S(2)}, u32[]{:S(2)}) collective-permute-start(bf16[384,128]{1,0:T(8,128)(2,1)S(1)} %get-tuple-element.122), channel_id=1, source_target_pairs={{0,16},{8,24},{16,0},{24,8},{1,17},{9,25},{17,1},{25,9},{2,18},{10... | collective-permute-start | bytes 294920 | tf_op jit(solution)/shard_map/ppermute | solution.py:167
  106.2 16.2 %collective-permute-start.3 = (bf16[384,128]{1,0:T(8,128)(2,1)S(1)}, bf16[384,128]{1,0:T(8,128)(2,1)S(1)}, u32[]{:S(2)}, u32[]{:S(2)}) collective-permute-start(bf16[384,128]{1,0:T(8,128)(2,1)S(1)} %get-tuple-element.123), channel_id=1, source_target_pairs={{0,8},{8,0},{16,24},{24,16},{1,9},{9,1},{17,25},{25,17},{2,10},{10... | collective-permute-start | bytes 294920 | tf_op jit(solution)/shard_map/ppermute | solution.py:167
  264.2 26.3 %collective-permute-start.14 = (bf16[384,128]{1,0:T(8,128)(2,1)S(1)}, bf16[384,128]{1,0:T(8,128)(2,1)S(1)}, u32[]{:S(2)}, u32[]{:S(2)}) collective-permute-start(bf16[384,128]{1,0:T(8,128)(2,1)S(1)} %get-tuple-element.113), channel_id=1, source_target_pairs={{0,24},{8,16},{16,8},{24,0},{1,25},{9,17},{17,9},{25,1},{2,26},{10... | collective-permute-start | bytes 294920 | tf_op jit(solution)/shard_map/ppermute | solution.py:167
  265.7 25.3 %collective-permute-start.13 = (bf16[384,128]{1,0:T(8,128)(2,1)S(1)}, bf16[384,128]{1,0:T(8,128)(2,1)S(1)}, u32[]{:S(2)}, u32[]{:S(2)}) collective-permute-start(bf16[384,128]{1,0:T(8,128)(2,1)S(1)} %get-tuple-element.114), channel_id=1, source_target_pairs={{0,16},{8,24},{16,0},{24,8},{1,17},{9,25},{17,1},{25,9},{2,18},{10... | collective-permute-start | bytes 294920 | tf_op jit(solution)/shard_map/ppermute | solution.py:167
  267.2 23.9 %collective-permute-start.12 = (bf16[384,128]{1,0:T(8,128)(2,1)S(1)}, bf16[384,128]{1,0:T(8,128)(2,1)S(1)}, u32[]{:S(2)}, u32[]{:S(2)}) collective-permute-start(bf16[384,128]{1,0:T(8,128)(2,1)S(1)} %get-tuple-element.115), channel_id=1, source_target_pairs={{0,8},{8,0},{16,24},{24,16},{1,9},{9,1},{17,25},{25,17},{2,10},{10... | collective-permute-start | bytes 294920 | tf_op jit(solution)/shard_map/ppermute | solution.py:167
  273.0 42.9 %collective-permute-start.20 = (bf16[384,128]{1,0:T(8,128)(2,1)S(1)}, bf16[384,128]{1,0:T(8,128)(2,1)S(1)}, u32[]{:S(2)}, u32[]{:S(2)}) collective-permute-start(bf16[384,128]{1,0:T(8,128)(2,1)S(1)} %get-tuple-element.109), channel_id=1, source_target_pairs={{0,24},{8,16},{16,8},{24,0},{1,25},{9,17},{17,9},{25,1},{2,26},{10... | collective-permute-start | bytes 294920 | tf_op jit(solution)/shard_map/ppermute | solution.py:167
  274.5 41.9 %collective-permute-start.19 = (bf16[384,128]{1,0:T(8,128)(2,1)S(1)}, bf16[384,128]{1,0:T(8,128)(2,1)S(1)}, u32[]{:S(2)}, u32[]{:S(2)}) collective-permute-start(bf16[384,128]{1,0:T(8,128)(2,1)S(1)} %get-tuple-element.110), channel_id=1, source_target_pairs={{0,16},{8,24},{16,0},{24,8},{1,17},{9,25},{17,1},{25,9},{2,18},{10... | collective-permute-start | bytes 294920 | tf_op jit(solution)/shard_map/ppermute | solution.py:167
  290.5 25.9 %collective-permute-start.18 = (bf16[384,128]{1,0:T(8,128)(2,1)S(1)}, bf16[384,128]{1,0:T(8,128)(2,1)S(1)}, u32[]{:S(2)}, u32[]{:S(2)}) collective-permute-start(bf16[384,128]{1,0:T(8,128)(2,1)S(1)} %get-tuple-element.111), channel_id=1, source_target_pairs={{0,8},{8,0},{16,24},{24,16},{1,9},{9,1},{17,25},{25,17},{2,10},{10... | collective-permute-start | bytes 294920 | tf_op jit(solution)/shard_map/ppermute | solution.py:167
  312.9 27.6 %collective-permute-start.17 = (bf16[384,384]{1,0:T(8,128)(2,1)}, bf16[384,384]{1,0:T(8,128)(2,1)}, u32[]{:S(2)}, u32[]{:S(2)}) collective-permute-start(bf16[384,384]{1,0:T(8,128)(2,1)} %get-tuple-element.83), channel_id=1, source_target_pairs={{0,24},{8,16},{16,8},{24,0},{1,25},{9,17},{17,9},{25,1},{2,26},{10... | collective-permute-start | bytes 884744 | tf_op jit(solution)/shard_map/ppermute | solution.py:167
  314.3 28.5 %collective-permute-start.16 = (bf16[384,384]{1,0:T(8,128)(2,1)}, bf16[384,384]{1,0:T(8,128)(2,1)}, u32[]{:S(2)}, u32[]{:S(2)}) collective-permute-start(bf16[384,384]{1,0:T(8,128)(2,1)} %get-tuple-element.84), channel_id=1, source_target_pairs={{0,16},{8,24},{16,0},{24,8},{1,17},{9,25},{17,1},{25,9},{2,18},{10... | collective-permute-start | bytes 884744 | tf_op jit(solution)/shard_map/ppermute | solution.py:167
  315.8 27.0 %collective-permute-start.15 = (bf16[384,384]{1,0:T(8,128)(2,1)}, bf16[384,384]{1,0:T(8,128)(2,1)}, u32[]{:S(2)}, u32[]{:S(2)}) collective-permute-start(bf16[384,384]{1,0:T(8,128)(2,1)} %get-tuple-element.85), channel_id=1, source_target_pairs={{0,8},{8,0},{16,24},{24,16},{1,9},{9,1},{17,25},{25,17},{2,10},{10... | collective-permute-start | bytes 884744 | tf_op jit(solution)/shard_map/ppermute | solution.py:167
  337.5 10.8 %collective-permute-start.23 = (bf16[384,384]{1,0:T(8,128)(2,1)S(1)}, bf16[384,384]{1,0:T(8,128)(2,1)S(1)}, u32[]{:S(2)}, u32[]{:S(2)}) collective-permute-start(bf16[384,384]{1,0:T(8,128)(2,1)S(1)} %get-tuple-element.79), channel_id=1, source_target_pairs={{0,24},{8,16},{16,8},{24,0},{1,25},{9,17},{17,9},{25,1},{2,26},{10... | collective-permute-start | bytes 884744 | tf_op jit(solution)/shard_map/ppermute | solution.py:167
  339.1 12.4 %collective-permute-start.22 = (bf16[384,384]{1,0:T(8,128)(2,1)S(1)}, bf16[384,384]{1,0:T(8,128)(2,1)S(1)}, u32[]{:S(2)}, u32[]{:S(2)}) collective-permute-start(bf16[384,384]{1,0:T(8,128)(2,1)S(1)} %get-tuple-element.80), channel_id=1, source_target_pairs={{0,16},{8,24},{16,0},{24,8},{1,17},{9,25},{17,1},{25,9},{2,18},{10... | collective-permute-start | bytes 884744 | tf_op jit(solution)/shard_map/ppermute | solution.py:167
  340.5 10.9 %collective-permute-start.21 = (bf16[384,384]{1,0:T(8,128)(2,1)S(1)}, bf16[384,384]{1,0:T(8,128)(2,1)S(1)}, u32[]{:S(2)}, u32[]{:S(2)}) collective-permute-start(bf16[384,384]{1,0:T(8,128)(2,1)S(1)} %get-tuple-element.81), channel_id=1, source_target_pairs={{0,8},{8,0},{16,24},{24,16},{1,9},{9,1},{17,25},{25,17},{2,10},{10... | collective-permute-start | bytes 884744 | tf_op jit(solution)/shard_map/ppermute | solution.py:167
  342.8 22.6 %collective-permute-start.34 = (bf16[1024,512]{1,0:T(8,128)(2,1)}, bf16[1024,512]{1,0:T(8,128)(2,1)}, u32[]{:S(2)}, u32[]{:S(2)}) collective-permute-start(bf16[1024,512]{1,0:T(8,128)(2,1)} %convolution_convert_fusion.3), channel_id=1, source_target_pairs={{0,1},{1,0},{2,3},{3,2},{4,5},{5,4},{6,7},{7,6},{8,9},{9,8},{10,11... | collective-permute-start | bytes 3145736 | tf_op jit(solution)/shard_map/ppermute | solution.py:358
  342.8 138.2 %collective-permute-start.44 = (bf16[1024,2688]{1,0:T(8,128)(2,1)}, bf16[1024,2688]{1,0:T(8,128)(2,1)}, u32[]{:S(2)}, u32[]{:S(2)}) collective-permute-start(bf16[1024,2688]{1,0:T(8,128)(2,1)} %convolution_convert_fusion), channel_id=1, source_target_pairs={{0,1},{1,0},{2,3},{3,2},{4,5},{5,4},{6,7},{7,6},{8,9},{9,8},{10,11... | collective-permute-start | bytes 16515080 | tf_op jit(solution)/shard_map/ppermute | solution.py:358
  348.3 58.7 %collective-permute-start.54 = (bf16[2624,512]{1,0:T(8,128)(2,1)}, bf16[2624,512]{1,0:T(8,128)(2,1)}, u32[]{:S(2)}, u32[]{:S(2)}) collective-permute-start(bf16[2624,512]{1,0:T(8,128)(2,1)} %convolution_convert_fusion.1), channel_id=1, source_target_pairs={{0,1},{1,0},{2,3},{3,2},{4,5},{5,4},{6,7},{7,6},{8,9},{9,8},{10,11... | collective-permute-start | bytes 8060936 | tf_op jit(solution)/shard_map/ppermute | solution.py:358
  398.3 32.2 %collective-permute-start.24 = (bf16[1024,1536]{1,0:T(8,128)(2,1)S(1)}, bf16[1024,1536]{1,0:T(8,128)(2,1)S(1)}, u32[]{:S(2)}, u32[]{:S(2)}) collective-permute-start(bf16[1024,1536]{1,0:T(8,128)(2,1)S(1)} %convolution_convert_fusion.2), channel_id=1, source_target_pairs={{0,1},{1,0},{2,3},{3,2},{4,5},{5,4},{6,7},{7,6},{8,9},{9,8},{10,11... | collective-permute-start | bytes 9437192 | tf_op jit(solution)/shard_map/ppermute | solution.py:358
  410.7 17.5 %collective-permute-start.57 = (bf16[2,328,512]{2,1,0:T(8,128)(2,1)S(1)}, bf16[2,328,512]{2,1,0:T(8,128)(2,1)S(1)}, u32[]{:S(2)}, u32[]{:S(2)}) collective-permute-start(bf16[2,328,512]{2,1,0:T(8,128)(2,1)S(1)} %dynamic-slice_bitcast_fusion.7), channel_id=1, source_target_pairs={{0,8},{8,0},{16,24},{24,16},{1,9},{9,1},{17,25},{25,17},{2,10},{10... | collective-permute-start | bytes 2015240 | tf_op jit(solution)/shard_map/ppermute | solution.py:358
  411.1 17.6 %collective-permute-start.55 = (bf16[2,328,512]{2,1,0:T(8,128)(2,1)S(1)}, bf16[2,328,512]{2,1,0:T(8,128)(2,1)S(1)}, u32[]{:S(2)}, u32[]{:S(2)}) collective-permute-start(bf16[2,328,512]{2,1,0:T(8,128)(2,1)S(1)} %dynamic-slice_bitcast_fusion.8), channel_id=1, source_target_pairs={{0,16},{8,24},{16,0},{24,8},{1,17},{9,25},{17,1},{25,9},{2,18},{10... | collective-permute-start | bytes 2015240 | tf_op jit(solution)/shard_map/ppermute | solution.py:358
  444.3 18.0 %collective-permute-start.27 = (bf16[2,128,1536]{2,1,0:T(8,128)(2,1)}, bf16[2,128,1536]{2,1,0:T(8,128)(2,1)S(1)}, u32[]{:S(2)}, u32[]{:S(2)}) collective-permute-start(bf16[2,128,1536]{2,1,0:T(8,128)(2,1)} %dynamic-slice_bitcast_fusion.2), channel_id=1, source_target_pairs={{0,8},{8,0},{16,24},{24,16},{1,9},{9,1},{17,25},{25,17},{2,10},{10... | collective-permute-start | bytes 2359304 | tf_op jit(solution)/shard_map/ppermute | solution.py:358
  452.2 20.5 %collective-permute-start.25 = (bf16[2,128,1536]{2,1,0:T(8,128)(2,1)S(1)}, bf16[2,128,1536]{2,1,0:T(8,128)(2,1)S(1)}, u32[]{:S(2)}, u32[]{:S(2)}) collective-permute-start(bf16[2,128,1536]{2,1,0:T(8,128)(2,1)S(1)} %dynamic-slice_bitcast_fusion.3), channel_id=1, source_target_pairs={{0,16},{8,24},{16,0},{24,8},{1,17},{9,25},{17,1},{25,9},{2,18},{10... | collective-permute-start | bytes 2359304 | tf_op jit(solution)/shard_map/ppermute | solution.py:358
  458.4 10.0 %collective-permute-start.61 = (bf16[656,128]{1,0:T(8,128)(2,1)S(1)}, bf16[656,128]{1,0:T(8,128)(2,1)S(1)}, u32[]{:S(2)}, u32[]{:S(2)}) collective-permute-start(bf16[656,128]{1,0:T(8,128)(2,1)S(1)} %add_convert_fusion.7), channel_id=1, source_target_pairs={{0,4},{2,6},{4,0},{6,2},{1,5},{3,7},{5,1},{7,3},{8,12},{10,14},{12... | collective-permute-start | bytes 503816 | tf_op jit(solution)/shard_map/ppermute | solution.py:358
  462.6 15.2 %collective-permute-start.28 = (bf16[128,1536]{1,0:T(8,128)(2,1)S(1)}, bf16[128,1536]{1,0:T(8,128)(2,1)S(1)}, u32[]{:S(2)}, u32[]{:S(2)}) collective-permute-start(bf16[128,1536]{1,0:T(8,128)(2,1)S(1)} %dynamic-slice_bitcast_fusion.10), channel_id=1, source_target_pairs={{0,16},{8,24},{16,0},{24,8},{1,17},{9,25},{17,1},{25,9},{2,18},{10... | collective-permute-start | bytes 1179656 | tf_op jit(solution)/shard_map/ppermute | solution.py:358
  487.1 26.0 %collective-permute-start.47 = (bf16[2,128,2688]{2,1,0:T(8,128)(2,1)S(1)}, bf16[2,128,2688]{2,1,0:T(8,128)(2,1)S(1)}, u32[]{:S(2)}, u32[]{:S(2)}) collective-permute-start(bf16[2,128,2688]{2,1,0:T(8,128)(2,1)S(1)} %dynamic-slice_bitcast_fusion), channel_id=1, source_target_pairs={{0,8},{8,0},{16,24},{24,16},{1,9},{9,1},{17,25},{25,17},{2,10},{10... | collective-permute-start | bytes 4128776 | tf_op jit(solution)/shard_map/ppermute | solution.py:358
  490.2 51.7 %collective-permute-start.63 = (bf16[656,512]{1,0:T(8,128)(2,1)S(1)}, bf16[656,512]{1,0:T(8,128)(2,1)S(1)}, u32[]{:S(2)}, u32[]{:S(2)}) collective-permute-start(bf16[656,512]{1,0:T(8,128)(2,1)S(1)} %pad_maximum_fusion.13), channel_id=1, source_target_pairs={{0,1},{1,0},{2,3},{3,2},{4,5},{5,4},{6,7},{7,6},{8,9},{9,8},{10,11... | collective-permute-start | bytes 2015240 | tf_op jit(solution)/shard_map/ppermute | solution.py:358
  490.4 33.0 %collective-permute-start.45 = (bf16[2,128,2688]{2,1,0:T(8,128)(2,1)S(1)}, bf16[2,128,2688]{2,1,0:T(8,128)(2,1)S(1)}, u32[]{:S(2)}, u32[]{:S(2)}) collective-permute-start(bf16[2,128,2688]{2,1,0:T(8,128)(2,1)S(1)} %dynamic-slice_bitcast_fusion.1), channel_id=1, source_target_pairs={{0,16},{8,24},{16,0},{24,8},{1,17},{9,25},{17,1},{25,9},{2,18},{10... | collective-permute-start | bytes 4128776 | tf_op jit(solution)/shard_map/ppermute | solution.py:358
  497.6 43.6 %collective-permute-start.30 = (bf16[64,1536]{1,0:T(8,128)(2,1)S(1)}, bf16[64,1536]{1,0:T(8,128)(2,1)S(1)}, u32[]{:S(2)}, u32[]{:S(2)}) collective-permute-start(bf16[64,1536]{1,0:T(8,128)(2,1)S(1)} %dynamic-slice_bitcast_fusion.17), channel_id=1, source_target_pairs={{0,4},{2,6},{4,0},{6,2},{1,5},{3,7},{5,1},{7,3},{8,12},{10,14},{12... | collective-permute-start | bytes 589832 | tf_op jit(solution)/shard_map/ppermute | solution.py:358
  513.5 24.2 %collective-permute-start.48 = (bf16[128,2688]{1,0:T(8,128)(2,1)S(1)}, bf16[128,2688]{1,0:T(8,128)(2,1)S(1)}, u32[]{:S(2)}, u32[]{:S(2)}) collective-permute-start(bf16[128,2688]{1,0:T(8,128)(2,1)S(1)} %dynamic-slice_bitcast_fusion.5), channel_id=1, source_target_pairs={{0,16},{8,24},{16,0},{24,8},{1,17},{9,25},{17,1},{25,9},{2,18},{10... | collective-permute-start | bytes 2064392 | tf_op jit(solution)/shard_map/ppermute | solution.py:358
  523.8 16.7 %collective-permute-start.46 = (bf16[128,2688]{1,0:T(8,128)(2,1)S(1)}, bf16[128,2688]{1,0:T(8,128)(2,1)S(1)}, u32[]{:S(2)}, u32[]{:S(2)}) collective-permute-start(bf16[128,2688]{1,0:T(8,128)(2,1)S(1)} %dynamic-slice_bitcast_fusion.6), channel_id=1, source_target_pairs={{0,8},{8,0},{16,24},{24,16},{1,9},{9,1},{17,25},{25,17},{2,10},{10... | collective-permute-start | bytes 2064392 | tf_op jit(solution)/shard_map/ppermute | solution.py:358
  540.9 20.0 %collective-permute-start.49 = (bf16[128,2688]{1,0:T(8,128)(2,1)S(1)}, bf16[128,2688]{1,0:T(8,128)(2,1)S(1)}, u32[]{:S(2)}, u32[]{:S(2)}) collective-permute-start(bf16[128,2688]{1,0:T(8,128)(2,1)S(1)} %dynamic-slice_bitcast_fusion.4), channel_id=1, source_target_pairs={{0,2},{2,0},{4,6},{6,4},{1,3},{3,1},{5,7},{7,5},{8,10},{10,8},{12,... | collective-permute-start | bytes 2064392 | tf_op jit(solution)/shard_map/ppermute | solution.py:358
  541.3 43.5 %collective-permute-start.31 = (bf16[64,1536]{1,0:T(8,128)(2,1)S(1)}, bf16[64,1536]{1,0:T(8,128)(2,1)S(1)}, u32[]{:S(2)}, u32[]{:S(2)}) collective-permute-start(bf16[64,1536]{1,0:T(8,128)(2,1)S(1)} %fusion.68), channel_id=1, source_target_pairs={{0,4},{2,6},{4,0},{6,2},{1,5},{3,7},{5,1},{7,3},{8,12},{10,14},{12... | collective-permute-start | bytes 589832 | tf_op jit(solution)/shard_map/ppermute | solution.py:358
  561.1 23.5 %collective-permute-start.50 = (bf16[64,2688]{1,0:T(8,128)(2,1)S(1)}, bf16[64,2688]{1,0:T(8,128)(2,1)S(1)}, u32[]{:S(2)}, u32[]{:S(2)}) collective-permute-start(bf16[64,2688]{1,0:T(8,128)(2,1)S(1)} %dynamic-slice_bitcast_fusion.12), channel_id=1, source_target_pairs={{0,4},{2,6},{4,0},{6,2},{1,5},{3,7},{5,1},{7,3},{8,12},{10,14},{12... | collective-permute-start | bytes 1032200 | tf_op jit(solution)/shard_map/ppermute | solution.py:358
  584.7 11.1 %collective-permute-start.51 = (bf16[64,2688]{1,0:T(8,128)(2,1)S(1)}, bf16[64,2688]{1,0:T(8,128)(2,1)S(1)}, u32[]{:S(2)}, u32[]{:S(2)}) collective-permute-start(bf16[64,2688]{1,0:T(8,128)(2,1)S(1)} %fusion.62), channel_id=1, source_target_pairs={{0,4},{2,6},{4,0},{6,2},{1,5},{3,7},{5,1},{7,3},{8,12},{10,14},{12... | collective-permute-start | bytes 1032200 | tf_op jit(solution)/shard_map/ppermute | solution.py:358
  584.9 19.3 %collective-permute-start.32 = (bf16[128,1536]{1,0:T(8,128)(2,1)S(1)}, bf16[128,1536]{1,0:T(8,128)(2,1)S(1)}, u32[]{:S(2)}, u32[]{:S(2)}) collective-permute-start(bf16[128,1536]{1,0:T(8,128)(2,1)S(1)} %pad_maximum_fusion.19), channel_id=1, source_target_pairs={{0,2},{2,0},{4,6},{6,4},{1,3},{3,1},{5,7},{7,5},{8,10},{10,8},{12,... | collective-permute-start | bytes 1179656 | tf_op jit(solution)/shard_map/ppermute | solution.py:358
  595.9 22.2 %collective-permute-start.52 = (bf16[128,2688]{1,0:T(8,128)(2,1)S(1)}, bf16[128,2688]{1,0:T(8,128)(2,1)S(1)}, u32[]{:S(2)}, u32[]{:S(2)}) collective-permute-start(bf16[128,2688]{1,0:T(8,128)(2,1)S(1)} %pad_maximum_fusion.11), channel_id=1, source_target_pairs={{0,2},{2,0},{4,6},{6,4},{1,3},{3,1},{5,7},{7,5},{8,10},{10,8},{12,... | collective-permute-start | bytes 2064392 | tf_op jit(solution)/shard_map/ppermute | solution.py:358
  604.4 14.2 %collective-permute-start.33 = (bf16[256,1536]{1,0:T(8,128)(2,1)S(1)}, bf16[256,1536]{1,0:T(8,128)(2,1)S(1)}, u32[]{:S(2)}, u32[]{:S(2)}) collective-permute-start(bf16[256,1536]{1,0:T(8,128)(2,1)S(1)} %pad_maximum_fusion.10), channel_id=1, source_target_pairs={{0,1},{1,0},{2,3},{3,2},{4,5},{5,4},{6,7},{7,6},{8,9},{9,8},{10,11... | collective-permute-start | bytes 2359304 | tf_op jit(solution)/shard_map/ppermute | solution.py:358
  (65 other events, 731.8 us)
Sparse Core Ops, SparseCore 0:
  10.5 48.2 all-gather.4
  61.2 44.4 all-gather.6
  108.2 69.5 all-gather.8
  180.1 41.6 all-gather.10

commit v3 on v2

--- a/solution.py
+++ b/solution.py
@@ -84,12 +84,22 @@
     out_ref[0, :, 2 * PAIR :] = got[:, 2 * PAIR :].astype(jnp.bfloat16)
 
 
-def project(me, first_normed, w_in, cos, sin, pair, group):
+def skipping(kernel, before, extra):
+    def body(*refs):
+        kernel(*refs[:before], *refs[before + extra :])
+
+    return body
+
+
+def untouched(after):
+    return [pl.BlockSpec(memory_space=pl.ANY)] * len(after)
+
+
+def project(me, first_normed, w_pair, cos, sin, group):
     rows = first_normed.shape[0]
-    pairs = D // PAIR // group
 
     def column(part):
-        return lambda d, me: (0, part * (D // PAIR) + (me[0] ^ d) * pairs + pair)
+        return lambda d, me: (0, part * group + (me[0] ^ d))
 
     return pl.pallas_call(
         project_kernel,
@@ -109,63 +119,119 @@
         out_shape=jax.ShapeDtypeStruct((group, rows, 3 * PAIR), jnp.bfloat16),
         compiler_params=compiler_params(),
         name="project",
-    )(me, first_normed, w_in, w_in, w_in, cos, sin)
+    )(me, first_normed, w_pair, w_pair, w_pair, cos, sin)
 
 
 def row_product_kernel(me_ref, x_ref, w_ref, out_ref):
     out_ref[0] = against(x_ref[...], w_ref[...]).astype(jnp.bfloat16)
 
 
-def row_product(me, left, weight, pair, group):
+def row_product(me, left, weight, pair, group, after=()):
     rows = left.shape[0]
     pairs = D // PAIR // group
     return pl.pallas_call(
-        row_product_kernel,
+        skipping(row_product_kernel, 3, len(after)),
         grid_spec=pltpu.PrefetchScalarGridSpec(
             num_scalar_prefetch=1,
             grid=(group,),
             in_specs=[
                 pl.BlockSpec((rows, D), lambda d, me: (0, 0)),
                 pl.BlockSpec((PAIR, D), lambda d, me: ((me[0] ^ d) * pairs + pair, 0)),
+                *untouched(after),
             ],
             out_specs=pl.BlockSpec((1, rows, PAIR), lambda d, me: (d, 0, 0)),
         ),
         out_shape=jax.ShapeDtypeStruct((group, rows, PAIR), jnp.bfloat16),
         compiler_params=compiler_params(),
         name="row_product",
-    )(me, left, weight)
-
-
-def place_kernel(me_ref, *refs):
-    out_ref = refs[-1]
-    for index, ref in enumerate(refs[:-1]):
-        out_ref[:, index * PAIR : (index + 1) * PAIR] = ref[0]
-
-
-def place(me, pieces, parts, group):
-    rows = pieces[0].shape[1]
+    )(me, left, weight, *after)
+
+
+def run_copies(pairs_of, sems):
+    copies = [
+        pltpu.make_async_copy(source, target, sems.at[index])
+        for index, (source, target) in enumerate(pairs_of)
+    ]
+    for copy in copies:
+        copy.start()
+    for copy in copies:
+        copy.wait()
+
+
+def place(me, pieces, parts, group, after=()):
+    rows = pieces[0][0].shape[0]
     pairs = len(pieces)
+    flat = [piece for near in pieces for piece in near]
+
+    def kernel(me_ref, *refs):
+        out_ref, sems = refs[len(flat) + len(after) :]
+        moves = []
+        for pair in range(pairs):
+            for step in range(group):
+                owner = me_ref[0] ^ step
+                for part in range(parts):
+                    column = ((part * group + owner) * pairs + pair) * PAIR
+                    moves.append(
+                        (
+                            refs[pair * group + step].at[:, part * PAIR : (part + 1) * PAIR],
+                            out_ref.at[:, pl.ds(pl.multiple_of(column, PAIR), PAIR)],
+                        )
+                    )
+        run_copies(moves, sems)
+
     return pl.pallas_call(
-        place_kernel,
-        grid_spec=pltpu.PrefetchScalarGridSpec(
-            num_scalar_prefetch=1,
-            grid=(parts, group),
-            in_specs=[pl.BlockSpec((1, rows, PAIR), lambda j, d, me: (d, 0, j))] * pairs,
-            out_specs=pl.BlockSpec(
-                (rows, pairs * PAIR), lambda j, d, me: (0, j * group + (me[0] ^ d))
-            ),
-        ),
-        out_shape=jax.ShapeDtypeStruct((rows, parts * D), jnp.bfloat16),
+        kernel,
+        in_specs=[pl.BlockSpec(memory_space=pltpu.SMEM)] + untouched(flat) + untouched(after),
+        out_specs=pl.BlockSpec(memory_space=pl.ANY),
+        out_shape=jax.ShapeDtypeStruct((rows, parts * group * pairs * PAIR), jnp.bfloat16),
+        scratch_shapes=[pltpu.SemaphoreType.DMA((len(flat) * parts,))],
         compiler_params=compiler_params(),
         name="place",
-    )(me, *pieces)
+    )(me, *flat, *after)
+
+
+def exchange(array, axis, mask, size):
+    return lax.ppermute(array, axis, [(i, i ^ mask) for i in range(size)])
 
 
 def swap_heads(pieces, group):
-    got = [pieces[0]]
-    for step in range(1, group):
-        got.append(lax.ppermute(pieces[step], "grp", [(i, i ^ step) for i in range(group)]))
-    return jnp.stack(got)
+    return [pieces[0]] + [exchange(pieces[d], "grp", d, group) for d in range(1, group)]
+
+
+def gather_rows(half, me_core, group):
+    if group != 4:
+        return lax.all_gather(half, ("grp", "core"), axis=0, tiled=True)
+    rows, columns = half.shape
+    middle = rows // 2
+    first = exchange(half, "grp", 1, group)
+    second = exchange(half, "grp", 2, group)
+    upper = exchange(second[:middle], "grp", 1, group)
+    lower = exchange(first[middle:], "grp", 2, group)
+    got = [half, first, second, upper, lower]
+    got += [exchange(piece, "core", 1, 2) for piece in got]
+
+    def kernel(index_ref, *refs):
+        out_ref, sems = refs[len(got) :]
+        moves = []
+        for side in range(2):
+            core = index_ref[1] ^ side
+            for slot, (step, offset) in enumerate(((0, 0), (1, 0), (2, 0), (3, 0), (3, middle))):
+                row = ((index_ref[0] ^ step) * 2 + core) * rows + offset
+                source = refs[side * 5 + slot]
+                moves.append(
+                    (source, out_ref.at[pl.ds(pl.multiple_of(row, middle), source.shape[0])])
+                )
+        run_copies(moves, sems)
+
+    return pl.pallas_call(
+        kernel,
+        in_specs=[pl.BlockSpec(memory_space=pltpu.SMEM)] + untouched(got),
+        out_specs=pl.BlockSpec(memory_space=pl.ANY),
+        out_shape=jax.ShapeDtypeStruct((2 * group * rows, columns), jnp.bfloat16),
+        scratch_shapes=[pltpu.SemaphoreType.DMA((len(got),))],
+        compiler_params=compiler_params(),
+        name="gather_rows",
+    )(me_core, *got)
 
 
 def attend_kernel(q_ref, k_ref, v_ref, qf_ref, kf_ref, own_v_ref, own_f_ref, out_ref, stat_ref, ke):
@@ -240,7 +306,7 @@
 
 def attend_back_kernel(
     q_ref, k_ref, v_ref, qf_ref, kf_ref, stat_ref, att_ref, grad_ref, cos_ref, sin_ref,
-    own_cos_ref, own_sin_ref, dq_ref, dk_ref, dv_ref, ke, ve, kt, dk_sum, dv_sum,
+    own_cos_ref, own_sin_ref, out_ref, ke, ve, kt, dk_sum, dv_sum,
 ):
     @pl.when(pl.program_id(0) == 0)
     def _():
@@ -287,15 +353,21 @@
     )
     row = lax.broadcasted_iota(jnp.int32, turned_grads[0].shape, 0)
     grad_query = jnp.where(row < HEAD, turned_grads[0], turned_grads[1]).T * HEAD ** (-0.5)
-    dq_ref[...] = turned(grad_query, own_cos_ref[...], -own_sin_ref[...]).astype(jnp.bfloat16)
+    block = query.shape[0]
+    own = pl.ds(pl.multiple_of(pl.program_id(0) * block, block), block)
+    out_ref[own, :PAIR] = turned(grad_query, own_cos_ref[...], -own_sin_ref[...]).astype(
+        jnp.bfloat16
+    )
 
     @pl.when(pl.program_id(0) == pl.num_programs(0) - 1)
     def _():
-        dk_ref[...] = turned(dk_sum[...], cos_ref[...], -sin_ref[...]).astype(jnp.bfloat16)
-        dv_ref[...] = dv_sum[...].astype(jnp.bfloat16)
-
-
-def attend_back(qkv, query_side, key_side, stat, attended, grad, cos, sin):
+        out_ref[:, PAIR : 2 * PAIR] = turned(dk_sum[...], cos_ref[...], -sin_ref[...]).astype(
+            jnp.bfloat16
+        )
+        out_ref[:, 2 * PAIR :] = dv_sum[...].astype(jnp.bfloat16)
+
+
+def attend_back(qkv, query_side, key_side, stat, attended, grad, cos, sin, after=()):
     rows = qkv.shape[0]
     block = block_rows(rows)
 
@@ -305,16 +377,15 @@
     def whole(part):
         return pl.BlockSpec((rows, PAIR), lambda i: (0, part))
 
-    out = jax.ShapeDtypeStruct((rows, PAIR), jnp.bfloat16)
     return pl.pallas_call(
-        attend_back_kernel,
+        skipping(attend_back_kernel, 12, len(after)),
         grid=(rows // block,),
         in_specs=[
             some(0), whole(1), whole(2), some(0), whole(0), some(0), some(0), some(0),
-            whole(0), whole(0), some(0), some(0),
+            whole(0), whole(0), some(0), some(0), *untouched(after),
         ],
-        out_specs=[some(0), whole(0), whole(0)],
-        out_shape=[out, out, out],
+        out_specs=pl.BlockSpec((rows, 3 * PAIR), lambda i: (0, 0)),
+        out_shape=jax.ShapeDtypeStruct((rows, 3 * PAIR), jnp.bfloat16),
         scratch_shapes=[
             pltpu.VMEM((rows, 2 * PAIR), jnp.bfloat16),
             pltpu.VMEM((rows, 2 * PAIR), jnp.bfloat16),
@@ -324,7 +395,7 @@
         ],
         compiler_params=compiler_params(),
         name="attend_back",
-    )(qkv, qkv, qkv, query_side, key_side, stat, attended, grad, cos, sin, cos, sin)
+    )(qkv, qkv, qkv, query_side, key_side, stat, attended, grad, cos, sin, cos, sin, *after)
 
 
 def product(left, right):
@@ -354,76 +425,91 @@
     )
 
 
-def exchange(array, axis, mask, size):
-    return lax.ppermute(array, axis, [(i, i ^ mask) for i in range(size)])
-
-
 def pick(array, index, axis):
     return lax.dynamic_index_in_dim(array, index, axis, keepdims=False)
 
 
-def halved(array, axis, mask, size, dim):
-    bit = (lax.axis_index(axis) // mask) % 2
-    got = exchange(pick(array, 1 - bit, dim), axis, mask, size)
-    kept = pick(array, bit, dim)
-    return (kept.astype(jnp.float32) + got.astype(jnp.float32)).astype(jnp.bfloat16)
-
-
-def doubled(array, axis, mask, size, dim):
-    bit = (lax.axis_index(axis) // mask) % 2
-    got = exchange(array, axis, mask, size)
-    low = jnp.where(bit == 0, array, got)
-    high = jnp.where(bit == 0, got, array)
-    return jnp.concatenate([low, high], axis=dim)
-
-
-def scatter_rows(array, order, group):
-    bits = group.bit_length() - 1
-    rows, columns = array.shape[-2:]
-    array = array.reshape((2,) * bits + (rows, columns))
-    left = list(range(bits))
-    for bit in order:
-        place_of = left.index(bit)
-        array = halved(array, "grp", 1 << (bits - 1 - bit), group, place_of)
-        left.pop(place_of)
-    return array
-
-
-def reduce_weight(left, right, core, group, far):
+def added(*terms):
+    return sum(term.astype(jnp.float32) for term in terms).astype(jnp.bfloat16)
+
+
+def halved(array, mask, group, dim):
+    bit = (lax.axis_index("grp") // mask) % 2
+    got = exchange(pick(array, 1 - bit, dim), "grp", mask, group)
+    return added(pick(array, bit, dim), got)
+
+
+def core_sum(left, right, core):
     columns = right.shape[1] // 2
     theirs = lax.dynamic_slice_in_dim(right, (1 - core) * columns, columns, 1)
     mine = lax.dynamic_slice_in_dim(right, core * columns, columns, 1)
     sent = exchange(contract(left, theirs).astype(jnp.bfloat16), "core", 1, 2)
-    share = (contract(left, mine) + sent.astype(jnp.float32)).astype(jnp.bfloat16)
-    rows = share.shape[0] // group
-    share = share.reshape(group, rows, columns)
-    bits = group.bit_length() - 1
-    forth = tuple(range(bits))
-    share = jnp.concatenate(
-        [
-            scatter_rows(share[:, : rows // 2], forth, group),
-            scatter_rows(share[:, rows // 2 :], forth[::-1], group),
-        ],
-        axis=0,
-    )
-    by_rows = rows % (16 * far) == 0
-    dim = 0 if by_rows else 1
-    masks = []
+    return (contract(left, mine) + sent.astype(jnp.float32)).astype(jnp.bfloat16)
+
+
+def group_first(share, group):
+    rows, columns = share.shape[0] // group, share.shape[1]
+    if group != 4:
+        return (lax.psum_scatter(share, "grp", scatter_dimension=0, tiled=True),)
+    share = share.reshape(2, 2, rows, columns)
+    return (
+        halved(share[:, :, : rows // 2], 2, group, 0),
+        halved(share[:, :, rows // 2 :], 1, group, 1),
+    )
+
+
+def group_second(halves, group):
+    if group != 4:
+        return halves[0]
+    return jnp.concatenate([halved(halves[0], 1, group, 0), halved(halves[1], 2, group, 0)], axis=0)
+
+
+def far_scatter(share, far):
+    if far > 4:
+        return lax.psum(share, "far")
+    rows, columns = share.shape
+    own = lax.axis_index("far")
+    if rows % (16 * far) == 0:
+        chunk = rows // far
+        pieces = [lax.dynamic_slice_in_dim(share, (own ^ d) * chunk, chunk, 0) for d in range(far)]
+    else:
+        chunk = columns // far
+        pieces = [lax.dynamic_slice_in_dim(share, (own ^ d) * chunk, chunk, 1) for d in range(far)]
+    return added(pieces[0], *[exchange(pieces[d], "far", d, far) for d in range(1, far)])
+
+
+def far_gather(chunk, rows, far):
+    if far > 4:
+        return chunk
+    pieces = [chunk] + [exchange(chunk, "far", d, far) for d in range(1, far)]
+    own = lax.axis_index("far")
     mask = 1
     while mask < far:
-        size = share.shape[dim]
-        if size % 2 == 0 and (by_rows or size % (2 * PAIR) == 0):
-            shape = share.shape
-            split = (2, shape[0] // 2, shape[1]) if by_rows else (shape[0], 2, shape[1] // 2)
-            share = halved(share.reshape(split), "far", mask, far, dim)
-            masks.append(mask)
-        else:
-            got = exchange(share, "far", mask, far)
-            share = (share.astype(jnp.float32) + got.astype(jnp.float32)).astype(jnp.bfloat16)
+        swap = (own // mask) % 2 == 1
+        pieces = [jnp.where(swap, pieces[j ^ mask], pieces[j]) for j in range(far)]
         mask *= 2
-    for mask in masks[::-1]:
-        share = doubled(share, "far", mask, far, dim)
-    return doubled(share, "core", 1, 2, 1).astype(jnp.float32)
+    return jnp.concatenate(pieces, axis=0 if rows % (16 * far) == 0 else 1)
+
+
+def finished(chunk, rows, core, far):
+    share = far_gather(chunk, rows, far)
+    other = exchange(share, "core", 1, 2)
+    low = jnp.where(core == 0, share, other)
+    high = jnp.where(core == 0, other, share)
+    return jnp.concatenate([low, high], axis=1).astype(jnp.float32)
+
+
+def pair_columns(weight, pair, pairs):
+    blocks = range(pair, weight.shape[1] // PAIR, pairs)
+    return jnp.concatenate([weight[:, j * PAIR : (j + 1) * PAIR] for j in blocks], axis=1)
+
+
+def merged_columns(parts):
+    pairs = len(parts)
+    blocks = range(pairs * parts[0].shape[1] // PAIR)
+    return jnp.concatenate(
+        [parts[j % pairs][:, j // pairs * PAIR : (j // pairs + 1) * PAIR] for j in blocks], axis=1
+    )
 
 
 def spread_halves(array):
@@ -469,18 +555,27 @@
     gains_square,
 ):
     me = lax.axis_index("grp")
+    core = lax.axis_index("core")
     me_list = me.reshape(1).astype(jnp.int32)
-    core = lax.axis_index("core")
+    me_core = jnp.stack([me, core]).astype(jnp.int32)
     pairs = D // PAIR // group
     masters = (inproj, outproj, upproj, downproj, norm_gains)
-    w_in = gather_weight(inproj, core)
-    gains_low = lax.all_gather(norm_gains.astype(jnp.bfloat16), "grp", axis=0, tiled=True)
-    w_out = gather_weight(outproj, core)
+    own_rows = tokens.shape[1]
+    own_gains = norm_gains.shape[0]
+    w_pairs = [
+        gather_rows(
+            own_half(pair_columns(inproj, pair, pairs), core).astype(jnp.bfloat16), me_core, group
+        )
+        for pair in range(pairs)
+    ]
     w_up = gather_weight(spread_halves(upproj), core)
     w_down = gather_weight(downproj, core)
-    gains = gains_low.astype(jnp.float32)
-    all_ids = lax.all_gather(slot_ids, "grp", axis=1, tiled=True)[0]
-    own_rows = tokens.shape[1]
+    w_out = gather_rows(own_half(outproj, core).astype(jnp.bfloat16), me_core, group)
+    packed = jnp.concatenate([norm_gains[:, 0], norm_gains[:, 1], slot_ids[0].astype(jnp.float32)])
+    packed = lax.all_gather(packed.astype(jnp.bfloat16), "grp", axis=0, tiled=False)
+    gain_one = packed[:, :own_gains].reshape(D).astype(jnp.float32)
+    gain_two = packed[:, own_gains : 2 * own_gains].reshape(D).astype(jnp.float32)
+    all_ids = packed[:, 2 * own_gains :].astype(jnp.int32).reshape(group * own_rows)
     group_rows = all_ids.shape[0]
     order = me ^ jnp.arange(group, dtype=jnp.int32)
     near_ids = all_ids.reshape(group, own_rows)[order].reshape(group_rows)
@@ -489,13 +584,13 @@
     query_side, key_side = slot_features(near_ids)
     live = (slot_ids[0] >= 0).astype(jnp.bfloat16)
     inputs = tokens[0].astype(jnp.float32)
-    first_normed = layer_norm(inputs, gains[:, 0]).astype(jnp.bfloat16)
+    first_normed = layer_norm(inputs, gain_one).astype(jnp.bfloat16)
     cos_near = cos.reshape(group, own_rows, PAIR)
     sin_near = sin.reshape(group, own_rows, PAIR)
     qkv, stats, attended_near, attended_here = [], [], [], []
     for pair in range(pairs):
-        pieces = project(me_list, first_normed, w_in, cos_near, sin_near, pair, group)
-        qkv.append(swap_heads(pieces, group).reshape(group_rows, 3 * PAIR))
+        pieces = project(me_list, first_normed, w_pairs[pair], cos_near, sin_near, group)
+        qkv.append(jnp.concatenate(swap_heads(pieces, group), axis=0))
     for pair in range(pairs):
         mixed, stat = attend(qkv[pair], query_side, key_side)
         stats.append(stat)
@@ -503,7 +598,7 @@
         attended_here.append(swap_heads(mixed.reshape(group, own_rows, PAIR), group))
     attended = place(me_list, attended_here, 1, group)
     middle = inputs + product(attended, w_out)
-    second_normed = layer_norm(middle, gains[:, 1]).astype(jnp.bfloat16)
+    second_normed = layer_norm(middle, gain_two).astype(jnp.bfloat16)
     gate_up = product(second_normed, w_up)
     gate = gate_up[:, :FF]
     upward = gate_up[:, FF_WIDE : FF_WIDE + FF]
@@ -516,26 +611,51 @@
         jnp.bfloat16
     )
     grad_second = against(grad_gate_up, w_up)
-    _, second_back = jax.vjp(lambda v: layer_norm(v, gains[:, 1]), middle)
+    _, second_back = jax.vjp(lambda v: layer_norm(v, gain_two), middle)
     (grad_from_norm,) = second_back(grad_second)
     grad_middle = grad_top.astype(jnp.float32) + grad_from_norm
     grad_branch = grad_middle.astype(jnp.bfloat16)
-    total_down = reduce_weight(hidden, grad_top, core, group, far)
-    total_up = joined_halves(reduce_weight(second_normed, grad_gate_up, core, group, far))
-    pieces_here = []
+    down_rows, up_rows, out_rows = downproj.shape[0], upproj.shape[0], outproj.shape[0]
+    down_share = core_sum(hidden, grad_top, core)
+    up_share = core_sum(second_normed, grad_gate_up, core)
+    grad_near = []
     for pair in range(pairs):
-        sent = row_product(me_list, grad_branch, w_out, pair, group)
-        grad_near = swap_heads(sent, group).reshape(group_rows, PAIR)
+        sent = row_product(
+            me_list, grad_branch, w_out, pair, group, (down_share,) if pair == 0 else ()
+        )
+        grad_near.append(jnp.concatenate(swap_heads(sent, group), axis=0))
+    down_halves = group_first(down_share, group)
+    out_share = core_sum(attended, grad_branch, core)
+    waits = [(*down_halves, up_share)]
+    down_half = group_second(down_halves, group)
+    up_halves = group_first(up_share, group)
+    waits.append((down_half, *up_halves, out_share))
+    grads_here = []
+    for pair in range(pairs):
         grads = attend_back(
-            qkv[pair], query_side, key_side, stats[pair], attended_near[pair], grad_near, cos, sin
+            qkv[pair], query_side, key_side, stats[pair], attended_near[pair], grad_near[pair],
+            cos, sin, waits[pair],
         )
-        joined = jnp.concatenate(grads, axis=1).reshape(group, own_rows, 3 * PAIR)
-        pieces_here.append(swap_heads(joined, group))
-    total_out = reduce_weight(attended, grad_branch, core, group, far)
-    grad_projected = place(me_list, pieces_here, 3, group)
-    total_in = reduce_weight(first_normed, grad_projected, core, group, far)
-    grad_first = against(grad_projected, w_in)
-    _, first_back = jax.vjp(lambda v: layer_norm(v, gains[:, 0]), inputs)
+        grads_here.append(swap_heads(grads.reshape(group, own_rows, 3 * PAIR), group))
+    up_half = group_second(up_halves, group)
+    down_chunk = far_scatter(down_half, far)
+    out_halves = group_first(out_share, group)
+    waits = [(down_chunk, *out_halves), ()]
+    in_shares, grad_first = [], 0.0
+    for pair in range(pairs):
+        grad_projected = place(me_list, [grads_here[pair]], 3, group, waits[pair])
+        in_shares.append(core_sum(first_normed, grad_projected, core))
+        grad_first = grad_first + against(grad_projected, w_pairs[pair])
+    up_chunk = far_scatter(up_half, far)
+    out_chunk = far_scatter(group_second(out_halves, group), far)
+    in_chunks = [
+        far_scatter(group_second(group_first(share, group), group), far) for share in in_shares
+    ]
+    total_down = finished(down_chunk, down_rows, core, far)
+    total_up = joined_halves(finished(up_chunk, up_rows, core, far))
+    total_out = finished(out_chunk, out_rows, core, far)
+    total_in = merged_columns([finished(chunk, inproj.shape[0], core, far) for chunk in in_chunks])
+    _, first_back = jax.vjp(lambda v: layer_norm(v, gain_one), inputs)
     (grad_inputs,) = first_back(grad_first)
     input_grad = (grad_middle + grad_inputs).astype(jnp.bfloat16)
     low_in = inproj.astype(jnp.bfloat16).astype(jnp.float32)

time: 652 us -> 985 us (1.51)
  Pallas kernels: 86 us -> 434 us
  waiting for transfers between devices: 281 us -> 170 us
  starting transfers between devices: 65.3 us -> 120 us
  local copies, waits for them, and re-layouts: 36.1 us -> 61.4 us
  blocking collectives: 17.6 us -> 28.9 us
    pallas_call x6 -> x10, Pallas kernels: 53.5 us -> 401 us  [the longest x3 260 us: gather_rows(): pl.pallas_call(kernel, in_specs=[pl.BlockSpec(memory_space=pltpu.SMEM)] +...]
    ppermute x40 -> x111, starting transfers between devices: 33.3 us -> 120 us  [exchange(): return lax.ppermute(array, axis, [(i, i ^ mask) for i in range(size)])]
    all_gather x4 -> x2, waiting for transfers between devices: 79.8 us -> 0.02 us  [gather_weight(): lax.all_gather(own_half(weight, core).astype(jnp.bfloat16), ('grp', 'core...]
    ppermute x24 -> x0, starting transfers between devices: 31.8 us -> none  [swap_heads(): lax.ppermute(pieces[step], 'grp', [(i, i ^ step) for i in range(group)])]
    ppermute x24 -> x0, waiting for transfers between devices: 17.9 us -> none  [swap_heads(): lax.ppermute(pieces[step], 'grp', [(i, i ^ step) for i in range(group)])]
    unnamed x96 -> x249, local copies, waits for them, and re-layouts: 11.2 us -> 28.3 us
    ppermute x40 -> x111, waiting for transfers between devices: 183 us -> 169 us  [exchange(): return lax.ppermute(array, axis, [(i, i ^ mask) for i in range(size)])]
    all_gather x2 -> x1, blocking collectives: 17.6 us -> 28.9 us  [local(): lax.all_gather(packed.astype(jnp.bfloat16), 'grp', axis=0, tiled=False)]
  transfers between devices with their start and end apart: 68 -> 113, of which waited for: 38 -> 42; matrix products, arithmetic and copies ran while one was open for 18% -> 14% of each run, Pallas kernels for 13% -> 44%
where the time goes in v3:
time: 985 us; the launch traced here: 981 us
  Pallas kernels  434 us (44%)
  waiting for transfers between devices  170 us (17%)
  starting transfers between devices  120 us (12%)
  other arithmetic  78.9 us (8%)
  matrix products  71.8 us (7%)
  local copies, waits for them, and re-layouts  61.4 us (6%)
  blocking collectives  28.9 us (3%)
  between operations  16.7 us (2%)
    pallas_call x3, Pallas kernels, gather_rows(): pl.pallas_call(kernel, in_specs=[pl.BlockSpec(memory_space=pltpu.SMEM)] +...  260 us
    ppermute x111, waiting for transfers between devices, exchange(): return lax.ppermute(array, axis, [(i, i ^ mask) for i in range(size)])  169 us
    ppermute x111, starting transfers between devices, exchange(): return lax.ppermute(array, axis, [(i, i ^ mask) for i in range(size)])  120 us
    pallas_call x3, Pallas kernels, place(): pl.pallas_call(kernel, in_specs=[pl.BlockSpec(memory_space=pltpu.SMEM)] +...  98.9 us
    pallas_call x2, Pallas kernels, attend_back(): pl.pallas_call(skipping(attend_back_kernel, 12, len(after)), grid=(rows /...  34.1 us
    dot_general x4, matrix products, against(): lax.dot_general(left, right, (((1,), (1,)), ((), ())), preferred_element_...  30.6 us
    all_gather x1, blocking collectives, local(): lax.all_gather(packed.astype(jnp.bfloat16), 'grp', axis=0, tiled=False)  28.9 us
    unnamed x249, local copies, waits for them, and re-layouts  28.3 us
  transfers between devices with their start and end apart: 113, of which 42 were waited for; matrix products, arithmetic and copies ran while one was open for 14% of the time, Pallas kernels for 44%

profile of v3, /device:TPU:0, one launch (start us, length us, event | category | flops | bytes accessed | tf_op | source)
XLA Modules:
  0.0 981.0 jit_solution(10679638300791992932)
XLA Ops:
  32.9 28.9 %all-gather = bf16[4,1,896]{2,1,0:T(2,128)(2,1)S(1)} all-gather(bf16[1,1,896]{2,1,0:T(2,128)(2,1)S(1)} %maximum_bitcast_fusion), channel_id=1, replica_groups=mesh['grp'=4,'far'=4,'core'=2] {'grp'}, dimensions={0}, use_global_device_ids=true | all-gather | bytes 8960 | tf_op jit(solution)/shard_map/all_gather | solution.py:575
  81.0 5.1 fusion.43
  87.9 4.3 fusion.42
  93.9 5.4 collective-permute-done.2.refs_3_
  104.1 97.1 %gather_rows.3.wq_ref.wk_ref.wv_ref = bf16[1024,1536]{1,0:T(8,128)(2,1)} custom-call(s32[2]{0:T(128)} %pad_add_fusion.index_ref, bf16[128,1536]{1,0:T(8,128)(2,1)} %copy-done.33, bf16[128,1536]{1,0:T(8,128)(2,1)} %copy-done.42, bf16[128,1536]{1,0:T(8,128)(2,1)} %copy-done.43, bf16[64,1536]{1,0:T(8,128)(2,1)} %copy-done.65, bf16[64,1536]{1,0:T(8,128)(2,1)} %copy-done.66, ...), custom_call_target="tpu_custom_call" | custom-call | tf_op jit(solution)/shard_map/gather_rows/pallas_call | solution.py:226
  201.3 5.9 project.2
  216.7 97.2 %gather_rows.4.wq_ref.wk_ref.wv_ref = bf16[1024,1536]{1,0:T(8,128)(2,1)} custom-call(s32[2]{0:T(128)} %pad_add_fusion.index_ref, bf16[128,1536]{1,0:T(8,128)(2,1)} %copy-done.32, bf16[128,1536]{1,0:T(8,128)(2,1)} %copy-done.40, bf16[128,1536]{1,0:T(8,128)(2,1)} %copy-done.41, bf16[64,1536]{1,0:T(8,128)(2,1)} %copy-done.63, bf16[64,1536]{1,0:T(8,128)(2,1)} %copy-done.64, ...), custom_call_target="tpu_custom_call" | custom-call | tf_op jit(solution)/shard_map/gather_rows/pallas_call | solution.py:226
  313.9 5.9 project.3
  327.9 10.9 %collective-permute-done.32.refs_3_ = bf16[64,1024]{1,0:T(8,128)(2,1)S(1)} collective-permute-done((bf16[64,1024]{1,0:T(8,128)(2,1)S(1)}, bf16[64,1024]{1,0:T(8,128)(2,1)S(1)}, u32[]{:S(2)}, u32[]{:S(2)}) %collective-permute-start.32) | collective-permute-done | bytes 131104 | tf_op jit(solution)/shard_map/ppermute | solution.py:194
  341.8 10.3 %attend.2 = (bf16[1536,128]{1,0:T(8,128)(2,1)}, f32[1536,128]{1,0:T(8,128)}) custom-call(bf16[1536,384]{1,0:T(8,128)(2,1)} %pad_maximum_fusion.3.q_ref.k_ref.v_ref.own_v_ref.refs_0_.refs_1_.refs_2_, bf16[1536,384]{1,0:T(8,128)(2,1)} %pad_maximum_fusion.3.q_ref.k_ref.v_ref.own_v_ref.refs_0_.refs_1_.refs_2_, ...), custom_call_target="tpu_custom_call" | custom-call | tf_op jit(solution)/shard_map/attend/pallas_call | solution.py:281
  353.8 10.5 %attend.3 = (bf16[1536,128]{1,0:T(8,128)(2,1)}, f32[1536,128]{1,0:T(8,128)}) custom-call(bf16[1536,384]{1,0:T(8,128)(2,1)} %pad_maximum_fusion.4.q_ref.k_ref.v_ref.own_v_ref.refs_0_.refs_1_.refs_2_, bf16[1536,384]{1,0:T(8,128)(2,1)} %pad_maximum_fusion.4.q_ref.k_ref.v_ref.own_v_ref.refs_0_.refs_1_.refs_2_, ...), custom_call_target="tpu_custom_call" | custom-call | tf_op jit(solution)/shard_map/attend/pallas_call | solution.py:281
  373.6 65.4 %gather_rows.5.refs_2_ = bf16[1024,1024]{1,0:T(8,128)(2,1)} custom-call(s32[2]{0:T(128)} %pad_add_fusion.index_ref, bf16[128,1024]{1,0:T(8,128)(2,1)} %copy-done.37, bf16[128,1024]{1,0:T(8,128)(2,1)} %copy-done.47, bf16[128,1024]{1,0:T(8,128)(2,1)} %copy-done.48, bf16[64,1024]{1,0:T(8,128)(2,1)} %copy-done.71, bf16[64,1024]{1,0:T(8,128)(2,1)} %copy-done.72, ...), custom_call_target="tpu_custom_call" | custom-call | tf_op jit(solution)/shard_map/gather_rows/pallas_call | solution.py:226
  439.8 25.0 %place.3 = bf16[384,1024]{1,0:T(8,128)(2,1)} custom-call(s32[1]{0:T(128)} %bitcast.1.me_ref.refs_0_, bf16[384,128]{1,0:T(8,128)(2,1)} %get-tuple-element.153.refs_0_, bf16[384,128]{1,0:T(8,128)(2,1)} %copy-done.75, bf16[384,128]{1,0:T(8,128)(2,1)} %copy-done.76, bf16[384,128]{1,0:T(8,128)(2,1)} %copy-done.77, bf16[384,128]{1,0:T(8,128)(2,1)} %get-tuple-element.149.refs_4_, ...), custom_call_target="tpu_custom_call" | custom-call | tf_op jit(solution)/shard_map/place/pallas_call | solution.py:182
  468.1 11.2 %fusion.140 = f32[384,5376]{1,0:T(8,128)} fusion(bf16[1024,5376]{1,0:T(8,128)(2,1)} %all-gather.4.cloned.1.call-done, f32[384,1024]{1,0:T(8,128)S(1)} %get-tuple-element.172, f32[1024]{0:T(1024)S(1)} %bitcast.254, f32[384]{0:T(512)S(1)} %fusion.110, f32[384]{0:T(512)S(1)} %broadcast_multiply_fusion), kind=kOutput, calls=%fused_computation.450 | convolution fusion | flops 4229431296 | bytes 20847616 | tf_op jit(solution)/shard_map/dot_general | solution.py:402
  479.3 16.3 %add_convert_fusion.2 = (bf16[384,2624]{1,0:T(8,128)(2,1)}, f32[384,2624]{1,0:T(8,128)}, f32[384,2624]{1,0:T(8,128)}) fusion(f32[384,5376]{1,0:T(8,128)} %fusion.140, bf16[384,1024]{1,0:T(8,128)(2,1)S(1)} %bitcast_multiply_fusion, bf16[2624,1024]{1,0:T(8,128)(2,1)} %all-gather.6.cloned.1.call-done), kind=kOutput, calls=%fused_computation.23 | convolution fusion | flops 2137153536 | bytes 24297472 | tf_op jit(solution)/shard_map/dot_general | solution.py:412
  495.6 6.0 multiply_convert_fusion
  501.6 9.8 multiply_reduce_fusion.2
  513.7 4.3 row_product.3
  523.9 5.4 convolution_convert_fusion
  541.1 4.0 collective-permute-done.56
  550.6 3.4 collective-permute-start.93
  561.3 3.4 collective-permute-start.94
  570.0 4.3 collective-permute-done.44
  575.6 6.6 collective-permute-done.43
  586.0 3.8 collective-permute-done.49
  590.7 3.4 collective-permute-start.53
  595.2 4.2 row_product.2
  599.4 8.9 collective-permute-done.52
  626.0 5.8 add_convert_fusion.refs_14_
  637.9 4.0 multiply_subtract_fusion.2
  641.9 17.0 %attend_back.2 = bf16[1536,384]{1,0:T(8,128)(2,1)} custom-call(bf16[1536,384]{1,0:T(8,128)(2,1)} %pad_maximum_fusion.3.q_ref.k_ref.v_ref.own_v_ref.refs_0_.refs_1_.refs_2_, bf16[1536,384]{1,0:T(8,128)(2,1)} %pad_maximum_fusion.3.q_ref.k_ref.v_ref.own_v_ref.refs_0_.refs_1_.refs_2_, ...), custom_call_target="tpu_custom_call" | custom-call | tf_op jit(solution)/shard_map/attend_back/pallas_call | solution.py:380
  666.7 4.1 collective-permute-done.46.refs_1_
  670.8 10.0 %collective-permute-done.47.refs_2_ = bf16[384,384]{1,0:T(8,128)(2,1)S(1)} collective-permute-done((bf16[384,384]{1,0:T(8,128)(2,1)S(1)}, bf16[384,384]{1,0:T(8,128)(2,1)S(1)}, u32[]{:S(2)}, u32[]{:S(2)}) %collective-permute-start.47) | collective-permute-done | bytes 294944 | tf_op jit(solution)/shard_map/ppermute | solution.py:194
  682.1 36.9 %place.4 = bf16[384,1536]{1,0:T(8,128)(2,1)} custom-call(s32[1]{0:T(128)} %bitcast.1.me_ref.refs_0_, bf16[384,384]{1,0:T(8,128)(2,1)} %get-tuple-element.96.refs_0_, bf16[384,384]{1,0:T(8,128)(2,1)} %copy-done.55, bf16[384,384]{1,0:T(8,128)(2,1)} %copy-done.57, bf16[384,384]{1,0:T(8,128)(2,1)} %copy-done.59, bf16[656,128]{1,0:T(8,128)(2,1)} %copy-done.34, ...), custom_call_target="tpu_custom_call" | custom-call | tf_op jit(solution)/shard_map/place/pallas_call | solution.py:182
  719.1 3.5 convolution_convert_fusion.3
  727.5 17.1 %attend_back.3 = bf16[1536,384]{1,0:T(8,128)(2,1)} custom-call(bf16[1536,384]{1,0:T(8,128)(2,1)} %pad_maximum_fusion.4.q_ref.k_ref.v_ref.own_v_ref.refs_0_.refs_1_.refs_2_, bf16[1536,384]{1,0:T(8,128)(2,1)} %pad_maximum_fusion.4.q_ref.k_ref.v_ref.own_v_ref.refs_0_.refs_1_.refs_2_, ...), custom_call_target="tpu_custom_call" | custom-call | tf_op jit(solution)/shard_map/attend_back/pallas_call | solution.py:380
  752.1 4.6 collective-permute-done.62.refs_1_
  757.8 4.0 collective-permute-done.63.refs_2_
  764.2 36.9 %place.5 = bf16[384,1536]{1,0:T(8,128)(2,1)} custom-call(s32[1]{0:T(128)} %bitcast.1.me_ref.refs_0_, bf16[384,384]{1,0:T(8,128)(2,1)} %get-tuple-element.100.refs_0_, bf16[384,384]{1,0:T(8,128)(2,1)} %collective-permute-done.62.refs_1_, bf16[384,384]{1,0:T(8,128)(2,1)} %copy-done.56, bf16[384,384]{1,0:T(8,128)(2,1)} %copy-done.58), custom_call_target="tpu_custom_call" | custom-call | tf_op jit(solution)/shard_map/place/pallas_call | solution.py:182
  815.6 6.0 collective-permute-done.66
  836.8 10.9 %collective-permute-start.70 = (bf16[64,768]{1,0:T(8,128)(2,1)S(1)}, bf16[64,768]{1,0:T(8,128)(2,1)S(1)}, u32[]{:S(2)}, u32[]{:S(2)}) collective-permute-start(bf16[64,768]{1,0:T(8,128)(2,1)S(1)} %get-tuple-element.135), channel_id=1, source_target_pairs={{0,2},{2,0},{4,6},{6,4},{1,3},{3,1},{5,7},{7,5},{8,10},{10,8},{12,... | collective-permute-start | bytes 294920 | tf_op jit(solution)/shard_map/ppermute | solution.py:194
  848.7 17.0 %collective-permute-done.71 = bf16[64,768]{1,0:T(8,128)(2,1)S(1)} collective-permute-done((bf16[64,768]{1,0:T(8,128)(2,1)S(1)}, bf16[64,768]{1,0:T(8,128)(2,1)S(1)}, u32[]{:S(2)}, u32[]{:S(2)}) %collective-permute-start.71) | collective-permute-done | bytes 98336 | tf_op jit(solution)/shard_map/ppermute | solution.py:194
  873.3 4.2 collective-permute-done.74
  877.7 7.3 collective-permute-done.103
  885.0 21.5 %collective-permute-done.104 = bf16[64,2688]{1,0:T(8,128)(2,1)S(1)} collective-permute-done((bf16[64,2688]{1,0:T(8,128)(2,1)S(1)}, bf16[64,2688]{1,0:T(8,128)(2,1)S(1)}, u32[]{:S(2)}, u32[]{:S(2)}) %collective-permute-start.104) | collective-permute-done | bytes 344096 | tf_op jit(solution)/shard_map/ppermute | solution.py:194
  910.0 9.1 collective-permute-done.78
  951.7 11.2 %multiply_subtract_fusion = (f32[256,5248]{1,0:T(8,128)}, f32[256,5248]{1,0:T(8,128)}, f32[256,5248]{1,0:T(8,128)}, f32[256]{0:T(256)S(1)}) fusion(f32[256,5248]{1,0:T(8,128)S(1)} %bitcast.241, f32[256,2624]{1,0:T(8,128)S(1)} %get-tuple-element.49, f32[256,2624]{1,0:T(8,128)S(1)} %get-tuple-element.48, f32[256,5248]{1,0:T(8,128)} %param.33, ...), kind=kLoop, calls=%fused_computation.15 | loop fusion | flops 26869504 | bytes 37618688 | tf_op jit(solution)/shard_map/sub | solution.py:532
  966.9 6.3 multiply_subtract_fusion.1
  (627 shorter events, 260.3 us)
Async XLA Ops:
  7.2 460.9 %all-gather.4.cloned.1.call-start = ((), (), s32[]{:S(2)}) async-start(), calls=%async_computation | async-start | bytes 12386304 | tf_op jit(solution)/shard_map/all_gather | solution.py:423
  12.6 466.6 %all-gather.6.cloned.1.call-start = ((), (), s32[]{:S(2)}) async-start(), calls=%async_computation.1 | async-start | bytes 6045696 | tf_op jit(solution)/shard_map/all_gather | solution.py:423
  25.2 62.2 %collective-permute-start = (bf16[128,1536]{1,0:T(8,128)(2,1)S(1)}, bf16[128,1536]{1,0:T(8,128)(2,1)S(1)}, u32[]{:S(2)}, u32[]{:S(2)}) collective-permute-start(bf16[128,1536]{1,0:T(8,128)(2,1)S(1)} %dynamic-slice_convert_fusion.2.refs_0_), channel_id=1, source_target_pairs={{0,8},{8,0},{16,24},{24,16},{1,9},{9,1},{17,25},{25,17},{2,10},{10... | collective-permute-start | bytes 1179656 | tf_op jit(solution)/shard_map/ppermute | solution.py:194
  28.3 59.1 %collective-permute-start.1 = (bf16[128,1536]{1,0:T(8,128)(2,1)S(1)}, bf16[128,1536]{1,0:T(8,128)(2,1)S(1)}, u32[]{:S(2)}, u32[]{:S(2)}) collective-permute-start(bf16[128,1536]{1,0:T(8,128)(2,1)S(1)} %dynamic-slice_convert_fusion.2.refs_0_), channel_id=1, source_target_pairs={{0,16},{8,24},{16,0},{24,8},{1,17},{9,25},{17,1},{25,9},{2,18},{10... | collective-permute-start | bytes 1179656 | tf_op jit(solution)/shard_map/ppermute | solution.py:194
  29.8 62.4 %collective-permute-start.4 = (bf16[128,1536]{1,0:T(8,128)(2,1)S(1)}, bf16[128,1536]{1,0:T(8,128)(2,1)S(1)}, u32[]{:S(2)}, u32[]{:S(2)}) collective-permute-start(bf16[128,1536]{1,0:T(8,128)(2,1)S(1)} %dynamic-slice_convert_fusion.2.refs_0_), channel_id=1, source_target_pairs={{0,1},{1,0},{2,3},{3,2},{4,5},{5,4},{6,7},{7,6},{8,9},{9,8},{10,11... | collective-permute-start | bytes 1179656 | tf_op jit(solution)/shard_map/ppermute | solution.py:194
  29.9 63.0 %collective-permute-start.15 = (bf16[128,1536]{1,0:T(8,128)(2,1)S(1)}, bf16[128,1536]{1,0:T(8,128)(2,1)S(1)}, u32[]{:S(2)}, u32[]{:S(2)}) collective-permute-start(bf16[128,1536]{1,0:T(8,128)(2,1)S(1)} %dynamic-slice_convert_fusion.1.refs_0_), channel_id=1, source_target_pairs={{0,8},{8,0},{16,24},{24,16},{1,9},{9,1},{17,25},{25,17},{2,10},{10... | collective-permute-start | bytes 1179656 | tf_op jit(solution)/shard_map/ppermute | solution.py:194
  30.5 63.3 %collective-permute-start.16 = (bf16[128,1536]{1,0:T(8,128)(2,1)S(1)}, bf16[128,1536]{1,0:T(8,128)(2,1)S(1)}, u32[]{:S(2)}, u32[]{:S(2)}) collective-permute-start(bf16[128,1536]{1,0:T(8,128)(2,1)S(1)} %dynamic-slice_convert_fusion.1.refs_0_), channel_id=1, source_target_pairs={{0,16},{8,24},{16,0},{24,8},{1,17},{9,25},{17,1},{25,9},{2,18},{10... | collective-permute-start | bytes 1179656 | tf_op jit(solution)/shard_map/ppermute | solution.py:194
  93.8 114.8 %collective-permute-start.19 = (bf16[128,1536]{1,0:T(8,128)(2,1)S(1)}, bf16[128,1536]{1,0:T(8,128)(2,1)S(1)}, u32[]{:S(2)}, u32[]{:S(2)}) collective-permute-start(bf16[128,1536]{1,0:T(8,128)(2,1)S(1)} %dynamic-slice_convert_fusion.1.refs_0_), channel_id=1, source_target_pairs={{0,1},{1,0},{2,3},{3,2},{4,5},{5,4},{6,7},{7,6},{8,9},{9,8},{10,11... | collective-permute-start | bytes 1179656 | tf_op jit(solution)/shard_map/ppermute | solution.py:194
  99.2 111.6 %collective-permute-start.20 = (bf16[128,1536]{1,0:T(8,128)(2,1)S(1)}, bf16[128,1536]{1,0:T(8,128)(2,1)S(1)}, u32[]{:S(2)}, u32[]{:S(2)}) collective-permute-start(bf16[128,1536]{1,0:T(8,128)(2,1)S(1)} %collective-permute-done.15.refs_1_), channel_id=1, source_target_pairs={{0,1},{1,0},{2,3},{3,2},{4,5},{5,4},{6,7},{7,6},{8,9},{9,8},{10,11... | collective-permute-start | bytes 1179656 | tf_op jit(solution)/shard_map/ppermute | solution.py:194
  99.5 111.9 %collective-permute-start.21 = (bf16[128,1536]{1,0:T(8,128)(2,1)S(1)}, bf16[128,1536]{1,0:T(8,128)(2,1)S(1)}, u32[]{:S(2)}, u32[]{:S(2)}) collective-permute-start(bf16[128,1536]{1,0:T(8,128)(2,1)S(1)} %collective-permute-done.16.refs_2_), channel_id=1, source_target_pairs={{0,1},{1,0},{2,3},{3,2},{4,5},{5,4},{6,7},{7,6},{8,9},{9,8},{10,11... | collective-permute-start | bytes 1179656 | tf_op jit(solution)/shard_map/ppermute | solution.py:194
  102.0 107.5 %collective-permute-start.17 = (bf16[64,1536]{1,0:T(8,128)(2,1)S(1)}, bf16[64,1536]{1,0:T(8,128)(2,1)S(1)}, u32[]{:S(2)}, u32[]{:S(2)}) collective-permute-start(bf16[64,1536]{1,0:T(8,128)(2,1)S(1)} %slice.472), channel_id=1, source_target_pairs={{0,8},{8,0},{16,24},{24,16},{1,9},{9,1},{17,25},{25,17},{2,10},{10... | collective-permute-start | bytes 589832 | tf_op jit(solution)/shard_map/ppermute | solution.py:194
  103.4 107.5 %collective-permute-start.18 = (bf16[64,1536]{1,0:T(8,128)(2,1)S(1)}, bf16[64,1536]{1,0:T(8,128)(2,1)S(1)}, u32[]{:S(2)}, u32[]{:S(2)}) collective-permute-start(bf16[64,1536]{1,0:T(8,128)(2,1)S(1)} %slice.473), channel_id=1, source_target_pairs={{0,16},{8,24},{16,0},{24,8},{1,17},{9,25},{17,1},{25,9},{2,18},{10... | collective-permute-start | bytes 589832 | tf_op jit(solution)/shard_map/ppermute | solution.py:194
  208.6 112.6 %collective-permute-start.30 = (bf16[128,1024]{1,0:T(8,128)(2,1)S(1)}, bf16[128,1024]{1,0:T(8,128)(2,1)S(1)}, u32[]{:S(2)}, u32[]{:S(2)}) collective-permute-start(bf16[128,1024]{1,0:T(8,128)(2,1)S(1)} %dynamic-slice_convert_fusion.3.refs_0_), channel_id=1, source_target_pairs={{0,8},{8,0},{16,24},{24,16},{1,9},{9,1},{17,25},{25,17},{2,10},{10... | collective-permute-start | bytes 786440 | tf_op jit(solution)/shard_map/ppermute | solution.py:194
  209.5 113.1 %collective-permute-start.31 = (bf16[128,1024]{1,0:T(8,128)(2,1)S(1)}, bf16[128,1024]{1,0:T(8,128)(2,1)S(1)}, u32[]{:S(2)}, u32[]{:S(2)}) collective-permute-start(bf16[128,1024]{1,0:T(8,128)(2,1)S(1)} %dynamic-slice_convert_fusion.3.refs_0_), channel_id=1, source_target_pairs={{0,16},{8,24},{16,0},{24,8},{1,17},{9,25},{17,1},{25,9},{2,18},{10... | collective-permute-start | bytes 786440 | tf_op jit(solution)/shard_map/ppermute | solution.py:194
  211.4 112.7 %collective-permute-start.11 = (bf16[384,384]{1,0:T(8,128)(2,1)S(1)}, bf16[384,384]{1,0:T(8,128)(2,1)S(1)}, u32[]{:S(2)}, u32[]{:S(2)}) collective-permute-start(bf16[384,384]{1,0:T(8,128)(2,1)S(1)} %get-tuple-element.106), channel_id=1, source_target_pairs={{0,24},{8,16},{16,8},{24,0},{1,25},{9,17},{17,9},{25,1},{2,26},{10... | collective-permute-start | bytes 884744 | tf_op jit(solution)/shard_map/ppermute | solution.py:194
  214.5 110.4 %collective-permute-start.10 = (bf16[384,384]{1,0:T(8,128)(2,1)S(1)}, bf16[384,384]{1,0:T(8,128)(2,1)S(1)}, u32[]{:S(2)}, u32[]{:S(2)}) collective-permute-start(bf16[384,384]{1,0:T(8,128)(2,1)S(1)} %get-tuple-element.107), channel_id=1, source_target_pairs={{0,16},{8,24},{16,0},{24,8},{1,17},{9,25},{17,1},{25,9},{2,18},{10... | collective-permute-start | bytes 884744 | tf_op jit(solution)/shard_map/ppermute | solution.py:194
  216.0 110.3 %collective-permute-start.9 = (bf16[384,384]{1,0:T(8,128)(2,1)S(1)}, bf16[384,384]{1,0:T(8,128)(2,1)S(1)}, u32[]{:S(2)}, u32[]{:S(2)}) collective-permute-start(bf16[384,384]{1,0:T(8,128)(2,1)S(1)} %get-tuple-element.108), channel_id=1, source_target_pairs={{0,8},{8,0},{16,24},{24,16},{1,9},{9,1},{17,25},{25,17},{2,10},{10... | collective-permute-start | bytes 884744 | tf_op jit(solution)/shard_map/ppermute | solution.py:194
  321.2 18.4 %collective-permute-start.26 = (bf16[384,384]{1,0:T(8,128)(2,1)S(1)}, bf16[384,384]{1,0:T(8,128)(2,1)S(1)}, u32[]{:S(2)}, u32[]{:S(2)}) collective-permute-start(bf16[384,384]{1,0:T(8,128)(2,1)S(1)} %get-tuple-element.102), channel_id=1, source_target_pairs={{0,24},{8,16},{16,8},{24,0},{1,25},{9,17},{17,9},{25,1},{2,26},{10... | collective-permute-start | bytes 884744 | tf_op jit(solution)/shard_map/ppermute | solution.py:194
  338.8 25.5 %collective-permute-start.34 = (bf16[128,1024]{1,0:T(8,128)(2,1)S(1)}, bf16[128,1024]{1,0:T(8,128)(2,1)S(1)}, u32[]{:S(2)}, u32[]{:S(2)}) collective-permute-start(bf16[128,1024]{1,0:T(8,128)(2,1)S(1)} %dynamic-slice_convert_fusion.3.refs_0_), channel_id=1, source_target_pairs={{0,1},{1,0},{2,3},{3,2},{4,5},{5,4},{6,7},{7,6},{8,9},{9,8},{10,11... | collective-permute-start | bytes 786440 | tf_op jit(solution)/shard_map/ppermute | solution.py:194
  339.6 27.5 %collective-permute-start.35 = (bf16[128,1024]{1,0:T(8,128)(2,1)S(1)}, bf16[128,1024]{1,0:T(8,128)(2,1)S(1)}, u32[]{:S(2)}, u32[]{:S(2)}) collective-permute-start(bf16[128,1024]{1,0:T(8,128)(2,1)S(1)} %collective-permute-done.30.refs_1_), channel_id=1, source_target_pairs={{0,1},{1,0},{2,3},{3,2},{4,5},{5,4},{6,7},{7,6},{8,9},{9,8},{10,11... | collective-permute-start | bytes 786440 | tf_op jit(solution)/shard_map/ppermute | solution.py:194
  339.6 28.5 %collective-permute-start.36 = (bf16[128,1024]{1,0:T(8,128)(2,1)S(1)}, bf16[128,1024]{1,0:T(8,128)(2,1)S(1)}, u32[]{:S(2)}, u32[]{:S(2)}) collective-permute-start(bf16[128,1024]{1,0:T(8,128)(2,1)S(1)} %collective-permute-done.31.refs_2_), channel_id=1, source_target_pairs={{0,1},{1,0},{2,3},{3,2},{4,5},{5,4},{6,7},{7,6},{8,9},{9,8},{10,11... | collective-permute-start | bytes 786440 | tf_op jit(solution)/shard_map/ppermute | solution.py:194
  340.1 29.6 %collective-permute-start.37 = (bf16[64,1024]{1,0:T(8,128)(2,1)S(1)}, bf16[64,1024]{1,0:T(8,128)(2,1)S(1)}, u32[]{:S(2)}, u32[]{:S(2)}) collective-permute-start(bf16[64,1024]{1,0:T(8,128)(2,1)S(1)} %collective-permute-done.32.refs_3_), channel_id=1, source_target_pairs={{0,1},{1,0},{2,3},{3,2},{4,5},{5,4},{6,7},{7,6},{8,9},{9,8},{10,11... | collective-permute-start | bytes 393224 | tf_op jit(solution)/shard_map/ppermute | solution.py:194
  340.2 30.4 %collective-permute-start.38 = (bf16[64,1024]{1,0:T(8,128)(2,1)S(1)}, bf16[64,1024]{1,0:T(8,128)(2,1)S(1)}, u32[]{:S(2)}, u32[]{:S(2)}) collective-permute-start(bf16[64,1024]{1,0:T(8,128)(2,1)S(1)} %collective-permute-done.33.refs_4_), channel_id=1, source_target_pairs={{0,1},{1,0},{2,3},{3,2},{4,5},{5,4},{6,7},{7,6},{8,9},{9,8},{10,11... | collective-permute-start | bytes 393224 | tf_op jit(solution)/shard_map/ppermute | solution.py:194
  367.1 72.0 %collective-permute-start.13 = (bf16[384,128]{1,0:T(8,128)(2,1)S(1)}, bf16[384,128]{1,0:T(8,128)(2,1)S(1)}, u32[]{:S(2)}, u32[]{:S(2)}) collective-permute-start(bf16[384,128]{1,0:T(8,128)(2,1)S(1)} %get-tuple-element.151), channel_id=1, source_target_pairs={{0,16},{8,24},{16,0},{24,8},{1,17},{9,25},{17,1},{25,9},{2,18},{10... | collective-permute-start | bytes 294920 | tf_op jit(solution)/shard_map/ppermute | solution.py:194
  368.1 71.0 %collective-permute-start.14 = (bf16[384,128]{1,0:T(8,128)(2,1)S(1)}, bf16[384,128]{1,0:T(8,128)(2,1)S(1)}, u32[]{:S(2)}, u32[]{:S(2)}) collective-permute-start(bf16[384,128]{1,0:T(8,128)(2,1)S(1)} %get-tuple-element.150), channel_id=1, source_target_pairs={{0,24},{8,16},{16,8},{24,0},{1,25},{9,17},{17,9},{25,1},{2,26},{10... | collective-permute-start | bytes 294920 | tf_op jit(solution)/shard_map/ppermute | solution.py:194
  369.7 69.4 %collective-permute-start.27 = (bf16[384,128]{1,0:T(8,128)(2,1)}, bf16[384,128]{1,0:T(8,128)(2,1)S(1)}, u32[]{:S(2)}, u32[]{:S(2)}) collective-permute-start(bf16[384,128]{1,0:T(8,128)(2,1)} %get-tuple-element.148), channel_id=1, source_target_pairs={{0,8},{8,0},{16,24},{24,16},{1,9},{9,1},{17,25},{25,17},{2,10},{10... | collective-permute-start | bytes 294920 | tf_op jit(solution)/shard_map/ppermute | solution.py:194
  370.6 68.5 %collective-permute-start.28 = (bf16[384,128]{1,0:T(8,128)(2,1)S(1)}, bf16[384,128]{1,0:T(8,128)(2,1)S(1)}, u32[]{:S(2)}, u32[]{:S(2)}) collective-permute-start(bf16[384,128]{1,0:T(8,128)(2,1)S(1)} %get-tuple-element.147), channel_id=1, source_target_pairs={{0,16},{8,24},{16,0},{24,8},{1,17},{9,25},{17,1},{25,9},{2,18},{10... | collective-permute-start | bytes 294920 | tf_op jit(solution)/shard_map/ppermute | solution.py:194
  371.6 67.6 %collective-permute-start.29 = (bf16[384,128]{1,0:T(8,128)(2,1)S(1)}, bf16[384,128]{1,0:T(8,128)(2,1)S(1)}, u32[]{:S(2)}, u32[]{:S(2)}) collective-permute-start(bf16[384,128]{1,0:T(8,128)(2,1)S(1)} %get-tuple-element.146), channel_id=1, source_target_pairs={{0,24},{8,16},{16,8},{24,0},{1,25},{9,17},{17,9},{25,1},{2,26},{10... | collective-permute-start | bytes 294920 | tf_op jit(solution)/shard_map/ppermute | solution.py:194
  519.2 42.0 %collective-permute-start.59 = (bf16[384,128]{1,0:T(8,128)(2,1)S(1)}, bf16[384,128]{1,0:T(8,128)(2,1)S(1)}, u32[]{:S(2)}, u32[]{:S(2)}) collective-permute-start(bf16[384,128]{1,0:T(8,128)(2,1)S(1)} %get-tuple-element.143), channel_id=1, source_target_pairs={{0,24},{8,16},{16,8},{24,0},{1,25},{9,17},{17,9},{25,1},{2,26},{10... | collective-permute-start | bytes 294920 | tf_op jit(solution)/shard_map/ppermute | solution.py:194
  523.0 31.0 %collective-permute-start.39 = (bf16[2624,512]{1,0:T(8,128)(2,1)S(1)}, bf16[2624,512]{1,0:T(8,128)(2,1)S(1)}, u32[]{:S(2)}, u32[]{:S(2)}) collective-permute-start(bf16[2624,512]{1,0:T(8,128)(2,1)S(1)} %convolution_convert_fusion.1), channel_id=1, source_target_pairs={{0,1},{1,0},{2,3},{3,2},{4,5},{5,4},{6,7},{7,6},{8,9},{9,8},{10,11... | collective-permute-start | bytes 8060936 | tf_op jit(solution)/shard_map/ppermute | solution.py:194
  529.3 96.7 %collective-permute-start.45 = (bf16[1024,2688]{1,0:T(8,128)(2,1)}, bf16[1024,2688]{1,0:T(8,128)(2,1)}, u32[]{:S(2)}, u32[]{:S(2)}) collective-permute-start(bf16[1024,2688]{1,0:T(8,128)(2,1)} %convolution_convert_fusion), channel_id=1, source_target_pairs={{0,1},{1,0},{2,3},{3,2},{4,5},{5,4},{6,7},{7,6},{8,9},{9,8},{10,11... | collective-permute-start | bytes 16515080 | tf_op jit(solution)/shard_map/ppermute | solution.py:194
  635.8 86.8 %collective-permute-start.60 = (bf16[2,128,2688]{2,1,0:T(8,128)(2,1)}, bf16[2,128,2688]{2,1,0:T(8,128)(2,1)}, u32[]{:S(2)}, u32[]{:S(2)}) collective-permute-start(bf16[2,128,2688]{2,1,0:T(8,128)(2,1)} %dynamic-slice_bitcast_fusion.1), channel_id=1, source_target_pairs={{0,16},{8,24},{16,0},{24,8},{1,17},{9,25},{17,1},{25,9},{2,18},{10... | collective-permute-start | bytes 4128776 | tf_op jit(solution)/shard_map/ppermute | solution.py:194
  662.0 18.7 %collective-permute-start.47 = (bf16[384,384]{1,0:T(8,128)(2,1)S(1)}, bf16[384,384]{1,0:T(8,128)(2,1)S(1)}, u32[]{:S(2)}, u32[]{:S(2)}) collective-permute-start(bf16[384,384]{1,0:T(8,128)(2,1)S(1)} %get-tuple-element.94), channel_id=1, source_target_pairs={{0,16},{8,24},{16,0},{24,8},{1,17},{9,25},{17,1},{25,9},{2,18},{10... | collective-permute-start | bytes 884744 | tf_op jit(solution)/shard_map/ppermute | solution.py:194
  663.1 17.6 %collective-permute-start.48 = (bf16[384,384]{1,0:T(8,128)(2,1)S(1)}, bf16[384,384]{1,0:T(8,128)(2,1)S(1)}, u32[]{:S(2)}, u32[]{:S(2)}) collective-permute-start(bf16[384,384]{1,0:T(8,128)(2,1)S(1)} %get-tuple-element.93), channel_id=1, source_target_pairs={{0,24},{8,16},{16,8},{24,0},{1,25},{9,17},{17,9},{25,1},{2,26},{10... | collective-permute-start | bytes 884744 | tf_op jit(solution)/shard_map/ppermute | solution.py:194
  665.5 58.8 %collective-permute-start.61 = (bf16[2,128,2688]{2,1,0:T(8,128)(2,1)}, bf16[2,128,2688]{2,1,0:T(8,128)(2,1)}, u32[]{:S(2)}, u32[]{:S(2)}) collective-permute-start(bf16[2,128,2688]{2,1,0:T(8,128)(2,1)} %dynamic-slice_bitcast_fusion), channel_id=1, source_target_pairs={{0,8},{8,0},{16,24},{24,16},{1,9},{9,1},{17,25},{25,17},{2,10},{10... | collective-permute-start | bytes 4128776 | tf_op jit(solution)/shard_map/ppermute | solution.py:194
  722.6 85.9 %collective-permute-start.65 = (bf16[1024,768]{1,0:T(8,128)(2,1)}, bf16[1024,768]{1,0:T(8,128)(2,1)}, u32[]{:S(2)}, u32[]{:S(2)}) collective-permute-start(bf16[1024,768]{1,0:T(8,128)(2,1)} %convolution_convert_fusion.3), channel_id=1, source_target_pairs={{0,1},{1,0},{2,3},{3,2},{4,5},{5,4},{6,7},{7,6},{8,9},{9,8},{10,11... | collective-permute-start | bytes 4718600 | tf_op jit(solution)/shard_map/ppermute | solution.py:194
  750.3 63.9 %collective-permute-start.98 = (bf16[128,2688]{1,0:T(8,128)(2,1)S(1)}, bf16[128,2688]{1,0:T(8,128)(2,1)S(1)}, u32[]{:S(2)}, u32[]{:S(2)}) collective-permute-start(bf16[128,2688]{1,0:T(8,128)(2,1)S(1)} %dynamic-slice_bitcast_fusion.3), channel_id=1, source_target_pairs={{0,8},{8,0},{16,24},{24,16},{1,9},{9,1},{17,25},{25,17},{2,10},{10... | collective-permute-start | bytes 2064392 | tf_op jit(solution)/shard_map/ppermute | solution.py:194
  756.7 57.6 %collective-permute-start.99 = (bf16[128,2688]{1,0:T(8,128)(2,1)}, bf16[128,2688]{1,0:T(8,128)(2,1)}, u32[]{:S(2)}, u32[]{:S(2)}) collective-permute-start(bf16[128,2688]{1,0:T(8,128)(2,1)} %dynamic-slice_bitcast_fusion.2), channel_id=1, source_target_pairs={{0,16},{8,24},{16,0},{24,8},{1,17},{9,25},{17,1},{25,9},{2,18},{10... | collective-permute-start | bytes 2064392 | tf_op jit(solution)/shard_map/ppermute | solution.py:194
  832.1 36.1 %collective-permute-start.102 = (bf16[64,2688]{1,0:T(8,128)(2,1)S(1)}, bf16[64,2688]{1,0:T(8,128)(2,1)S(1)}, u32[]{:S(2)}, u32[]{:S(2)}) collective-permute-start(bf16[64,2688]{1,0:T(8,128)(2,1)S(1)} %get-tuple-element.90), channel_id=1, source_target_pairs={{0,6},{2,4},{4,2},{6,0},{1,7},{3,5},{5,3},{7,1},{8,14},{10,12},{12... | collective-permute-start | bytes 1032200 | tf_op jit(solution)/shard_map/ppermute | solution.py:194
  833.8 34.4 %collective-permute-start.101 = (bf16[64,2688]{1,0:T(8,128)(2,1)S(1)}, bf16[64,2688]{1,0:T(8,128)(2,1)S(1)}, u32[]{:S(2)}, u32[]{:S(2)}) collective-permute-start(bf16[64,2688]{1,0:T(8,128)(2,1)S(1)} %get-tuple-element.89), channel_id=1, source_target_pairs={{0,4},{2,6},{4,0},{6,2},{1,5},{3,7},{5,1},{7,3},{8,12},{10,14},{12... | collective-permute-start | bytes 1032200 | tf_op jit(solution)/shard_map/ppermute | solution.py:194
  833.8 36.4 %collective-permute-start.100 = (bf16[64,2688]{1,0:T(8,128)(2,1)S(1)}, bf16[64,2688]{1,0:T(8,128)(2,1)S(1)}, u32[]{:S(2)}, u32[]{:S(2)}) collective-permute-start(bf16[64,2688]{1,0:T(8,128)(2,1)S(1)} %get-tuple-element.88), channel_id=1, source_target_pairs={{0,2},{2,0},{4,6},{6,4},{1,3},{3,1},{5,7},{7,5},{8,10},{10,8},{12,... | collective-permute-start | bytes 1032200 | tf_op jit(solution)/shard_map/ppermute | solution.py:194
  836.5 29.1 %collective-permute-start.71 = (bf16[64,768]{1,0:T(8,128)(2,1)S(1)}, bf16[64,768]{1,0:T(8,128)(2,1)S(1)}, u32[]{:S(2)}, u32[]{:S(2)}) collective-permute-start(bf16[64,768]{1,0:T(8,128)(2,1)S(1)} %get-tuple-element.136), channel_id=1, source_target_pairs={{0,4},{2,6},{4,0},{6,2},{1,5},{3,7},{5,1},{7,3},{8,12},{10,14},{12... | collective-permute-start | bytes 294920 | tf_op jit(solution)/shard_map/ppermute | solution.py:194
  836.8 28.9 %collective-permute-start.70 = (bf16[64,768]{1,0:T(8,128)(2,1)S(1)}, bf16[64,768]{1,0:T(8,128)(2,1)S(1)}, u32[]{:S(2)}, u32[]{:S(2)}) collective-permute-start(bf16[64,768]{1,0:T(8,128)(2,1)S(1)} %get-tuple-element.135), channel_id=1, source_target_pairs={{0,2},{2,0},{4,6},{6,4},{1,3},{3,1},{5,7},{7,5},{8,10},{10,8},{12,... | collective-permute-start | bytes 294920 | tf_op jit(solution)/shard_map/ppermute | solution.py:194
  865.6 41.1 %collective-permute-start.77 = (bf16[1024,768]{1,0:T(8,128)(2,1)S(1)}, bf16[1024,768]{1,0:T(8,128)(2,1)S(1)}, u32[]{:S(2)}, u32[]{:S(2)}) collective-permute-start(bf16[1024,768]{1,0:T(8,128)(2,1)S(1)} %convolution_convert_fusion.2), channel_id=1, source_target_pairs={{0,1},{1,0},{2,3},{3,2},{4,5},{5,4},{6,7},{7,6},{8,9},{9,8},{10,11... | collective-permute-start | bytes 4718600 | tf_op jit(solution)/shard_map/ppermute | solution.py:194
  873.3 33.2 %collective-permute-start.104 = (bf16[64,2688]{1,0:T(8,128)(2,1)S(1)}, bf16[64,2688]{1,0:T(8,128)(2,1)S(1)}, u32[]{:S(2)}, u32[]{:S(2)}) collective-permute-start(bf16[64,2688]{1,0:T(8,128)(2,1)S(1)} %add_convert_fusion.8), channel_id=1, source_target_pairs={{0,4},{2,6},{4,0},{6,2},{1,5},{3,7},{5,1},{7,3},{8,12},{10,14},{12... | collective-permute-start | bytes 1032200 | tf_op jit(solution)/shard_map/ppermute | solution.py:194
  877.5 29.0 %collective-permute-start.105 = (bf16[64,2688]{1,0:T(8,128)(2,1)S(1)}, bf16[64,2688]{1,0:T(8,128)(2,1)S(1)}, u32[]{:S(2)}, u32[]{:S(2)}) collective-permute-start(bf16[64,2688]{1,0:T(8,128)(2,1)S(1)} %add_convert_fusion.8), channel_id=1, source_target_pairs={{0,2},{2,0},{4,6},{6,4},{1,3},{3,1},{5,7},{7,5},{8,10},{10,8},{12,... | collective-permute-start | bytes 1032200 | tf_op jit(solution)/shard_map/ppermute | solution.py:194
  877.6 32.3 %collective-permute-start.76 = (bf16[256,768]{1,0:T(8,128)(2,1)S(1)}, bf16[256,768]{1,0:T(8,128)(2,1)S(1)}, u32[]{:S(2)}, u32[]{:S(2)}) collective-permute-start(bf16[256,768]{1,0:T(8,128)(2,1)S(1)} %pad_maximum_fusion.10), channel_id=1, source_target_pairs={{0,1},{1,0},{2,3},{3,2},{4,5},{5,4},{6,7},{7,6},{8,9},{9,8},{10,11... | collective-permute-start | bytes 1179656 | tf_op jit(solution)/shard_map/ppermute | solution.py:194
  909.0 39.6 %collective-permute-start.106 = (bf16[256,2688]{1,0:T(8,128)(2,1)S(1)}, bf16[256,2688]{1,0:T(8,128)(2,1)S(1)}, u32[]{:S(2)}, u32[]{:S(2)}) collective-permute-start(bf16[256,2688]{1,0:T(8,128)(2,1)S(1)} %pad_maximum_fusion.1), channel_id=1, source_target_pairs={{0,1},{1,0},{2,3},{3,2},{4,5},{5,4},{6,7},{7,6},{8,9},{9,8},{10,11... | collective-permute-start | bytes 4128776 | tf_op jit(solution)/shard_map/ppermute | solution.py:194
  (171 other events, 2174.4 us)
Sparse Core Ops, SparseCore 0:
  12.8 79.7 all-gather.3
  95.0 45.7 all-gather.5

commit v4 on v3

--- a/solution.py
+++ b/solution.py
@@ -73,9 +73,35 @@
     return pltpu.CompilerParams(vmem_limit_bytes=VMEM_BYTES)
 
 
-def project_kernel(me_ref, x_ref, wq_ref, wk_ref, wv_ref, cos_ref, sin_ref, out_ref):
-    weights = jnp.concatenate([wq_ref[...], wk_ref[...], wv_ref[...]], axis=1)
-    got = jnp.dot(x_ref[...], weights, preferred_element_type=jnp.float32)
+def lower_kernel(pairs, group, core_ref, w_ref, out_ref):
+    for pair in range(pairs):
+        for owner in range(group):
+            for part in range(3):
+                source = ((part * group + owner) * pairs + pair) * PAIR
+                target = ((pair * group + owner) * 3 + part) * PAIR
+                out_ref[:, target : target + PAIR] = w_ref[:, source : source + PAIR].astype(
+                    jnp.bfloat16
+                )
+
+
+def lower_half(core, weight, group):
+    rows, columns = weight.shape[0] // 2, weight.shape[1]
+    return pl.pallas_call(
+        functools.partial(lower_kernel, D // PAIR // group, group),
+        grid_spec=pltpu.PrefetchScalarGridSpec(
+            num_scalar_prefetch=1,
+            grid=(1,),
+            in_specs=[pl.BlockSpec((rows, columns), lambda i, core: (core[0], 0))],
+            out_specs=pl.BlockSpec((rows, columns), lambda i, core: (0, 0)),
+        ),
+        out_shape=jax.ShapeDtypeStruct((rows, columns), jnp.bfloat16),
+        compiler_params=compiler_params(),
+        name="lower_half",
+    )(core, weight)
+
+
+def project_kernel(me_ref, x_ref, w_ref, cos_ref, sin_ref, out_ref):
+    got = jnp.dot(x_ref[...], w_ref[...], preferred_element_type=jnp.float32)
     cos, sin = cos_ref[0], sin_ref[0]
     query = turned(got[:, :PAIR], cos, sin) * HEAD ** (-0.5)
     keys = turned(got[:, PAIR : 2 * PAIR], cos, sin)
@@ -95,12 +121,8 @@
     return [pl.BlockSpec(memory_space=pl.ANY)] * len(after)
 
 
-def project(me, first_normed, w_pair, cos, sin, group):
+def project(me, first_normed, w_in, cos, sin, pair, group):
     rows = first_normed.shape[0]
-
-    def column(part):
-        return lambda d, me: (0, part * group + (me[0] ^ d))
-
     return pl.pallas_call(
         project_kernel,
         grid_spec=pltpu.PrefetchScalarGridSpec(
@@ -108,9 +130,7 @@
             grid=(group,),
             in_specs=[
                 pl.BlockSpec((rows, D), lambda d, me: (0, 0)),
-                pl.BlockSpec((D, PAIR), column(0)),
-                pl.BlockSpec((D, PAIR), column(1)),
-                pl.BlockSpec((D, PAIR), column(2)),
+                pl.BlockSpec((D, 3 * PAIR), lambda d, me: (0, pair * group + (me[0] ^ d))),
                 pl.BlockSpec((1, rows, PAIR), lambda d, me: (0, 0, 0)),
                 pl.BlockSpec((1, rows, PAIR), lambda d, me: (0, 0, 0)),
             ],
@@ -119,7 +139,7 @@
         out_shape=jax.ShapeDtypeStruct((group, rows, 3 * PAIR), jnp.bfloat16),
         compiler_params=compiler_params(),
         name="project",
-    )(me, first_normed, w_pair, w_pair, w_pair, cos, sin)
+    )(me, first_normed, w_in, cos, sin)
 
 
 def row_product_kernel(me_ref, x_ref, w_ref, out_ref):
@@ -147,44 +167,30 @@
     )(me, left, weight, *after)
 
 
-def run_copies(pairs_of, sems):
-    copies = [
-        pltpu.make_async_copy(source, target, sems.at[index])
-        for index, (source, target) in enumerate(pairs_of)
-    ]
-    for copy in copies:
-        copy.start()
-    for copy in copies:
-        copy.wait()
-
-
-def place(me, pieces, parts, group, after=()):
-    rows = pieces[0][0].shape[0]
+def place(me, pieces, group, after=()):
+    rows, width = pieces[0][0].shape
     pairs = len(pieces)
     flat = [piece for near in pieces for piece in near]
 
     def kernel(me_ref, *refs):
-        out_ref, sems = refs[len(flat) + len(after) :]
-        moves = []
-        for pair in range(pairs):
-            for step in range(group):
-                owner = me_ref[0] ^ step
-                for part in range(parts):
-                    column = ((part * group + owner) * pairs + pair) * PAIR
-                    moves.append(
-                        (
-                            refs[pair * group + step].at[:, part * PAIR : (part + 1) * PAIR],
-                            out_ref.at[:, pl.ds(pl.multiple_of(column, PAIR), PAIR)],
-                        )
-                    )
-        run_copies(moves, sems)
+        out_ref = refs[-1]
+        for step in range(group):
+
+            @pl.when(pl.program_id(0) == step)
+            def _():
+                for pair in range(pairs):
+                    out_ref[:, pair * width : (pair + 1) * width] = refs[pair * group + step][...]
 
     return pl.pallas_call(
         kernel,
-        in_specs=[pl.BlockSpec(memory_space=pltpu.SMEM)] + untouched(flat) + untouched(after),
-        out_specs=pl.BlockSpec(memory_space=pl.ANY),
-        out_shape=jax.ShapeDtypeStruct((rows, parts * group * pairs * PAIR), jnp.bfloat16),
-        scratch_shapes=[pltpu.SemaphoreType.DMA((len(flat) * parts,))],
+        grid_spec=pltpu.PrefetchScalarGridSpec(
+            num_scalar_prefetch=1,
+            grid=(group,),
+            in_specs=[pl.BlockSpec((rows, width), lambda d, me: (0, 0))] * len(flat)
+            + untouched(after),
+            out_specs=pl.BlockSpec((rows, pairs * width), lambda d, me: (0, me[0] ^ d)),
+        ),
+        out_shape=jax.ShapeDtypeStruct((rows, group * pairs * width), jnp.bfloat16),
         compiler_params=compiler_params(),
         name="place",
     )(me, *flat, *after)
@@ -196,42 +202,6 @@
 
 def swap_heads(pieces, group):
     return [pieces[0]] + [exchange(pieces[d], "grp", d, group) for d in range(1, group)]
-
-
-def gather_rows(half, me_core, group):
-    if group != 4:
-        return lax.all_gather(half, ("grp", "core"), axis=0, tiled=True)
-    rows, columns = half.shape
-    middle = rows // 2
-    first = exchange(half, "grp", 1, group)
-    second = exchange(half, "grp", 2, group)
-    upper = exchange(second[:middle], "grp", 1, group)
-    lower = exchange(first[middle:], "grp", 2, group)
-    got = [half, first, second, upper, lower]
-    got += [exchange(piece, "core", 1, 2) for piece in got]
-
-    def kernel(index_ref, *refs):
-        out_ref, sems = refs[len(got) :]
-        moves = []
-        for side in range(2):
-            core = index_ref[1] ^ side
-            for slot, (step, offset) in enumerate(((0, 0), (1, 0), (2, 0), (3, 0), (3, middle))):
-                row = ((index_ref[0] ^ step) * 2 + core) * rows + offset
-                source = refs[side * 5 + slot]
-                moves.append(
-                    (source, out_ref.at[pl.ds(pl.multiple_of(row, middle), source.shape[0])])
-                )
-        run_copies(moves, sems)
-
-    return pl.pallas_call(
-        kernel,
-        in_specs=[pl.BlockSpec(memory_space=pltpu.SMEM)] + untouched(got),
-        out_specs=pl.BlockSpec(memory_space=pl.ANY),
-        out_shape=jax.ShapeDtypeStruct((2 * group * rows, columns), jnp.bfloat16),
-        scratch_shapes=[pltpu.SemaphoreType.DMA((len(got),))],
-        compiler_params=compiler_params(),
-        name="gather_rows",
-    )(me_core, *got)
 
 
 def attend_kernel(q_ref, k_ref, v_ref, qf_ref, kf_ref, own_v_ref, own_f_ref, out_ref, stat_ref, ke):
@@ -433,18 +403,27 @@
     return sum(term.astype(jnp.float32) for term in terms).astype(jnp.bfloat16)
 
 
+def delayed(value, after):
+    return lax.optimization_barrier((value, after))[0]
+
+
 def halved(array, mask, group, dim):
     bit = (lax.axis_index("grp") // mask) % 2
     got = exchange(pick(array, 1 - bit, dim), "grp", mask, group)
     return added(pick(array, bit, dim), got)
 
 
-def core_sum(left, right, core):
+def core_theirs(left, right, core):
     columns = right.shape[1] // 2
     theirs = lax.dynamic_slice_in_dim(right, (1 - core) * columns, columns, 1)
+    return contract(left, theirs).astype(jnp.bfloat16)
+
+
+def core_mine(left, right, core, sent):
+    columns = right.shape[1] // 2
     mine = lax.dynamic_slice_in_dim(right, core * columns, columns, 1)
-    sent = exchange(contract(left, theirs).astype(jnp.bfloat16), "core", 1, 2)
-    return (contract(left, mine) + sent.astype(jnp.float32)).astype(jnp.bfloat16)
+    got = exchange(sent, "core", 1, 2)
+    return (contract(left, mine) + got.astype(jnp.float32)).astype(jnp.bfloat16)
 
 
 def group_first(share, group):
@@ -464,61 +443,54 @@
     return jnp.concatenate([halved(halves[0], 1, group, 0), halved(halves[1], 2, group, 0)], axis=0)
 
 
-def far_scatter(share, far):
+def far_masks(far):
+    return [1 << bit for bit in range(far.bit_length() - 1)]
+
+
+def far_scatter(share, far, waits=((), ())):
     if far > 4:
         return lax.psum(share, "far")
-    rows, columns = share.shape
-    own = lax.axis_index("far")
-    if rows % (16 * far) == 0:
-        chunk = rows // far
-        pieces = [lax.dynamic_slice_in_dim(share, (own ^ d) * chunk, chunk, 0) for d in range(far)]
-    else:
-        chunk = columns // far
-        pieces = [lax.dynamic_slice_in_dim(share, (own ^ d) * chunk, chunk, 1) for d in range(far)]
-    return added(pieces[0], *[exchange(pieces[d], "far", d, far) for d in range(1, far)])
-
-
-def far_gather(chunk, rows, far):
-    if far > 4:
-        return chunk
-    pieces = [chunk] + [exchange(chunk, "far", d, far) for d in range(1, far)]
-    own = lax.axis_index("far")
-    mask = 1
-    while mask < far:
-        swap = (own // mask) % 2 == 1
-        pieces = [jnp.where(swap, pieces[j ^ mask], pieces[j]) for j in range(far)]
-        mask *= 2
-    return jnp.concatenate(pieces, axis=0 if rows % (16 * far) == 0 else 1)
-
-
-def finished(chunk, rows, core, far):
-    share = far_gather(chunk, rows, far)
-    other = exchange(share, "core", 1, 2)
-    low = jnp.where(core == 0, share, other)
-    high = jnp.where(core == 0, other, share)
-    return jnp.concatenate([low, high], axis=1).astype(jnp.float32)
-
-
-def pair_columns(weight, pair, pairs):
-    blocks = range(pair, weight.shape[1] // PAIR, pairs)
-    return jnp.concatenate([weight[:, j * PAIR : (j + 1) * PAIR] for j in blocks], axis=1)
-
-
-def merged_columns(parts):
+    for mask, after in zip(far_masks(far), waits):
+        bit = (lax.axis_index("far") // mask) % 2
+        rows = share.shape[0] // 2
+        got = exchange(
+            lax.dynamic_slice_in_dim(share, (1 - bit) * rows, rows, 0), "far", mask, far
+        )
+        kept = lax.dynamic_slice_in_dim(share, bit * rows, rows, 0)
+        share = added(delayed(kept, after), got)
+    return share
+
+
+def doubled(array, axis, mask, size, dim, after):
+    bit = (lax.axis_index(axis) // mask) % 2
+    got = exchange(array, axis, mask, size)
+    array = delayed(array, after)
+    low = jnp.where(bit == 0, array, got)
+    high = jnp.where(bit == 0, got, array)
+    return jnp.concatenate([low, high], axis=dim)
+
+
+def spread(share, far, waits=((), ())):
+    if far <= 4:
+        for mask, after in zip(far_masks(far)[::-1], waits):
+            share = doubled(share, "far", mask, far, 0, after)
+    return share
+
+
+def merged_columns(parts, group):
     pairs = len(parts)
-    blocks = range(pairs * parts[0].shape[1] // PAIR)
-    return jnp.concatenate(
-        [parts[j % pairs][:, j // pairs * PAIR : (j // pairs + 1) * PAIR] for j in blocks], axis=1
-    )
+    blocks = []
+    for part in range(3):
+        for owner in range(group):
+            for pair in range(pairs):
+                column = (owner * 3 + part) * PAIR
+                blocks.append(parts[pair][:, column : column + PAIR])
+    return jnp.concatenate(blocks, axis=1)
 
 
 def spread_halves(array):
     spare = ((0, 0), (0, FF_WIDE - FF))
     return jnp.concatenate([jnp.pad(array[:, :FF], spare), jnp.pad(array[:, FF:], spare)], axis=1)
-
-
-def joined_halves(array):
-    return jnp.concatenate([array[:, :FF], array[:, FF_WIDE : FF_WIDE + FF]], axis=1)
 
 
 def gated(gate, upward):
@@ -557,20 +529,16 @@
     me = lax.axis_index("grp")
     core = lax.axis_index("core")
     me_list = me.reshape(1).astype(jnp.int32)
-    me_core = jnp.stack([me, core]).astype(jnp.int32)
+    core_list = core.reshape(1).astype(jnp.int32)
     pairs = D // PAIR // group
     masters = (inproj, outproj, upproj, downproj, norm_gains)
     own_rows = tokens.shape[1]
     own_gains = norm_gains.shape[0]
-    w_pairs = [
-        gather_rows(
-            own_half(pair_columns(inproj, pair, pairs), core).astype(jnp.bfloat16), me_core, group
-        )
-        for pair in range(pairs)
-    ]
-    w_up = gather_weight(spread_halves(upproj), core)
+    both = ("grp", "core")
+    w_in = lax.all_gather(lower_half(core_list, inproj, group), both, axis=0, tiled=True)
+    w_outup = gather_weight(jnp.concatenate([outproj, spread_halves(upproj)], axis=1), core)
     w_down = gather_weight(downproj, core)
-    w_out = gather_rows(own_half(outproj, core).astype(jnp.bfloat16), me_core, group)
+    w_out, w_up = w_outup[:, :D], w_outup[:, D:]
     packed = jnp.concatenate([norm_gains[:, 0], norm_gains[:, 1], slot_ids[0].astype(jnp.float32)])
     packed = lax.all_gather(packed.astype(jnp.bfloat16), "grp", axis=0, tiled=False)
     gain_one = packed[:, :own_gains].reshape(D).astype(jnp.float32)
@@ -589,14 +557,14 @@
     sin_near = sin.reshape(group, own_rows, PAIR)
     qkv, stats, attended_near, attended_here = [], [], [], []
     for pair in range(pairs):
-        pieces = project(me_list, first_normed, w_pairs[pair], cos_near, sin_near, group)
+        pieces = project(me_list, first_normed, w_in, cos_near, sin_near, pair, group)
         qkv.append(jnp.concatenate(swap_heads(pieces, group), axis=0))
     for pair in range(pairs):
         mixed, stat = attend(qkv[pair], query_side, key_side)
         stats.append(stat)
         attended_near.append(mixed)
         attended_here.append(swap_heads(mixed.reshape(group, own_rows, PAIR), group))
-    attended = place(me_list, attended_here, 1, group)
+    attended = place(me_list, attended_here, group)
     middle = inputs + product(attended, w_out)
     second_normed = layer_norm(middle, gain_two).astype(jnp.bfloat16)
     gate_up = product(second_normed, w_up)
@@ -610,26 +578,33 @@
     grad_gate_up = spread_halves(jnp.concatenate(gate_back(grad_hidden), axis=1)).astype(
         jnp.bfloat16
     )
+    grad_down = contract(hidden, grad_top).astype(jnp.bfloat16)
+    up_theirs = core_theirs(second_normed, grad_gate_up, core)
+    grad_gate_up, up_theirs, grad_down = lax.optimization_barrier(
+        (grad_gate_up, up_theirs, grad_down)
+    )
     grad_second = against(grad_gate_up, w_up)
     _, second_back = jax.vjp(lambda v: layer_norm(v, gain_two), middle)
     (grad_from_norm,) = second_back(grad_second)
     grad_middle = grad_top.astype(jnp.float32) + grad_from_norm
     grad_branch = grad_middle.astype(jnp.bfloat16)
-    down_rows, up_rows, out_rows = downproj.shape[0], upproj.shape[0], outproj.shape[0]
-    down_share = core_sum(hidden, grad_top, core)
-    up_share = core_sum(second_normed, grad_gate_up, core)
+    down_share = lax.psum_scatter(grad_down, both, scatter_dimension=0, tiled=True)
     grad_near = []
     for pair in range(pairs):
-        sent = row_product(
-            me_list, grad_branch, w_out, pair, group, (down_share,) if pair == 0 else ()
-        )
+        after = (up_theirs, grad_down) if pair == 0 else (sent,)
+        sent = row_product(me_list, grad_branch, w_outup, pair, group, after)
         grad_near.append(jnp.concatenate(swap_heads(sent, group), axis=0))
-    down_halves = group_first(down_share, group)
-    out_share = core_sum(attended, grad_branch, core)
-    waits = [(*down_halves, up_share)]
-    down_half = group_second(down_halves, group)
+    out_theirs = core_theirs(attended, grad_branch, core)
+    up_share = jnp.concatenate(
+        [
+            core_mine(second_normed, grad_gate_up, core, up_theirs),
+            core_mine(attended, grad_branch, core, out_theirs),
+        ],
+        axis=1,
+    )
     up_halves = group_first(up_share, group)
-    waits.append((down_half, *up_halves, out_share))
+    up_half = group_second(up_halves, group)
+    waits = [(up_share,), up_halves]
     grads_here = []
     for pair in range(pairs):
         grads = attend_back(
@@ -637,24 +612,37 @@
             cos, sin, waits[pair],
         )
         grads_here.append(swap_heads(grads.reshape(group, own_rows, 3 * PAIR), group))
-    up_half = group_second(up_halves, group)
-    down_chunk = far_scatter(down_half, far)
-    out_halves = group_first(out_share, group)
-    waits = [(down_chunk, *out_halves), ()]
-    in_shares, grad_first = [], 0.0
+    grads_placed, in_theirs, grad_first = [], [], 0.0
     for pair in range(pairs):
-        grad_projected = place(me_list, [grads_here[pair]], 3, group, waits[pair])
-        in_shares.append(core_sum(first_normed, grad_projected, core))
-        grad_first = grad_first + against(grad_projected, w_pairs[pair])
-    up_chunk = far_scatter(up_half, far)
-    out_chunk = far_scatter(group_second(out_halves, group), far)
-    in_chunks = [
-        far_scatter(group_second(group_first(share, group), group), far) for share in in_shares
+        after = (up_half,) if pair == 0 else (in_theirs[0],)
+        placed = place(me_list, [grads_here[pair]], group, after)
+        grads_placed.append(placed)
+        in_theirs.append(core_theirs(first_normed, placed, core))
+    in_shares = [
+        core_mine(first_normed, grads_placed[pair], core, in_theirs[pair]) for pair in range(pairs)
     ]
-    total_down = finished(down_chunk, down_rows, core, far)
-    total_up = joined_halves(finished(up_chunk, up_rows, core, far))
-    total_out = finished(out_chunk, out_rows, core, far)
-    total_in = merged_columns([finished(chunk, inproj.shape[0], core, far) for chunk in in_chunks])
+    in_firsts = [delayed(group_first(share, group), in_theirs[-1]) for share in in_shares]
+    in_halves = [group_second(first, group) for first in in_firsts]
+    in_chunks = [far_scatter(half, far) for half in in_halves]
+    for pair in range(pairs):
+        width = 3 * PAIR * group
+        part = w_in[:, pair * width : (pair + 1) * width]
+        grad_first = grad_first + against(grads_placed[pair], part)
+    up_chunk = far_scatter(up_half, far, (in_theirs[-1], in_shares[-1]))
+    up_chunk = spread(up_chunk, far, (in_firsts[-1], in_halves[-1]))
+    total_up = doubled(up_chunk, "core", 1, 2, 1, in_chunks[-1]).astype(jnp.float32)
+    wide = up_chunk.shape[1]
+    total_out = jnp.concatenate([total_up[:, FF_WIDE:wide], total_up[:, wide + FF_WIDE :]], axis=1)
+    total_up = jnp.concatenate(
+        [total_up[:, :FF], total_up[:, wide : wide + FF]], axis=1
+    )
+    down_share = lax.psum(delayed(down_share, in_theirs[0]), "far")
+    total_down = doubled(
+        delayed(down_share, in_halves[-1]), "core", 1, 2, 0, in_chunks[-1]
+    ).astype(jnp.float32)
+    total_in = merged_columns(
+        [doubled(spread(chunk, far), "core", 1, 2, 1, ()) for chunk in in_chunks], group
+    ).astype(jnp.float32)
     _, first_back = jax.vjp(lambda v: layer_norm(v, gain_one), inputs)
     (grad_inputs,) = first_back(grad_first)
     input_grad = (grad_middle + grad_inputs).astype(jnp.bfloat16)

time: 985 us -> 638 us (0.65)
  Pallas kernels: 434 us -> 87 us
  waiting for transfers between devices: 170 us -> 274 us
  starting transfers between devices: 120 us -> 50 us
  local copies, waits for them, and re-layouts: 61.4 us -> 37.6 us
  blocking collectives: 28.9 us -> 9.73 us
  matrix products: 71.8 us -> 83.8 us
    pallas_call x6 -> x4, Pallas kernels: 359 us -> 11.6 us  [the longest x3 9.16 us: place(): pl.pallas_call(kernel, grid_spec=pltpu.PrefetchScalarGridSpec(num_scalar_...]
    ppermute x111 -> x56, starting transfers between devices: 120 us -> 49.7 us  [exchange(): return lax.ppermute(array, axis, [(i, i ^ mask) for i in range(size)])]
    all_gather x2, waiting for transfers between devices: 0.02 us -> 51.4 us  [gather_weight(): lax.all_gather(own_half(weight, core).astype(jnp.bfloat16), ('grp', 'core...]
    ppermute x111 -> x56, waiting for transfers between devices: 169 us -> 199 us  [exchange(): return lax.ppermute(array, axis, [(i, i ^ mask) for i in range(size)])]
    all_gather x0 -> x1, waiting for transfers between devices: none -> 22.6 us  [local(): lax.all_gather(lower_half(core_list, inproj, group), both, axis=0, tiled=...]
    all_gather x1, blocking collectives: 28.9 us -> 9.73 us  [local(): lax.all_gather(packed.astype(jnp.bfloat16), 'grp', axis=0, tiled=False)]
    unnamed x249 -> x152, local copies, waits for them, and re-layouts: 28.3 us -> 15.3 us
    dot_general x10 -> x9, matrix products: 23.9 us -> 33.8 us  [contract(): lax.dot_general(left, right, (((0,), (0,)), ((), ())), preferred_element_...]
  transfers between devices with their start and end apart: 113 -> 61, of which waited for: 42 -> 25; matrix products, arithmetic and copies ran while one was open for 14% -> 20% of each run, Pallas kernels for 44% -> 13%
where the time goes in v4:
time: 638 us; the launch traced here: 627 us
  waiting for transfers between devices  274 us (43%)
  Pallas kernels  87 us (14%)
  matrix products  83.8 us (13%)
  other arithmetic  70.4 us (11%)
  starting transfers between devices  50 us (8%)
  local copies, waits for them, and re-layouts  37.6 us (6%)
  between operations  15.3 us (2%)
  blocking collectives  9.73 us (2%)
    ppermute x56, waiting for transfers between devices, exchange(): return lax.ppermute(array, axis, [(i, i ^ mask) for i in range(size)])  199 us
    all_gather x2, waiting for transfers between devices, gather_weight(): lax.all_gather(own_half(weight, core).astype(jnp.bfloat16), ('grp', 'core...  51.4 us
    ppermute x56, starting transfers between devices, exchange(): return lax.ppermute(array, axis, [(i, i ^ mask) for i in range(size)])  49.7 us
    pallas_call x2, Pallas kernels, attend_back(): pl.pallas_call(skipping(attend_back_kernel, 12, len(after)), grid=(rows /...  34.1 us
    dot_general x9, matrix products, contract(): lax.dot_general(left, right, (((0,), (0,)), ((), ())), preferred_element_...  33.8 us
    dot_general x4, matrix products, against(): lax.dot_general(left, right, (((1,), (1,)), ((), ())), preferred_element_...  29 us
    sub x5, other arithmetic, adam_update(): return (mean_new, square_new, weight - rate * (step_size + 0.01 * weight))  23.2 us
    all_gather x1, waiting for transfers between devices, local(): lax.all_gather(lower_half(core_list, inproj, group), both, axis=0, tiled=...  22.6 us
  transfers between devices with their start and end apart: 61, of which 25 were waited for; matrix products, arithmetic and copies ran while one was open for 20% of the time, Pallas kernels for 13%

profile of v4, /device:TPU:0, one launch (start us, length us, event | category | flops | bytes accessed | tf_op | source)
XLA Modules:
  0.0 627.4 jit_solution(3936057692746135209)
XLA Ops:
  17.9 9.7 %all-gather = bf16[4,1,896]{2,1,0:T(2,128)(2,1)S(1)} all-gather(bf16[1,1,896]{2,1,0:T(2,128)(2,1)S(1)} %maximum_bitcast_fusion), channel_id=1, replica_groups=mesh['grp'=4,'far'=4,'core'=2] {'grp'}, dimensions={0}, use_global_device_ids=true | all-gather | bytes 8960 | tf_op jit(solution)/shard_map/all_gather | solution.py:543
  30.7 4.3 fusion.62
  36.2 22.6 %all-gather.5.cloned.1.call-done.w_ref = bf16[1024,3072]{1,0:T(8,128)(2,1)} async-done(((bf16[128,3072]{1,0:T(8,128)(2,1)}), bf16[1024,3072]{1,0:T(8,128)(2,1)}) %all-gather.5.cloned.1.call-update) | async-done | bytes 6291472 | tf_op jit(solution)/shard_map/all_gather | solution.py:538
  58.8 5.8 project.2
  71.3 6.0 project.3
  82.4 6.4 %collective-permute-done.1 = bf16[384,384]{1,0:T(8,128)(2,1)S(1)} collective-permute-done((bf16[384,384]{1,0:T(8,128)(2,1)S(1)}, bf16[384,384]{1,0:T(8,128)(2,1)S(1)}, u32[]{:S(2)}, u32[]{:S(2)}) %collective-permute-start.1) | collective-permute-done | bytes 294944 | tf_op jit(solution)/shard_map/ppermute | solution.py:200
  88.8 4.3 collective-permute-done
  94.3 10.2 %attend.2 = (bf16[1536,128]{1,0:T(8,128)(2,1)}, f32[1536,128]{1,0:T(8,128)}) custom-call(bf16[1536,384]{1,0:T(8,128)(2,1)} %pad_maximum_fusion.6.q_ref.k_ref.v_ref.own_v_ref.refs_0_.refs_1_.refs_2_, bf16[1536,384]{1,0:T(8,128)(2,1)} %pad_maximum_fusion.6.q_ref.k_ref.v_ref.own_v_ref.refs_0_.refs_1_.refs_2_, ...), custom_call_target="tpu_custom_call" | custom-call | tf_op jit(solution)/shard_map/attend/pallas_call | solution.py:251
  109.7 3.4 collective-permute-done.6
  114.2 10.2 %attend.3 = (bf16[1536,128]{1,0:T(8,128)(2,1)}, f32[1536,128]{1,0:T(8,128)}) custom-call(bf16[1536,384]{1,0:T(8,128)(2,1)} %pad_maximum_fusion.7.q_ref.k_ref.v_ref.own_v_ref.refs_0_.refs_1_.refs_2_, bf16[1536,384]{1,0:T(8,128)(2,1)} %pad_maximum_fusion.7.q_ref.k_ref.v_ref.own_v_ref.refs_0_.refs_1_.refs_2_, ...), custom_call_target="tpu_custom_call" | custom-call | tf_op jit(solution)/shard_map/attend/pallas_call | solution.py:251
  129.7 4.2 collective-permute-done.9.refs_5_
  138.4 3.1 place.3
  141.4 23.2 %all-gather.7.cloned.1.call-done.refs_2_ = bf16[1024,6400]{1,0:T(8,128)(2,1)} async-done(((bf16[128,6400]{1,0:T(8,128)(2,1)}), bf16[1024,6400]{1,0:T(8,128)(2,1)}) %all-gather.7.cloned.1.call-update) | async-done | bytes 13107216 | tf_op jit(solution)/shard_map/all_gather | solution.py:393
  164.6 2.9 fusion.129
  168.7 12.0 %fusion.2 = f32[384,5376]{1,0:T(8,128)} fusion(bf16[1024,6400]{1,0:T(8,128)(2,1)} %all-gather.7.cloned.1.call-done.refs_2_, f32[384,1024]{1,0:T(8,128)S(1)} %get-tuple-element.163, f32[1024]{0:T(1024)S(1)} %bitcast.206, f32[384]{0:T(512)S(1)} %fusion.104, f32[384]{0:T(512)S(1)} %broadcast_multiply_fusion), kind=kOutput, calls=%fused_computation.5 | convolution fusion | flops 4229431296 | bytes 20847616 | tf_op jit(solution)/shard_map/dot_general | solution.py:372
  180.6 28.2 %all-gather.9.cloned.1.call-done = bf16[2624,1024]{1,0:T(8,128)(2,1)} async-done(((bf16[328,1024]{1,0:T(8,128)(2,1)}), bf16[2624,1024]{1,0:T(8,128)(2,1)}) %all-gather.9.cloned.1.call-update) | async-done | bytes 5373968 | tf_op jit(solution)/shard_map/all_gather | solution.py:393
  208.8 15.9 %add_convert_fusion.1 = (bf16[384,2624]{1,0:T(8,128)(2,1)}, f32[384,2624]{1,0:T(8,128)}, f32[384,2624]{1,0:T(8,128)}) fusion(f32[384,5376]{1,0:T(8,128)} %fusion.2, bf16[2624,1024]{1,0:T(8,128)(2,1)} %all-gather.9.cloned.1.call-done, bf16[1,384,1024]{2,1,0:T(8,128)(2,1)S(1)} %copy-done.30, bf16[384]{0:T(512)(128)(2,1)S(1)} %fusion.105), kind=kOutput, calls=%fused_computation.31 | convolution fusion | flops 2137546752 | bytes 24298240 | tf_op jit(solution)/shard_map/dot_general | solution.py:382
  224.8 6.0 multiply_convert_fusion
  230.7 6.4 %convolution_convert_fusion.refs_4_ = bf16[2624,1024]{1,0:T(8,128)(2,1)} fusion(bf16[384,2624]{1,0:T(8,128)(2,1)} %get-tuple-element.75, bf16[1,384,1024]{2,1,0:T(8,128)(2,1)S(1)} %copy-done.30, bf16[384]{0:T(512)(128)(2,1)S(1)} %fusion.105), kind=kOutput, calls=%fused_computation.17 | convolution fusion | flops 2066677760 | bytes 8176384 | tf_op jit(solution)/shard_map/dot_general | solution.py:376
  239.2 5.1 convolution_convert_fusion.1.refs_3_
  244.6 8.6 %multiply_reduce_fusion.1 = (f32[384]{0:T(512)S(1)}, f32[384,1024]{1,0:T(8,128)S(1)}) fusion(f32[384,1024]{1,0:T(8,128)S(1)} %copy-done.19, f32[384]{0:T(512)S(1)} %broadcast_multiply_fusion, f32[1024]{0:T(1024)S(1)} %bitcast.208, bf16[384,5376]{1,0:T(8,128)(2,1)} %copy-done.24, bf16[1024,6400]{1,0:T(8,128)(2,1)} %all-gather.7.cloned.1.call-done.refs_2_), kind=kOutput, calls=%fused_computation.114 | convolution fusion | flops 4229430784 | bytes 18291712 | tf_op jit(solution)/shard_map/dot_general | solution.py:382
  257.4 4.3 fusion.63
  261.8 4.4 row_product.2.refs_3_
  266.2 4.7 row_product.3
  278.3 2.9 add_convert_fusion.4
  281.3 6.9 %add_convert_fusion = bf16[1024,2688]{1,0:T(8,128)(2,1)} fusion(bf16[1024,2688]{1,0:T(8,128)(2,1)} %collective-permute-done.15, bf16[384,5376]{1,0:T(8,128)(2,1)S(1)} %copy-done.25, s32[]{:T(128)S(6)} %select_n.368, f32[384,1024]{1,0:T(8,128)S(1)} %copy-done.19, f32[1024]{0:T(1024)S(1)} %bitcast.209, f32[384]{0:T(512)S(1)} %fusion.104, ...), kind=kOutput, calls=%fused_computation.2 | convolution fusion | flops 2123759616 | bytes 14655492 | tf_op jit(solution)/shard_map/dot_general | solution.py:376
  288.2 3.4 pad_maximum_fusion.refs_12_
  297.2 6.1 fusion.57
  308.0 37.9 %collective-permute-done.12 = bf16[384,128]{1,0:T(8,128)(2,1)S(1)} collective-permute-done((bf16[384,128]{1,0:T(8,128)(2,1)S(1)}, bf16[384,128]{1,0:T(8,128)(2,1)S(1)}, u32[]{:S(2)}, u32[]{:S(2)}) %collective-permute-start.12) | collective-permute-done | bytes 98336 | tf_op jit(solution)/shard_map/ppermute | solution.py:200
  350.4 17.1 %attend_back.2 = bf16[1536,384]{1,0:T(8,128)(2,1)} custom-call(bf16[1536,384]{1,0:T(8,128)(2,1)} %pad_maximum_fusion.6.q_ref.k_ref.v_ref.own_v_ref.refs_0_.refs_1_.refs_2_, bf16[1536,384]{1,0:T(8,128)(2,1)} %pad_maximum_fusion.6.q_ref.k_ref.v_ref.own_v_ref.refs_0_.refs_1_.refs_2_, ...), custom_call_target="tpu_custom_call" | custom-call | tf_op jit(solution)/shard_map/attend_back/pallas_call | solution.py:350
  374.5 19.7 %collective-permute-done.20 = bf16[2,128,3200]{2,1,0:T(8,128)(2,1)S(1)} collective-permute-done((bf16[2,128,3200]{2,1,0:T(8,128)(2,1)}, bf16[2,128,3200]{2,1,0:T(8,128)(2,1)S(1)}, u32[]{:S(2)}, u32[]{:S(2)}) %collective-permute-start.20) | collective-permute-done | bytes 1638432 | tf_op jit(solution)/shard_map/ppermute | solution.py:200
  395.7 17.0 %attend_back.3 = bf16[1536,384]{1,0:T(8,128)(2,1)} custom-call(bf16[1536,384]{1,0:T(8,128)(2,1)} %pad_maximum_fusion.7.q_ref.k_ref.v_ref.own_v_ref.refs_0_.refs_1_.refs_2_, bf16[1536,384]{1,0:T(8,128)(2,1)} %pad_maximum_fusion.7.q_ref.k_ref.v_ref.own_v_ref.refs_0_.refs_1_.refs_2_, ...), custom_call_target="tpu_custom_call" | custom-call | tf_op jit(solution)/shard_map/attend_back/pallas_call | solution.py:350
  417.5 21.4 %collective-permute-done.21 = bf16[128,3200]{1,0:T(8,128)(2,1)S(1)} collective-permute-done((bf16[128,3200]{1,0:T(8,128)(2,1)S(1)}, bf16[128,3200]{1,0:T(8,128)(2,1)S(1)}, u32[]{:S(2)}, u32[]{:S(2)}) %collective-permute-start.21) | collective-permute-done | bytes 819232 | tf_op jit(solution)/shard_map/ppermute | solution.py:200
  445.0 3.6 convolution_convert_fusion.3.refs_4_
  453.5 3.2 place.5
  466.9 5.2 collective-permute-done.50
  485.8 18.2 %collective-permute-done.51 = bf16[64,3200]{1,0:T(8,128)(2,1)S(1)} collective-permute-done((bf16[64,3200]{1,0:T(8,128)(2,1)S(1)}, bf16[64,3200]{1,0:T(8,128)(2,1)S(1)}, u32[]{:S(2)}, u32[]{:S(2)}) %collective-permute-start.51) | collective-permute-done | bytes 409632 | tf_op jit(solution)/shard_map/ppermute | solution.py:200
  509.1 25.7 %collective-permute-done.52 = bf16[64,3200]{1,0:T(8,128)(2,1)S(1)} collective-permute-done((bf16[64,3200]{1,0:T(8,128)(2,1)S(1)}, bf16[64,3200]{1,0:T(8,128)(2,1)S(1)}, u32[]{:S(2)}, u32[]{:S(2)}) %collective-permute-start.52) | collective-permute-done | bytes 409632 | tf_op jit(solution)/shard_map/ppermute | solution.py:200
  538.4 21.9 %collective-permute-done.35 = bf16[128,768]{1,0:T(8,128)(2,1)S(1)} collective-permute-done((bf16[128,768]{1,0:T(8,128)(2,1)S(1)}, bf16[128,768]{1,0:T(8,128)(2,1)S(1)}, u32[]{:S(2)}, u32[]{:S(2)}) %collective-permute-start.35) | collective-permute-done | bytes 196640 | tf_op jit(solution)/shard_map/ppermute | solution.py:200
  561.2 3.4 collective-permute-done.45
  565.4 2.9 collective-permute-done.36
  568.4 5.4 collective-permute-done.46
  576.9 3.3 collective-permute-done.47
  580.4 4.2 collective-permute-done.38
  584.7 3.7 collective-permute-done.48
  592.1 4.2 multiply_subtract_fusion.2
  599.1 5.0 multiply_subtract_fusion.1
  608.9 11.2 %multiply_subtract_fusion = (f32[256,5248]{1,0:T(8,128)}, f32[256,5248]{1,0:T(8,128)}, f32[256,5248]{1,0:T(8,128)}, f32[256]{0:T(256)S(1)}) fusion(f32[256,5248]{1,0:T(8,128)S(1)} %bitcast.195, f32[256,2624]{1,0:T(8,128)S(1)} %get-tuple-element.81, f32[256,2624]{1,0:T(8,128)S(1)} %get-tuple-element.80, f32[256,5248]{1,0:T(8,128)} %param.33, ...), kind=kLoop, calls=%fused_computation.26 | loop fusion | flops 26869504 | bytes 37618688 | tf_op jit(solution)/shard_map/sub | solution.py:504
  (398 shorter events, 146.7 us)
Async XLA Ops:
  7.2 51.6 %all-gather.5.cloned.1.call-start = ((), (), s32[]{:S(2)}) async-start(), calls=%async_computation.1 | async-start | bytes 7077888 | tf_op jit(solution)/shard_map/all_gather | solution.py:538
  9.7 154.9 %all-gather.7.cloned.1.call-start = ((), (), s32[]{:S(2)}) async-start(), calls=%async_computation.2 | async-start | bytes 14745600 | tf_op jit(solution)/shard_map/all_gather | solution.py:393
  15.4 193.4 %all-gather.9.cloned.1.call-start = ((), (), s32[]{:S(2)}) async-start(), calls=%async_computation.3 | async-start | bytes 6045696 | tf_op jit(solution)/shard_map/all_gather | solution.py:393
  17.8 449.1 %reduce-scatter.2.cloned.1.call-start = ((), (), s32[]{:S(2)}) async-start(), calls=%async_computation.4 | async-start | bytes 6045696 | tf_op jit(solution)/shard_map/reduce_scatter | solution.py:591
  66.0 15.9 %collective-permute-start.2 = (bf16[384,384]{1,0:T(8,128)(2,1)S(1)}, bf16[384,384]{1,0:T(8,128)(2,1)S(1)}, u32[]{:S(2)}, u32[]{:S(2)}) collective-permute-start(bf16[384,384]{1,0:T(8,128)(2,1)S(1)} %get-tuple-element.109), channel_id=1, source_target_pairs={{0,24},{8,16},{16,8},{24,0},{1,25},{9,17},{17,9},{25,1},{2,26},{10... | collective-permute-start | bytes 884744 | tf_op jit(solution)/shard_map/ppermute | solution.py:200
  67.5 21.3 %collective-permute-start.1 = (bf16[384,384]{1,0:T(8,128)(2,1)S(1)}, bf16[384,384]{1,0:T(8,128)(2,1)S(1)}, u32[]{:S(2)}, u32[]{:S(2)}) collective-permute-start(bf16[384,384]{1,0:T(8,128)(2,1)S(1)} %get-tuple-element.110), channel_id=1, source_target_pairs={{0,16},{8,24},{16,0},{24,8},{1,17},{9,25},{17,1},{25,9},{2,18},{10... | collective-permute-start | bytes 884744 | tf_op jit(solution)/shard_map/ppermute | solution.py:200
  69.0 24.2 %collective-permute-start = (bf16[384,384]{1,0:T(8,128)(2,1)S(1)}, bf16[384,384]{1,0:T(8,128)(2,1)S(1)}, u32[]{:S(2)}, u32[]{:S(2)}) collective-permute-start(bf16[384,384]{1,0:T(8,128)(2,1)S(1)} %get-tuple-element.111), channel_id=1, source_target_pairs={{0,8},{8,0},{16,24},{24,16},{1,9},{9,1},{17,25},{25,17},{2,10},{10... | collective-permute-start | bytes 884744 | tf_op jit(solution)/shard_map/ppermute | solution.py:200
  78.7 30.1 %collective-permute-start.8 = (bf16[384,384]{1,0:T(8,128)(2,1)S(1)}, bf16[384,384]{1,0:T(8,128)(2,1)S(1)}, u32[]{:S(2)}, u32[]{:S(2)}) collective-permute-start(bf16[384,384]{1,0:T(8,128)(2,1)S(1)} %get-tuple-element.105), channel_id=1, source_target_pairs={{0,24},{8,16},{16,8},{24,0},{1,25},{9,17},{17,9},{25,1},{2,26},{10... | collective-permute-start | bytes 884744 | tf_op jit(solution)/shard_map/ppermute | solution.py:200
  80.1 29.6 %collective-permute-start.7 = (bf16[384,384]{1,0:T(8,128)(2,1)S(1)}, bf16[384,384]{1,0:T(8,128)(2,1)S(1)}, u32[]{:S(2)}, u32[]{:S(2)}) collective-permute-start(bf16[384,384]{1,0:T(8,128)(2,1)S(1)} %get-tuple-element.106), channel_id=1, source_target_pairs={{0,16},{8,24},{16,0},{24,8},{1,17},{9,25},{17,1},{25,9},{2,18},{10... | collective-permute-start | bytes 884744 | tf_op jit(solution)/shard_map/ppermute | solution.py:200
  81.8 31.3 %collective-permute-start.6 = (bf16[384,384]{1,0:T(8,128)(2,1)S(1)}, bf16[384,384]{1,0:T(8,128)(2,1)S(1)}, u32[]{:S(2)}, u32[]{:S(2)}) collective-permute-start(bf16[384,384]{1,0:T(8,128)(2,1)S(1)} %get-tuple-element.107), channel_id=1, source_target_pairs={{0,8},{8,0},{16,24},{24,16},{1,9},{9,1},{17,25},{25,17},{2,10},{10... | collective-permute-start | bytes 884744 | tf_op jit(solution)/shard_map/ppermute | solution.py:200
  106.2 22.2 %collective-permute-start.3 = (bf16[384,128]{1,0:T(8,128)(2,1)S(1)}, bf16[384,128]{1,0:T(8,128)(2,1)S(1)}, u32[]{:S(2)}, u32[]{:S(2)}) collective-permute-start(bf16[384,128]{1,0:T(8,128)(2,1)S(1)} %get-tuple-element.142), channel_id=1, source_target_pairs={{0,8},{8,0},{16,24},{24,16},{1,9},{9,1},{17,25},{25,17},{2,10},{10... | collective-permute-start | bytes 294920 | tf_op jit(solution)/shard_map/ppermute | solution.py:200
  107.5 22.2 %collective-permute-start.4 = (bf16[384,128]{1,0:T(8,128)(2,1)S(1)}, bf16[384,128]{1,0:T(8,128)(2,1)S(1)}, u32[]{:S(2)}, u32[]{:S(2)}) collective-permute-start(bf16[384,128]{1,0:T(8,128)(2,1)S(1)} %get-tuple-element.141), channel_id=1, source_target_pairs={{0,16},{8,24},{16,0},{24,8},{1,17},{9,25},{17,1},{25,9},{2,18},{10... | collective-permute-start | bytes 294920 | tf_op jit(solution)/shard_map/ppermute | solution.py:200
  108.7 21.0 %collective-permute-start.5 = (bf16[384,128]{1,0:T(8,128)(2,1)S(1)}, bf16[384,128]{1,0:T(8,128)(2,1)S(1)}, u32[]{:S(2)}, u32[]{:S(2)}) collective-permute-start(bf16[384,128]{1,0:T(8,128)(2,1)S(1)} %get-tuple-element.140), channel_id=1, source_target_pairs={{0,24},{8,16},{16,8},{24,0},{1,25},{9,17},{17,9},{25,1},{2,26},{10... | collective-permute-start | bytes 294920 | tf_op jit(solution)/shard_map/ppermute | solution.py:200
  244.3 37.0 %collective-permute-start.15 = (bf16[1024,2688]{1,0:T(8,128)(2,1)}, bf16[1024,2688]{1,0:T(8,128)(2,1)}, u32[]{:S(2)}, u32[]{:S(2)}) collective-permute-start(bf16[1024,2688]{1,0:T(8,128)(2,1)} %convolution_convert_fusion.1.refs_3_), channel_id=1, source_target_pairs={{0,1},{1,0},{2,3},{3,2},{4,5},{5,4},{6,7},{7,6},{8,9},{9,8},{10,11... | collective-permute-start | bytes 16515080 | tf_op jit(solution)/shard_map/ppermute | solution.py:200
  257.2 19.9 %collective-permute-start.16 = (bf16[1024,512]{1,0:T(8,128)(2,1)}, bf16[1024,512]{1,0:T(8,128)(2,1)}, u32[]{:S(2)}, u32[]{:S(2)}) collective-permute-start(bf16[1024,512]{1,0:T(8,128)(2,1)} %convolution_convert_fusion.4), channel_id=1, source_target_pairs={{0,1},{1,0},{2,3},{3,2},{4,5},{5,4},{6,7},{7,6},{8,9},{9,8},{10,11... | collective-permute-start | bytes 3145736 | tf_op jit(solution)/shard_map/ppermute | solution.py:200
  261.7 276.6 %all-reduce.5.cloned.1.call-start = ((), (), s32[]{:S(2)}) async-start(), calls=%async_computation.5 | async-start | bytes 1343488 | tf_op jit(solution)/shard_map/psum | solution.py:639
  272.8 30.5 %collective-permute-start.26 = (bf16[384,128]{1,0:T(8,128)(2,1)}, bf16[384,128]{1,0:T(8,128)(2,1)}, u32[]{:S(2)}, u32[]{:S(2)}) collective-permute-start(bf16[384,128]{1,0:T(8,128)(2,1)} %get-tuple-element.133), channel_id=1, source_target_pairs={{0,24},{8,16},{16,8},{24,0},{1,25},{9,17},{17,9},{25,1},{2,26},{10... | collective-permute-start | bytes 294920 | tf_op jit(solution)/shard_map/ppermute | solution.py:200
  274.0 30.8 %collective-permute-start.25 = (bf16[384,128]{1,0:T(8,128)(2,1)}, bf16[384,128]{1,0:T(8,128)(2,1)}, u32[]{:S(2)}, u32[]{:S(2)}) collective-permute-start(bf16[384,128]{1,0:T(8,128)(2,1)} %get-tuple-element.134), channel_id=1, source_target_pairs={{0,16},{8,24},{16,0},{24,8},{1,17},{9,25},{17,1},{25,9},{2,18},{10... | collective-permute-start | bytes 294920 | tf_op jit(solution)/shard_map/ppermute | solution.py:200
  275.5 30.2 %collective-permute-start.24 = (bf16[384,128]{1,0:T(8,128)(2,1)}, bf16[384,128]{1,0:T(8,128)(2,1)}, u32[]{:S(2)}, u32[]{:S(2)}) collective-permute-start(bf16[384,128]{1,0:T(8,128)(2,1)} %get-tuple-element.135), channel_id=1, source_target_pairs={{0,8},{8,0},{16,24},{24,16},{1,9},{9,1},{17,25},{25,17},{2,10},{10... | collective-permute-start | bytes 294920 | tf_op jit(solution)/shard_map/ppermute | solution.py:200
  277.1 30.3 %collective-permute-start.14 = (bf16[384,128]{1,0:T(8,128)(2,1)}, bf16[384,128]{1,0:T(8,128)(2,1)}, u32[]{:S(2)}, u32[]{:S(2)}) collective-permute-start(bf16[384,128]{1,0:T(8,128)(2,1)} %get-tuple-element.129), channel_id=1, source_target_pairs={{0,24},{8,16},{16,8},{24,0},{1,25},{9,17},{17,9},{25,1},{2,26},{10... | collective-permute-start | bytes 294920 | tf_op jit(solution)/shard_map/ppermute | solution.py:200
  294.7 78.7 %collective-permute-start.22 = (bf16[2,128,3200]{2,1,0:T(8,128)(2,1)S(1)}, bf16[2,128,3200]{2,1,0:T(8,128)(2,1)S(1)}, u32[]{:S(2)}, u32[]{:S(2)}) collective-permute-start(bf16[2,128,3200]{2,1,0:T(8,128)(2,1)S(1)} %dynamic-slice_bitcast_fusion), channel_id=1, source_target_pairs={{0,8},{8,0},{16,24},{24,16},{1,9},{9,1},{17,25},{25,17},{2,10},{10... | collective-permute-start | bytes 4915208 | tf_op jit(solution)/shard_map/ppermute | solution.py:200
  304.8 41.1 %collective-permute-start.12 = (bf16[384,128]{1,0:T(8,128)(2,1)S(1)}, bf16[384,128]{1,0:T(8,128)(2,1)S(1)}, u32[]{:S(2)}, u32[]{:S(2)}) collective-permute-start(bf16[384,128]{1,0:T(8,128)(2,1)S(1)} %copy-done.45), channel_id=1, source_target_pairs={{0,8},{8,0},{16,24},{24,16},{1,9},{9,1},{17,25},{25,17},{2,10},{10... | collective-permute-start | bytes 294920 | tf_op jit(solution)/shard_map/ppermute | solution.py:200
  348.9 45.3 %collective-permute-start.20 = (bf16[2,128,3200]{2,1,0:T(8,128)(2,1)}, bf16[2,128,3200]{2,1,0:T(8,128)(2,1)S(1)}, u32[]{:S(2)}, u32[]{:S(2)}) collective-permute-start(bf16[2,128,3200]{2,1,0:T(8,128)(2,1)} %dynamic-slice_bitcast_fusion.1), channel_id=1, source_target_pairs={{0,16},{8,24},{16,0},{24,8},{1,17},{9,25},{17,1},{25,9},{2,18},{10... | collective-permute-start | bytes 4915208 | tf_op jit(solution)/shard_map/ppermute | solution.py:200
  369.9 72.0 %collective-permute-start.17 = (bf16[384,384]{1,0:T(8,128)(2,1)}, bf16[384,384]{1,0:T(8,128)(2,1)}, u32[]{:S(2)}, u32[]{:S(2)}) collective-permute-start(bf16[384,384]{1,0:T(8,128)(2,1)} %get-tuple-element.98), channel_id=1, source_target_pairs={{0,8},{8,0},{16,24},{24,16},{1,9},{9,1},{17,25},{25,17},{2,10},{10... | collective-permute-start | bytes 884744 | tf_op jit(solution)/shard_map/ppermute | solution.py:200
  370.4 71.7 %collective-permute-start.18 = (bf16[384,384]{1,0:T(8,128)(2,1)}, bf16[384,384]{1,0:T(8,128)(2,1)}, u32[]{:S(2)}, u32[]{:S(2)}) collective-permute-start(bf16[384,384]{1,0:T(8,128)(2,1)} %get-tuple-element.97), channel_id=1, source_target_pairs={{0,16},{8,24},{16,0},{24,8},{1,17},{9,25},{17,1},{25,9},{2,18},{10... | collective-permute-start | bytes 884744 | tf_op jit(solution)/shard_map/ppermute | solution.py:200
  370.7 71.4 %collective-permute-start.19 = (bf16[384,384]{1,0:T(8,128)(2,1)}, bf16[384,384]{1,0:T(8,128)(2,1)}, u32[]{:S(2)}, u32[]{:S(2)}) collective-permute-start(bf16[384,384]{1,0:T(8,128)(2,1)} %get-tuple-element.96), channel_id=1, source_target_pairs={{0,24},{8,16},{16,8},{24,0},{1,25},{9,17},{17,9},{25,1},{2,26},{10... | collective-permute-start | bytes 884744 | tf_op jit(solution)/shard_map/ppermute | solution.py:200
  373.8 42.7 %collective-permute-start.23 = (bf16[128,3200]{1,0:T(8,128)(2,1)S(1)}, bf16[128,3200]{1,0:T(8,128)(2,1)S(1)}, u32[]{:S(2)}, u32[]{:S(2)}) collective-permute-start(bf16[128,3200]{1,0:T(8,128)(2,1)S(1)} %dynamic-slice_bitcast_fusion.2), channel_id=1, source_target_pairs={{0,16},{8,24},{16,0},{24,8},{1,17},{9,25},{17,1},{25,9},{2,18},{10... | collective-permute-start | bytes 2457608 | tf_op jit(solution)/shard_map/ppermute | solution.py:200
  415.1 37.7 %collective-permute-start.27 = (bf16[384,384]{1,0:T(8,128)(2,1)}, bf16[384,384]{1,0:T(8,128)(2,1)S(1)}, u32[]{:S(2)}, u32[]{:S(2)}) collective-permute-start(bf16[384,384]{1,0:T(8,128)(2,1)} %get-tuple-element.102), channel_id=1, source_target_pairs={{0,8},{8,0},{16,24},{24,16},{1,9},{9,1},{17,25},{25,17},{2,10},{10... | collective-permute-start | bytes 884744 | tf_op jit(solution)/shard_map/ppermute | solution.py:200
  416.5 22.3 %collective-permute-start.21 = (bf16[128,3200]{1,0:T(8,128)(2,1)S(1)}, bf16[128,3200]{1,0:T(8,128)(2,1)S(1)}, u32[]{:S(2)}, u32[]{:S(2)}) collective-permute-start(bf16[128,3200]{1,0:T(8,128)(2,1)S(1)} %dynamic-slice_bitcast_fusion.3), channel_id=1, source_target_pairs={{0,8},{8,0},{16,24},{24,16},{1,9},{9,1},{17,25},{25,17},{2,10},{10... | collective-permute-start | bytes 2457608 | tf_op jit(solution)/shard_map/ppermute | solution.py:200
  438.9 14.0 %collective-permute-start.28 = (bf16[384,384]{1,0:T(8,128)(2,1)}, bf16[384,384]{1,0:T(8,128)(2,1)}, u32[]{:S(2)}, u32[]{:S(2)}) collective-permute-start(bf16[384,384]{1,0:T(8,128)(2,1)} %get-tuple-element.101), channel_id=1, source_target_pairs={{0,16},{8,24},{16,0},{24,8},{1,17},{9,25},{17,1},{25,9},{2,18},{10... | collective-permute-start | bytes 884744 | tf_op jit(solution)/shard_map/ppermute | solution.py:200
  448.6 27.5 %collective-permute-start.30 = (bf16[1024,768]{1,0:T(8,128)(2,1)}, bf16[1024,768]{1,0:T(8,128)(2,1)}, u32[]{:S(2)}, u32[]{:S(2)}) collective-permute-start(bf16[1024,768]{1,0:T(8,128)(2,1)} %convolution_convert_fusion.3.refs_4_), channel_id=1, source_target_pairs={{0,1},{1,0},{2,3},{3,2},{4,5},{5,4},{6,7},{7,6},{8,9},{9,8},{10,11... | collective-permute-start | bytes 4718600 | tf_op jit(solution)/shard_map/ppermute | solution.py:200
  451.1 21.0 %collective-permute-start.50 = (bf16[128,3200]{1,0:T(8,128)(2,1)}, bf16[128,3200]{1,0:T(8,128)(2,1)}, u32[]{:S(2)}, u32[]{:S(2)}) collective-permute-start(bf16[128,3200]{1,0:T(8,128)(2,1)} %get-tuple-element.89), channel_id=1, source_target_pairs={{0,2},{2,0},{4,6},{6,4},{1,3},{3,1},{5,7},{7,5},{8,10},{10,8},{12,... | collective-permute-start | bytes 2457608 | tf_op jit(solution)/shard_map/ppermute | solution.py:200
  466.6 15.3 %collective-permute-start.40 = (bf16[1024,768]{1,0:T(8,128)(2,1)}, bf16[1024,768]{1,0:T(8,128)(2,1)}, u32[]{:S(2)}, u32[]{:S(2)}) collective-permute-start(bf16[1024,768]{1,0:T(8,128)(2,1)} %convolution_convert_fusion.2), channel_id=1, source_target_pairs={{0,1},{1,0},{2,3},{3,2},{4,5},{5,4},{6,7},{7,6},{8,9},{9,8},{10,11... | collective-permute-start | bytes 4718600 | tf_op jit(solution)/shard_map/ppermute | solution.py:200
  473.5 30.5 %collective-permute-start.51 = (bf16[64,3200]{1,0:T(8,128)(2,1)S(1)}, bf16[64,3200]{1,0:T(8,128)(2,1)S(1)}, u32[]{:S(2)}, u32[]{:S(2)}) collective-permute-start(bf16[64,3200]{1,0:T(8,128)(2,1)S(1)} %get-tuple-element.115), channel_id=1, source_target_pairs={{0,4},{2,6},{4,0},{6,2},{1,5},{3,7},{5,1},{7,3},{8,12},{10,14},{12... | collective-permute-start | bytes 1228808 | tf_op jit(solution)/shard_map/ppermute | solution.py:200
  478.8 25.4 %collective-permute-start.31 = (bf16[2,128,768]{2,1,0:T(8,128)(2,1)S(1)}, bf16[2,128,768]{2,1,0:T(8,128)(2,1)S(1)}, u32[]{:S(2)}, u32[]{:S(2)}) collective-permute-start(bf16[2,128,768]{2,1,0:T(8,128)(2,1)S(1)} %dynamic-slice_bitcast_fusion.7), channel_id=1, source_target_pairs={{0,16},{8,24},{16,0},{24,8},{1,17},{9,25},{17,1},{25,9},{2,18},{10... | collective-permute-start | bytes 1179656 | tf_op jit(solution)/shard_map/ppermute | solution.py:200
  480.5 23.8 %collective-permute-start.32 = (bf16[2,128,768]{2,1,0:T(8,128)(2,1)S(1)}, bf16[2,128,768]{2,1,0:T(8,128)(2,1)S(1)}, u32[]{:S(2)}, u32[]{:S(2)}) collective-permute-start(bf16[2,128,768]{2,1,0:T(8,128)(2,1)S(1)} %dynamic-slice_bitcast_fusion.6), channel_id=1, source_target_pairs={{0,8},{8,0},{16,24},{24,16},{1,9},{9,1},{17,25},{25,17},{2,10},{10... | collective-permute-start | bytes 1179656 | tf_op jit(solution)/shard_map/ppermute | solution.py:200
  484.5 23.0 %collective-permute-start.41 = (bf16[2,128,768]{2,1,0:T(8,128)(2,1)S(1)}, bf16[2,128,768]{2,1,0:T(8,128)(2,1)S(1)}, u32[]{:S(2)}, u32[]{:S(2)}) collective-permute-start(bf16[2,128,768]{2,1,0:T(8,128)(2,1)S(1)} %dynamic-slice_bitcast_fusion.5), channel_id=1, source_target_pairs={{0,16},{8,24},{16,0},{24,8},{1,17},{9,25},{17,1},{25,9},{2,18},{10... | collective-permute-start | bytes 1179656 | tf_op jit(solution)/shard_map/ppermute | solution.py:200
  485.1 22.5 %collective-permute-start.42 = (bf16[2,128,768]{2,1,0:T(8,128)(2,1)S(1)}, bf16[2,128,768]{2,1,0:T(8,128)(2,1)S(1)}, u32[]{:S(2)}, u32[]{:S(2)}) collective-permute-start(bf16[2,128,768]{2,1,0:T(8,128)(2,1)S(1)} %dynamic-slice_bitcast_fusion.4), channel_id=1, source_target_pairs={{0,8},{8,0},{16,24},{24,16},{1,9},{9,1},{17,25},{25,17},{2,10},{10... | collective-permute-start | bytes 1179656 | tf_op jit(solution)/shard_map/ppermute | solution.py:200
  504.1 30.7 %collective-permute-start.52 = (bf16[64,3200]{1,0:T(8,128)(2,1)S(1)}, bf16[64,3200]{1,0:T(8,128)(2,1)S(1)}, u32[]{:S(2)}, u32[]{:S(2)}) collective-permute-start(bf16[64,3200]{1,0:T(8,128)(2,1)S(1)} %add_convert_fusion.8), channel_id=1, source_target_pairs={{0,4},{2,6},{4,0},{6,2},{1,5},{3,7},{5,1},{7,3},{8,12},{10,14},{12... | collective-permute-start | bytes 1228808 | tf_op jit(solution)/shard_map/ppermute | solution.py:200
  504.4 30.5 %collective-permute-start.33 = (bf16[128,768]{1,0:T(8,128)(2,1)S(1)}, bf16[128,768]{1,0:T(8,128)(2,1)S(1)}, u32[]{:S(2)}, u32[]{:S(2)}) collective-permute-start(bf16[128,768]{1,0:T(8,128)(2,1)S(1)} %dynamic-slice_bitcast_fusion.11), channel_id=1, source_target_pairs={{0,8},{8,0},{16,24},{24,16},{1,9},{9,1},{17,25},{25,17},{2,10},{10... | collective-permute-start | bytes 589832 | tf_op jit(solution)/shard_map/ppermute | solution.py:200
  506.0 29.1 %collective-permute-start.34 = (bf16[128,768]{1,0:T(8,128)(2,1)S(1)}, bf16[128,768]{1,0:T(8,128)(2,1)S(1)}, u32[]{:S(2)}, u32[]{:S(2)}) collective-permute-start(bf16[128,768]{1,0:T(8,128)(2,1)S(1)} %dynamic-slice_bitcast_fusion.10), channel_id=1, source_target_pairs={{0,16},{8,24},{16,0},{24,8},{1,17},{9,25},{17,1},{25,9},{2,18},{10... | collective-permute-start | bytes 589832 | tf_op jit(solution)/shard_map/ppermute | solution.py:200
  507.8 29.8 %collective-permute-start.43 = (bf16[128,768]{1,0:T(8,128)(2,1)S(1)}, bf16[128,768]{1,0:T(8,128)(2,1)S(1)}, u32[]{:S(2)}, u32[]{:S(2)}) collective-permute-start(bf16[128,768]{1,0:T(8,128)(2,1)S(1)} %dynamic-slice_bitcast_fusion.9), channel_id=1, source_target_pairs={{0,8},{8,0},{16,24},{24,16},{1,9},{9,1},{17,25},{25,17},{2,10},{10... | collective-permute-start | bytes 589832 | tf_op jit(solution)/shard_map/ppermute | solution.py:200
  508.4 29.3 %collective-permute-start.44 = (bf16[128,768]{1,0:T(8,128)(2,1)S(1)}, bf16[128,768]{1,0:T(8,128)(2,1)S(1)}, u32[]{:S(2)}, u32[]{:S(2)}) collective-permute-start(bf16[128,768]{1,0:T(8,128)(2,1)S(1)} %dynamic-slice_bitcast_fusion.8), channel_id=1, source_target_pairs={{0,16},{8,24},{16,0},{24,8},{1,17},{9,25},{17,1},{25,9},{2,18},{10... | collective-permute-start | bytes 589832 | tf_op jit(solution)/shard_map/ppermute | solution.py:200
  534.9 53.7 %collective-permute-start.53 = (bf16[128,3200]{1,0:T(8,128)(2,1)S(1)}, bf16[128,3200]{1,0:T(8,128)(2,1)S(1)}, u32[]{:S(2)}, u32[]{:S(2)}) collective-permute-start(bf16[128,3200]{1,0:T(8,128)(2,1)S(1)} %pad_maximum_fusion.9), channel_id=1, source_target_pairs={{0,2},{2,0},{4,6},{6,4},{1,3},{3,1},{5,7},{7,5},{8,10},{10,8},{12,... | collective-permute-start | bytes 2457608 | tf_op jit(solution)/shard_map/ppermute | solution.py:200
  535.6 24.7 %collective-permute-start.35 = (bf16[128,768]{1,0:T(8,128)(2,1)S(1)}, bf16[128,768]{1,0:T(8,128)(2,1)S(1)}, u32[]{:S(2)}, u32[]{:S(2)}) collective-permute-start(bf16[128,768]{1,0:T(8,128)(2,1)S(1)} %get-tuple-element.127), channel_id=1, source_target_pairs={{0,2},{2,0},{4,6},{6,4},{1,3},{3,1},{5,7},{7,5},{8,10},{10,8},{12,... | collective-permute-start | bytes 589832 | tf_op jit(solution)/shard_map/ppermute | solution.py:200
  538.2 26.4 %collective-permute-start.45 = (bf16[128,768]{1,0:T(8,128)(2,1)S(1)}, bf16[128,768]{1,0:T(8,128)(2,1)S(1)}, u32[]{:S(2)}, u32[]{:S(2)}) collective-permute-start(bf16[128,768]{1,0:T(8,128)(2,1)S(1)} %get-tuple-element.123), channel_id=1, source_target_pairs={{0,2},{2,0},{4,6},{6,4},{1,3},{3,1},{5,7},{7,5},{8,10},{10,8},{12,... | collective-permute-start | bytes 589832 | tf_op jit(solution)/shard_map/ppermute | solution.py:200
  538.3 51.1 %collective-permute-start.55 = (bf16[328,1024]{1,0:T(8,128)(2,1)}, bf16[328,1024]{1,0:T(8,128)(2,1)S(1)}, u32[]{:S(2)}, u32[]{:S(2)}) collective-permute-start(bf16[328,1024]{1,0:T(8,128)(2,1)} %all-reduce.5.cloned.1.call-done), channel_id=1, source_target_pairs={{0,1},{1,0},{2,3},{3,2},{4,5},{5,4},{6,7},{7,6},{8,9},{9,8},{10,11... | collective-permute-start | bytes 2015240 | tf_op jit(solution)/shard_map/ppermute | solution.py:200
  588.9 15.2 %collective-permute-start.54 = (bf16[256,3200]{1,0:T(8,128)(2,1)S(1)}, bf16[256,3200]{1,0:T(8,128)(2,1)S(1)}, u32[]{:S(2)}, u32[]{:S(2)}) collective-permute-start(bf16[256,3200]{1,0:T(8,128)(2,1)S(1)} %pad_maximum_fusion.3), channel_id=1, source_target_pairs={{0,1},{1,0},{2,3},{3,2},{4,5},{5,4},{6,7},{7,6},{8,9},{9,8},{10,11... | collective-permute-start | bytes 4915208 | tf_op jit(solution)/shard_map/ppermute | solution.py:200
  (76 other events, 645.9 us)
Sparse Core Ops, SparseCore 0:
  10.5 48.3 all-gather.4
  61.3 103.2 all-gather.6
  167.1 41.6 all-gather.8
  261.9 69.0 reduce-scatter.1
  467.0 64.7 all-reduce.4

commit v5 on v4

--- a/solution.py
+++ b/solution.py
@@ -121,10 +121,10 @@
     return [pl.BlockSpec(memory_space=pl.ANY)] * len(after)
 
 
-def project(me, first_normed, w_in, cos, sin, pair, group):
+def project(me, first_normed, w_in, cos, sin, pair, group, after=()):
     rows = first_normed.shape[0]
     return pl.pallas_call(
-        project_kernel,
+        skipping(project_kernel, 5, len(after)),
         grid_spec=pltpu.PrefetchScalarGridSpec(
             num_scalar_prefetch=1,
             grid=(group,),
@@ -133,22 +133,23 @@
                 pl.BlockSpec((D, 3 * PAIR), lambda d, me: (0, pair * group + (me[0] ^ d))),
                 pl.BlockSpec((1, rows, PAIR), lambda d, me: (0, 0, 0)),
                 pl.BlockSpec((1, rows, PAIR), lambda d, me: (0, 0, 0)),
+                *untouched(after),
             ],
             out_specs=pl.BlockSpec((1, rows, 3 * PAIR), lambda d, me: (d, 0, 0)),
         ),
         out_shape=jax.ShapeDtypeStruct((group, rows, 3 * PAIR), jnp.bfloat16),
         compiler_params=compiler_params(),
         name="project",
-    )(me, first_normed, w_in, cos, sin)
+    )(me, first_normed, w_in, cos, sin, *after)
 
 
 def row_product_kernel(me_ref, x_ref, w_ref, out_ref):
     out_ref[0] = against(x_ref[...], w_ref[...]).astype(jnp.bfloat16)
 
 
-def row_product(me, left, weight, pair, group, after=()):
+def row_product(me, left, weight, group, after=()):
     rows = left.shape[0]
-    pairs = D // PAIR // group
+    wide = D // group
     return pl.pallas_call(
         skipping(row_product_kernel, 3, len(after)),
         grid_spec=pltpu.PrefetchScalarGridSpec(
@@ -156,12 +157,12 @@
             grid=(group,),
             in_specs=[
                 pl.BlockSpec((rows, D), lambda d, me: (0, 0)),
-                pl.BlockSpec((PAIR, D), lambda d, me: ((me[0] ^ d) * pairs + pair, 0)),
+                pl.BlockSpec((wide, D), lambda d, me: (me[0] ^ d, 0)),
                 *untouched(after),
             ],
-            out_specs=pl.BlockSpec((1, rows, PAIR), lambda d, me: (d, 0, 0)),
+            out_specs=pl.BlockSpec((1, rows, wide), lambda d, me: (d, 0, 0)),
         ),
-        out_shape=jax.ShapeDtypeStruct((group, rows, PAIR), jnp.bfloat16),
+        out_shape=jax.ShapeDtypeStruct((group, rows, wide), jnp.bfloat16),
         compiler_params=compiler_params(),
         name="row_product",
     )(me, left, weight, *after)
@@ -202,6 +203,43 @@
 
 def swap_heads(pieces, group):
     return [pieces[0]] + [exchange(pieces[d], "grp", d, group) for d in range(1, group)]
+
+
+def assemble_kernel(me_ref, own_ref, other_ref, out_ref):
+    @pl.when(pl.program_id(1) == 0)
+    def _():
+        out_ref[...] = own_ref[0]
+
+    @pl.when(pl.program_id(1) == 1)
+    def _():
+        out_ref[...] = other_ref[0]
+
+
+def near_parts(part, group):
+    return jnp.stack([part] + [exchange(part, "grp", d, group) for d in range(1, group)])
+
+
+def gather_direct(own, me_core, group, by_rows):
+    other = exchange(own, "core", 1, 2)
+    rows, columns = own.shape[1:]
+    if by_rows:
+        shape = (2 * group * rows, columns)
+        target = lambda d, side, me: ((me[0] ^ d) * 2 + (me[1] ^ side), 0)
+    else:
+        shape = (group * rows, 2 * columns)
+        target = lambda d, side, me: (me[0] ^ d, me[1] ^ side)
+    return pl.pallas_call(
+        assemble_kernel,
+        grid_spec=pltpu.PrefetchScalarGridSpec(
+            num_scalar_prefetch=1,
+            grid=(group, 2),
+            in_specs=[pl.BlockSpec((1, rows, columns), lambda d, side, me: (d, 0, 0))] * 2,
+            out_specs=pl.BlockSpec((rows, columns), target),
+        ),
+        out_shape=jax.ShapeDtypeStruct(shape, jnp.bfloat16),
+        compiler_params=compiler_params(),
+        name="assemble",
+    )(me_core, own, other)
 
 
 def attend_kernel(q_ref, k_ref, v_ref, qf_ref, kf_ref, own_v_ref, own_f_ref, out_ref, stat_ref, ke):
@@ -238,7 +276,7 @@
     return 512 if rows <= 2048 else 256
 
 
-def attend(qkv, query_side, key_side):
+def attend(qkv, query_side, key_side, after=()):
     rows = qkv.shape[0]
     block = block_rows(rows)
 
@@ -249,9 +287,11 @@
         return pl.BlockSpec((rows, PAIR), lambda i: (0, part))
 
     return pl.pallas_call(
-        attend_kernel,
+        skipping(attend_kernel, 7, len(after)),
         grid=(rows // block,),
-        in_specs=[some(0), whole(1), whole(2), some(0), whole(0), some(2), some(0)],
+        in_specs=[
+            some(0), whole(1), whole(2), some(0), whole(0), some(2), some(0), *untouched(after),
+        ],
         out_specs=[some(0), some(0)],
         out_shape=[
             jax.ShapeDtypeStruct((rows, PAIR), jnp.bfloat16),
@@ -260,7 +300,7 @@
         scratch_shapes=[pltpu.VMEM((rows, 2 * PAIR), jnp.bfloat16)],
         compiler_params=compiler_params(),
         name="attend",
-    )(qkv, qkv, qkv, query_side, key_side, qkv, key_side)
+    )(qkv, qkv, qkv, query_side, key_side, qkv, key_side, *after)
 
 
 def in_three(column, lane):
@@ -337,7 +377,7 @@
         out_ref[:, 2 * PAIR :] = dv_sum[...].astype(jnp.bfloat16)
 
 
-def attend_back(qkv, query_side, key_side, stat, attended, grad, cos, sin, after=()):
+def attend_back(qkv, query_side, key_side, stat, attended, grad, cos, sin, pair, after=()):
     rows = qkv.shape[0]
     block = block_rows(rows)
 
@@ -351,7 +391,7 @@
         skipping(attend_back_kernel, 12, len(after)),
         grid=(rows // block,),
         in_specs=[
-            some(0), whole(1), whole(2), some(0), whole(0), some(0), some(0), some(0),
+            some(0), whole(1), whole(2), some(0), whole(0), some(0), some(0), some(pair),
             whole(0), whole(0), some(0), some(0), *untouched(after),
         ],
         out_specs=pl.BlockSpec((rows, 3 * PAIR), lambda i: (0, 0)),
@@ -407,10 +447,10 @@
     return lax.optimization_barrier((value, after))[0]
 
 
-def halved(array, mask, group, dim):
+def halved(array, mask, group, dim, after=()):
     bit = (lax.axis_index("grp") // mask) % 2
     got = exchange(pick(array, 1 - bit, dim), "grp", mask, group)
-    return added(pick(array, bit, dim), got)
+    return added(delayed(pick(array, bit, dim), after), got)
 
 
 def core_theirs(left, right, core):
@@ -437,10 +477,12 @@
     )
 
 
-def group_second(halves, group):
+def group_second(halves, group, after=()):
     if group != 4:
         return halves[0]
-    return jnp.concatenate([halved(halves[0], 1, group, 0), halved(halves[1], 2, group, 0)], axis=0)
+    return jnp.concatenate(
+        [halved(halves[0], 1, group, 0, after), halved(halves[1], 2, group, 0, after)], axis=0
+    )
 
 
 def far_masks(far):
@@ -477,14 +519,15 @@
     return share
 
 
-def merged_columns(parts, group):
-    pairs = len(parts)
+def merged_columns(total, pairs, group):
+    half = 3 * PAIR * group // 2
     blocks = []
     for part in range(3):
         for owner in range(group):
             for pair in range(pairs):
-                column = (owner * 3 + part) * PAIR
-                blocks.append(parts[pair][:, column : column + PAIR])
+                side, within = divmod((owner * 3 + part) * PAIR, half)
+                column = (side * pairs + pair) * half + within
+                blocks.append(total[:, column : column + PAIR])
     return jnp.concatenate(blocks, axis=1)
 
 
@@ -536,9 +579,10 @@
     own_gains = norm_gains.shape[0]
     both = ("grp", "core")
     w_in = lax.all_gather(lower_half(core_list, inproj, group), both, axis=0, tiled=True)
-    w_outup = gather_weight(jnp.concatenate([outproj, spread_halves(upproj)], axis=1), core)
-    w_down = gather_weight(downproj, core)
-    w_out, w_up = w_outup[:, :D], w_outup[:, D:]
+    me_core = jnp.stack([me, core]).astype(jnp.int32)
+    near_out = near_parts(own_half(outproj, core).astype(jnp.bfloat16), group)
+    w_out = gather_direct(near_out, me_core, group, True)
+    w_up = gather_weight(spread_halves(upproj), core)
     packed = jnp.concatenate([norm_gains[:, 0], norm_gains[:, 1], slot_ids[0].astype(jnp.float32)])
     packed = lax.all_gather(packed.astype(jnp.bfloat16), "grp", axis=0, tiled=False)
     gain_one = packed[:, :own_gains].reshape(D).astype(jnp.float32)
@@ -555,15 +599,19 @@
     first_normed = layer_norm(inputs, gain_one).astype(jnp.bfloat16)
     cos_near = cos.reshape(group, own_rows, PAIR)
     sin_near = sin.reshape(group, own_rows, PAIR)
-    qkv, stats, attended_near, attended_here = [], [], [], []
+    qkv, stats, attended_near, attended_here, first_sent = [], [], [], [], []
     for pair in range(pairs):
-        pieces = project(me_list, first_normed, w_in, cos_near, sin_near, pair, group)
+        after = (near_out,) if pair == 0 else (first_sent[0],)
+        pieces = project(me_list, first_normed, w_in, cos_near, sin_near, pair, group, after)
+        first_sent.append(pieces)
         qkv.append(jnp.concatenate(swap_heads(pieces, group), axis=0))
     for pair in range(pairs):
-        mixed, stat = attend(qkv[pair], query_side, key_side)
+        mixed, stat = attend(qkv[pair], query_side, key_side, [qkv[-1]] + stats[-1:])
         stats.append(stat)
         attended_near.append(mixed)
         attended_here.append(swap_heads(mixed.reshape(group, own_rows, PAIR), group))
+    low_down = lax.dynamic_slice_in_dim(downproj, core * (D // 2), D // 2, 1).astype(jnp.bfloat16)
+    w_down = gather_direct(near_parts(delayed(low_down, qkv[-1]), group), me_core, group, False)
     attended = place(me_list, attended_here, group)
     middle = inputs + product(attended, w_out)
     second_normed = layer_norm(middle, gain_two).astype(jnp.bfloat16)
@@ -573,28 +621,23 @@
     hidden = gated(gate, upward).astype(jnp.bfloat16)
     result = middle + product(hidden, w_down)
     grad_top = cotangent[0] * live[:, None]
-    grad_hidden = against(grad_top, w_down)
+    grad_down = contract(hidden, grad_top).astype(jnp.bfloat16)
+    grad_hidden = against(delayed(grad_top, grad_down), w_down)
     _, gate_back = jax.vjp(gated, gate, upward)
     grad_gate_up = spread_halves(jnp.concatenate(gate_back(grad_hidden), axis=1)).astype(
         jnp.bfloat16
     )
-    grad_down = contract(hidden, grad_top).astype(jnp.bfloat16)
+    down_share = lax.psum_scatter(grad_down, both, scatter_dimension=0, tiled=True)
     up_theirs = core_theirs(second_normed, grad_gate_up, core)
-    grad_gate_up, up_theirs, grad_down = lax.optimization_barrier(
-        (grad_gate_up, up_theirs, grad_down)
-    )
+    grad_gate_up, up_theirs = lax.optimization_barrier((grad_gate_up, up_theirs))
     grad_second = against(grad_gate_up, w_up)
     _, second_back = jax.vjp(lambda v: layer_norm(v, gain_two), middle)
     (grad_from_norm,) = second_back(grad_second)
     grad_middle = grad_top.astype(jnp.float32) + grad_from_norm
     grad_branch = grad_middle.astype(jnp.bfloat16)
-    down_share = lax.psum_scatter(grad_down, both, scatter_dimension=0, tiled=True)
-    grad_near = []
-    for pair in range(pairs):
-        after = (up_theirs, grad_down) if pair == 0 else (sent,)
-        sent = row_product(me_list, grad_branch, w_outup, pair, group, after)
-        grad_near.append(jnp.concatenate(swap_heads(sent, group), axis=0))
-    out_theirs = core_theirs(attended, grad_branch, core)
+    sent = row_product(me_list, grad_branch, w_out, group, (up_theirs,))
+    grad_near = jnp.concatenate(swap_heads(sent, group), axis=0)
+    out_theirs = core_theirs(attended, delayed(grad_branch, sent), core)
     up_share = jnp.concatenate(
         [
             core_mine(second_normed, grad_gate_up, core, up_theirs),
@@ -602,47 +645,48 @@
         ],
         axis=1,
     )
-    up_halves = group_first(up_share, group)
+    up_halves = group_first(delayed(up_share, grad_near), group)
     up_half = group_second(up_halves, group)
-    waits = [(up_share,), up_halves]
-    grads_here = []
+    grads_here, grads_near = [], [up_share, down_share]
     for pair in range(pairs):
         grads = attend_back(
-            qkv[pair], query_side, key_side, stats[pair], attended_near[pair], grad_near[pair],
-            cos, sin, waits[pair],
+            qkv[pair], query_side, key_side, stats[pair], attended_near[pair], grad_near,
+            cos, sin, pair, grads_near,
         )
+        grads_near = [grads, *up_halves]
         grads_here.append(swap_heads(grads.reshape(group, own_rows, 3 * PAIR), group))
+    down_share = lax.psum(down_share, "far")
     grads_placed, in_theirs, grad_first = [], [], 0.0
     for pair in range(pairs):
-        after = (up_half,) if pair == 0 else (in_theirs[0],)
+        after = (up_half,) if pair == 0 else (in_theirs[0], down_share)
         placed = place(me_list, [grads_here[pair]], group, after)
         grads_placed.append(placed)
         in_theirs.append(core_theirs(first_normed, placed, core))
-    in_shares = [
-        core_mine(first_normed, grads_placed[pair], core, in_theirs[pair]) for pair in range(pairs)
-    ]
-    in_firsts = [delayed(group_first(share, group), in_theirs[-1]) for share in in_shares]
-    in_halves = [group_second(first, group) for first in in_firsts]
-    in_chunks = [far_scatter(half, far) for half in in_halves]
+    in_share = jnp.concatenate(
+        [
+            core_mine(first_normed, grads_placed[pair], core, in_theirs[pair])
+            for pair in range(pairs)
+        ],
+        axis=1,
+    )
+    in_first = group_first(in_share, group)
+    in_half = group_second(in_first, group)
+    in_chunk = far_scatter(in_half, far)
     for pair in range(pairs):
         width = 3 * PAIR * group
         part = w_in[:, pair * width : (pair + 1) * width]
         grad_first = grad_first + against(grads_placed[pair], part)
-    up_chunk = far_scatter(up_half, far, (in_theirs[-1], in_shares[-1]))
-    up_chunk = spread(up_chunk, far, (in_firsts[-1], in_halves[-1]))
-    total_up = doubled(up_chunk, "core", 1, 2, 1, in_chunks[-1]).astype(jnp.float32)
+    up_chunk = far_scatter(up_half, far, (in_theirs[-1], in_share))
+    up_chunk = spread(up_chunk, far, (in_first, in_half))
+    total_up = doubled(up_chunk, "core", 1, 2, 1, in_chunk).astype(jnp.float32)
     wide = up_chunk.shape[1]
     total_out = jnp.concatenate([total_up[:, FF_WIDE:wide], total_up[:, wide + FF_WIDE :]], axis=1)
-    total_up = jnp.concatenate(
-        [total_up[:, :FF], total_up[:, wide : wide + FF]], axis=1
-    )
-    down_share = lax.psum(delayed(down_share, in_theirs[0]), "far")
+    total_up = jnp.concatenate([total_up[:, :FF], total_up[:, wide : wide + FF]], axis=1)
     total_down = doubled(
-        delayed(down_share, in_halves[-1]), "core", 1, 2, 0, in_chunks[-1]
+        delayed(down_share, in_share), "core", 1, 2, 0, in_half
     ).astype(jnp.float32)
-    total_in = merged_columns(
-        [doubled(spread(chunk, far), "core", 1, 2, 1, ()) for chunk in in_chunks], group
-    ).astype(jnp.float32)
+    total_in = merged_columns(doubled(spread(in_chunk, far), "core", 1, 2, 1, ()), pairs, group)
+    total_in = total_in.astype(jnp.float32)
     _, first_back = jax.vjp(lambda v: layer_norm(v, gain_one), inputs)
     (grad_inputs,) = first_back(grad_first)
     input_grad = (grad_middle + grad_inputs).astype(jnp.bfloat16)

time: 638 us -> 655 us (1.027); the launches traced: 627 us -> 651 us
  matrix products: 83.8 us -> 68.4 us
  blocking collectives: 9.73 us -> 23.2 us
  Pallas kernels: 87 us -> 97.5 us
    all_gather x2 -> x1, waiting for transfers between devices: 51.4 us -> 0.01 us  [gather_weight(): lax.all_gather(own_half(weight, core).astype(jnp.bfloat16), ('grp', 'core...]
    ppermute x56 -> x52, waiting for transfers between devices: 199 us -> 249 us  [exchange(): return lax.ppermute(array, axis, [(i, i ^ mask) for i in range(size)])]
    psum x1, waiting for transfers between devices: 0.01 us -> 17.1 us  [local(): down_share = lax.psum(down_share, 'far')]
    pallas_call x4 -> x6, Pallas kernels: 32.3 us -> 47.2 us  [the longest x2 20.5 us: attend(): pl.pallas_call(skipping(attend_kernel, 7, len(after)), grid=(rows // bloc...]
    all_gather x1, blocking collectives: 9.73 us -> 23.2 us  [local(): lax.all_gather(packed.astype(jnp.bfloat16), 'grp', axis=0, tiled=False)]
    convert_element_type x0 -> x1, other arithmetic: none -> 10.3 us  [local(): hidden = gated(gate, upward).astype(jnp.bfloat16)]
    all_gather x1, waiting for transfers between devices: 22.6 us -> 13.6 us  [local(): lax.all_gather(lower_half(core_list, inproj, group), both, axis=0, tiled=...]
    dot_general x3, matrix products: 21 us -> 14.3 us  [product(): return jnp.dot(left, right, preferred_element_type=jnp.float32)]
  transfers between devices with their start and end apart: 61 -> 56, of which waited for: 25 -> 25; matrix products, arithmetic and copies ran while one was open for 20% -> 17% of each run, Pallas kernels for 13% -> 12%
where the time goes in v5:
time: 655 us; the launch traced here: 651 us
  waiting for transfers between devices  280 us (43%)
  Pallas kernels  97.5 us (15%)
  other arithmetic  76.8 us (12%)
  matrix products  68.4 us (10%)
  starting transfers between devices  55.1 us (8%)
  local copies, waits for them, and re-layouts  34.5 us (5%)
  blocking collectives  23.2 us (4%)
  between operations  15.5 us (2%)
    ppermute x52, waiting for transfers between devices, exchange(): return lax.ppermute(array, axis, [(i, i ^ mask) for i in range(size)])  249 us
    ppermute x52, starting transfers between devices, exchange(): return lax.ppermute(array, axis, [(i, i ^ mask) for i in range(size)])  55 us
    pallas_call x2, Pallas kernels, attend_back(): pl.pallas_call(skipping(attend_back_kernel, 12, len(after)), grid=(rows /...  34.1 us
    dot_general x9, matrix products, contract(): lax.dot_general(left, right, (((0,), (0,)), ((), ())), preferred_element_...  29.7 us
    dot_general x4, matrix products, against(): lax.dot_general(left, right, (((1,), (1,)), ((), ())), preferred_element_...  24.4 us
    all_gather x1, blocking collectives, local(): lax.all_gather(packed.astype(jnp.bfloat16), 'grp', axis=0, tiled=False)  23.2 us
    sub x5, other arithmetic, adam_update(): return (mean_new, square_new, weight - rate * (step_size + 0.01 * weight))  23.2 us
    pallas_call x2, Pallas kernels, attend(): pl.pallas_call(skipping(attend_kernel, 7, len(after)), grid=(rows // bloc...  20.5 us
  transfers between devices with their start and end apart: 56, of which 25 were waited for; matrix products, arithmetic and copies ran while one was open for 17% of the time, Pallas kernels for 12%

profile of v5, /device:TPU:0, one launch (start us, length us, event | category | flops | bytes accessed | tf_op | source)
XLA Modules:
  0.0 651.1 jit_solution(8917669294005357020)
XLA Ops:
  15.6 4.0 collective-permute-start.2
  20.2 23.2 %all-gather = bf16[4,1,896]{2,1,0:T(2,128)(2,1)S(1)} all-gather(bf16[1,1,896]{2,1,0:T(2,128)(2,1)S(1)} %maximum_bitcast_fusion), channel_id=1, replica_groups=mesh['grp'=4,'far'=4,'core'=2] {'grp'}, dimensions={0}, use_global_device_ids=true | all-gather | bytes 8960 | tf_op jit(solution)/shard_map/all_gather | solution.py:587
  47.8 4.6 fusion.46
  53.5 13.6 %all-gather.4.cloned.1.call-done.refs_2_ = bf16[1024,3072]{1,0:T(8,128)(2,1)} async-done(((bf16[128,3072]{1,0:T(8,128)(2,1)}), bf16[1024,3072]{1,0:T(8,128)(2,1)}) %all-gather.4.cloned.1.call-update) | async-done | bytes 6291472 | tf_op jit(solution)/shard_map/all_gather | solution.py:581
  67.1 5.8 project.2.refs_5_
  72.9 5.9 project.3
  85.4 12.2 %collective-permute-done.8 = bf16[384,384]{1,0:T(8,128)(2,1)S(1)} collective-permute-done((bf16[384,384]{1,0:T(8,128)(2,1)S(1)}, bf16[384,384]{1,0:T(8,128)(2,1)S(1)}, u32[]{:S(2)}, u32[]{:S(2)}) %collective-permute-start.8) | collective-permute-done | bytes 294944 | tf_op jit(solution)/shard_map/ppermute | solution.py:201
  97.5 6.0 collective-permute-done.7
  103.6 4.3 collective-permute-done.6
  112.5 26.2 %collective-permute-done.18 = bf16[656,512]{1,0:T(8,128)(2,1)S(1)} collective-permute-done((bf16[656,512]{1,0:T(8,128)(2,1)S(1)}, bf16[656,512]{1,0:T(8,128)(2,1)S(1)}, u32[]{:S(2)}, u32[]{:S(2)}) %collective-permute-start.18) | collective-permute-done | bytes 671776 | tf_op jit(solution)/shard_map/ppermute | solution.py:201
  138.7 17.0 %collective-permute-done.17 = bf16[656,512]{1,0:T(8,128)(2,1)S(1)} collective-permute-done((bf16[656,512]{1,0:T(8,128)(2,1)S(1)}, bf16[656,512]{1,0:T(8,128)(2,1)S(1)}, u32[]{:S(2)}, u32[]{:S(2)}) %collective-permute-start.17) | collective-permute-done | bytes 671776 | tf_op jit(solution)/shard_map/ppermute | solution.py:201
  155.7 11.7 %collective-permute-done.16 = bf16[656,512]{1,0:T(8,128)(2,1)S(1)} collective-permute-done((bf16[656,512]{1,0:T(8,128)(2,1)S(1)}, bf16[656,512]{1,0:T(8,128)(2,1)S(1)}, u32[]{:S(2)}, u32[]{:S(2)}) %collective-permute-start.16) | collective-permute-done | bytes 671776 | tf_op jit(solution)/shard_map/ppermute | solution.py:201
  176.8 5.5 collective-permute-done.5
  182.3 4.9 collective-permute-done.4
  189.6 10.3 %attend.2 = (bf16[1536,128]{1,0:T(8,128)(2,1)}, f32[1536,128]{1,0:T(8,128)}) custom-call(bf16[1536,384]{1,0:T(8,128)(2,1)} %pad_maximum_fusion.8.refs_0_.refs_1_.refs_2_.refs_5_, bf16[1536,384]{1,0:T(8,128)(2,1)} %pad_maximum_fusion.8.refs_0_.refs_1_.refs_2_.refs_5_, bf16[1536,384]{1,0:T(8,128)(2,1)} %pad_maximum_fusion.8.refs_0_.refs_1_.refs_2_.refs_5_, ...), custom_call_target="tpu_custom_call" | custom-call | tf_op jit(solution)/shard_map/attend/pallas_call | solution.py:289
  205.0 10.2 %attend.3 = (bf16[1536,128]{1,0:T(8,128)(2,1)}, f32[1536,128]{1,0:T(8,128)}) custom-call(bf16[1536,384]{1,0:T(8,128)(2,1)} %pad_maximum_fusion.9.refs_7_.refs_0_.refs_1_.refs_2_.refs_5_, bf16[1536,384]{1,0:T(8,128)(2,1)} %pad_maximum_fusion.9.refs_7_.refs_0_.refs_1_.refs_2_.refs_5_, ...), custom_call_target="tpu_custom_call" | custom-call | tf_op jit(solution)/shard_map/attend/pallas_call | solution.py:289
  221.1 6.3 assemble.2.refs_2_
  235.3 8.8 %assemble.3 = bf16[2624,1024]{1,0:T(8,128)(2,1)} custom-call(s32[2]{0:T(128)} %pad_add_fusion.me_ref, bf16[4,656,512]{2,1,0:T(8,128)(2,1)} %copy-done.8, bf16[4,656,512]{2,1,0:T(8,128)(2,1)} %collective-permute-done.19.other_ref), custom_call_target="tpu_custom_call" | custom-call | tf_op jit(solution)/shard_map/assemble/pallas_call | solution.py:231
  244.1 8.1 %fusion.100 = f32[384,5376]{1,0:T(8,128)S(1)} fusion(bf16[1024,5376]{1,0:T(8,128)(2,1)} %all-gather.6.cloned.1.call-done, f32[384,1024]{1,0:T(8,128)S(1)} %copy-done.15, f32[1024]{0:T(1024)S(1)} %bitcast.183, f32[384]{0:T(512)S(1)} %fusion.75, f32[384]{0:T(512)S(1)} %broadcast_multiply_fusion), kind=kOutput, calls=%fused_computation.304 | convolution fusion | flops 4229431296 | bytes 20847616 | tf_op jit(solution)/shard_map/dot_general | solution.py:412
  252.3 10.3 %multiply_convert_fusion.1 = (bf16[384,2624]{1,0:T(8,128)(2,1)S(1)}, f32[384,2624]{1,0:T(8,128)}) fusion(f32[384,5376]{1,0:T(8,128)S(1)} %fusion.100), kind=kLoop, calls=%fused_computation.27 | loop fusion | flops 66502656 | bytes 14106624 | tf_op jit(solution)/shard_map/convert_element_type | solution.py:621
  263.9 4.7 convolution_convert_fusion.1
  268.6 10.2 %add_convert_fusion.1 = (bf16[384,2624]{1,0:T(8,128)(2,1)S(1)}, bf16[384,2624]{1,0:T(8,128)(2,1)S(1)}) fusion(f32[384,2624]{1,0:T(8,128)} %get-tuple-element.69, f32[384,5376]{1,0:T(8,128)} %copy-done.10, bf16[384,1024]{1,0:T(8,128)(2,1)S(1)} %copy-done.36, bf16[2624,1024]{1,0:T(8,128)(2,1)} %assemble.3), kind=kOutput, calls=%fused_computation.26 | convolution fusion | flops 2081734656 | bytes 22282240 | tf_op jit(solution)/shard_map/dot_general | solution.py:422
  279.2 5.2 convolution_convert_fusion.refs_3_
  284.4 8.7 %multiply_reduce_fusion.1 = (f32[384]{0:T(512)S(1)}, f32[384,1024]{1,0:T(8,128)S(1)}) fusion(f32[384,1024]{1,0:T(8,128)S(1)} %copy-done.15, f32[384]{0:T(512)S(1)} %broadcast_multiply_fusion, f32[1024]{0:T(1024)S(1)} %bitcast.185, bf16[384,5376]{1,0:T(8,128)(2,1)} %copy-done.18, bf16[1024,5376]{1,0:T(8,128)(2,1)} %all-gather.6.cloned.1.call-done), kind=kOutput, calls=%fused_computation.108 | convolution fusion | flops 4229430784 | bytes 18291712 | tf_op jit(solution)/shard_map/dot_general | solution.py:422
  295.9 4.8 row_product.1
  307.9 4.9 collective-permute-done.22
  321.6 7.0 %add_convert_fusion = bf16[1024,2688]{1,0:T(8,128)(2,1)} fusion(bf16[1024,2688]{1,0:T(8,128)(2,1)} %collective-permute-done.23, bf16[384,5376]{1,0:T(8,128)(2,1)S(1)} %copy-done.19, s32[]{:T(128)S(6)} %select_n.304, f32[384,1024]{1,0:T(8,128)S(1)} %copy-done.15, f32[1024]{0:T(1024)S(1)} %bitcast.186, f32[384]{0:T(512)S(1)} %copy-done.57, f32[384]{0:T(512)S(1)} %copy-done.49), kind=kOutput, calls=%fused_computation.2 | convolution fusion | flops 2123759616 | bytes 14655492 | tf_op jit(solution)/shard_map/dot_general | solution.py:416
  328.6 3.9 pad_maximum_fusion.refs_12_
  336.9 4.3 fusion.47
  346.5 43.2 %collective-permute-done.30 = bf16[2,128,3200]{2,1,0:T(8,128)(2,1)S(1)} collective-permute-done((bf16[2,128,3200]{2,1,0:T(8,128)(2,1)S(1)}, bf16[2,128,3200]{2,1,0:T(8,128)(2,1)S(1)}, u32[]{:S(2)}, u32[]{:S(2)}) %collective-permute-start.30) | collective-permute-done | bytes 1638432 | tf_op jit(solution)/shard_map/ppermute | solution.py:201
  393.0 17.2 %collective-permute-done.31 = bf16[128,3200]{1,0:T(8,128)(2,1)S(1)} collective-permute-done((bf16[128,3200]{1,0:T(8,128)(2,1)S(1)}, bf16[128,3200]{1,0:T(8,128)(2,1)S(1)}, u32[]{:S(2)}, u32[]{:S(2)}) %collective-permute-start.31) | collective-permute-done | bytes 819232 | tf_op jit(solution)/shard_map/ppermute | solution.py:201
  412.3 17.0 %attend_back.2.refs_12_ = bf16[1536,384]{1,0:T(8,128)(2,1)} custom-call(bf16[1536,384]{1,0:T(8,128)(2,1)} %pad_maximum_fusion.8.refs_0_.refs_1_.refs_2_.refs_5_, bf16[1536,384]{1,0:T(8,128)(2,1)} %pad_maximum_fusion.8.refs_0_.refs_1_.refs_2_.refs_5_, bf16[1536,384]{1,0:T(8,128)(2,1)} %pad_maximum_fusion.8.refs_0_.refs_1_.refs_2_.refs_5_, ...), custom_call_target="tpu_custom_call" | custom-call | tf_op jit(solution)/shard_map/attend_back/pallas_call | solution.py:390
  433.3 17.1 %attend_back.3 = bf16[1536,384]{1,0:T(8,128)(2,1)} custom-call(bf16[1536,384]{1,0:T(8,128)(2,1)} %pad_maximum_fusion.9.refs_7_.refs_0_.refs_1_.refs_2_.refs_5_, bf16[1536,384]{1,0:T(8,128)(2,1)} %pad_maximum_fusion.9.refs_7_.refs_0_.refs_1_.refs_2_.refs_5_, bf16[1536,384]{1,0:T(8,128)(2,1)} %pad_maximum_fusion.9.refs_7_.refs_0_.refs_1_.refs_2_.refs_5_, ...), custom_call_target="tpu_custom_call" | custom-call | tf_op jit(solution)/shard_map/attend_back/pallas_call | solution.py:390
  461.2 19.3 %collective-permute-done.26.refs_2_ = bf16[384,384]{1,0:T(8,128)(2,1)} collective-permute-done((bf16[384,384]{1,0:T(8,128)(2,1)}, bf16[384,384]{1,0:T(8,128)(2,1)}, u32[]{:S(2)}, u32[]{:S(2)}) %collective-permute-start.26) | collective-permute-done | bytes 294944 | tf_op jit(solution)/shard_map/ppermute | solution.py:201
  488.8 17.1 %all-reduce.5.cloned.1.call-done.refs_5_ = bf16[328,1024]{1,0:T(8,128)(2,1)} async-done(((bf16[328,1024]{1,0:T(8,128)(2,1)}), bf16[328,1024]{1,0:T(8,128)(2,1)}) %all-reduce.5.cloned.1.call-update) | async-done | bytes 671760 | tf_op jit(solution)/shard_map/psum | solution.py:658
  509.3 3.8 fusion.14
  520.8 3.6 collective-permute-start.47
  531.4 11.8 %collective-permute-done.47 = bf16[64,3200]{1,0:T(8,128)(2,1)S(1)} collective-permute-done((bf16[64,3200]{1,0:T(8,128)(2,1)S(1)}, bf16[64,3200]{1,0:T(8,128)(2,1)S(1)}, u32[]{:S(2)}, u32[]{:S(2)}) %collective-permute-start.47) | collective-permute-done | bytes 409632 | tf_op jit(solution)/shard_map/ppermute | solution.py:201
  543.5 4.8 collective-permute-done.37
  551.6 11.8 %collective-permute-done.48 = bf16[64,3200]{1,0:T(8,128)(2,1)S(1)} collective-permute-done((bf16[64,3200]{1,0:T(8,128)(2,1)S(1)}, bf16[64,3200]{1,0:T(8,128)(2,1)S(1)}, u32[]{:S(2)}, u32[]{:S(2)}) %collective-permute-start.48) | collective-permute-done | bytes 409632 | tf_op jit(solution)/shard_map/ppermute | solution.py:201
  566.6 9.8 %collective-permute-done.41 = bf16[128,1536]{1,0:T(8,128)(2,1)S(1)} collective-permute-done((bf16[128,1536]{1,0:T(8,128)(2,1)S(1)}, bf16[128,1536]{1,0:T(8,128)(2,1)S(1)}, u32[]{:S(2)}, u32[]{:S(2)}) %collective-permute-start.41) | collective-permute-done | bytes 393248 | tf_op jit(solution)/shard_map/ppermute | solution.py:201
  577.3 17.8 %collective-permute-done.42 = bf16[64,1536]{1,0:T(8,128)(2,1)S(1)} collective-permute-done((bf16[64,1536]{1,0:T(8,128)(2,1)S(1)}, bf16[64,1536]{1,0:T(8,128)(2,1)S(1)}, u32[]{:S(2)}, u32[]{:S(2)}) %collective-permute-start.42) | collective-permute-done | bytes 196640 | tf_op jit(solution)/shard_map/ppermute | solution.py:201
  595.2 3.4 collective-permute-start.43
  598.7 8.7 %collective-permute-done.43 = bf16[64,1536]{1,0:T(8,128)(2,1)S(1)} collective-permute-done((bf16[64,1536]{1,0:T(8,128)(2,1)S(1)}, bf16[64,1536]{1,0:T(8,128)(2,1)S(1)}, u32[]{:S(2)}, u32[]{:S(2)}) %collective-permute-start.43) | collective-permute-done | bytes 196640 | tf_op jit(solution)/shard_map/ppermute | solution.py:201
  607.6 4.1 multiply_subtract_fusion.2
  611.7 5.7 collective-permute-done.44
  622.8 5.0 multiply_subtract_fusion.1
  632.5 11.2 %multiply_subtract_fusion = (f32[256,5248]{1,0:T(8,128)}, f32[256,5248]{1,0:T(8,128)}, f32[256,5248]{1,0:T(8,128)}, f32[256]{0:T(256)S(1)}) fusion(f32[256,5248]{1,0:T(8,128)S(1)} %bitcast.165, f32[256,2624]{1,0:T(8,128)S(1)} %get-tuple-element.77, f32[256,2624]{1,0:T(8,128)S(1)} %get-tuple-element.76, f32[256,5248]{1,0:T(8,128)} %param.33, ...), kind=kLoop, calls=%fused_computation.21 | loop fusion | flops 26869504 | bytes 37618688 | tf_op jit(solution)/shard_map/sub | solution.py:547
  (402 shorter events, 150.7 us)
Async XLA Ops:
  7.2 59.9 %all-gather.4.cloned.1.call-start = ((), (), s32[]{:S(2)}) async-start(), calls=%async_computation.1 | async-start | bytes 7077888 | tf_op jit(solution)/shard_map/all_gather | solution.py:581
  9.7 234.4 %all-gather.6.cloned.1.call-start = ((), (), s32[]{:S(2)}) async-start(), calls=%async_computation.2 | async-start | bytes 12386304 | tf_op jit(solution)/shard_map/all_gather | solution.py:433
  15.2 397.2 %reduce-scatter.2.cloned.1.call-start = ((), (), s32[]{:S(2)}) async-start(), calls=%async_computation.3 | async-start | bytes 6045696 | tf_op jit(solution)/shard_map/reduce_scatter | solution.py:630
  15.6 36.8 %collective-permute-start.2 = (bf16[128,1024]{1,0:T(8,128)(2,1)S(1)}, bf16[128,1024]{1,0:T(8,128)(2,1)S(1)}, u32[]{:S(2)}, u32[]{:S(2)}) collective-permute-start(bf16[128,1024]{1,0:T(8,128)(2,1)S(1)} %dynamic-slice_convert_fusion.1), channel_id=1, source_target_pairs={{0,24},{8,16},{16,8},{24,0},{1,25},{9,17},{17,9},{25,1},{2,26},{10... | collective-permute-start | bytes 786440 | tf_op jit(solution)/shard_map/ppermute | solution.py:201
  19.6 32.8 %collective-permute-start.1 = (bf16[128,1024]{1,0:T(8,128)(2,1)S(1)}, bf16[128,1024]{1,0:T(8,128)(2,1)S(1)}, u32[]{:S(2)}, u32[]{:S(2)}) collective-permute-start(bf16[128,1024]{1,0:T(8,128)(2,1)S(1)} %dynamic-slice_convert_fusion.1), channel_id=1, source_target_pairs={{0,16},{8,24},{16,0},{24,8},{1,17},{9,25},{17,1},{25,9},{2,18},{10... | collective-permute-start | bytes 786440 | tf_op jit(solution)/shard_map/ppermute | solution.py:201
  20.1 32.3 %collective-permute-start = (bf16[128,1024]{1,0:T(8,128)(2,1)S(1)}, bf16[128,1024]{1,0:T(8,128)(2,1)S(1)}, u32[]{:S(2)}, u32[]{:S(2)}) collective-permute-start(bf16[128,1024]{1,0:T(8,128)(2,1)S(1)} %dynamic-slice_convert_fusion.1), channel_id=1, source_target_pairs={{0,8},{8,0},{16,24},{24,16},{1,9},{9,1},{17,25},{25,17},{2,10},{10... | collective-permute-start | bytes 786440 | tf_op jit(solution)/shard_map/ppermute | solution.py:201
  80.4 17.1 %collective-permute-start.8 = (bf16[384,384]{1,0:T(8,128)(2,1)S(1)}, bf16[384,384]{1,0:T(8,128)(2,1)S(1)}, u32[]{:S(2)}, u32[]{:S(2)}) collective-permute-start(bf16[384,384]{1,0:T(8,128)(2,1)S(1)} %get-tuple-element.113), channel_id=1, source_target_pairs={{0,24},{8,16},{16,8},{24,0},{1,25},{9,17},{17,9},{25,1},{2,26},{10... | collective-permute-start | bytes 884744 | tf_op jit(solution)/shard_map/ppermute | solution.py:201
  81.7 21.9 %collective-permute-start.7 = (bf16[384,384]{1,0:T(8,128)(2,1)S(1)}, bf16[384,384]{1,0:T(8,128)(2,1)S(1)}, u32[]{:S(2)}, u32[]{:S(2)}) collective-permute-start(bf16[384,384]{1,0:T(8,128)(2,1)S(1)} %get-tuple-element.114), channel_id=1, source_target_pairs={{0,16},{8,24},{16,0},{24,8},{1,17},{9,25},{17,1},{25,9},{2,18},{10... | collective-permute-start | bytes 884744 | tf_op jit(solution)/shard_map/ppermute | solution.py:201
  83.2 24.7 %collective-permute-start.6 = (bf16[384,384]{1,0:T(8,128)(2,1)S(1)}, bf16[384,384]{1,0:T(8,128)(2,1)S(1)}, u32[]{:S(2)}, u32[]{:S(2)}) collective-permute-start(bf16[384,384]{1,0:T(8,128)(2,1)S(1)} %get-tuple-element.115), channel_id=1, source_target_pairs={{0,8},{8,0},{16,24},{24,16},{1,9},{9,1},{17,25},{25,17},{2,10},{10... | collective-permute-start | bytes 884744 | tf_op jit(solution)/shard_map/ppermute | solution.py:201
  109.0 29.7 %collective-permute-start.18 = (bf16[656,512]{1,0:T(8,128)(2,1)S(1)}, bf16[656,512]{1,0:T(8,128)(2,1)S(1)}, u32[]{:S(2)}, u32[]{:S(2)}) collective-permute-start(bf16[656,512]{1,0:T(8,128)(2,1)S(1)} %dynamic-slice_convert_fusion), channel_id=1, source_target_pairs={{0,24},{8,16},{16,8},{24,0},{1,25},{9,17},{17,9},{25,1},{2,26},{10... | collective-permute-start | bytes 2015240 | tf_op jit(solution)/shard_map/ppermute | solution.py:201
  110.5 45.1 %collective-permute-start.17 = (bf16[656,512]{1,0:T(8,128)(2,1)S(1)}, bf16[656,512]{1,0:T(8,128)(2,1)S(1)}, u32[]{:S(2)}, u32[]{:S(2)}) collective-permute-start(bf16[656,512]{1,0:T(8,128)(2,1)S(1)} %dynamic-slice_convert_fusion), channel_id=1, source_target_pairs={{0,16},{8,24},{16,0},{24,8},{1,17},{9,25},{17,1},{25,9},{2,18},{10... | collective-permute-start | bytes 2015240 | tf_op jit(solution)/shard_map/ppermute | solution.py:201
  110.8 56.5 %collective-permute-start.16 = (bf16[656,512]{1,0:T(8,128)(2,1)S(1)}, bf16[656,512]{1,0:T(8,128)(2,1)S(1)}, u32[]{:S(2)}, u32[]{:S(2)}) collective-permute-start(bf16[656,512]{1,0:T(8,128)(2,1)S(1)} %dynamic-slice_convert_fusion), channel_id=1, source_target_pairs={{0,8},{8,0},{16,24},{24,16},{1,9},{9,1},{17,25},{25,17},{2,10},{10... | collective-permute-start | bytes 2015240 | tf_op jit(solution)/shard_map/ppermute | solution.py:201
  167.7 67.6 %collective-permute-start.19 = (bf16[4,656,512]{2,1,0:T(8,128)(2,1)S(1)}, bf16[4,656,512]{2,1,0:T(8,128)(2,1)}, u32[]{:S(2)}, u32[]{:S(2)}) collective-permute-start(bf16[4,656,512]{2,1,0:T(8,128)(2,1)S(1)} %pad_maximum_fusion.3.own_ref), channel_id=1, source_target_pairs={{0,1},{1,0},{2,3},{3,2},{4,5},{5,4},{6,7},{7,6},{8,9},{9,8},{10,11... | collective-permute-start | bytes 8060936 | tf_op jit(solution)/shard_map/ppermute | solution.py:201
  169.6 47.3 %collective-permute-start.15 = (bf16[4,128,1024]{2,1,0:T(8,128)(2,1)}, bf16[4,128,1024]{2,1,0:T(8,128)(2,1)}, u32[]{:S(2)}, u32[]{:S(2)}) collective-permute-start(bf16[4,128,1024]{2,1,0:T(8,128)(2,1)} %pad_maximum_fusion.10.refs_5_.own_ref), channel_id=1, source_target_pairs={{0,1},{1,0},{2,3},{3,2},{4,5},{5,4},{6,7},{7,6},{8,9},{9,8},{10,11... | collective-permute-start | bytes 3145736 | tf_op jit(solution)/shard_map/ppermute | solution.py:201
  171.2 11.1 %collective-permute-start.5 = (bf16[384,384]{1,0:T(8,128)(2,1)}, bf16[384,384]{1,0:T(8,128)(2,1)}, u32[]{:S(2)}, u32[]{:S(2)}) collective-permute-start(bf16[384,384]{1,0:T(8,128)(2,1)} %get-tuple-element.117), channel_id=1, source_target_pairs={{0,24},{8,16},{16,8},{24,0},{1,25},{9,17},{17,9},{25,1},{2,26},{10... | collective-permute-start | bytes 884744 | tf_op jit(solution)/shard_map/ppermute | solution.py:201
  171.2 16.1 %collective-permute-start.4 = (bf16[384,384]{1,0:T(8,128)(2,1)}, bf16[384,384]{1,0:T(8,128)(2,1)}, u32[]{:S(2)}, u32[]{:S(2)}) collective-permute-start(bf16[384,384]{1,0:T(8,128)(2,1)} %get-tuple-element.118), channel_id=1, source_target_pairs={{0,16},{8,24},{16,0},{24,8},{1,17},{9,25},{17,1},{25,9},{2,18},{10... | collective-permute-start | bytes 884744 | tf_op jit(solution)/shard_map/ppermute | solution.py:201
  173.7 13.6 %collective-permute-start.3 = (bf16[384,384]{1,0:T(8,128)(2,1)}, bf16[384,384]{1,0:T(8,128)(2,1)}, u32[]{:S(2)}, u32[]{:S(2)}) collective-permute-start(bf16[384,384]{1,0:T(8,128)(2,1)} %get-tuple-element.119), channel_id=1, source_target_pairs={{0,8},{8,0},{16,24},{24,16},{1,9},{9,1},{17,25},{25,17},{2,10},{10... | collective-permute-start | bytes 884744 | tf_op jit(solution)/shard_map/ppermute | solution.py:201
  201.5 16.4 %collective-permute-start.9 = (bf16[384,128]{1,0:T(8,128)(2,1)S(1)}, bf16[384,128]{1,0:T(8,128)(2,1)S(1)}, u32[]{:S(2)}, u32[]{:S(2)}) collective-permute-start(bf16[384,128]{1,0:T(8,128)(2,1)S(1)} %get-tuple-element.146), channel_id=1, source_target_pairs={{0,8},{8,0},{16,24},{24,16},{1,9},{9,1},{17,25},{25,17},{2,10},{10... | collective-permute-start | bytes 294920 | tf_op jit(solution)/shard_map/ppermute | solution.py:201
  202.5 16.5 %collective-permute-start.10 = (bf16[384,128]{1,0:T(8,128)(2,1)S(1)}, bf16[384,128]{1,0:T(8,128)(2,1)S(1)}, u32[]{:S(2)}, u32[]{:S(2)}) collective-permute-start(bf16[384,128]{1,0:T(8,128)(2,1)S(1)} %get-tuple-element.145), channel_id=1, source_target_pairs={{0,16},{8,24},{16,0},{24,8},{1,17},{9,25},{17,1},{25,9},{2,18},{10... | collective-permute-start | bytes 294920 | tf_op jit(solution)/shard_map/ppermute | solution.py:201
  203.6 23.8 %collective-permute-start.11 = (bf16[384,128]{1,0:T(8,128)(2,1)S(1)}, bf16[384,128]{1,0:T(8,128)(2,1)S(1)}, u32[]{:S(2)}, u32[]{:S(2)}) collective-permute-start(bf16[384,128]{1,0:T(8,128)(2,1)S(1)} %get-tuple-element.144), channel_id=1, source_target_pairs={{0,24},{8,16},{16,8},{24,0},{1,25},{9,17},{17,9},{25,1},{2,26},{10... | collective-permute-start | bytes 294920 | tf_op jit(solution)/shard_map/ppermute | solution.py:201
  217.0 10.5 %collective-permute-start.12 = (bf16[384,128]{1,0:T(8,128)(2,1)S(1)}, bf16[384,128]{1,0:T(8,128)(2,1)S(1)}, u32[]{:S(2)}, u32[]{:S(2)}) collective-permute-start(bf16[384,128]{1,0:T(8,128)(2,1)S(1)} %get-tuple-element.142), channel_id=1, source_target_pairs={{0,8},{8,0},{16,24},{24,16},{1,9},{9,1},{17,25},{25,17},{2,10},{10... | collective-permute-start | bytes 294920 | tf_op jit(solution)/shard_map/ppermute | solution.py:201
  284.4 37.2 %collective-permute-start.23 = (bf16[1024,2688]{1,0:T(8,128)(2,1)}, bf16[1024,2688]{1,0:T(8,128)(2,1)}, u32[]{:S(2)}, u32[]{:S(2)}) collective-permute-start(bf16[1024,2688]{1,0:T(8,128)(2,1)} %convolution_convert_fusion.refs_3_), channel_id=1, source_target_pairs={{0,1},{1,0},{2,3},{3,2},{4,5},{5,4},{6,7},{7,6},{8,9},{9,8},{10,11... | collective-permute-start | bytes 16515080 | tf_op jit(solution)/shard_map/ppermute | solution.py:201
  302.4 15.9 %collective-permute-start.24 = (bf16[1024,512]{1,0:T(8,128)(2,1)}, bf16[1024,512]{1,0:T(8,128)(2,1)}, u32[]{:S(2)}, u32[]{:S(2)}) collective-permute-start(bf16[1024,512]{1,0:T(8,128)(2,1)} %convolution_convert_fusion.4), channel_id=1, source_target_pairs={{0,1},{1,0},{2,3},{3,2},{4,5},{5,4},{6,7},{7,6},{8,9},{9,8},{10,11... | collective-permute-start | bytes 3145736 | tf_op jit(solution)/shard_map/ppermute | solution.py:201
  305.2 10.7 %collective-permute-start.21 = (bf16[384,256]{1,0:T(8,128)(2,1)}, bf16[384,256]{1,0:T(8,128)(2,1)}, u32[]{:S(2)}, u32[]{:S(2)}) collective-permute-start(bf16[384,256]{1,0:T(8,128)(2,1)} %get-tuple-element.134), channel_id=1, source_target_pairs={{0,16},{8,24},{16,0},{24,8},{1,17},{9,25},{17,1},{25,9},{2,18},{10... | collective-permute-start | bytes 589832 | tf_op jit(solution)/shard_map/ppermute | solution.py:201
  336.1 53.6 %collective-permute-start.30 = (bf16[2,128,3200]{2,1,0:T(8,128)(2,1)S(1)}, bf16[2,128,3200]{2,1,0:T(8,128)(2,1)S(1)}, u32[]{:S(2)}, u32[]{:S(2)}) collective-permute-start(bf16[2,128,3200]{2,1,0:T(8,128)(2,1)S(1)} %get-tuple-element.83), channel_id=1, source_target_pairs={{0,8},{8,0},{16,24},{24,16},{1,9},{9,1},{17,25},{25,17},{2,10},{10... | collective-permute-start | bytes 4915208 | tf_op jit(solution)/shard_map/ppermute | solution.py:201
  341.4 50.4 %collective-permute-start.28 = (bf16[2,128,3200]{2,1,0:T(8,128)(2,1)S(1)}, bf16[2,128,3200]{2,1,0:T(8,128)(2,1)S(1)}, u32[]{:S(2)}, u32[]{:S(2)}) collective-permute-start(bf16[2,128,3200]{2,1,0:T(8,128)(2,1)S(1)} %get-tuple-element.85), channel_id=1, source_target_pairs={{0,16},{8,24},{16,0},{24,8},{1,17},{9,25},{17,1},{25,9},{2,18},{10... | collective-permute-start | bytes 4915208 | tf_op jit(solution)/shard_map/ppermute | solution.py:201
  390.3 19.9 %collective-permute-start.31 = (bf16[128,3200]{1,0:T(8,128)(2,1)S(1)}, bf16[128,3200]{1,0:T(8,128)(2,1)S(1)}, u32[]{:S(2)}, u32[]{:S(2)}) collective-permute-start(bf16[128,3200]{1,0:T(8,128)(2,1)S(1)} %get-tuple-element.95), channel_id=1, source_target_pairs={{0,16},{8,24},{16,0},{24,8},{1,17},{9,25},{17,1},{25,9},{2,18},{10... | collective-permute-start | bytes 2457608 | tf_op jit(solution)/shard_map/ppermute | solution.py:201
  392.3 19.8 %collective-permute-start.29 = (bf16[128,3200]{1,0:T(8,128)(2,1)S(1)}, bf16[128,3200]{1,0:T(8,128)(2,1)S(1)}, u32[]{:S(2)}, u32[]{:S(2)}) collective-permute-start(bf16[128,3200]{1,0:T(8,128)(2,1)S(1)} %get-tuple-element.93), channel_id=1, source_target_pairs={{0,8},{8,0},{16,24},{24,16},{1,9},{9,1},{17,25},{25,17},{2,10},{10... | collective-permute-start | bytes 2457608 | tf_op jit(solution)/shard_map/ppermute | solution.py:201
  429.3 76.6 %all-reduce.5.cloned.1.call-start = ((), (), s32[]{:S(2)}) async-start(), calls=%async_computation.4 | async-start | bytes 1343488 | tf_op jit(solution)/shard_map/psum | solution.py:658
  431.5 25.6 %collective-permute-start.25 = (bf16[384,384]{1,0:T(8,128)(2,1)S(1)}, bf16[384,384]{1,0:T(8,128)(2,1)S(1)}, u32[]{:S(2)}, u32[]{:S(2)}) collective-permute-start(bf16[384,384]{1,0:T(8,128)(2,1)S(1)} %get-tuple-element.106), channel_id=1, source_target_pairs={{0,8},{8,0},{16,24},{24,16},{1,9},{9,1},{17,25},{25,17},{2,10},{10... | collective-permute-start | bytes 884744 | tf_op jit(solution)/shard_map/ppermute | solution.py:201
  452.7 36.1 %collective-permute-start.32 = (bf16[384,384]{1,0:T(8,128)(2,1)}, bf16[384,384]{1,0:T(8,128)(2,1)}, u32[]{:S(2)}, u32[]{:S(2)}) collective-permute-start(bf16[384,384]{1,0:T(8,128)(2,1)} %get-tuple-element.110), channel_id=1, source_target_pairs={{0,8},{8,0},{16,24},{24,16},{1,9},{9,1},{17,25},{25,17},{2,10},{10... | collective-permute-start | bytes 884744 | tf_op jit(solution)/shard_map/ppermute | solution.py:201
  454.2 34.6 %collective-permute-start.33 = (bf16[384,384]{1,0:T(8,128)(2,1)}, bf16[384,384]{1,0:T(8,128)(2,1)}, u32[]{:S(2)}, u32[]{:S(2)}) collective-permute-start(bf16[384,384]{1,0:T(8,128)(2,1)} %get-tuple-element.109), channel_id=1, source_target_pairs={{0,16},{8,24},{16,0},{24,8},{1,17},{9,25},{17,1},{25,9},{2,18},{10... | collective-permute-start | bytes 884744 | tf_op jit(solution)/shard_map/ppermute | solution.py:201
  455.0 33.8 %collective-permute-start.34 = (bf16[384,384]{1,0:T(8,128)(2,1)}, bf16[384,384]{1,0:T(8,128)(2,1)}, u32[]{:S(2)}, u32[]{:S(2)}) collective-permute-start(bf16[384,384]{1,0:T(8,128)(2,1)} %get-tuple-element.108), channel_id=1, source_target_pairs={{0,24},{8,16},{16,8},{24,0},{1,25},{9,17},{17,9},{25,1},{2,26},{10... | collective-permute-start | bytes 884744 | tf_op jit(solution)/shard_map/ppermute | solution.py:201
  456.2 24.2 %collective-permute-start.26 = (bf16[384,384]{1,0:T(8,128)(2,1)}, bf16[384,384]{1,0:T(8,128)(2,1)}, u32[]{:S(2)}, u32[]{:S(2)}) collective-permute-start(bf16[384,384]{1,0:T(8,128)(2,1)} %get-tuple-element.105), channel_id=1, source_target_pairs={{0,16},{8,24},{16,0},{24,8},{1,17},{9,25},{17,1},{25,9},{2,18},{10... | collective-permute-start | bytes 884744 | tf_op jit(solution)/shard_map/ppermute | solution.py:201
  457.8 24.2 %collective-permute-start.27 = (bf16[384,384]{1,0:T(8,128)(2,1)}, bf16[384,384]{1,0:T(8,128)(2,1)S(1)}, u32[]{:S(2)}, u32[]{:S(2)}) collective-permute-start(bf16[384,384]{1,0:T(8,128)(2,1)} %get-tuple-element.104), channel_id=1, source_target_pairs={{0,24},{8,16},{16,8},{24,0},{1,25},{9,17},{17,9},{25,1},{2,26},{10... | collective-permute-start | bytes 884744 | tf_op jit(solution)/shard_map/ppermute | solution.py:201
  480.5 38.9 %collective-permute-start.46 = (bf16[128,3200]{1,0:T(8,128)(2,1)S(1)}, bf16[128,3200]{1,0:T(8,128)(2,1)}, u32[]{:S(2)}, u32[]{:S(2)}) collective-permute-start(bf16[128,3200]{1,0:T(8,128)(2,1)S(1)} %get-tuple-element.91), channel_id=1, source_target_pairs={{0,2},{2,0},{4,6},{6,4},{1,3},{3,1},{5,7},{7,5},{8,10},{10,8},{12,... | collective-permute-start | bytes 2457608 | tf_op jit(solution)/shard_map/ppermute | solution.py:201
  488.8 35.6 %collective-permute-start.35 = (bf16[1024,768]{1,0:T(8,128)(2,1)}, bf16[1024,768]{1,0:T(8,128)(2,1)}, u32[]{:S(2)}, u32[]{:S(2)}) collective-permute-start(bf16[1024,768]{1,0:T(8,128)(2,1)} %convolution_convert_fusion.3.refs_4_), channel_id=1, source_target_pairs={{0,1},{1,0},{2,3},{3,2},{4,5},{5,4},{6,7},{7,6},{8,9},{9,8},{10,11... | collective-permute-start | bytes 4718600 | tf_op jit(solution)/shard_map/ppermute | solution.py:201
  520.8 22.4 %collective-permute-start.47 = (bf16[64,3200]{1,0:T(8,128)(2,1)S(1)}, bf16[64,3200]{1,0:T(8,128)(2,1)S(1)}, u32[]{:S(2)}, u32[]{:S(2)}) collective-permute-start(bf16[64,3200]{1,0:T(8,128)(2,1)S(1)} %get-tuple-element.123), channel_id=1, source_target_pairs={{0,4},{2,6},{4,0},{6,2},{1,5},{3,7},{5,1},{7,3},{8,12},{10,14},{12... | collective-permute-start | bytes 1228808 | tf_op jit(solution)/shard_map/ppermute | solution.py:201
  528.6 19.7 %collective-permute-start.37 = (bf16[2,128,1536]{2,1,0:T(8,128)(2,1)S(1)}, bf16[2,128,1536]{2,1,0:T(8,128)(2,1)S(1)}, u32[]{:S(2)}, u32[]{:S(2)}) collective-permute-start(bf16[2,128,1536]{2,1,0:T(8,128)(2,1)S(1)} %get-tuple-element.101), channel_id=1, source_target_pairs={{0,16},{8,24},{16,0},{24,8},{1,17},{9,25},{17,1},{25,9},{2,18},{10... | collective-permute-start | bytes 2359304 | tf_op jit(solution)/shard_map/ppermute | solution.py:201
  530.4 19.4 %collective-permute-start.39 = (bf16[2,128,1536]{2,1,0:T(8,128)(2,1)S(1)}, bf16[2,128,1536]{2,1,0:T(8,128)(2,1)S(1)}, u32[]{:S(2)}, u32[]{:S(2)}) collective-permute-start(bf16[2,128,1536]{2,1,0:T(8,128)(2,1)S(1)} %get-tuple-element.99), channel_id=1, source_target_pairs={{0,8},{8,0},{16,24},{24,16},{1,9},{9,1},{17,25},{25,17},{2,10},{10... | collective-permute-start | bytes 2359304 | tf_op jit(solution)/shard_map/ppermute | solution.py:201
  543.3 20.0 %collective-permute-start.48 = (bf16[64,3200]{1,0:T(8,128)(2,1)S(1)}, bf16[64,3200]{1,0:T(8,128)(2,1)S(1)}, u32[]{:S(2)}, u32[]{:S(2)}) collective-permute-start(bf16[64,3200]{1,0:T(8,128)(2,1)S(1)} %add_convert_fusion.14), channel_id=1, source_target_pairs={{0,4},{2,6},{4,0},{6,2},{1,5},{3,7},{5,1},{7,3},{8,12},{10,14},{12... | collective-permute-start | bytes 1228808 | tf_op jit(solution)/shard_map/ppermute | solution.py:201
  543.4 55.2 %collective-permute-start.51 = (bf16[328,1024]{1,0:T(8,128)(2,1)S(1)}, bf16[328,1024]{1,0:T(8,128)(2,1)S(1)}, u32[]{:S(2)}, u32[]{:S(2)}) collective-permute-start(bf16[328,1024]{1,0:T(8,128)(2,1)S(1)} %copy-done.24), channel_id=1, source_target_pairs={{0,1},{1,0},{2,3},{3,2},{4,5},{5,4},{6,7},{7,6},{8,9},{9,8},{10,11... | collective-permute-start | bytes 2015240 | tf_op jit(solution)/shard_map/ppermute | solution.py:201
  548.6 14.9 %collective-permute-start.38 = (bf16[128,1536]{1,0:T(8,128)(2,1)S(1)}, bf16[128,1536]{1,0:T(8,128)(2,1)S(1)}, u32[]{:S(2)}, u32[]{:S(2)}) collective-permute-start(bf16[128,1536]{1,0:T(8,128)(2,1)S(1)} %get-tuple-element.131), channel_id=1, source_target_pairs={{0,8},{8,0},{16,24},{24,16},{1,9},{9,1},{17,25},{25,17},{2,10},{10... | collective-permute-start | bytes 1179656 | tf_op jit(solution)/shard_map/ppermute | solution.py:201
  550.1 13.5 %collective-permute-start.40 = (bf16[128,1536]{1,0:T(8,128)(2,1)S(1)}, bf16[128,1536]{1,0:T(8,128)(2,1)S(1)}, u32[]{:S(2)}, u32[]{:S(2)}) collective-permute-start(bf16[128,1536]{1,0:T(8,128)(2,1)S(1)} %get-tuple-element.129), channel_id=1, source_target_pairs={{0,16},{8,24},{16,0},{24,8},{1,17},{9,25},{17,1},{25,9},{2,18},{10... | collective-permute-start | bytes 1179656 | tf_op jit(solution)/shard_map/ppermute | solution.py:201
  564.4 12.0 %collective-permute-start.41 = (bf16[128,1536]{1,0:T(8,128)(2,1)S(1)}, bf16[128,1536]{1,0:T(8,128)(2,1)S(1)}, u32[]{:S(2)}, u32[]{:S(2)}) collective-permute-start(bf16[128,1536]{1,0:T(8,128)(2,1)S(1)} %get-tuple-element.127), channel_id=1, source_target_pairs={{0,2},{2,0},{4,6},{6,4},{1,3},{3,1},{5,7},{7,5},{8,10},{10,8},{12,... | collective-permute-start | bytes 1179656 | tf_op jit(solution)/shard_map/ppermute | solution.py:201
  564.6 53.0 %collective-permute-start.49 = (bf16[128,3200]{1,0:T(8,128)(2,1)S(1)}, bf16[128,3200]{1,0:T(8,128)(2,1)S(1)}, u32[]{:S(2)}, u32[]{:S(2)}) collective-permute-start(bf16[128,3200]{1,0:T(8,128)(2,1)S(1)} %pad_maximum_fusion.13), channel_id=1, source_target_pairs={{0,2},{2,0},{4,6},{6,4},{1,3},{3,1},{5,7},{7,5},{8,10},{10,8},{12,... | collective-permute-start | bytes 2457608 | tf_op jit(solution)/shard_map/ppermute | solution.py:201
  576.6 18.5 %collective-permute-start.42 = (bf16[64,1536]{1,0:T(8,128)(2,1)S(1)}, bf16[64,1536]{1,0:T(8,128)(2,1)S(1)}, u32[]{:S(2)}, u32[]{:S(2)}) collective-permute-start(bf16[64,1536]{1,0:T(8,128)(2,1)S(1)} %get-tuple-element.139), channel_id=1, source_target_pairs={{0,4},{2,6},{4,0},{6,2},{1,5},{3,7},{5,1},{7,3},{8,12},{10,14},{12... | collective-permute-start | bytes 589832 | tf_op jit(solution)/shard_map/ppermute | solution.py:201
  595.2 12.2 %collective-permute-start.43 = (bf16[64,1536]{1,0:T(8,128)(2,1)S(1)}, bf16[64,1536]{1,0:T(8,128)(2,1)S(1)}, u32[]{:S(2)}, u32[]{:S(2)}) collective-permute-start(bf16[64,1536]{1,0:T(8,128)(2,1)S(1)} %add_convert_fusion.18), channel_id=1, source_target_pairs={{0,4},{2,6},{4,0},{6,2},{1,5},{3,7},{5,1},{7,3},{8,12},{10,14},{12... | collective-permute-start | bytes 589832 | tf_op jit(solution)/shard_map/ppermute | solution.py:201
  (84 other events, 876.3 us)
Sparse Core Ops, SparseCore 0:
  10.5 56.5 all-gather.3
  69.6 104.7 all-gather.5
  308.0 73.5 reduce-scatter.1
  457.2 48.7 all-reduce.4

commit v6 on v5

--- a/solution.py
+++ b/solution.py
@@ -215,8 +215,19 @@
         out_ref[...] = other_ref[0]
 
 
-def near_parts(part, group):
-    return jnp.stack([part] + [exchange(part, "grp", d, group) for d in range(1, group)])
+def near_first(part, group):
+    steps = (1, 2) if group == 4 else range(1, group)
+    return [exchange(part, "grp", d, group) for d in steps]
+
+
+def near_second(part, near, group, after, later):
+    if group == 4:
+        rows = part.shape[0] // 2
+        first, second = delayed(tuple(near), after)
+        upper = exchange(second[:rows], "grp", 1, group)
+        lower = exchange(first[rows:], "grp", 2, group)
+        near = [first, second, jnp.concatenate([upper, lower], axis=0)]
+    return jnp.stack([delayed(part, later), *near])
 
 
 def gather_direct(own, me_core, group, by_rows):
@@ -240,6 +251,29 @@
         compiler_params=compiler_params(),
         name="assemble",
     )(me_core, own, other)
+
+
+def update_kernel(rate, w_ref, m_ref, s_ref, grad_ref, mean_ref, square_ref, new_ref):
+    mean, square, new = adam_update(
+        w_ref[...], m_ref[...], s_ref[...], grad_ref[...].astype(jnp.float32), rate
+    )
+    mean_ref[...] = mean
+    square_ref[...] = square
+    new_ref[...] = new
+
+
+def update_after(weight, mean, square, grad, rate, after):
+    rows, columns = weight.shape
+    block = pl.BlockSpec((32, columns), lambda i: (i, 0))
+    return pl.pallas_call(
+        skipping(functools.partial(update_kernel, rate), 4, len(after)),
+        grid=(rows // 32,),
+        in_specs=[block] * 4 + untouched(after),
+        out_specs=[block] * 3,
+        out_shape=[jax.ShapeDtypeStruct(weight.shape, jnp.float32)] * 3,
+        compiler_params=compiler_params(),
+        name="update_inproj",
+    )(weight, mean, square, grad, *after)
 
 
 def attend_kernel(q_ref, k_ref, v_ref, qf_ref, kf_ref, own_v_ref, own_f_ref, out_ref, stat_ref, ke):
@@ -466,14 +500,14 @@
     return (contract(left, mine) + got.astype(jnp.float32)).astype(jnp.bfloat16)
 
 
-def group_first(share, group):
+def group_first(share, group, after=()):
     rows, columns = share.shape[0] // group, share.shape[1]
     if group != 4:
         return (lax.psum_scatter(share, "grp", scatter_dimension=0, tiled=True),)
     share = share.reshape(2, 2, rows, columns)
     return (
-        halved(share[:, :, : rows // 2], 2, group, 0),
-        halved(share[:, :, rows // 2 :], 1, group, 1),
+        halved(share[:, :, : rows // 2], 2, group, 0, after),
+        halved(share[:, :, rows // 2 :], 1, group, 1, after),
     )
 
 
@@ -491,16 +525,18 @@
 
 def far_scatter(share, far, waits=((), ())):
     if far > 4:
-        return lax.psum(share, "far")
+        return [lax.psum(share, "far")]
+    stages = [share]
     for mask, after in zip(far_masks(far), waits):
+        share = stages[-1]
         bit = (lax.axis_index("far") // mask) % 2
         rows = share.shape[0] // 2
         got = exchange(
             lax.dynamic_slice_in_dim(share, (1 - bit) * rows, rows, 0), "far", mask, far
         )
         kept = lax.dynamic_slice_in_dim(share, bit * rows, rows, 0)
-        share = added(delayed(kept, after), got)
-    return share
+        stages.append(added(delayed(kept, after), got))
+    return stages
 
 
 def doubled(array, axis, mask, size, dim, after):
@@ -580,9 +616,8 @@
     both = ("grp", "core")
     w_in = lax.all_gather(lower_half(core_list, inproj, group), both, axis=0, tiled=True)
     me_core = jnp.stack([me, core]).astype(jnp.int32)
-    near_out = near_parts(own_half(outproj, core).astype(jnp.bfloat16), group)
-    w_out = gather_direct(near_out, me_core, group, True)
-    w_up = gather_weight(spread_halves(upproj), core)
+    w_outup = gather_weight(jnp.concatenate([outproj, spread_halves(upproj)], axis=1), core)
+    w_out, w_up = w_outup[:, :D], w_outup[:, D:]
     packed = jnp.concatenate([norm_gains[:, 0], norm_gains[:, 1], slot_ids[0].astype(jnp.float32)])
     packed = lax.all_gather(packed.astype(jnp.bfloat16), "grp", axis=0, tiled=False)
     gain_one = packed[:, :own_gains].reshape(D).astype(jnp.float32)
@@ -601,18 +636,24 @@
     sin_near = sin.reshape(group, own_rows, PAIR)
     qkv, stats, attended_near, attended_here, first_sent = [], [], [], [], []
     for pair in range(pairs):
-        after = (near_out,) if pair == 0 else (first_sent[0],)
+        after = first_sent[:1]
         pieces = project(me_list, first_normed, w_in, cos_near, sin_near, pair, group, after)
         first_sent.append(pieces)
-        qkv.append(jnp.concatenate(swap_heads(pieces, group), axis=0))
+        qkv.append(swap_heads(pieces, group))
+    low_down = lax.dynamic_slice_in_dim(downproj, core * (D // 2), D // 2, 1).astype(jnp.bfloat16)
     for pair in range(pairs):
-        mixed, stat = attend(qkv[pair], query_side, key_side, [qkv[-1]] + stats[-1:])
+        qkv[pair] = jnp.concatenate([delayed(qkv[pair][0], stats[-1:]), *qkv[pair][1:]], axis=0)
+        if pair == pairs - 1:
+            low_down = delayed(low_down, qkv[pair])
+            near_down = near_first(low_down, group)
+        mixed, stat = attend(qkv[pair], query_side, key_side)
         stats.append(stat)
         attended_near.append(mixed)
+        mixed = delayed(mixed, attended_here[:1])
         attended_here.append(swap_heads(mixed.reshape(group, own_rows, PAIR), group))
-    low_down = lax.dynamic_slice_in_dim(downproj, core * (D // 2), D // 2, 1).astype(jnp.bfloat16)
-    w_down = gather_direct(near_parts(delayed(low_down, qkv[-1]), group), me_core, group, False)
     attended = place(me_list, attended_here, group)
+    near_down = near_second(low_down, near_down, group, stats[-1], attended)
+    w_down = gather_direct(near_down, me_core, group, False)
     middle = inputs + product(attended, w_out)
     second_normed = layer_norm(middle, gain_two).astype(jnp.bfloat16)
     gate_up = product(second_normed, w_up)
@@ -635,7 +676,7 @@
     (grad_from_norm,) = second_back(grad_second)
     grad_middle = grad_top.astype(jnp.float32) + grad_from_norm
     grad_branch = grad_middle.astype(jnp.bfloat16)
-    sent = row_product(me_list, grad_branch, w_out, group, (up_theirs,))
+    sent = row_product(me_list, grad_branch, w_outup, group, (up_theirs,))
     grad_near = jnp.concatenate(swap_heads(sent, group), axis=0)
     out_theirs = core_theirs(attended, delayed(grad_branch, sent), core)
     up_share = jnp.concatenate(
@@ -645,20 +686,24 @@
         ],
         axis=1,
     )
-    up_halves = group_first(delayed(up_share, grad_near), group)
-    up_half = group_second(up_halves, group)
-    grads_here, grads_near = [], [up_share, down_share]
+    grads_here, grads_near = [], [up_share]
     for pair in range(pairs):
         grads = attend_back(
             qkv[pair], query_side, key_side, stats[pair], attended_near[pair], grad_near,
             cos, sin, pair, grads_near,
         )
-        grads_near = [grads, *up_halves]
+        if pair == 0:
+            up_halves = group_first(delayed(up_share, grad_near), group, grads)
+            grads_near = [grads, down_share, *up_halves]
+        if pair == pairs - 1:
+            up_half = group_second(up_halves, group, grads)
+        if pair > 0:
+            grads = delayed(grads, grads_here[0])
         grads_here.append(swap_heads(grads.reshape(group, own_rows, 3 * PAIR), group))
     down_share = lax.psum(down_share, "far")
     grads_placed, in_theirs, grad_first = [], [], 0.0
     for pair in range(pairs):
-        after = (up_half,) if pair == 0 else (in_theirs[0], down_share)
+        after = (up_half,) if pair == 0 else (in_theirs[0],)
         placed = place(me_list, [grads_here[pair]], group, after)
         grads_placed.append(placed)
         in_theirs.append(core_theirs(first_normed, placed, core))
@@ -671,25 +716,35 @@
     )
     in_first = group_first(in_share, group)
     in_half = group_second(in_first, group)
-    in_chunk = far_scatter(in_half, far)
+    in_stages = far_scatter(in_half, far)
+    in_chunk, in_early = in_stages[-1], in_stages[min(1, len(in_stages) - 1)]
     for pair in range(pairs):
         width = 3 * PAIR * group
         part = w_in[:, pair * width : (pair + 1) * width]
         grad_first = grad_first + against(grads_placed[pair], part)
-    up_chunk = far_scatter(up_half, far, (in_theirs[-1], in_share))
+    up_chunk = far_scatter(up_half, far, (in_theirs[-1], in_share))[-1]
     up_chunk = spread(up_chunk, far, (in_first, in_half))
-    total_up = doubled(up_chunk, "core", 1, 2, 1, in_chunk).astype(jnp.float32)
+    up_final = doubled(up_chunk, "core", 1, 2, 1, in_early)
+    total_up = up_final.astype(jnp.float32)
     wide = up_chunk.shape[1]
     total_out = jnp.concatenate([total_up[:, FF_WIDE:wide], total_up[:, wide + FF_WIDE :]], axis=1)
     total_up = jnp.concatenate([total_up[:, :FF], total_up[:, wide : wide + FF]], axis=1)
     total_down = doubled(
-        delayed(down_share, in_share), "core", 1, 2, 0, in_half
+        delayed(down_share, in_first), "core", 1, 2, 0, in_early
     ).astype(jnp.float32)
-    total_in = merged_columns(doubled(spread(in_chunk, far), "core", 1, 2, 1, ()), pairs, group)
-    total_in = total_in.astype(jnp.float32)
     _, first_back = jax.vjp(lambda v: layer_norm(v, gain_one), inputs)
     (grad_inputs,) = first_back(grad_first)
     input_grad = (grad_middle + grad_inputs).astype(jnp.bfloat16)
+    means = (inproj_mean, outproj_mean, upproj_mean, downproj_mean, gains_mean)
+    squares = (inproj_square, outproj_square, upproj_square, downproj_square, gains_square)
+
+    def update(index, total):
+        return adam_update(masters[index], means[index], squares[index], total, rate_list[index])
+
+    updates = [None, update(1, total_out), update(2, total_up), update(3, total_down), None]
+    in_share = doubled(spread(in_chunk, far, ((), ())), "core", 1, 2, 1, ())
+    low_total = merged_columns(in_share, pairs, group)
+    total_in = low_total.astype(jnp.float32)
     low_in = inproj.astype(jnp.bfloat16).astype(jnp.float32)
     low_up = upproj.astype(jnp.bfloat16).astype(jnp.float32)
     low_gains = norm_gains.astype(jnp.bfloat16).astype(jnp.float32)
@@ -697,13 +752,11 @@
         jnp.stack([jnp.sum(low_in * total_in, axis=1), jnp.sum(low_up * total_up, axis=1)], axis=1)
         / low_gains
     )
-    totals = (total_in, total_out, total_up, total_down, total_gains)
-    means = (inproj_mean, outproj_mean, upproj_mean, downproj_mean, gains_mean)
-    squares = (inproj_square, outproj_square, upproj_square, downproj_square, gains_square)
-    updates = [
-        adam_update(masters[index], means[index], squares[index], totals[index], rate_list[index])
-        for index in range(5)
-    ]
+    updates[0] = update_after(
+        inproj, inproj_mean, inproj_square, low_total, rate_list[0],
+        [updates[index][2] for index in (1, 2, 3)],
+    )
+    updates[4] = update(4, total_gains)
     return (
         result.astype(jnp.bfloat16)[None],
         input_grad[None],

time: 655 us -> 568 us (0.87)
  waiting for transfers between devices: 280 us -> 202 us
  blocking collectives: 23.2 us -> 9.73 us
    ppermute x52 -> x49, waiting for transfers between devices: 249 us -> 179 us  [exchange(): return lax.ppermute(array, axis, [(i, i ^ mask) for i in range(size)])]
    psum x1, waiting for transfers between devices: 17.1 us -> 0.01 us  [local(): down_share = lax.psum(down_share, 'far')]
    all_gather x1, blocking collectives: 23.2 us -> 9.73 us  [local(): lax.all_gather(packed.astype(jnp.bfloat16), 'grp', axis=0, tiled=False)]
    pallas_call x0 -> x1, Pallas kernels: none -> 10 us  [update_after(): pl.pallas_call(skipping(functools.partial(update_kernel, rate), 4, len(af...]
    all_gather x1, waiting for transfers between devices: 13.6 us -> 22.3 us  [local(): lax.all_gather(lower_half(core_list, inproj, group), both, axis=0, tiled=...]
    pallas_call x2 -> x1, Pallas kernels: 15.1 us -> 8.87 us  [gather_direct(): pl.pallas_call(assemble_kernel, grid_spec=pltpu.PrefetchScalarGridSpec(nu...]
    sub x5 -> x4, other arithmetic: 23.2 us -> 18.3 us  [adam_update(): return (mean_new, square_new, weight - rate * (step_size + 0.01 * weight))]
    unnamed x178 -> x173, local copies, waits for them, and re-layouts: 15.3 us -> 10.8 us
  transfers between devices with their start and end apart: 56 -> 53, of which waited for: 25 -> 28; matrix products, arithmetic and copies ran while one was open for 17% -> 20% of each run, Pallas kernels for 12% -> 16%
where the time goes in v6:
time: 568 us; the launch traced here: 564 us
  waiting for transfers between devices  202 us (36%)
  Pallas kernels  102 us (18%)
  other arithmetic  75 us (13%)
  matrix products  71.5 us (13%)
  starting transfers between devices  54.2 us (10%)
  local copies, waits for them, and re-layouts  34.5 us (6%)
  between operations  15.6 us (3%)
  blocking collectives  9.73 us (2%)
    ppermute x49, waiting for transfers between devices, exchange(): return lax.ppermute(array, axis, [(i, i ^ mask) for i in range(size)])  179 us
    ppermute x49, starting transfers between devices, exchange(): return lax.ppermute(array, axis, [(i, i ^ mask) for i in range(size)])  53.9 us
    pallas_call x2, Pallas kernels, attend_back(): pl.pallas_call(skipping(attend_back_kernel, 12, len(after)), grid=(rows /...  34.3 us
    dot_general x9, matrix products, contract(): lax.dot_general(left, right, (((0,), (0,)), ((), ())), preferred_element_...  29.8 us
    dot_general x4, matrix products, against(): lax.dot_general(left, right, (((1,), (1,)), ((), ())), preferred_element_...  24.4 us
    all_gather x1, waiting for transfers between devices, local(): lax.all_gather(lower_half(core_list, inproj, group), both, axis=0, tiled=...  22.3 us
    pallas_call x2, Pallas kernels, attend(): pl.pallas_call(skipping(attend_kernel, 7, len(after)), grid=(rows // bloc...  20.5 us
    sub x4, other arithmetic, adam_update(): return (mean_new, square_new, weight - rate * (step_size + 0.01 * weight))  18.3 us
  transfers between devices with their start and end apart: 53, of which 28 were waited for; matrix products, arithmetic and copies ran while one was open for 20% of the time, Pallas kernels for 16%

profile of v6, /device:TPU:0, one launch (start us, length us, event | category | flops | bytes accessed | tf_op | source)
XLA Modules:
  0.0 563.8 jit_solution(16170793131228115987)
XLA Ops:
  15.5 9.7 %all-gather = bf16[4,1,896]{2,1,0:T(2,128)(2,1)S(1)} all-gather(bf16[1,1,896]{2,1,0:T(2,128)(2,1)S(1)} %maximum_bitcast_fusion.1), channel_id=1, replica_groups=mesh['grp'=4,'far'=4,'core'=2] {'grp'}, dimensions={0}, use_global_device_ids=true | all-gather | bytes 8960 | tf_op jit(solution)/shard_map/all_gather | solution.py:622
  28.9 4.5 fusion.55
  36.4 22.3 %all-gather.4.cloned.1.call-done.refs_2_ = bf16[1024,3072]{1,0:T(8,128)(2,1)} async-done(((bf16[128,3072]{1,0:T(8,128)(2,1)}), bf16[1024,3072]{1,0:T(8,128)(2,1)}) %all-gather.4.cloned.1.call-update) | async-done | bytes 6291472 | tf_op jit(solution)/shard_map/all_gather | solution.py:617
  58.7 5.8 %project.2.refs_5_ = bf16[4,384,384]{2,1,0:T(8,128)(2,1)} custom-call(s32[1]{0:T(128)} %bitcast.1.refs_0_.me_ref, bf16[384,1024]{1,0:T(8,128)(2,1)} %fusion.40.refs_1_, bf16[1024,3072]{1,0:T(8,128)(2,1)} %all-gather.4.cloned.1.call-done.refs_2_, f32[4,384,128]{2,1,0:T(8,128)} %get-tuple-element.177.refs_3_, f32[4,384,128]{2,1,0:T(8,128)} %get-tuple-element.176.refs_4_), custom_call_target="tpu_custom_call" | custom-call | tf_op jit(solution)/shard_map/project/pallas_call | solution.py:126
  71.0 6.1 %project.3 = bf16[4,384,384]{2,1,0:T(8,128)(2,1)} custom-call(s32[1]{0:T(128)} %bitcast.1.refs_0_.me_ref, bf16[384,1024]{1,0:T(8,128)(2,1)} %fusion.40.refs_1_, bf16[1024,3072]{1,0:T(8,128)(2,1)} %all-gather.4.cloned.1.call-done.refs_2_, f32[4,384,128]{2,1,0:T(8,128)} %get-tuple-element.177.refs_3_, f32[4,384,128]{2,1,0:T(8,128)} %get-tuple-element.176.refs_4_, ...), custom_call_target="tpu_custom_call" | custom-call | tf_op jit(solution)/shard_map/project/pallas_call | solution.py:126
  82.6 6.1 %collective-permute-done.1 = bf16[384,384]{1,0:T(8,128)(2,1)S(1)} collective-permute-done((bf16[384,384]{1,0:T(8,128)(2,1)S(1)}, bf16[384,384]{1,0:T(8,128)(2,1)S(1)}, u32[]{:S(2)}, u32[]{:S(2)}) %collective-permute-start.1) | collective-permute-done | bytes 294944 | tf_op jit(solution)/shard_map/ppermute | solution.py:201
  88.7 4.3 collective-permute-done
  94.2 10.2 %attend.2 = (bf16[1536,128]{1,0:T(8,128)(2,1)}, f32[1536,128]{1,0:T(8,128)}) custom-call(bf16[1536,384]{1,0:T(8,128)(2,1)} %pad_maximum_fusion.8.refs_0_.refs_1_.refs_2_.refs_5_, bf16[1536,384]{1,0:T(8,128)(2,1)} %pad_maximum_fusion.8.refs_0_.refs_1_.refs_2_.refs_5_, bf16[1536,384]{1,0:T(8,128)(2,1)} %pad_maximum_fusion.8.refs_0_.refs_1_.refs_2_.refs_5_, ...), custom_call_target="tpu_custom_call" | custom-call | tf_op jit(solution)/shard_map/attend/pallas_call | solution.py:323
  105.8 6.8 %collective-permute-done.8 = bf16[384,384]{1,0:T(8,128)(2,1)S(1)} collective-permute-done((bf16[384,384]{1,0:T(8,128)(2,1)S(1)}, bf16[384,384]{1,0:T(8,128)(2,1)S(1)}, u32[]{:S(2)}, u32[]{:S(2)}) %collective-permute-start.8) | collective-permute-done | bytes 294944 | tf_op jit(solution)/shard_map/ppermute | solution.py:201
  118.9 10.3 %attend.3 = (bf16[1536,128]{1,0:T(8,128)(2,1)}, f32[1536,128]{1,0:T(8,128)}) custom-call(bf16[1536,384]{1,0:T(8,128)(2,1)} %copy-done, bf16[1536,384]{1,0:T(8,128)(2,1)} %copy-done, bf16[1536,384]{1,0:T(8,128)(2,1)} %copy-done, bf16[1536,128]{1,0:T(8,128)(2,1)} %get-tuple-element.173.refs_3_, bf16[1536,128]{1,0:T(8,128)(2,1)} %get-tuple-element.172.refs_4_.refs_6_, ...), custom_call_target="tpu_custom_call" | custom-call | tf_op jit(solution)/shard_map/attend/pallas_call | solution.py:323
  129.2 15.4 %collective-permute-done.12 = bf16[656,512]{1,0:T(8,128)(2,1)S(1)} collective-permute-done((bf16[656,512]{1,0:T(8,128)(2,1)S(1)}, bf16[656,512]{1,0:T(8,128)(2,1)S(1)}, u32[]{:S(2)}, u32[]{:S(2)}) %collective-permute-start.12) | collective-permute-done | bytes 671776 | tf_op jit(solution)/shard_map/ppermute | solution.py:201
  148.7 3.8 collective-permute-done.4.refs_2_
  158.7 12.8 %collective-permute-done.9.refs_5_ = bf16[384,128]{1,0:T(8,128)(2,1)S(1)} collective-permute-done((bf16[384,128]{1,0:T(8,128)(2,1)S(1)}, bf16[384,128]{1,0:T(8,128)(2,1)S(1)}, u32[]{:S(2)}, u32[]{:S(2)}) %collective-permute-start.9) | collective-permute-done | bytes 98336 | tf_op jit(solution)/shard_map/ppermute | solution.py:201
  171.6 3.9 collective-permute-done.11.refs_7_
  184.5 8.9 %assemble.1 = bf16[2624,1024]{1,0:T(8,128)(2,1)} custom-call(s32[2]{0:T(128)} %pad_add_fusion.me_ref, bf16[4,656,512]{2,1,0:T(8,128)(2,1)} %copy-done.10, bf16[4,656,512]{2,1,0:T(8,128)(2,1)} %collective-permute-done.16.other_ref), custom_call_target="tpu_custom_call" | custom-call | tf_op jit(solution)/shard_map/assemble/pallas_call | solution.py:242
  196.6 7.8 %fusion.2 = f32[384,5376]{1,0:T(8,128)S(1)} fusion(bf16[1024,6400]{1,0:T(8,128)(2,1)} %all-gather.6.cloned.1.call-done.refs_2_, f32[384,1024]{1,0:T(8,128)S(1)} %get-tuple-element.181, f32[1024]{0:T(1024)S(1)} %bitcast.170, f32[384]{0:T(512)S(1)} %fusion.84, f32[384]{0:T(512)S(1)} %broadcast_multiply_fusion), kind=kOutput, calls=%fused_computation.5 | convolution fusion | flops 4229431296 | bytes 20847616 | tf_op jit(solution)/shard_map/dot_general | solution.py:446
  204.4 10.3 %multiply_convert_fusion.1 = (bf16[384,2624]{1,0:T(8,128)(2,1)S(1)}, f32[384,2624]{1,0:T(8,128)}) fusion(f32[384,5376]{1,0:T(8,128)S(1)} %fusion.2), kind=kLoop, calls=%fused_computation.28 | loop fusion | flops 66502656 | bytes 14106624 | tf_op jit(solution)/shard_map/convert_element_type | solution.py:662
  216.0 4.7 convolution_convert_fusion.1
  220.8 10.2 %add_convert_fusion.1 = (bf16[384,2624]{1,0:T(8,128)(2,1)S(1)}, bf16[384,2624]{1,0:T(8,128)(2,1)S(1)}) fusion(f32[384,2624]{1,0:T(8,128)} %get-tuple-element.92, f32[384,5376]{1,0:T(8,128)} %copy-done.11, bf16[384,1024]{1,0:T(8,128)(2,1)S(1)} %copy-done.35, bf16[2624,1024]{1,0:T(8,128)(2,1)} %assemble.1), kind=kOutput, calls=%fused_computation.27 | convolution fusion | flops 2081734656 | bytes 22282240 | tf_op jit(solution)/shard_map/dot_general | solution.py:456
  231.4 5.2 convolution_convert_fusion.refs_3_
  236.7 8.6 %multiply_reduce_fusion.2 = (f32[384]{0:T(512)S(1)}, f32[384,1024]{1,0:T(8,128)S(1)}) fusion(f32[384,1024]{1,0:T(8,128)S(1)} %get-tuple-element.181, f32[384]{0:T(512)S(1)} %broadcast_multiply_fusion, f32[1024]{0:T(1024)S(1)} %bitcast.172, bf16[384,5376]{1,0:T(8,128)(2,1)} %copy-done.21, bf16[1024,6400]{1,0:T(8,128)(2,1)} %all-gather.6.cloned.1.call-done.refs_2_), kind=kOutput, calls=%fused_computation.109 | convolution fusion | flops 4229430784 | bytes 18291712 | tf_op jit(solution)/shard_map/dot_general | solution.py:456
  248.2 5.0 row_product.1
  256.1 3.3 collective-permute-start.19
  260.6 4.9 collective-permute-done.19
  265.5 3.7 collective-permute-done.18
  271.6 3.3 add_convert_fusion.6
  274.9 7.1 %add_convert_fusion = bf16[1024,2688]{1,0:T(8,128)(2,1)} fusion(bf16[1024,2688]{1,0:T(8,128)(2,1)} %collective-permute-done.20, bf16[384,5376]{1,0:T(8,128)(2,1)S(1)} %copy-done.22, s32[]{:T(128)S(6)} %select_n.303, f32[384,1024]{1,0:T(8,128)S(1)} %get-tuple-element.181, f32[1024]{0:T(1024)S(1)} %bitcast.173, f32[384]{0:T(512)S(1)} %copy-done.55, ...), kind=kOutput, calls=%fused_computation.2 | convolution fusion | flops 2123759616 | bytes 14655492 | tf_op jit(solution)/shard_map/dot_general | solution.py:450
  282.0 3.4 pad_maximum_fusion.refs_12_
  292.4 4.4 fusion.56
  296.8 6.6 %fusion.50 = bf16[1,384,1024]{2,1,0:T(8,128)(2,1)} fusion(f32[384,1024]{1,0:T(8,128)S(1)} %copy-done.17, bf16[384,2624]{1,0:T(8,128)(2,1)} %copy-done.28, bf16[2624,1024]{1,0:T(8,128)(2,1)} %assemble.1), kind=kOutput, calls=%fused_computation.120 | convolution fusion | flops 2064384000 | bytes 9748480 | tf_op jit(solution)/shard_map/dot_general | solution.py:446
  304.5 17.2 %attend_back.2.refs_12_ = bf16[1536,384]{1,0:T(8,128)(2,1)} custom-call(bf16[1536,384]{1,0:T(8,128)(2,1)} %pad_maximum_fusion.8.refs_0_.refs_1_.refs_2_.refs_5_, bf16[1536,384]{1,0:T(8,128)(2,1)} %pad_maximum_fusion.8.refs_0_.refs_1_.refs_2_.refs_5_, bf16[1536,384]{1,0:T(8,128)(2,1)} %pad_maximum_fusion.8.refs_0_.refs_1_.refs_2_.refs_5_, ...), custom_call_target="tpu_custom_call" | custom-call | tf_op jit(solution)/shard_map/attend_back/pallas_call | solution.py:424
  327.4 17.1 %collective-permute-done.26 = bf16[2,128,3200]{2,1,0:T(8,128)(2,1)} collective-permute-done((bf16[2,128,3200]{2,1,0:T(8,128)(2,1)}, bf16[2,128,3200]{2,1,0:T(8,128)(2,1)}, u32[]{:S(2)}, u32[]{:S(2)}) %collective-permute-start.26) | collective-permute-done | bytes 1638432 | tf_op jit(solution)/shard_map/ppermute | solution.py:201
  353.0 17.1 %attend_back.3 = bf16[1536,384]{1,0:T(8,128)(2,1)} custom-call(bf16[1536,384]{1,0:T(8,128)(2,1)} %copy-done, bf16[1536,384]{1,0:T(8,128)(2,1)} %copy-done, bf16[1536,384]{1,0:T(8,128)(2,1)} %copy-done, bf16[1536,128]{1,0:T(8,128)(2,1)} %get-tuple-element.173.refs_3_, bf16[1536,128]{1,0:T(8,128)(2,1)} %get-tuple-element.172.refs_4_.refs_6_, ...), custom_call_target="tpu_custom_call" | custom-call | tf_op jit(solution)/shard_map/attend_back/pallas_call | solution.py:424
  376.1 4.0 collective-permute-done.28
  386.9 3.2 convolution_convert_fusion.3.refs_4_
  397.3 3.8 fusion.19
  407.7 17.0 %collective-permute-done.43 = bf16[128,3200]{1,0:T(8,128)(2,1)} collective-permute-done((bf16[128,3200]{1,0:T(8,128)(2,1)}, bf16[128,3200]{1,0:T(8,128)(2,1)}, u32[]{:S(2)}, u32[]{:S(2)}) %collective-permute-start.43) | collective-permute-done | bytes 819232 | tf_op jit(solution)/shard_map/ppermute | solution.py:201
  435.7 22.2 %collective-permute-done.44 = bf16[64,3200]{1,0:T(8,128)(2,1)S(1)} collective-permute-done((bf16[64,3200]{1,0:T(8,128)(2,1)S(1)}, bf16[64,3200]{1,0:T(8,128)(2,1)S(1)}, u32[]{:S(2)}, u32[]{:S(2)}) %collective-permute-start.44) | collective-permute-done | bytes 409632 | tf_op jit(solution)/shard_map/ppermute | solution.py:201
  461.4 7.2 %collective-permute-done.35 = bf16[128,1536]{1,0:T(8,128)(2,1)S(1)} collective-permute-done((bf16[128,1536]{1,0:T(8,128)(2,1)S(1)}, bf16[128,1536]{1,0:T(8,128)(2,1)S(1)}, u32[]{:S(2)}, u32[]{:S(2)}) %collective-permute-start.35) | collective-permute-done | bytes 393248 | tf_op jit(solution)/shard_map/ppermute | solution.py:201
  470.2 4.5 collective-permute-start.38
  474.7 3.6 collective-permute-done.45
  478.4 8.2 %collective-permute-done.38 = bf16[128,1536]{1,0:T(8,128)(2,1)S(1)} collective-permute-done((bf16[128,1536]{1,0:T(8,128)(2,1)S(1)}, bf16[128,1536]{1,0:T(8,128)(2,1)S(1)}, u32[]{:S(2)}, u32[]{:S(2)}) %collective-permute-start.38) | collective-permute-done | bytes 393248 | tf_op jit(solution)/shard_map/ppermute | solution.py:201
  488.7 9.1 %collective-permute-done.39 = bf16[64,1536]{1,0:T(8,128)(2,1)S(1)} collective-permute-done((bf16[64,1536]{1,0:T(8,128)(2,1)S(1)}, bf16[64,1536]{1,0:T(8,128)(2,1)S(1)}, u32[]{:S(2)}, u32[]{:S(2)}) %collective-permute-start.39) | collective-permute-done | bytes 196640 | tf_op jit(solution)/shard_map/ppermute | solution.py:201
  498.2 15.2 %collective-permute-done.40 = bf16[64,1536]{1,0:T(8,128)(2,1)S(1)} collective-permute-done((bf16[64,1536]{1,0:T(8,128)(2,1)S(1)}, bf16[64,1536]{1,0:T(8,128)(2,1)S(1)}, u32[]{:S(2)}, u32[]{:S(2)}) %collective-permute-start.40) | collective-permute-done | bytes 196640 | tf_op jit(solution)/shard_map/ppermute | solution.py:201
  516.1 4.2 multiply_subtract_fusion.1
  520.3 4.2 collective-permute-done.41
  534.9 11.2 %multiply_subtract_fusion = (f32[256,5248]{1,0:T(8,128)}, f32[256,5248]{1,0:T(8,128)}, f32[256,5248]{1,0:T(8,128)}, f32[256]{0:T(256)S(1)}) fusion(f32[256,5248]{1,0:T(8,128)S(1)} %bitcast.158, f32[256,2624]{1,0:T(8,128)S(1)} %get-tuple-element.99, f32[256,2624]{1,0:T(8,128)S(1)} %get-tuple-element.98, f32[256,5248]{1,0:T(8,128)} %param.28, ...), kind=kLoop, calls=%fused_computation.22 | loop fusion | flops 26869504 | bytes 37618688 | tf_op jit(solution)/shard_map/sub | solution.py:583
  546.8 10.0 %update_inproj.1 = (f32[256,3072]{1,0:T(8,128)}, f32[256,3072]{1,0:T(8,128)}, f32[256,3072]{1,0:T(8,128)}) custom-call(f32[256,3072]{1,0:T(8,128)} %refs_0_.1, f32[256,3072]{1,0:T(8,128)} %refs_1_.1, f32[256,3072]{1,0:T(8,128)} %refs_2_.1, bf16[256,3072]{1,0:T(8,128)(2,1)} %copy-done.15, f32[256,1024]{1,0:T(8,128)} %get-tuple-element.86.refs_4_, ...), custom_call_target="tpu_custom_call" | custom-call | tf_op jit(solution)/shard_map/update_inproj/pallas_call | solution.py:268
  (390 shorter events, 149.8 us)
Async XLA Ops:
  7.2 51.6 %all-gather.4.cloned.1.call-start = ((), (), s32[]{:S(2)}) async-start(), calls=%async_computation.1 | async-start | bytes 7077888 | tf_op jit(solution)/shard_map/all_gather | solution.py:617
  9.7 183.7 %all-gather.6.cloned.1.call-start = ((), (), s32[]{:S(2)}) async-start(), calls=%async_computation.2 | async-start | bytes 14745600 | tf_op jit(solution)/shard_map/all_gather | solution.py:467
  15.4 337.6 %reduce-scatter.2.cloned.1.call-start = ((), (), s32[]{:S(2)}) async-start(), calls=%async_computation.3 | async-start | bytes 6045696 | tf_op jit(solution)/shard_map/reduce_scatter | solution.py:671
  65.9 14.6 %collective-permute-start.2 = (bf16[384,384]{1,0:T(8,128)(2,1)S(1)}, bf16[384,384]{1,0:T(8,128)(2,1)S(1)}, u32[]{:S(2)}, u32[]{:S(2)}) collective-permute-start(bf16[384,384]{1,0:T(8,128)(2,1)S(1)} %get-tuple-element.139), channel_id=1, source_target_pairs={{0,24},{8,16},{16,8},{24,0},{1,25},{9,17},{17,9},{25,1},{2,26},{10... | collective-permute-start | bytes 884744 | tf_op jit(solution)/shard_map/ppermute | solution.py:201
  67.4 21.3 %collective-permute-start.1 = (bf16[384,384]{1,0:T(8,128)(2,1)S(1)}, bf16[384,384]{1,0:T(8,128)(2,1)S(1)}, u32[]{:S(2)}, u32[]{:S(2)}) collective-permute-start(bf16[384,384]{1,0:T(8,128)(2,1)S(1)} %get-tuple-element.140), channel_id=1, source_target_pairs={{0,16},{8,24},{16,0},{24,8},{1,17},{9,25},{17,1},{25,9},{2,18},{10... | collective-permute-start | bytes 884744 | tf_op jit(solution)/shard_map/ppermute | solution.py:201
  68.9 24.2 %collective-permute-start = (bf16[384,384]{1,0:T(8,128)(2,1)S(1)}, bf16[384,384]{1,0:T(8,128)(2,1)S(1)}, u32[]{:S(2)}, u32[]{:S(2)}) collective-permute-start(bf16[384,384]{1,0:T(8,128)(2,1)S(1)} %get-tuple-element.141), channel_id=1, source_target_pairs={{0,8},{8,0},{16,24},{24,16},{1,9},{9,1},{17,25},{25,17},{2,10},{10... | collective-permute-start | bytes 884744 | tf_op jit(solution)/shard_map/ppermute | solution.py:201
  78.4 27.2 %collective-permute-start.6 = (bf16[384,384]{1,0:T(8,128)(2,1)S(1)}, bf16[384,384]{1,0:T(8,128)(2,1)S(1)}, u32[]{:S(2)}, u32[]{:S(2)}) collective-permute-start(bf16[384,384]{1,0:T(8,128)(2,1)S(1)} %get-tuple-element.136), channel_id=1, source_target_pairs={{0,8},{8,0},{16,24},{24,16},{1,9},{9,1},{17,25},{25,17},{2,10},{10... | collective-permute-start | bytes 884744 | tf_op jit(solution)/shard_map/ppermute | solution.py:201
  80.1 25.6 %collective-permute-start.7 = (bf16[384,384]{1,0:T(8,128)(2,1)S(1)}, bf16[384,384]{1,0:T(8,128)(2,1)S(1)}, u32[]{:S(2)}, u32[]{:S(2)}) collective-permute-start(bf16[384,384]{1,0:T(8,128)(2,1)S(1)} %get-tuple-element.135), channel_id=1, source_target_pairs={{0,16},{8,24},{16,0},{24,8},{1,17},{9,25},{17,1},{25,9},{2,18},{10... | collective-permute-start | bytes 884744 | tf_op jit(solution)/shard_map/ppermute | solution.py:201
  80.5 32.1 %collective-permute-start.8 = (bf16[384,384]{1,0:T(8,128)(2,1)S(1)}, bf16[384,384]{1,0:T(8,128)(2,1)S(1)}, u32[]{:S(2)}, u32[]{:S(2)}) collective-permute-start(bf16[384,384]{1,0:T(8,128)(2,1)S(1)} %get-tuple-element.134), channel_id=1, source_target_pairs={{0,24},{8,16},{16,8},{24,0},{1,25},{9,17},{17,9},{25,1},{2,26},{10... | collective-permute-start | bytes 884744 | tf_op jit(solution)/shard_map/ppermute | solution.py:201
  112.6 31.9 %collective-permute-start.12 = (bf16[656,512]{1,0:T(8,128)(2,1)S(1)}, bf16[656,512]{1,0:T(8,128)(2,1)S(1)}, u32[]{:S(2)}, u32[]{:S(2)}) collective-permute-start(bf16[656,512]{1,0:T(8,128)(2,1)S(1)} %dynamic-slice_convert_fusion), channel_id=1, source_target_pairs={{0,8},{8,0},{16,24},{24,16},{1,9},{9,1},{17,25},{25,17},{2,10},{10... | collective-permute-start | bytes 2015240 | tf_op jit(solution)/shard_map/ppermute | solution.py:201
  114.2 32.6 %collective-permute-start.13 = (bf16[656,512]{1,0:T(8,128)(2,1)S(1)}, bf16[656,512]{1,0:T(8,128)(2,1)S(1)}, u32[]{:S(2)}, u32[]{:S(2)}) collective-permute-start(bf16[656,512]{1,0:T(8,128)(2,1)S(1)} %dynamic-slice_convert_fusion), channel_id=1, source_target_pairs={{0,16},{8,24},{16,0},{24,8},{1,17},{9,25},{17,1},{25,9},{2,18},{10... | collective-permute-start | bytes 2015240 | tf_op jit(solution)/shard_map/ppermute | solution.py:201
  115.4 33.4 %collective-permute-start.3 = (bf16[384,128]{1,0:T(8,128)(2,1)S(1)}, bf16[384,128]{1,0:T(8,128)(2,1)S(1)}, u32[]{:S(2)}, u32[]{:S(2)}) collective-permute-start(bf16[384,128]{1,0:T(8,128)(2,1)S(1)} %get-tuple-element.168), channel_id=1, source_target_pairs={{0,8},{8,0},{16,24},{24,16},{1,9},{9,1},{17,25},{25,17},{2,10},{10... | collective-permute-start | bytes 294920 | tf_op jit(solution)/shard_map/ppermute | solution.py:201
  116.6 36.0 %collective-permute-start.4 = (bf16[384,128]{1,0:T(8,128)(2,1)S(1)}, bf16[384,128]{1,0:T(8,128)(2,1)S(1)}, u32[]{:S(2)}, u32[]{:S(2)}) collective-permute-start(bf16[384,128]{1,0:T(8,128)(2,1)S(1)} %get-tuple-element.167), channel_id=1, source_target_pairs={{0,16},{8,24},{16,0},{24,8},{1,17},{9,25},{17,1},{25,9},{2,18},{10... | collective-permute-start | bytes 294920 | tf_op jit(solution)/shard_map/ppermute | solution.py:201
  117.4 36.1 %collective-permute-start.5 = (bf16[384,128]{1,0:T(8,128)(2,1)S(1)}, bf16[384,128]{1,0:T(8,128)(2,1)S(1)}, u32[]{:S(2)}, u32[]{:S(2)}) collective-permute-start(bf16[384,128]{1,0:T(8,128)(2,1)S(1)} %get-tuple-element.166), channel_id=1, source_target_pairs={{0,24},{8,16},{16,8},{24,0},{1,25},{9,17},{17,9},{25,1},{2,26},{10... | collective-permute-start | bytes 294920 | tf_op jit(solution)/shard_map/ppermute | solution.py:201
  146.8 32.0 %collective-permute-start.15 = (bf16[328,512]{1,0:T(8,128)(2,1)S(1)}, bf16[328,512]{1,0:T(8,128)(2,1)S(1)}, u32[]{:S(2)}, u32[]{:S(2)}) collective-permute-start(bf16[328,512]{1,0:T(8,128)(2,1)S(1)} %slice.281), channel_id=1, source_target_pairs={{0,16},{8,24},{16,0},{24,8},{1,17},{9,25},{17,1},{25,9},{2,18},{10... | collective-permute-start | bytes 1007624 | tf_op jit(solution)/shard_map/ppermute | solution.py:201
  147.1 31.7 %collective-permute-start.14 = (bf16[328,512]{1,0:T(8,128)(2,1)S(1)}, bf16[328,512]{1,0:T(8,128)(2,1)S(1)}, u32[]{:S(2)}, u32[]{:S(2)}) collective-permute-start(bf16[328,512]{1,0:T(8,128)(2,1)S(1)} %slice.280), channel_id=1, source_target_pairs={{0,8},{8,0},{16,24},{24,16},{1,9},{9,1},{17,25},{25,17},{2,10},{10... | collective-permute-start | bytes 1007624 | tf_op jit(solution)/shard_map/ppermute | solution.py:201
  155.2 16.3 %collective-permute-start.9 = (bf16[384,128]{1,0:T(8,128)(2,1)S(1)}, bf16[384,128]{1,0:T(8,128)(2,1)S(1)}, u32[]{:S(2)}, u32[]{:S(2)}) collective-permute-start(bf16[384,128]{1,0:T(8,128)(2,1)S(1)} %get-tuple-element.164), channel_id=1, source_target_pairs={{0,8},{8,0},{16,24},{24,16},{1,9},{9,1},{17,25},{25,17},{2,10},{10... | collective-permute-start | bytes 294920 | tf_op jit(solution)/shard_map/ppermute | solution.py:201
  156.1 15.4 %collective-permute-start.10 = (bf16[384,128]{1,0:T(8,128)(2,1)S(1)}, bf16[384,128]{1,0:T(8,128)(2,1)S(1)}, u32[]{:S(2)}, u32[]{:S(2)}) collective-permute-start(bf16[384,128]{1,0:T(8,128)(2,1)S(1)} %get-tuple-element.163), channel_id=1, source_target_pairs={{0,16},{8,24},{16,0},{24,8},{1,17},{9,25},{17,1},{25,9},{2,18},{10... | collective-permute-start | bytes 294920 | tf_op jit(solution)/shard_map/ppermute | solution.py:201
  158.1 17.3 %collective-permute-start.11 = (bf16[384,128]{1,0:T(8,128)(2,1)S(1)}, bf16[384,128]{1,0:T(8,128)(2,1)S(1)}, u32[]{:S(2)}, u32[]{:S(2)}) collective-permute-start(bf16[384,128]{1,0:T(8,128)(2,1)S(1)} %get-tuple-element.162), channel_id=1, source_target_pairs={{0,24},{8,16},{16,8},{24,0},{1,25},{9,17},{17,9},{25,1},{2,26},{10... | collective-permute-start | bytes 294920 | tf_op jit(solution)/shard_map/ppermute | solution.py:201
  236.5 38.3 %collective-permute-start.20 = (bf16[1024,2688]{1,0:T(8,128)(2,1)}, bf16[1024,2688]{1,0:T(8,128)(2,1)}, u32[]{:S(2)}, u32[]{:S(2)}) collective-permute-start(bf16[1024,2688]{1,0:T(8,128)(2,1)} %convolution_convert_fusion.refs_3_), channel_id=1, source_target_pairs={{0,1},{1,0},{2,3},{3,2},{4,5},{5,4},{6,7},{7,6},{8,9},{9,8},{10,11... | collective-permute-start | bytes 16515080 | tf_op jit(solution)/shard_map/ppermute | solution.py:201
  255.0 16.6 %collective-permute-start.21 = (bf16[1024,512]{1,0:T(8,128)(2,1)}, bf16[1024,512]{1,0:T(8,128)(2,1)}, u32[]{:S(2)}, u32[]{:S(2)}) collective-permute-start(bf16[1024,512]{1,0:T(8,128)(2,1)} %convolution_convert_fusion.4), channel_id=1, source_target_pairs={{0,1},{1,0},{2,3},{3,2},{4,5},{5,4},{6,7},{7,6},{8,9},{9,8},{10,11... | collective-permute-start | bytes 3145736 | tf_op jit(solution)/shard_map/ppermute | solution.py:201
  259.4 9.7 %collective-permute-start.18 = (bf16[384,256]{1,0:T(8,128)(2,1)}, bf16[384,256]{1,0:T(8,128)(2,1)}, u32[]{:S(2)}, u32[]{:S(2)}) collective-permute-start(bf16[384,256]{1,0:T(8,128)(2,1)} %get-tuple-element.156), channel_id=1, source_target_pairs={{0,16},{8,24},{16,0},{24,8},{1,17},{9,25},{17,1},{25,9},{2,18},{10... | collective-permute-start | bytes 589832 | tf_op jit(solution)/shard_map/ppermute | solution.py:201
  290.6 53.9 %collective-permute-start.26 = (bf16[2,128,3200]{2,1,0:T(8,128)(2,1)}, bf16[2,128,3200]{2,1,0:T(8,128)(2,1)}, u32[]{:S(2)}, u32[]{:S(2)}) collective-permute-start(bf16[2,128,3200]{2,1,0:T(8,128)(2,1)} %get-tuple-element.105), channel_id=1, source_target_pairs={{0,8},{8,0},{16,24},{24,16},{1,9},{9,1},{17,25},{25,17},{2,10},{10... | collective-permute-start | bytes 4915208 | tf_op jit(solution)/shard_map/ppermute | solution.py:201
  303.6 46.1 %collective-permute-start.25 = (bf16[2,128,3200]{2,1,0:T(8,128)(2,1)S(1)}, bf16[2,128,3200]{2,1,0:T(8,128)(2,1)}, u32[]{:S(2)}, u32[]{:S(2)}) collective-permute-start(bf16[2,128,3200]{2,1,0:T(8,128)(2,1)S(1)} %get-tuple-element.107), channel_id=1, source_target_pairs={{0,16},{8,24},{16,0},{24,8},{1,17},{9,25},{17,1},{25,9},{2,18},{10... | collective-permute-start | bytes 4915208 | tf_op jit(solution)/shard_map/ppermute | solution.py:201
  324.0 46.3 %collective-permute-start.22 = (bf16[384,384]{1,0:T(8,128)(2,1)}, bf16[384,384]{1,0:T(8,128)(2,1)}, u32[]{:S(2)}, u32[]{:S(2)}) collective-permute-start(bf16[384,384]{1,0:T(8,128)(2,1)} %get-tuple-element.132), channel_id=1, source_target_pairs={{0,8},{8,0},{16,24},{24,16},{1,9},{9,1},{17,25},{25,17},{2,10},{10... | collective-permute-start | bytes 884744 | tf_op jit(solution)/shard_map/ppermute | solution.py:201
  324.9 45.4 %collective-permute-start.23 = (bf16[384,384]{1,0:T(8,128)(2,1)}, bf16[384,384]{1,0:T(8,128)(2,1)}, u32[]{:S(2)}, u32[]{:S(2)}) collective-permute-start(bf16[384,384]{1,0:T(8,128)(2,1)} %get-tuple-element.131), channel_id=1, source_target_pairs={{0,16},{8,24},{16,0},{24,8},{1,17},{9,25},{17,1},{25,9},{2,18},{10... | collective-permute-start | bytes 884744 | tf_op jit(solution)/shard_map/ppermute | solution.py:201
  325.5 44.8 %collective-permute-start.24 = (bf16[384,384]{1,0:T(8,128)(2,1)}, bf16[384,384]{1,0:T(8,128)(2,1)}, u32[]{:S(2)}, u32[]{:S(2)}) collective-permute-start(bf16[384,384]{1,0:T(8,128)(2,1)} %get-tuple-element.130), channel_id=1, source_target_pairs={{0,24},{8,16},{16,8},{24,0},{1,25},{9,17},{17,9},{25,1},{2,26},{10... | collective-permute-start | bytes 884744 | tf_op jit(solution)/shard_map/ppermute | solution.py:201
  347.5 32.6 %collective-permute-start.28 = (bf16[128,3200]{1,0:T(8,128)(2,1)}, bf16[128,3200]{1,0:T(8,128)(2,1)}, u32[]{:S(2)}, u32[]{:S(2)}) collective-permute-start(bf16[128,3200]{1,0:T(8,128)(2,1)} %get-tuple-element.117), channel_id=1, source_target_pairs={{0,16},{8,24},{16,0},{24,8},{1,17},{9,25},{17,1},{25,9},{2,18},{10... | collective-permute-start | bytes 2457608 | tf_op jit(solution)/shard_map/ppermute | solution.py:201
  352.7 28.7 %collective-permute-start.27 = (bf16[128,3200]{1,0:T(8,128)(2,1)}, bf16[128,3200]{1,0:T(8,128)(2,1)}, u32[]{:S(2)}, u32[]{:S(2)}) collective-permute-start(bf16[128,3200]{1,0:T(8,128)(2,1)} %get-tuple-element.115), channel_id=1, source_target_pairs={{0,8},{8,0},{16,24},{24,16},{1,9},{9,1},{17,25},{25,17},{2,10},{10... | collective-permute-start | bytes 2457608 | tf_op jit(solution)/shard_map/ppermute | solution.py:201
  370.1 91.3 %all-reduce.5.cloned.1.call-start = ((), (), s32[]{:S(2)}) async-start(), calls=%async_computation.4 | async-start | bytes 1343488 | tf_op jit(solution)/shard_map/psum | solution.py:703
  372.6 21.7 %collective-permute-start.29 = (bf16[384,384]{1,0:T(8,128)(2,1)}, bf16[384,384]{1,0:T(8,128)(2,1)}, u32[]{:S(2)}, u32[]{:S(2)}) collective-permute-start(bf16[384,384]{1,0:T(8,128)(2,1)} %get-tuple-element.128), channel_id=1, source_target_pairs={{0,8},{8,0},{16,24},{24,16},{1,9},{9,1},{17,25},{25,17},{2,10},{10... | collective-permute-start | bytes 884744 | tf_op jit(solution)/shard_map/ppermute | solution.py:201
  374.3 19.9 %collective-permute-start.30 = (bf16[384,384]{1,0:T(8,128)(2,1)}, bf16[384,384]{1,0:T(8,128)(2,1)}, u32[]{:S(2)}, u32[]{:S(2)}) collective-permute-start(bf16[384,384]{1,0:T(8,128)(2,1)} %get-tuple-element.127), channel_id=1, source_target_pairs={{0,16},{8,24},{16,0},{24,8},{1,17},{9,25},{17,1},{25,9},{2,18},{10... | collective-permute-start | bytes 884744 | tf_op jit(solution)/shard_map/ppermute | solution.py:201
  375.1 19.2 %collective-permute-start.31 = (bf16[384,384]{1,0:T(8,128)(2,1)}, bf16[384,384]{1,0:T(8,128)(2,1)}, u32[]{:S(2)}, u32[]{:S(2)}) collective-permute-start(bf16[384,384]{1,0:T(8,128)(2,1)} %get-tuple-element.126), channel_id=1, source_target_pairs={{0,24},{8,16},{16,8},{24,0},{1,25},{9,17},{17,9},{25,1},{2,26},{10... | collective-permute-start | bytes 884744 | tf_op jit(solution)/shard_map/ppermute | solution.py:201
  390.2 38.4 %collective-permute-start.32 = (bf16[1024,768]{1,0:T(8,128)(2,1)}, bf16[1024,768]{1,0:T(8,128)(2,1)}, u32[]{:S(2)}, u32[]{:S(2)}) collective-permute-start(bf16[1024,768]{1,0:T(8,128)(2,1)} %convolution_convert_fusion.3.refs_4_), channel_id=1, source_target_pairs={{0,1},{1,0},{2,3},{3,2},{4,5},{5,4},{6,7},{7,6},{8,9},{9,8},{10,11... | collective-permute-start | bytes 4718600 | tf_op jit(solution)/shard_map/ppermute | solution.py:201
  392.6 32.0 %collective-permute-start.43 = (bf16[128,3200]{1,0:T(8,128)(2,1)}, bf16[128,3200]{1,0:T(8,128)(2,1)}, u32[]{:S(2)}, u32[]{:S(2)}) collective-permute-start(bf16[128,3200]{1,0:T(8,128)(2,1)} %get-tuple-element.113), channel_id=1, source_target_pairs={{0,2},{2,0},{4,6},{6,4},{1,3},{3,1},{5,7},{7,5},{8,10},{10,8},{12,... | collective-permute-start | bytes 2457608 | tf_op jit(solution)/shard_map/ppermute | solution.py:201
  407.4 23.6 %collective-permute-start.33 = (bf16[1024,768]{1,0:T(8,128)(2,1)S(1)}, bf16[1024,768]{1,0:T(8,128)(2,1)S(1)}, u32[]{:S(2)}, u32[]{:S(2)}) collective-permute-start(bf16[1024,768]{1,0:T(8,128)(2,1)S(1)} %convolution_convert_fusion.2), channel_id=1, source_target_pairs={{0,1},{1,0},{2,3},{3,2},{4,5},{5,4},{6,7},{7,6},{8,9},{9,8},{10,11... | collective-permute-start | bytes 4718600 | tf_op jit(solution)/shard_map/ppermute | solution.py:201
  426.1 31.8 %collective-permute-start.44 = (bf16[64,3200]{1,0:T(8,128)(2,1)S(1)}, bf16[64,3200]{1,0:T(8,128)(2,1)S(1)}, u32[]{:S(2)}, u32[]{:S(2)}) collective-permute-start(bf16[64,3200]{1,0:T(8,128)(2,1)S(1)} %get-tuple-element.145), channel_id=1, source_target_pairs={{0,4},{2,6},{4,0},{6,2},{1,5},{3,7},{5,1},{7,3},{8,12},{10,14},{12... | collective-permute-start | bytes 1228808 | tf_op jit(solution)/shard_map/ppermute | solution.py:201
  432.8 25.3 %collective-permute-start.34 = (bf16[2,128,1536]{2,1,0:T(8,128)(2,1)S(1)}, bf16[2,128,1536]{2,1,0:T(8,128)(2,1)S(1)}, u32[]{:S(2)}, u32[]{:S(2)}) collective-permute-start(bf16[2,128,1536]{2,1,0:T(8,128)(2,1)S(1)} %get-tuple-element.123), channel_id=1, source_target_pairs={{0,16},{8,24},{16,0},{24,8},{1,17},{9,25},{17,1},{25,9},{2,18},{10... | collective-permute-start | bytes 2359304 | tf_op jit(solution)/shard_map/ppermute | solution.py:201
  434.0 24.9 %collective-permute-start.36 = (bf16[2,128,1536]{2,1,0:T(8,128)(2,1)S(1)}, bf16[2,128,1536]{2,1,0:T(8,128)(2,1)S(1)}, u32[]{:S(2)}, u32[]{:S(2)}) collective-permute-start(bf16[2,128,1536]{2,1,0:T(8,128)(2,1)S(1)} %get-tuple-element.121), channel_id=1, source_target_pairs={{0,8},{8,0},{16,24},{24,16},{1,9},{9,1},{17,25},{25,17},{2,10},{10... | collective-permute-start | bytes 2359304 | tf_op jit(solution)/shard_map/ppermute | solution.py:201
  458.0 20.3 %collective-permute-start.45 = (bf16[64,3200]{1,0:T(8,128)(2,1)S(1)}, bf16[64,3200]{1,0:T(8,128)(2,1)S(1)}, u32[]{:S(2)}, u32[]{:S(2)}) collective-permute-start(bf16[64,3200]{1,0:T(8,128)(2,1)S(1)} %add_convert_fusion.14), channel_id=1, source_target_pairs={{0,4},{2,6},{4,0},{6,2},{1,5},{3,7},{5,1},{7,3},{8,12},{10,14},{12... | collective-permute-start | bytes 1228808 | tf_op jit(solution)/shard_map/ppermute | solution.py:201
  458.4 10.2 %collective-permute-start.35 = (bf16[128,1536]{1,0:T(8,128)(2,1)S(1)}, bf16[128,1536]{1,0:T(8,128)(2,1)S(1)}, u32[]{:S(2)}, u32[]{:S(2)}) collective-permute-start(bf16[128,1536]{1,0:T(8,128)(2,1)S(1)} %get-tuple-element.153), channel_id=1, source_target_pairs={{0,8},{8,0},{16,24},{24,16},{1,9},{9,1},{17,25},{25,17},{2,10},{10... | collective-permute-start | bytes 1179656 | tf_op jit(solution)/shard_map/ppermute | solution.py:201
  459.2 10.2 %collective-permute-start.37 = (bf16[128,1536]{1,0:T(8,128)(2,1)S(1)}, bf16[128,1536]{1,0:T(8,128)(2,1)S(1)}, u32[]{:S(2)}, u32[]{:S(2)}) collective-permute-start(bf16[128,1536]{1,0:T(8,128)(2,1)S(1)} %get-tuple-element.151), channel_id=1, source_target_pairs={{0,16},{8,24},{16,0},{24,8},{1,17},{9,25},{17,1},{25,9},{2,18},{10... | collective-permute-start | bytes 1179656 | tf_op jit(solution)/shard_map/ppermute | solution.py:201
  461.4 36.6 %collective-permute-start.48 = (bf16[328,1024]{1,0:T(8,128)(2,1)}, bf16[328,1024]{1,0:T(8,128)(2,1)S(1)}, u32[]{:S(2)}, u32[]{:S(2)}) collective-permute-start(bf16[328,1024]{1,0:T(8,128)(2,1)} %all-reduce.5.cloned.1.call-done), channel_id=1, source_target_pairs={{0,1},{1,0},{2,3},{3,2},{4,5},{5,4},{6,7},{7,6},{8,9},{9,8},{10,11... | collective-permute-start | bytes 2015240 | tf_op jit(solution)/shard_map/ppermute | solution.py:201
  470.2 16.4 %collective-permute-start.38 = (bf16[128,1536]{1,0:T(8,128)(2,1)S(1)}, bf16[128,1536]{1,0:T(8,128)(2,1)S(1)}, u32[]{:S(2)}, u32[]{:S(2)}) collective-permute-start(bf16[128,1536]{1,0:T(8,128)(2,1)S(1)} %get-tuple-element.149), channel_id=1, source_target_pairs={{0,2},{2,0},{4,6},{6,4},{1,3},{3,1},{5,7},{7,5},{8,10},{10,8},{12,... | collective-permute-start | bytes 1179656 | tf_op jit(solution)/shard_map/ppermute | solution.py:201
  486.8 11.1 %collective-permute-start.39 = (bf16[64,1536]{1,0:T(8,128)(2,1)S(1)}, bf16[64,1536]{1,0:T(8,128)(2,1)S(1)}, u32[]{:S(2)}, u32[]{:S(2)}) collective-permute-start(bf16[64,1536]{1,0:T(8,128)(2,1)S(1)} %get-tuple-element.161), channel_id=1, source_target_pairs={{0,4},{2,6},{4,0},{6,2},{1,5},{3,7},{5,1},{7,3},{8,12},{10,14},{12... | collective-permute-start | bytes 589832 | tf_op jit(solution)/shard_map/ppermute | solution.py:201
  487.0 37.8 %collective-permute-start.46 = (bf16[128,3200]{1,0:T(8,128)(2,1)S(1)}, bf16[128,3200]{1,0:T(8,128)(2,1)S(1)}, u32[]{:S(2)}, u32[]{:S(2)}) collective-permute-start(bf16[128,3200]{1,0:T(8,128)(2,1)S(1)} %pad_maximum_fusion.11), channel_id=1, source_target_pairs={{0,2},{2,0},{4,6},{6,4},{1,3},{3,1},{5,7},{7,5},{8,10},{10,8},{12,... | collective-permute-start | bytes 2457608 | tf_op jit(solution)/shard_map/ppermute | solution.py:201
  498.0 15.4 %collective-permute-start.40 = (bf16[64,1536]{1,0:T(8,128)(2,1)S(1)}, bf16[64,1536]{1,0:T(8,128)(2,1)S(1)}, u32[]{:S(2)}, u32[]{:S(2)}) collective-permute-start(bf16[64,1536]{1,0:T(8,128)(2,1)S(1)} %add_convert_fusion.18), channel_id=1, source_target_pairs={{0,4},{2,6},{4,0},{6,2},{1,5},{3,7},{5,1},{7,3},{8,12},{10,14},{12... | collective-permute-start | bytes 589832 | tf_op jit(solution)/shard_map/ppermute | solution.py:201
  513.4 11.2 %collective-permute-start.41 = (bf16[128,1536]{1,0:T(8,128)(2,1)S(1)}, bf16[128,1536]{1,0:T(8,128)(2,1)S(1)}, u32[]{:S(2)}, u32[]{:S(2)}) collective-permute-start(bf16[128,1536]{1,0:T(8,128)(2,1)S(1)} %pad_maximum_fusion.14), channel_id=1, source_target_pairs={{0,2},{2,0},{4,6},{6,4},{1,3},{3,1},{5,7},{7,5},{8,10},{10,8},{12,... | collective-permute-start | bytes 1179656 | tf_op jit(solution)/shard_map/ppermute | solution.py:201
  (77 other events, 777.6 us)
Sparse Core Ops, SparseCore 0:
  10.5 48.2 all-gather.3
  61.2 124.0 all-gather.5
  260.7 74.1 reduce-scatter.1
  394.4 61.4 all-reduce.4

commit v7 on v6

--- a/solution.py
+++ b/solution.py
@@ -215,19 +215,14 @@
         out_ref[...] = other_ref[0]
 
 
-def near_first(part, group):
-    steps = (1, 2) if group == 4 else range(1, group)
-    return [exchange(part, "grp", d, group) for d in steps]
-
-
-def near_second(part, near, group, after, later):
-    if group == 4:
-        rows = part.shape[0] // 2
-        first, second = delayed(tuple(near), after)
-        upper = exchange(second[:rows], "grp", 1, group)
-        lower = exchange(first[rows:], "grp", 2, group)
-        near = [first, second, jnp.concatenate([upper, lower], axis=0)]
-    return jnp.stack([delayed(part, later), *near])
+def near_parts(part, group):
+    if group != 4:
+        return jnp.stack([part] + [exchange(part, "grp", d, group) for d in range(1, group)])
+    rows = part.shape[0] // 2
+    first, second = [exchange(part, "grp", d, group) for d in (1, 2)]
+    upper = exchange(second[:rows], "grp", 1, group)
+    lower = exchange(first[rows:], "grp", 2, group)
+    return jnp.stack([part, first, second, jnp.concatenate([upper, lower], axis=0)])
 
 
 def gather_direct(own, me_core, group, by_rows):
@@ -253,27 +248,36 @@
     )(me_core, own, other)
 
 
-def update_kernel(rate, w_ref, m_ref, s_ref, grad_ref, mean_ref, square_ref, new_ref):
-    mean, square, new = adam_update(
-        w_ref[...], m_ref[...], s_ref[...], grad_ref[...].astype(jnp.float32), rate
-    )
-    mean_ref[...] = mean
-    square_ref[...] = square
-    new_ref[...] = new
-
-
-def update_after(weight, mean, square, grad, rate, after):
-    rows, columns = weight.shape
-    block = pl.BlockSpec((32, columns), lambda i: (i, 0))
+def merge_kernel(pairs, group, core_ref, own_ref, other_ref, out_ref):
+    low, high = [], []
+    half = 3 * PAIR * group // 2
+    first = core_ref[0] == 0
+    for part in range(3):
+        for owner in range(group):
+            for pair in range(pairs):
+                side, within = divmod((owner * 3 + part) * PAIR, half)
+                source = pl.ds(pair * half + within, PAIR)
+                target = ((part * group + owner) * pairs + pair) * PAIR
+                own, other = own_ref[:, source], other_ref[:, source]
+                chosen = jnp.where(first, own, other) if side == 0 else jnp.where(first, other, own)
+                out_ref[:, target : target + PAIR] = chosen
+
+
+def merged_columns(core, own, other, pairs, group, after):
+    rows, columns = own.shape
+    block = pl.BlockSpec((rows, columns), lambda i, core: (0, 0))
     return pl.pallas_call(
-        skipping(functools.partial(update_kernel, rate), 4, len(after)),
-        grid=(rows // 32,),
-        in_specs=[block] * 4 + untouched(after),
-        out_specs=[block] * 3,
-        out_shape=[jax.ShapeDtypeStruct(weight.shape, jnp.float32)] * 3,
+        skipping(functools.partial(merge_kernel, pairs, group), 3, len(after)),
+        grid_spec=pltpu.PrefetchScalarGridSpec(
+            num_scalar_prefetch=1,
+            grid=(1,),
+            in_specs=[block, block, *untouched(after)],
+            out_specs=pl.BlockSpec((rows, 2 * columns), lambda i, core: (0, 0)),
+        ),
+        out_shape=jax.ShapeDtypeStruct((rows, 2 * columns), jnp.bfloat16),
         compiler_params=compiler_params(),
-        name="update_inproj",
-    )(weight, mean, square, grad, *after)
+        name="merge",
+    )(core, own, other, *after)
 
 
 def attend_kernel(q_ref, k_ref, v_ref, qf_ref, kf_ref, own_v_ref, own_f_ref, out_ref, stat_ref, ke):
@@ -523,18 +527,18 @@
     return [1 << bit for bit in range(far.bit_length() - 1)]
 
 
-def far_scatter(share, far, waits=((), ())):
+def far_scatter(share, far, waits=((), ()), dim=0):
     if far > 4:
         return [lax.psum(share, "far")]
     stages = [share]
     for mask, after in zip(far_masks(far), waits):
         share = stages[-1]
         bit = (lax.axis_index("far") // mask) % 2
-        rows = share.shape[0] // 2
+        size = share.shape[dim] // 2
         got = exchange(
-            lax.dynamic_slice_in_dim(share, (1 - bit) * rows, rows, 0), "far", mask, far
+            lax.dynamic_slice_in_dim(share, (1 - bit) * size, size, dim), "far", mask, far
         )
-        kept = lax.dynamic_slice_in_dim(share, bit * rows, rows, 0)
+        kept = lax.dynamic_slice_in_dim(share, bit * size, size, dim)
         stages.append(added(delayed(kept, after), got))
     return stages
 
@@ -548,23 +552,11 @@
     return jnp.concatenate([low, high], axis=dim)
 
 
-def spread(share, far, waits=((), ())):
+def spread(share, far, waits=((), ()), dim=0):
     if far <= 4:
         for mask, after in zip(far_masks(far)[::-1], waits):
-            share = doubled(share, "far", mask, far, 0, after)
+            share = doubled(share, "far", mask, far, dim, after)
     return share
-
-
-def merged_columns(total, pairs, group):
-    half = 3 * PAIR * group // 2
-    blocks = []
-    for part in range(3):
-        for owner in range(group):
-            for pair in range(pairs):
-                side, within = divmod((owner * 3 + part) * PAIR, half)
-                column = (side * pairs + pair) * half + within
-                blocks.append(total[:, column : column + PAIR])
-    return jnp.concatenate(blocks, axis=1)
 
 
 def spread_halves(array):
@@ -634,25 +626,29 @@
     first_normed = layer_norm(inputs, gain_one).astype(jnp.bfloat16)
     cos_near = cos.reshape(group, own_rows, PAIR)
     sin_near = sin.reshape(group, own_rows, PAIR)
+    shares = 2 * far if far <= 4 else 2
+    place_of = core * far + lax.axis_index("far") if far <= 4 else core
+    low_down = lax.dynamic_slice_in_dim(
+        downproj, place_of * (D // shares), D // shares, 1
+    ).astype(jnp.bfloat16)
+    near_down = near_parts(low_down, group)
     qkv, stats, attended_near, attended_here, first_sent = [], [], [], [], []
     for pair in range(pairs):
-        after = first_sent[:1]
+        after = first_sent[:1] + [near_down] * (pair == pairs - 1)
         pieces = project(me_list, first_normed, w_in, cos_near, sin_near, pair, group, after)
         first_sent.append(pieces)
         qkv.append(swap_heads(pieces, group))
-    low_down = lax.dynamic_slice_in_dim(downproj, core * (D // 2), D // 2, 1).astype(jnp.bfloat16)
     for pair in range(pairs):
         qkv[pair] = jnp.concatenate([delayed(qkv[pair][0], stats[-1:]), *qkv[pair][1:]], axis=0)
-        if pair == pairs - 1:
-            low_down = delayed(low_down, qkv[pair])
-            near_down = near_first(low_down, group)
         mixed, stat = attend(qkv[pair], query_side, key_side)
         stats.append(stat)
         attended_near.append(mixed)
         mixed = delayed(mixed, attended_here[:1])
         attended_here.append(swap_heads(mixed.reshape(group, own_rows, PAIR), group))
     attended = place(me_list, attended_here, group)
-    near_down = near_second(low_down, near_down, group, stats[-1], attended)
+    if far <= 4:
+        for mask, after in zip(far_masks(far), (qkv[0][:8], attended)):
+            near_down = doubled(near_down, "far", mask, far, 2, after)
     w_down = gather_direct(near_down, me_core, group, False)
     middle = inputs + product(attended, w_out)
     second_normed = layer_norm(middle, gain_two).astype(jnp.bfloat16)
@@ -686,7 +682,7 @@
         ],
         axis=1,
     )
-    grads_here, grads_near = [], [up_share]
+    grads_here, grads_near, in_theirs = [], [up_share], []
     for pair in range(pairs):
         grads = attend_back(
             qkv[pair], query_side, key_side, stats[pair], attended_near[pair], grad_near,
@@ -694,16 +690,18 @@
         )
         if pair == 0:
             up_halves = group_first(delayed(up_share, grad_near), group, grads)
-            grads_near = [grads, down_share, *up_halves]
+            grads_near = [grads, *up_halves]
+            down_share = delayed(down_share, grads)
         if pair == pairs - 1:
             up_half = group_second(up_halves, group, grads)
+            down_stages = far_scatter(down_share, far, (grads, in_theirs), 1)
+            down_early, down_share = down_stages[min(1, len(down_stages) - 1)], down_stages[-1]
         if pair > 0:
-            grads = delayed(grads, grads_here[0])
+            grads = delayed(grads, (grads_here[0], down_early))
         grads_here.append(swap_heads(grads.reshape(group, own_rows, 3 * PAIR), group))
-    down_share = lax.psum(down_share, "far")
-    grads_placed, in_theirs, grad_first = [], [], 0.0
+    grads_placed, grad_first = [], 0.0
     for pair in range(pairs):
-        after = (up_half,) if pair == 0 else (in_theirs[0],)
+        after = (up_half,) if pair == 0 else (in_theirs[0], down_share)
         placed = place(me_list, [grads_here[pair]], group, after)
         grads_placed.append(placed)
         in_theirs.append(core_theirs(first_normed, placed, core))
@@ -721,7 +719,7 @@
     for pair in range(pairs):
         width = 3 * PAIR * group
         part = w_in[:, pair * width : (pair + 1) * width]
-        grad_first = grad_first + against(grads_placed[pair], part)
+        grad_first = grad_first + against(delayed(grads_placed[pair], in_share), part)
     up_chunk = far_scatter(up_half, far, (in_theirs[-1], in_share))[-1]
     up_chunk = spread(up_chunk, far, (in_first, in_half))
     up_final = doubled(up_chunk, "core", 1, 2, 1, in_early)
@@ -729,9 +727,8 @@
     wide = up_chunk.shape[1]
     total_out = jnp.concatenate([total_up[:, FF_WIDE:wide], total_up[:, wide + FF_WIDE :]], axis=1)
     total_up = jnp.concatenate([total_up[:, :FF], total_up[:, wide : wide + FF]], axis=1)
-    total_down = doubled(
-        delayed(down_share, in_first), "core", 1, 2, 0, in_early
-    ).astype(jnp.float32)
+    down_share = spread(down_share, far, (in_share, in_first), 1)
+    total_down = doubled(down_share, "core", 1, 2, 0, in_early).astype(jnp.float32)
     _, first_back = jax.vjp(lambda v: layer_norm(v, gain_one), inputs)
     (grad_inputs,) = first_back(grad_first)
     input_grad = (grad_middle + grad_inputs).astype(jnp.bfloat16)
@@ -742,9 +739,11 @@
         return adam_update(masters[index], means[index], squares[index], total, rate_list[index])
 
     updates = [None, update(1, total_out), update(2, total_up), update(3, total_down), None]
-    in_share = doubled(spread(in_chunk, far, ((), ())), "core", 1, 2, 1, ())
-    low_total = merged_columns(in_share, pairs, group)
-    total_in = low_total.astype(jnp.float32)
+    in_chunk = spread(in_chunk, far)
+    total_in = merged_columns(
+        core_list, in_chunk, exchange(in_chunk, "core", 1, 2), pairs, group,
+        [updates[index][2] for index in (1, 2, 3)],
+    ).astype(jnp.float32)
     low_in = inproj.astype(jnp.bfloat16).astype(jnp.float32)
     low_up = upproj.astype(jnp.bfloat16).astype(jnp.float32)
     low_gains = norm_gains.astype(jnp.bfloat16).astype(jnp.float32)
@@ -752,10 +751,7 @@
         jnp.stack([jnp.sum(low_in * total_in, axis=1), jnp.sum(low_up * total_up, axis=1)], axis=1)
         / low_gains
     )
-    updates[0] = update_after(
-        inproj, inproj_mean, inproj_square, low_total, rate_list[0],
-        [updates[index][2] for index in (1, 2, 3)],
-    )
+    updates[0] = update(0, total_in)
     updates[4] = update(4, total_gains)
     return (
         result.astype(jnp.bfloat16)[None],

time: 568 us -> 542 us (0.954)
  waiting for transfers between devices: 202 us -> 174 us
  starting transfers between devices: 54.2 us -> 62.8 us
  Pallas kernels: 102 us -> 94.2 us
    all_gather x1, waiting for transfers between devices: 22.3 us -> 1.33 us  [local(): lax.all_gather(lower_half(core_list, inproj, group), both, axis=0, tiled=...]
    ppermute x49 -> x55, waiting for transfers between devices: 179 us -> 166 us  [exchange(): return lax.ppermute(array, axis, [(i, i ^ mask) for i in range(size)])]
    ppermute x49 -> x55, starting transfers between devices: 53.9 us -> 62.7 us  [exchange(): return lax.ppermute(array, axis, [(i, i ^ mask) for i in range(size)])]
    pallas_call x1, Pallas kernels: 10 us -> 2.95 us  [merged_columns(): pl.pallas_call(skipping(functools.partial(merge_kernel, pairs, group), 3,...]
    all_gather x1, waiting for transfers between devices: 0.02 us -> 6.73 us  [gather_weight(): lax.all_gather(own_half(weight, core).astype(jnp.bfloat16), ('grp', 'core...]
    sub x4 -> x5, other arithmetic: 18.3 us -> 24.9 us  [adam_update(): return (mean_new, square_new, weight - rate * (step_size + 0.01 * weight))]
    unnamed x173 -> x152, local copies, waits for them, and re-layouts: 10.8 us -> 11.8 us
  transfers between devices with their start and end apart: 53 -> 58, of which waited for: 28 -> 28; matrix products, arithmetic and copies ran while one was open for 20% -> 22% of each run, Pallas kernels for 16% -> 17%
where the time goes in v7:
time: 542 us; the launch traced here: 536 us
  waiting for transfers between devices  174 us (32%)
  Pallas kernels  94.2 us (17%)
  other arithmetic  77.8 us (14%)
  matrix products  67.6 us (12%)
  starting transfers between devices  62.8 us (12%)
  local copies, waits for them, and re-layouts  34.8 us (6%)
  between operations  15.6 us (3%)
  blocking collectives  9.63 us (2%)
    ppermute x55, waiting for transfers between devices, exchange(): return lax.ppermute(array, axis, [(i, i ^ mask) for i in range(size)])  166 us
    ppermute x55, starting transfers between devices, exchange(): return lax.ppermute(array, axis, [(i, i ^ mask) for i in range(size)])  62.7 us
    pallas_call x2, Pallas kernels, attend_back(): pl.pallas_call(skipping(attend_back_kernel, 12, len(after)), grid=(rows /...  34.3 us
    dot_general x9, matrix products, contract(): lax.dot_general(left, right, (((0,), (0,)), ((), ())), preferred_element_...  28.4 us
    sub x5, other arithmetic, adam_update(): return (mean_new, square_new, weight - rate * (step_size + 0.01 * weight))  24.9 us
    dot_general x4, matrix products, against(): lax.dot_general(left, right, (((1,), (1,)), ((), ())), preferred_element_...  21.9 us
    pallas_call x2, Pallas kernels, attend(): pl.pallas_call(skipping(attend_kernel, 7, len(after)), grid=(rows // bloc...  20.5 us
    dot_general x3, matrix products, product(): return jnp.dot(left, right, preferred_element_type=jnp.float32)  17.2 us
  transfers between devices with their start and end apart: 58, of which 28 were waited for; matrix products, arithmetic and copies ran while one was open for 22% of the time, Pallas kernels for 17%

profile of v7, /device:TPU:0, one launch (start us, length us, event | category | flops | bytes accessed | tf_op | source)
XLA Modules:
  0.0 536.3 jit_solution(5210947060157209917)
XLA Ops:
  16.4 3.0 collective-permute-start.6
  21.0 9.6 %all-gather = bf16[4,1,896]{2,1,0:T(2,128)(2,1)S(1)} all-gather(bf16[1,1,896]{2,1,0:T(2,128)(2,1)S(1)} %maximum_bitcast_fusion.1), channel_id=1, replica_groups=mesh['grp'=4,'far'=4,'core'=2] {'grp'}, dimensions={0}, use_global_device_ids=true | all-gather | bytes 8960 | tf_op jit(solution)/shard_map/all_gather | solution.py:614
  34.9 4.5 fusion.58
  52.2 7.8 %collective-permute-done.16 = bf16[4,656,128]{2,1,0:T(8,128)(2,1)S(1)} collective-permute-done((bf16[4,656,128]{2,1,0:T(8,128)(2,1)S(1)}, bf16[4,656,128]{2,1,0:T(8,128)(2,1)S(1)}, u32[]{:S(2)}, u32[]{:S(2)}) %collective-permute-start.16) | collective-permute-done | bytes 671776 | tf_op jit(solution)/shard_map/ppermute | solution.py:201
  61.4 5.8 %project.2.refs_5_ = bf16[4,384,384]{2,1,0:T(8,128)(2,1)} custom-call(s32[1]{0:T(128)} %bitcast.1.refs_0_.me_ref, bf16[384,1024]{1,0:T(8,128)(2,1)} %fusion.43.refs_1_, bf16[1024,3072]{1,0:T(8,128)(2,1)} %all-gather.4.cloned.1.call-done.refs_2_, f32[4,384,128]{2,1,0:T(8,128)} %get-tuple-element.189.refs_3_, f32[4,384,128]{2,1,0:T(8,128)} %get-tuple-element.188.refs_4_), custom_call_target="tpu_custom_call" | custom-call | tf_op jit(solution)/shard_map/project/pallas_call | solution.py:126
  74.7 5.9 %project.3 = bf16[4,384,384]{2,1,0:T(8,128)(2,1)} custom-call(s32[1]{0:T(128)} %bitcast.1.refs_0_.me_ref, bf16[384,1024]{1,0:T(8,128)(2,1)} %fusion.43.refs_1_, bf16[1024,3072]{1,0:T(8,128)(2,1)} %all-gather.4.cloned.1.call-done.refs_2_, f32[4,384,128]{2,1,0:T(8,128)} %get-tuple-element.189.refs_3_, f32[4,384,128]{2,1,0:T(8,128)} %get-tuple-element.188.refs_4_, ...), custom_call_target="tpu_custom_call" | custom-call | tf_op jit(solution)/shard_map/project/pallas_call | solution.py:126
  84.3 7.1 %collective-permute-done.1 = bf16[384,384]{1,0:T(8,128)(2,1)S(1)} collective-permute-done((bf16[384,384]{1,0:T(8,128)(2,1)S(1)}, bf16[384,384]{1,0:T(8,128)(2,1)S(1)}, u32[]{:S(2)}, u32[]{:S(2)}) %collective-permute-start.1) | collective-permute-done | bytes 294944 | tf_op jit(solution)/shard_map/ppermute | solution.py:201
  96.3 10.2 %attend.2 = (bf16[1536,128]{1,0:T(8,128)(2,1)}, f32[1536,128]{1,0:T(8,128)}) custom-call(bf16[1536,384]{1,0:T(8,128)(2,1)} %pad_maximum_fusion.9.refs_0_.refs_1_.refs_2_.refs_5_, bf16[1536,384]{1,0:T(8,128)(2,1)} %pad_maximum_fusion.9.refs_0_.refs_1_.refs_2_.refs_5_, bf16[1536,384]{1,0:T(8,128)(2,1)} %pad_maximum_fusion.9.refs_0_.refs_1_.refs_2_.refs_5_, ...), custom_call_target="tpu_custom_call" | custom-call | tf_op jit(solution)/shard_map/attend/pallas_call | solution.py:327
  112.1 3.8 collective-permute-done.12
  116.9 10.2 %attend.3 = (bf16[1536,128]{1,0:T(8,128)(2,1)}, f32[1536,128]{1,0:T(8,128)}) custom-call(bf16[1536,384]{1,0:T(8,128)(2,1)} %copy-done, bf16[1536,384]{1,0:T(8,128)(2,1)} %copy-done, bf16[1536,384]{1,0:T(8,128)(2,1)} %copy-done, bf16[1536,128]{1,0:T(8,128)(2,1)} %get-tuple-element.185.refs_3_, bf16[1536,128]{1,0:T(8,128)(2,1)} %get-tuple-element.184.refs_4_.refs_6_, ...), custom_call_target="tpu_custom_call" | custom-call | tf_op jit(solution)/shard_map/attend/pallas_call | solution.py:327
  132.5 4.6 collective-permute-done.13.refs_5_
  149.5 8.9 %assemble.1 = bf16[2624,1024]{1,0:T(8,128)(2,1)} custom-call(s32[2]{0:T(128)} %pad_add_fusion.me_ref, bf16[4,656,512]{2,1,0:T(8,128)(2,1)} %copy-done.10, bf16[4,656,512]{2,1,0:T(8,128)(2,1)} %collective-permute-done.18.other_ref), custom_call_target="tpu_custom_call" | custom-call | tf_op jit(solution)/shard_map/assemble/pallas_call | solution.py:237
  158.5 6.7 %all-gather.6.cloned.1.call-done.refs_2_ = bf16[1024,6400]{1,0:T(8,128)(2,1)} async-done(((bf16[128,6400]{1,0:T(8,128)(2,1)}), bf16[1024,6400]{1,0:T(8,128)(2,1)}) %all-gather.6.cloned.1.call-update) | async-done | bytes 13107216 | tf_op jit(solution)/shard_map/all_gather | solution.py:471
  165.2 2.9 fusion.111
  168.5 7.8 %fusion.2 = f32[384,5376]{1,0:T(8,128)S(1)} fusion(bf16[1024,6400]{1,0:T(8,128)(2,1)} %all-gather.6.cloned.1.call-done.refs_2_, f32[384,1024]{1,0:T(8,128)S(1)} %get-tuple-element.193, f32[1024]{0:T(1024)S(1)} %bitcast.170, f32[384]{0:T(512)S(1)} %fusion.87, f32[384]{0:T(512)S(1)} %broadcast_multiply_fusion), kind=kOutput, calls=%fused_computation.5 | convolution fusion | flops 4229431296 | bytes 20847616 | tf_op jit(solution)/shard_map/dot_general | solution.py:450
  176.3 10.3 %multiply_convert_fusion.1 = (bf16[384,2624]{1,0:T(8,128)(2,1)S(1)}, f32[384,2624]{1,0:T(8,128)}) fusion(f32[384,5376]{1,0:T(8,128)S(1)} %fusion.2), kind=kLoop, calls=%fused_computation.32 | loop fusion | flops 66502656 | bytes 14106624 | tf_op jit(solution)/shard_map/convert_element_type | solution.py:658
  187.9 4.7 convolution_convert_fusion.1
  192.6 10.2 %add_convert_fusion.1 = (bf16[384,2624]{1,0:T(8,128)(2,1)S(1)}, bf16[384,2624]{1,0:T(8,128)(2,1)S(1)}) fusion(f32[384,2624]{1,0:T(8,128)} %get-tuple-element.93, f32[384,5376]{1,0:T(8,128)} %copy-done.11, bf16[384,1024]{1,0:T(8,128)(2,1)S(1)} %copy-done.40, bf16[2624,1024]{1,0:T(8,128)(2,1)} %assemble.1), kind=kOutput, calls=%fused_computation.31 | convolution fusion | flops 2081734656 | bytes 22282240 | tf_op jit(solution)/shard_map/dot_general | solution.py:460
  203.2 5.1 convolution_convert_fusion.refs_3_
  208.6 8.6 %multiply_reduce_fusion.1 = (f32[384]{0:T(512)S(1)}, f32[384,1024]{1,0:T(8,128)S(1)}) fusion(f32[384,1024]{1,0:T(8,128)S(1)} %get-tuple-element.193, f32[384]{0:T(512)S(1)} %broadcast_multiply_fusion, f32[1024]{0:T(1024)S(1)} %bitcast.172, bf16[384,5376]{1,0:T(8,128)(2,1)} %copy-done.21, bf16[1024,6400]{1,0:T(8,128)(2,1)} %all-gather.6.cloned.1.call-done.refs_2_), kind=kOutput, calls=%fused_computation.116 | convolution fusion | flops 4229430784 | bytes 18291712 | tf_op jit(solution)/shard_map/dot_general | solution.py:460
  220.1 5.0 row_product.1
  232.1 4.8 collective-permute-done.21
  236.9 3.5 collective-permute-done.20
  242.7 3.1 add_convert_fusion.6
  245.8 7.0 %add_convert_fusion = bf16[1024,2688]{1,0:T(8,128)(2,1)} fusion(bf16[1024,2688]{1,0:T(8,128)(2,1)} %collective-permute-done.22, bf16[384,5376]{1,0:T(8,128)(2,1)S(1)} %copy-done.22, s32[]{:T(128)S(6)} %select_n.377, f32[384,1024]{1,0:T(8,128)S(1)} %get-tuple-element.193, f32[1024]{0:T(1024)S(1)} %bitcast.173, f32[384]{0:T(512)S(1)} %copy-done.56, ...), kind=kOutput, calls=%fused_computation.2 | convolution fusion | flops 2123759616 | bytes 14655492 | tf_op jit(solution)/shard_map/dot_general | solution.py:454
  252.8 3.7 pad_maximum_fusion.refs_12_
  262.6 4.3 fusion.59
  266.9 6.6 %fusion.53 = bf16[1,384,1024]{2,1,0:T(8,128)(2,1)} fusion(f32[384,1024]{1,0:T(8,128)S(1)} %copy-done.16, bf16[384,2624]{1,0:T(8,128)(2,1)} %copy-done.30, bf16[2624,1024]{1,0:T(8,128)(2,1)} %assemble.1), kind=kOutput, calls=%fused_computation.129 | convolution fusion | flops 2064384000 | bytes 9748480 | tf_op jit(solution)/shard_map/dot_general | solution.py:450
  274.8 17.1 %attend_back.2.refs_12_ = bf16[1536,384]{1,0:T(8,128)(2,1)} custom-call(bf16[1536,384]{1,0:T(8,128)(2,1)} %pad_maximum_fusion.9.refs_0_.refs_1_.refs_2_.refs_5_, bf16[1536,384]{1,0:T(8,128)(2,1)} %pad_maximum_fusion.9.refs_0_.refs_1_.refs_2_.refs_5_, bf16[1536,384]{1,0:T(8,128)(2,1)} %pad_maximum_fusion.9.refs_0_.refs_1_.refs_2_.refs_5_, ...), custom_call_target="tpu_custom_call" | custom-call | tf_op jit(solution)/shard_map/attend_back/pallas_call | solution.py:428
  297.7 16.9 %collective-permute-done.28 = bf16[2,128,3200]{2,1,0:T(8,128)(2,1)} collective-permute-done((bf16[2,128,3200]{2,1,0:T(8,128)(2,1)}, bf16[2,128,3200]{2,1,0:T(8,128)(2,1)}, u32[]{:S(2)}, u32[]{:S(2)}) %collective-permute-start.28) | collective-permute-done | bytes 1638432 | tf_op jit(solution)/shard_map/ppermute | solution.py:201
  321.2 17.2 %attend_back.3 = bf16[1536,384]{1,0:T(8,128)(2,1)} custom-call(bf16[1536,384]{1,0:T(8,128)(2,1)} %copy-done, bf16[1536,384]{1,0:T(8,128)(2,1)} %copy-done, bf16[1536,384]{1,0:T(8,128)(2,1)} %copy-done, bf16[1536,128]{1,0:T(8,128)(2,1)} %get-tuple-element.185.refs_3_, bf16[1536,128]{1,0:T(8,128)(2,1)} %get-tuple-element.184.refs_4_.refs_6_, ...), custom_call_target="tpu_custom_call" | custom-call | tf_op jit(solution)/shard_map/attend_back/pallas_call | solution.py:428
  339.7 8.8 %collective-permute-done.30 = bf16[128,3200]{1,0:T(8,128)(2,1)S(1)} collective-permute-done((bf16[128,3200]{1,0:T(8,128)(2,1)S(1)}, bf16[128,3200]{1,0:T(8,128)(2,1)S(1)}, u32[]{:S(2)}, u32[]{:S(2)}) %collective-permute-start.30) | collective-permute-done | bytes 819232 | tf_op jit(solution)/shard_map/ppermute | solution.py:201
  348.7 7.7 %collective-permute-done.29 = bf16[128,3200]{1,0:T(8,128)(2,1)S(1)} collective-permute-done((bf16[128,3200]{1,0:T(8,128)(2,1)S(1)}, bf16[128,3200]{1,0:T(8,128)(2,1)S(1)}, u32[]{:S(2)}, u32[]{:S(2)}) %collective-permute-start.29) | collective-permute-done | bytes 819232 | tf_op jit(solution)/shard_map/ppermute | solution.py:201
  363.3 2.9 place.4
  366.2 16.7 %collective-permute-done.32 = bf16[328,512]{1,0:T(8,128)(2,1)S(1)} collective-permute-done((bf16[328,512]{1,0:T(8,128)(2,1)S(1)}, bf16[328,512]{1,0:T(8,128)(2,1)S(1)}, u32[]{:S(2)}, u32[]{:S(2)}) %collective-permute-start.32) | collective-permute-done | bytes 335904 | tf_op jit(solution)/shard_map/ppermute | solution.py:201
  390.9 4.6 collective-permute-done.36
  397.7 2.8 place.5
  416.4 8.2 %collective-permute-done.48 = bf16[64,3200]{1,0:T(8,128)(2,1)S(1)} collective-permute-done((bf16[64,3200]{1,0:T(8,128)(2,1)S(1)}, bf16[64,3200]{1,0:T(8,128)(2,1)S(1)}, u32[]{:S(2)}, u32[]{:S(2)}) %collective-permute-start.48) | collective-permute-done | bytes 409632 | tf_op jit(solution)/shard_map/ppermute | solution.py:201
  426.4 3.9 collective-permute-start.53
  435.7 9.8 %collective-permute-done.49 = bf16[64,3200]{1,0:T(8,128)(2,1)S(1)} collective-permute-done((bf16[64,3200]{1,0:T(8,128)(2,1)S(1)}, bf16[64,3200]{1,0:T(8,128)(2,1)S(1)}, u32[]{:S(2)}, u32[]{:S(2)}) %collective-permute-start.49) | collective-permute-done | bytes 409632 | tf_op jit(solution)/shard_map/ppermute | solution.py:201
  449.0 11.8 %collective-permute-done.42 = bf16[128,1536]{1,0:T(8,128)(2,1)S(1)} collective-permute-done((bf16[128,1536]{1,0:T(8,128)(2,1)S(1)}, bf16[128,1536]{1,0:T(8,128)(2,1)S(1)}, u32[]{:S(2)}, u32[]{:S(2)}) %collective-permute-start.42) | collective-permute-done | bytes 393248 | tf_op jit(solution)/shard_map/ppermute | solution.py:201
  461.1 17.2 %collective-permute-done.50 = bf16[128,3200]{1,0:T(8,128)(2,1)S(1)} collective-permute-done((bf16[128,3200]{1,0:T(8,128)(2,1)S(1)}, bf16[128,3200]{1,0:T(8,128)(2,1)S(1)}, u32[]{:S(2)}, u32[]{:S(2)}) %collective-permute-start.50) | collective-permute-done | bytes 819232 | tf_op jit(solution)/shard_map/ppermute | solution.py:201
  479.9 8.7 %collective-permute-done.44 = bf16[64,1536]{1,0:T(8,128)(2,1)S(1)} collective-permute-done((bf16[64,1536]{1,0:T(8,128)(2,1)S(1)}, bf16[64,1536]{1,0:T(8,128)(2,1)S(1)}, u32[]{:S(2)}, u32[]{:S(2)}) %collective-permute-start.44) | collective-permute-done | bytes 196640 | tf_op jit(solution)/shard_map/ppermute | solution.py:201
  488.8 4.2 multiply_subtract_fusion.2
  493.0 5.9 %collective-permute-done.45 = bf16[128,1536]{1,0:T(8,128)(2,1)S(1)} collective-permute-done((bf16[128,1536]{1,0:T(8,128)(2,1)S(1)}, bf16[128,1536]{1,0:T(8,128)(2,1)S(1)}, u32[]{:S(2)}, u32[]{:S(2)}) %collective-permute-start.45) | collective-permute-done | bytes 393248 | tf_op jit(solution)/shard_map/ppermute | solution.py:201
  502.0 11.2 %multiply_subtract_fusion = (f32[256,5248]{1,0:T(8,128)}, f32[256,5248]{1,0:T(8,128)}, f32[256,5248]{1,0:T(8,128)}, f32[256]{0:T(256)S(1)}) fusion(f32[256,5248]{1,0:T(8,128)S(1)} %bitcast.159, f32[256,2624]{1,0:T(8,128)S(1)} %get-tuple-element.101, f32[256,2624]{1,0:T(8,128)S(1)} %get-tuple-element.100, f32[256,5248]{1,0:T(8,128)} %param.28, ...), kind=kLoop, calls=%fused_computation.26 | loop fusion | flops 26869504 | bytes 37618688 | tf_op jit(solution)/shard_map/sub | solution.py:575
  518.2 3.0 merge.1
  522.1 6.6 %multiply_subtract_fusion.1 = (f32[256,3072]{1,0:T(8,128)}, f32[256,3072]{1,0:T(8,128)}, f32[256,3072]{1,0:T(8,128)}, f32[256]{0:T(256)S(1)}) fusion(f32[256,3072]{1,0:T(8,128)S(1)} %copy-done.9, bf16[256,3072]{1,0:T(8,128)(2,1)} %merge.1, f32[256,3072]{1,0:T(8,128)S(1)} %copy-done.26, f32[256,3072]{1,0:T(8,128)} %param.26), kind=kLoop, calls=%fused_computation.65 | loop fusion | flops 15728384 | bytes 20448256 | tf_op jit(solution)/shard_map/sub | solution.py:575
  (389 shorter events, 159.6 us)
Async XLA Ops:
  7.2 54.2 %all-gather.4.cloned.1.call-start = ((), (), s32[]{:S(2)}) async-start(), calls=%async_computation.1 | async-start | bytes 7077888 | tf_op jit(solution)/shard_map/all_gather | solution.py:609
  9.7 155.5 %all-gather.6.cloned.1.call-start = ((), (), s32[]{:S(2)}) async-start(), calls=%async_computation.2 | async-start | bytes 14745600 | tf_op jit(solution)/shard_map/all_gather | solution.py:471
  15.4 344.9 %reduce-scatter.2.cloned.1.call-start = ((), (), s32[]{:S(2)}) async-start(), calls=%async_computation.3 | async-start | bytes 6045696 | tf_op jit(solution)/shard_map/reduce_scatter | solution.py:667
  16.4 24.1 %collective-permute-start.6 = (bf16[656,128]{1,0:T(8,128)(2,1)S(1)}, bf16[656,128]{1,0:T(8,128)(2,1)S(1)}, u32[]{:S(2)}, u32[]{:S(2)}) collective-permute-start(bf16[656,128]{1,0:T(8,128)(2,1)S(1)} %dynamic-slice_convert_fusion), channel_id=1, source_target_pairs={{0,8},{8,0},{16,24},{24,16},{1,9},{9,1},{17,25},{25,17},{2,10},{10... | collective-permute-start | bytes 503816 | tf_op jit(solution)/shard_map/ppermute | solution.py:201
  19.5 22.4 %collective-permute-start.7 = (bf16[656,128]{1,0:T(8,128)(2,1)S(1)}, bf16[656,128]{1,0:T(8,128)(2,1)S(1)}, u32[]{:S(2)}, u32[]{:S(2)}) collective-permute-start(bf16[656,128]{1,0:T(8,128)(2,1)S(1)} %dynamic-slice_convert_fusion), channel_id=1, source_target_pairs={{0,16},{8,24},{16,0},{24,8},{1,17},{9,25},{17,1},{25,9},{2,18},{10... | collective-permute-start | bytes 503816 | tf_op jit(solution)/shard_map/ppermute | solution.py:201
  48.7 11.2 %collective-permute-start.16 = (bf16[4,656,128]{2,1,0:T(8,128)(2,1)S(1)}, bf16[4,656,128]{2,1,0:T(8,128)(2,1)S(1)}, u32[]{:S(2)}, u32[]{:S(2)}) collective-permute-start(bf16[4,656,128]{2,1,0:T(8,128)(2,1)S(1)} %pad_maximum_fusion.15.refs_6_), channel_id=1, source_target_pairs={{0,2},{2,0},{4,6},{6,4},{1,3},{3,1},{5,7},{7,5},{8,10},{10,8},{12,... | collective-permute-start | bytes 2015240 | tf_op jit(solution)/shard_map/ppermute | solution.py:201
  68.5 15.1 %collective-permute-start.2 = (bf16[384,384]{1,0:T(8,128)(2,1)S(1)}, bf16[384,384]{1,0:T(8,128)(2,1)S(1)}, u32[]{:S(2)}, u32[]{:S(2)}) collective-permute-start(bf16[384,384]{1,0:T(8,128)(2,1)S(1)} %get-tuple-element.143), channel_id=1, source_target_pairs={{0,24},{8,16},{16,8},{24,0},{1,25},{9,17},{17,9},{25,1},{2,26},{10... | collective-permute-start | bytes 884744 | tf_op jit(solution)/shard_map/ppermute | solution.py:201
  70.1 21.2 %collective-permute-start.1 = (bf16[384,384]{1,0:T(8,128)(2,1)S(1)}, bf16[384,384]{1,0:T(8,128)(2,1)S(1)}, u32[]{:S(2)}, u32[]{:S(2)}) collective-permute-start(bf16[384,384]{1,0:T(8,128)(2,1)S(1)} %get-tuple-element.144), channel_id=1, source_target_pairs={{0,16},{8,24},{16,0},{24,8},{1,17},{9,25},{17,1},{25,9},{2,18},{10... | collective-permute-start | bytes 884744 | tf_op jit(solution)/shard_map/ppermute | solution.py:201
  71.5 23.7 %collective-permute-start = (bf16[384,384]{1,0:T(8,128)(2,1)S(1)}, bf16[384,384]{1,0:T(8,128)(2,1)S(1)}, u32[]{:S(2)}, u32[]{:S(2)}) collective-permute-start(bf16[384,384]{1,0:T(8,128)(2,1)S(1)} %get-tuple-element.145), channel_id=1, source_target_pairs={{0,8},{8,0},{16,24},{24,16},{1,9},{9,1},{17,25},{25,17},{2,10},{10... | collective-permute-start | bytes 884744 | tf_op jit(solution)/shard_map/ppermute | solution.py:201
  72.2 71.7 %collective-permute-start.17 = (bf16[4,656,256]{2,1,0:T(8,128)(2,1)S(1)}, bf16[4,656,256]{2,1,0:T(8,128)(2,1)S(1)}, u32[]{:S(2)}, u32[]{:S(2)}) collective-permute-start(bf16[4,656,256]{2,1,0:T(8,128)(2,1)S(1)} %pad_maximum_fusion.7), channel_id=1, source_target_pairs={{0,4},{2,6},{4,0},{6,2},{1,5},{3,7},{5,1},{7,3},{8,12},{10,14},{12... | collective-permute-start | bytes 4030472 | tf_op jit(solution)/shard_map/ppermute | solution.py:201
  81.9 27.9 %collective-permute-start.10 = (bf16[384,384]{1,0:T(8,128)(2,1)S(1)}, bf16[384,384]{1,0:T(8,128)(2,1)S(1)}, u32[]{:S(2)}, u32[]{:S(2)}) collective-permute-start(bf16[384,384]{1,0:T(8,128)(2,1)S(1)} %get-tuple-element.140), channel_id=1, source_target_pairs={{0,8},{8,0},{16,24},{24,16},{1,9},{9,1},{17,25},{25,17},{2,10},{10... | collective-permute-start | bytes 884744 | tf_op jit(solution)/shard_map/ppermute | solution.py:201
  83.6 27.4 %collective-permute-start.11 = (bf16[384,384]{1,0:T(8,128)(2,1)S(1)}, bf16[384,384]{1,0:T(8,128)(2,1)S(1)}, u32[]{:S(2)}, u32[]{:S(2)}) collective-permute-start(bf16[384,384]{1,0:T(8,128)(2,1)S(1)} %get-tuple-element.139), channel_id=1, source_target_pairs={{0,16},{8,24},{16,0},{24,8},{1,17},{9,25},{17,1},{25,9},{2,18},{10... | collective-permute-start | bytes 884744 | tf_op jit(solution)/shard_map/ppermute | solution.py:201
  91.4 24.5 %collective-permute-start.12 = (bf16[384,384]{1,0:T(8,128)(2,1)S(1)}, bf16[384,384]{1,0:T(8,128)(2,1)S(1)}, u32[]{:S(2)}, u32[]{:S(2)}) collective-permute-start(bf16[384,384]{1,0:T(8,128)(2,1)S(1)} %get-tuple-element.138), channel_id=1, source_target_pairs={{0,24},{8,16},{16,8},{24,0},{1,25},{9,17},{17,9},{25,1},{2,26},{10... | collective-permute-start | bytes 884744 | tf_op jit(solution)/shard_map/ppermute | solution.py:201
  108.3 18.9 %collective-permute-start.3 = (bf16[384,128]{1,0:T(8,128)(2,1)S(1)}, bf16[384,128]{1,0:T(8,128)(2,1)}, u32[]{:S(2)}, u32[]{:S(2)}) collective-permute-start(bf16[384,128]{1,0:T(8,128)(2,1)S(1)} %get-tuple-element.176), channel_id=1, source_target_pairs={{0,8},{8,0},{16,24},{24,16},{1,9},{9,1},{17,25},{25,17},{2,10},{10... | collective-permute-start | bytes 294920 | tf_op jit(solution)/shard_map/ppermute | solution.py:201
  109.8 17.4 %collective-permute-start.4 = (bf16[384,128]{1,0:T(8,128)(2,1)S(1)}, bf16[384,128]{1,0:T(8,128)(2,1)}, u32[]{:S(2)}, u32[]{:S(2)}) collective-permute-start(bf16[384,128]{1,0:T(8,128)(2,1)S(1)} %get-tuple-element.175), channel_id=1, source_target_pairs={{0,16},{8,24},{16,0},{24,8},{1,17},{9,25},{17,1},{25,9},{2,18},{10... | collective-permute-start | bytes 294920 | tf_op jit(solution)/shard_map/ppermute | solution.py:201
  111.0 16.2 %collective-permute-start.5 = (bf16[384,128]{1,0:T(8,128)(2,1)S(1)}, bf16[384,128]{1,0:T(8,128)(2,1)}, u32[]{:S(2)}, u32[]{:S(2)}) collective-permute-start(bf16[384,128]{1,0:T(8,128)(2,1)S(1)} %get-tuple-element.174), channel_id=1, source_target_pairs={{0,24},{8,16},{16,8},{24,0},{1,25},{9,17},{17,9},{25,1},{2,26},{10... | collective-permute-start | bytes 294920 | tf_op jit(solution)/shard_map/ppermute | solution.py:201
  131.1 10.1 %collective-permute-start.15 = (bf16[384,128]{1,0:T(8,128)(2,1)}, bf16[384,128]{1,0:T(8,128)(2,1)}, u32[]{:S(2)}, u32[]{:S(2)}) collective-permute-start(bf16[384,128]{1,0:T(8,128)(2,1)} %get-tuple-element.170), channel_id=1, source_target_pairs={{0,24},{8,16},{16,8},{24,0},{1,25},{9,17},{17,9},{25,1},{2,26},{10... | collective-permute-start | bytes 294920 | tf_op jit(solution)/shard_map/ppermute | solution.py:201
  208.3 37.4 %collective-permute-start.22 = (bf16[1024,2688]{1,0:T(8,128)(2,1)}, bf16[1024,2688]{1,0:T(8,128)(2,1)}, u32[]{:S(2)}, u32[]{:S(2)}) collective-permute-start(bf16[1024,2688]{1,0:T(8,128)(2,1)} %convolution_convert_fusion.refs_3_), channel_id=1, source_target_pairs={{0,1},{1,0},{2,3},{3,2},{4,5},{5,4},{6,7},{7,6},{8,9},{9,8},{10,11... | collective-permute-start | bytes 16515080 | tf_op jit(solution)/shard_map/ppermute | solution.py:201
  226.9 15.8 %collective-permute-start.23 = (bf16[1024,512]{1,0:T(8,128)(2,1)}, bf16[1024,512]{1,0:T(8,128)(2,1)}, u32[]{:S(2)}, u32[]{:S(2)}) collective-permute-start(bf16[1024,512]{1,0:T(8,128)(2,1)} %convolution_convert_fusion.4), channel_id=1, source_target_pairs={{0,1},{1,0},{2,3},{3,2},{4,5},{5,4},{6,7},{7,6},{8,9},{9,8},{10,11... | collective-permute-start | bytes 3145736 | tf_op jit(solution)/shard_map/ppermute | solution.py:201
  229.4 11.0 %collective-permute-start.20 = (bf16[384,256]{1,0:T(8,128)(2,1)}, bf16[384,256]{1,0:T(8,128)(2,1)}, u32[]{:S(2)}, u32[]{:S(2)}) collective-permute-start(bf16[384,256]{1,0:T(8,128)(2,1)} %get-tuple-element.160), channel_id=1, source_target_pairs={{0,16},{8,24},{16,0},{24,8},{1,17},{9,25},{17,1},{25,9},{2,18},{10... | collective-permute-start | bytes 589832 | tf_op jit(solution)/shard_map/ppermute | solution.py:201
  261.6 53.0 %collective-permute-start.28 = (bf16[2,128,3200]{2,1,0:T(8,128)(2,1)}, bf16[2,128,3200]{2,1,0:T(8,128)(2,1)}, u32[]{:S(2)}, u32[]{:S(2)}) collective-permute-start(bf16[2,128,3200]{2,1,0:T(8,128)(2,1)} %get-tuple-element.107), channel_id=1, source_target_pairs={{0,8},{8,0},{16,24},{24,16},{1,9},{9,1},{17,25},{25,17},{2,10},{10... | collective-permute-start | bytes 4915208 | tf_op jit(solution)/shard_map/ppermute | solution.py:201
  273.7 46.0 %collective-permute-start.27 = (bf16[2,128,3200]{2,1,0:T(8,128)(2,1)S(1)}, bf16[2,128,3200]{2,1,0:T(8,128)(2,1)S(1)}, u32[]{:S(2)}, u32[]{:S(2)}) collective-permute-start(bf16[2,128,3200]{2,1,0:T(8,128)(2,1)S(1)} %get-tuple-element.109), channel_id=1, source_target_pairs={{0,16},{8,24},{16,0},{24,8},{1,17},{9,25},{17,1},{25,9},{2,18},{10... | collective-permute-start | bytes 4915208 | tf_op jit(solution)/shard_map/ppermute | solution.py:201
  294.2 69.1 %collective-permute-start.24 = (bf16[384,384]{1,0:T(8,128)(2,1)}, bf16[384,384]{1,0:T(8,128)(2,1)}, u32[]{:S(2)}, u32[]{:S(2)}) collective-permute-start(bf16[384,384]{1,0:T(8,128)(2,1)} %get-tuple-element.136), channel_id=1, source_target_pairs={{0,8},{8,0},{16,24},{24,16},{1,9},{9,1},{17,25},{25,17},{2,10},{10... | collective-permute-start | bytes 884744 | tf_op jit(solution)/shard_map/ppermute | solution.py:201
  294.9 68.4 %collective-permute-start.25 = (bf16[384,384]{1,0:T(8,128)(2,1)}, bf16[384,384]{1,0:T(8,128)(2,1)}, u32[]{:S(2)}, u32[]{:S(2)}) collective-permute-start(bf16[384,384]{1,0:T(8,128)(2,1)} %get-tuple-element.135), channel_id=1, source_target_pairs={{0,16},{8,24},{16,0},{24,8},{1,17},{9,25},{17,1},{25,9},{2,18},{10... | collective-permute-start | bytes 884744 | tf_op jit(solution)/shard_map/ppermute | solution.py:201
  296.3 67.0 %collective-permute-start.26 = (bf16[384,384]{1,0:T(8,128)(2,1)}, bf16[384,384]{1,0:T(8,128)(2,1)}, u32[]{:S(2)}, u32[]{:S(2)}) collective-permute-start(bf16[384,384]{1,0:T(8,128)(2,1)} %get-tuple-element.134), channel_id=1, source_target_pairs={{0,24},{8,16},{16,8},{24,0},{1,25},{9,17},{17,9},{25,1},{2,26},{10... | collective-permute-start | bytes 884744 | tf_op jit(solution)/shard_map/ppermute | solution.py:201
  316.6 31.9 %collective-permute-start.30 = (bf16[128,3200]{1,0:T(8,128)(2,1)S(1)}, bf16[128,3200]{1,0:T(8,128)(2,1)S(1)}, u32[]{:S(2)}, u32[]{:S(2)}) collective-permute-start(bf16[128,3200]{1,0:T(8,128)(2,1)S(1)} %get-tuple-element.121), channel_id=1, source_target_pairs={{0,16},{8,24},{16,0},{24,8},{1,17},{9,25},{17,1},{25,9},{2,18},{10... | collective-permute-start | bytes 2457608 | tf_op jit(solution)/shard_map/ppermute | solution.py:201
  338.6 17.8 %collective-permute-start.29 = (bf16[128,3200]{1,0:T(8,128)(2,1)S(1)}, bf16[128,3200]{1,0:T(8,128)(2,1)S(1)}, u32[]{:S(2)}, u32[]{:S(2)}) collective-permute-start(bf16[128,3200]{1,0:T(8,128)(2,1)S(1)} %get-tuple-element.119), channel_id=1, source_target_pairs={{0,8},{8,0},{16,24},{24,16},{1,9},{9,1},{17,25},{25,17},{2,10},{10... | collective-permute-start | bytes 2457608 | tf_op jit(solution)/shard_map/ppermute | solution.py:201
  358.8 43.9 %collective-permute-start.47 = (bf16[128,3200]{1,0:T(8,128)(2,1)}, bf16[128,3200]{1,0:T(8,128)(2,1)S(1)}, u32[]{:S(2)}, u32[]{:S(2)}) collective-permute-start(bf16[128,3200]{1,0:T(8,128)(2,1)} %get-tuple-element.117), channel_id=1, source_target_pairs={{0,2},{2,0},{4,6},{6,4},{1,3},{3,1},{5,7},{7,5},{8,10},{10,8},{12,... | collective-permute-start | bytes 2457608 | tf_op jit(solution)/shard_map/ppermute | solution.py:201
  361.4 21.6 %collective-permute-start.32 = (bf16[328,512]{1,0:T(8,128)(2,1)S(1)}, bf16[328,512]{1,0:T(8,128)(2,1)S(1)}, u32[]{:S(2)}, u32[]{:S(2)}) collective-permute-start(bf16[328,512]{1,0:T(8,128)(2,1)S(1)} %get-tuple-element.165), channel_id=1, source_target_pairs={{0,2},{2,0},{4,6},{6,4},{1,3},{3,1},{5,7},{7,5},{8,10},{10,8},{12,... | collective-permute-start | bytes 1007624 | tf_op jit(solution)/shard_map/ppermute | solution.py:201
  383.9 11.7 %collective-permute-start.33 = (bf16[384,384]{1,0:T(8,128)(2,1)S(1)}, bf16[384,384]{1,0:T(8,128)(2,1)S(1)}, u32[]{:S(2)}, u32[]{:S(2)}) collective-permute-start(bf16[384,384]{1,0:T(8,128)(2,1)S(1)} %get-tuple-element.132), channel_id=1, source_target_pairs={{0,8},{8,0},{16,24},{24,16},{1,9},{9,1},{17,25},{25,17},{2,10},{10... | collective-permute-start | bytes 884744 | tf_op jit(solution)/shard_map/ppermute | solution.py:201
  385.4 11.5 %collective-permute-start.34 = (bf16[384,384]{1,0:T(8,128)(2,1)S(1)}, bf16[384,384]{1,0:T(8,128)(2,1)S(1)}, u32[]{:S(2)}, u32[]{:S(2)}) collective-permute-start(bf16[384,384]{1,0:T(8,128)(2,1)S(1)} %get-tuple-element.131), channel_id=1, source_target_pairs={{0,16},{8,24},{16,0},{24,8},{1,17},{9,25},{17,1},{25,9},{2,18},{10... | collective-permute-start | bytes 884744 | tf_op jit(solution)/shard_map/ppermute | solution.py:201
  386.7 10.1 %collective-permute-start.35 = (bf16[384,384]{1,0:T(8,128)(2,1)S(1)}, bf16[384,384]{1,0:T(8,128)(2,1)S(1)}, u32[]{:S(2)}, u32[]{:S(2)}) collective-permute-start(bf16[384,384]{1,0:T(8,128)(2,1)S(1)} %get-tuple-element.130), channel_id=1, source_target_pairs={{0,24},{8,16},{16,8},{24,0},{1,25},{9,17},{17,9},{25,1},{2,26},{10... | collective-permute-start | bytes 884744 | tf_op jit(solution)/shard_map/ppermute | solution.py:201
  395.6 29.1 %collective-permute-start.52 = (bf16[328,256]{1,0:T(8,128)(2,1)S(1)}, bf16[328,256]{1,0:T(8,128)(2,1)S(1)}, u32[]{:S(2)}, u32[]{:S(2)}) collective-permute-start(bf16[328,256]{1,0:T(8,128)(2,1)S(1)} %add_convert_fusion.20.refs_5_), channel_id=1, source_target_pairs={{0,4},{2,6},{4,0},{6,2},{1,5},{3,7},{5,1},{7,3},{8,12},{10,14},{12... | collective-permute-start | bytes 503816 | tf_op jit(solution)/shard_map/ppermute | solution.py:201
  402.9 21.6 %collective-permute-start.48 = (bf16[64,3200]{1,0:T(8,128)(2,1)S(1)}, bf16[64,3200]{1,0:T(8,128)(2,1)S(1)}, u32[]{:S(2)}, u32[]{:S(2)}) collective-permute-start(bf16[64,3200]{1,0:T(8,128)(2,1)S(1)} %get-tuple-element.149), channel_id=1, source_target_pairs={{0,4},{2,6},{4,0},{6,2},{1,5},{3,7},{5,1},{7,3},{8,12},{10,14},{12... | collective-permute-start | bytes 1228808 | tf_op jit(solution)/shard_map/ppermute | solution.py:201
  413.1 19.7 %collective-permute-start.38 = (bf16[2,128,1536]{2,1,0:T(8,128)(2,1)S(1)}, bf16[2,128,1536]{2,1,0:T(8,128)(2,1)S(1)}, u32[]{:S(2)}, u32[]{:S(2)}) collective-permute-start(bf16[2,128,1536]{2,1,0:T(8,128)(2,1)S(1)} %get-tuple-element.125), channel_id=1, source_target_pairs={{0,16},{8,24},{16,0},{24,8},{1,17},{9,25},{17,1},{25,9},{2,18},{10... | collective-permute-start | bytes 2359304 | tf_op jit(solution)/shard_map/ppermute | solution.py:201
  414.5 19.5 %collective-permute-start.40 = (bf16[2,128,1536]{2,1,0:T(8,128)(2,1)S(1)}, bf16[2,128,1536]{2,1,0:T(8,128)(2,1)S(1)}, u32[]{:S(2)}, u32[]{:S(2)}) collective-permute-start(bf16[2,128,1536]{2,1,0:T(8,128)(2,1)S(1)} %get-tuple-element.123), channel_id=1, source_target_pairs={{0,8},{8,0},{16,24},{24,16},{1,9},{9,1},{17,25},{25,17},{2,10},{10... | collective-permute-start | bytes 2359304 | tf_op jit(solution)/shard_map/ppermute | solution.py:201
  424.6 20.9 %collective-permute-start.49 = (bf16[64,3200]{1,0:T(8,128)(2,1)S(1)}, bf16[64,3200]{1,0:T(8,128)(2,1)S(1)}, u32[]{:S(2)}, u32[]{:S(2)}) collective-permute-start(bf16[64,3200]{1,0:T(8,128)(2,1)S(1)} %add_convert_fusion.14), channel_id=1, source_target_pairs={{0,4},{2,6},{4,0},{6,2},{1,5},{3,7},{5,1},{7,3},{8,12},{10,14},{12... | collective-permute-start | bytes 1228808 | tf_op jit(solution)/shard_map/ppermute | solution.py:201
  426.4 22.4 %collective-permute-start.53 = (bf16[328,512]{1,0:T(8,128)(2,1)S(1)}, bf16[328,512]{1,0:T(8,128)(2,1)S(1)}, u32[]{:S(2)}, u32[]{:S(2)}) collective-permute-start(bf16[328,512]{1,0:T(8,128)(2,1)S(1)} %pad_maximum_fusion.18), channel_id=1, source_target_pairs={{0,2},{2,0},{4,6},{6,4},{1,3},{3,1},{5,7},{7,5},{8,10},{10,8},{12,... | collective-permute-start | bytes 1007624 | tf_op jit(solution)/shard_map/ppermute | solution.py:201
  433.1 12.6 %collective-permute-start.39 = (bf16[128,1536]{1,0:T(8,128)(2,1)S(1)}, bf16[128,1536]{1,0:T(8,128)(2,1)S(1)}, u32[]{:S(2)}, u32[]{:S(2)}) collective-permute-start(bf16[128,1536]{1,0:T(8,128)(2,1)S(1)} %get-tuple-element.157), channel_id=1, source_target_pairs={{0,8},{8,0},{16,24},{24,16},{1,9},{9,1},{17,25},{25,17},{2,10},{10... | collective-permute-start | bytes 1179656 | tf_op jit(solution)/shard_map/ppermute | solution.py:201
  434.3 11.5 %collective-permute-start.41 = (bf16[128,1536]{1,0:T(8,128)(2,1)S(1)}, bf16[128,1536]{1,0:T(8,128)(2,1)S(1)}, u32[]{:S(2)}, u32[]{:S(2)}) collective-permute-start(bf16[128,1536]{1,0:T(8,128)(2,1)S(1)} %get-tuple-element.155), channel_id=1, source_target_pairs={{0,16},{8,24},{16,0},{24,8},{1,17},{9,25},{17,1},{25,9},{2,18},{10... | collective-permute-start | bytes 1179656 | tf_op jit(solution)/shard_map/ppermute | solution.py:201
  446.6 14.2 %collective-permute-start.42 = (bf16[128,1536]{1,0:T(8,128)(2,1)S(1)}, bf16[128,1536]{1,0:T(8,128)(2,1)S(1)}, u32[]{:S(2)}, u32[]{:S(2)}) collective-permute-start(bf16[128,1536]{1,0:T(8,128)(2,1)S(1)} %get-tuple-element.153), channel_id=1, source_target_pairs={{0,2},{2,0},{4,6},{6,4},{1,3},{3,1},{5,7},{7,5},{8,10},{10,8},{12,... | collective-permute-start | bytes 1179656 | tf_op jit(solution)/shard_map/ppermute | solution.py:201
  446.8 31.6 %collective-permute-start.50 = (bf16[128,3200]{1,0:T(8,128)(2,1)S(1)}, bf16[128,3200]{1,0:T(8,128)(2,1)S(1)}, u32[]{:S(2)}, u32[]{:S(2)}) collective-permute-start(bf16[128,3200]{1,0:T(8,128)(2,1)S(1)} %pad_maximum_fusion.12), channel_id=1, source_target_pairs={{0,2},{2,0},{4,6},{6,4},{1,3},{3,1},{5,7},{7,5},{8,10},{10,8},{12,... | collective-permute-start | bytes 2457608 | tf_op jit(solution)/shard_map/ppermute | solution.py:201
  449.0 12.1 %collective-permute-start.54 = (bf16[328,1024]{1,0:T(8,128)(2,1)S(1)}, bf16[328,1024]{1,0:T(8,128)(2,1)S(1)}, u32[]{:S(2)}, u32[]{:S(2)}) collective-permute-start(bf16[328,1024]{1,0:T(8,128)(2,1)S(1)} %pad_maximum_fusion.16), channel_id=1, source_target_pairs={{0,1},{1,0},{2,3},{3,2},{4,5},{5,4},{6,7},{7,6},{8,9},{9,8},{10,11... | collective-permute-start | bytes 2015240 | tf_op jit(solution)/shard_map/ppermute | solution.py:201
  461.0 17.6 %collective-permute-start.43 = (bf16[64,1536]{1,0:T(8,128)(2,1)S(1)}, bf16[64,1536]{1,0:T(8,128)(2,1)S(1)}, u32[]{:S(2)}, u32[]{:S(2)}) collective-permute-start(bf16[64,1536]{1,0:T(8,128)(2,1)S(1)} %get-tuple-element.169), channel_id=1, source_target_pairs={{0,4},{2,6},{4,0},{6,2},{1,5},{3,7},{5,1},{7,3},{8,12},{10,14},{12... | collective-permute-start | bytes 589832 | tf_op jit(solution)/shard_map/ppermute | solution.py:201
  478.6 10.0 %collective-permute-start.44 = (bf16[64,1536]{1,0:T(8,128)(2,1)S(1)}, bf16[64,1536]{1,0:T(8,128)(2,1)S(1)}, u32[]{:S(2)}, u32[]{:S(2)}) collective-permute-start(bf16[64,1536]{1,0:T(8,128)(2,1)S(1)} %add_convert_fusion.19), channel_id=1, source_target_pairs={{0,4},{2,6},{4,0},{6,2},{1,5},{3,7},{5,1},{7,3},{8,12},{10,14},{12... | collective-permute-start | bytes 589832 | tf_op jit(solution)/shard_map/ppermute | solution.py:201
  479.8 19.3 %collective-permute-start.51 = (bf16[256,3200]{1,0:T(8,128)(2,1)S(1)}, bf16[256,3200]{1,0:T(8,128)(2,1)S(1)}, u32[]{:S(2)}, u32[]{:S(2)}) collective-permute-start(bf16[256,3200]{1,0:T(8,128)(2,1)S(1)} %pad_maximum_fusion.5), channel_id=1, source_target_pairs={{0,1},{1,0},{2,3},{3,2},{4,5},{5,4},{6,7},{7,6},{8,9},{9,8},{10,11... | collective-permute-start | bytes 4915208 | tf_op jit(solution)/shard_map/ppermute | solution.py:201
  488.7 10.2 %collective-permute-start.45 = (bf16[128,1536]{1,0:T(8,128)(2,1)S(1)}, bf16[128,1536]{1,0:T(8,128)(2,1)S(1)}, u32[]{:S(2)}, u32[]{:S(2)}) collective-permute-start(bf16[128,1536]{1,0:T(8,128)(2,1)S(1)} %pad_maximum_fusion.17), channel_id=1, source_target_pairs={{0,2},{2,0},{4,6},{6,4},{1,3},{3,1},{5,7},{7,5},{8,10},{10,8},{12,... | collective-permute-start | bytes 1179656 | tf_op jit(solution)/shard_map/ppermute | solution.py:201
  499.1 18.3 %collective-permute-start.46 = (bf16[256,1536]{1,0:T(8,128)(2,1)S(1)}, bf16[256,1536]{1,0:T(8,128)(2,1)S(1)}, u32[]{:S(2)}, u32[]{:S(2)}) collective-permute-start(bf16[256,1536]{1,0:T(8,128)(2,1)S(1)} %pad_maximum_fusion.14.refs_1_), channel_id=1, source_target_pairs={{0,1},{1,0},{2,3},{3,2},{4,5},{5,4},{6,7},{7,6},{8,9},{9,8},{10,11... | collective-permute-start | bytes 2359304 | tf_op jit(solution)/shard_map/ppermute | solution.py:201
  (83 other events, 852.4 us)
Sparse Core Ops, SparseCore 0:
  10.5 50.8 all-gather.3
  63.8 101.3 all-gather.5
  232.2 72.3 reduce-scatter.1

commit v8 on v7

--- a/solution.py
+++ b/solution.py
@@ -1,4 +1,5 @@
 import functools
+import math
 
 import jax
 import jax.numpy as jnp
@@ -562,10 +563,6 @@
 def spread_halves(array):
     spare = ((0, 0), (0, FF_WIDE - FF))
     return jnp.concatenate([jnp.pad(array[:, :FF], spare), jnp.pad(array[:, FF:], spare)], axis=1)
-
-
-def gated(gate, upward):
-    return jax.nn.gelu(gate, approximate=False) * upward
 
 
 def adam_update(weight, mean, square, grad, rate):
@@ -619,7 +616,7 @@
     order = me ^ jnp.arange(group, dtype=jnp.int32)
     near_ids = all_ids.reshape(group, own_rows)[order].reshape(group_rows)
     where_at = positions(all_ids).reshape(group, own_rows)[order].reshape(group_rows)
-    cos, sin = pair_tables(where_at)
+    cos, sin = lax.optimization_barrier(pair_tables(where_at))
     query_side, key_side = slot_features(near_ids)
     live = (slot_ids[0] >= 0).astype(jnp.bfloat16)
     inputs = tokens[0].astype(jnp.float32)
@@ -655,15 +652,15 @@
     gate_up = product(second_normed, w_up)
     gate = gate_up[:, :FF]
     upward = gate_up[:, FF_WIDE : FF_WIDE + FF]
-    hidden = gated(gate, upward).astype(jnp.bfloat16)
-    result = middle + product(hidden, w_down)
+    below = 0.5 + 0.5 * lax.erf(gate * 0.5**0.5)
+    hidden = (gate * below * upward).astype(jnp.bfloat16)
     grad_top = cotangent[0] * live[:, None]
     grad_down = contract(hidden, grad_top).astype(jnp.bfloat16)
     grad_hidden = against(delayed(grad_top, grad_down), w_down)
-    _, gate_back = jax.vjp(gated, gate, upward)
-    grad_gate_up = spread_halves(jnp.concatenate(gate_back(grad_hidden), axis=1)).astype(
-        jnp.bfloat16
-    )
+    slope = below + gate * jnp.exp(-0.5 * gate * gate) * (2.0 * math.pi) ** -0.5
+    grad_gate_up = spread_halves(
+        jnp.concatenate([grad_hidden * upward * slope, grad_hidden * gate * below], axis=1)
+    ).astype(jnp.bfloat16)
     down_share = lax.psum_scatter(grad_down, both, scatter_dimension=0, tiled=True)
     up_theirs = core_theirs(second_normed, grad_gate_up, core)
     grad_gate_up, up_theirs = lax.optimization_barrier((grad_gate_up, up_theirs))
@@ -690,18 +687,16 @@
         )
         if pair == 0:
             up_halves = group_first(delayed(up_share, grad_near), group, grads)
-            grads_near = [grads, *up_halves]
-            down_share = delayed(down_share, grads)
+            grads_near = [grads, down_share, *up_halves]
+            result = middle + product(delayed(hidden, grads), w_down)
         if pair == pairs - 1:
             up_half = group_second(up_halves, group, grads)
-            down_stages = far_scatter(down_share, far, (grads, in_theirs), 1)
-            down_early, down_share = down_stages[min(1, len(down_stages) - 1)], down_stages[-1]
         if pair > 0:
-            grads = delayed(grads, (grads_here[0], down_early))
+            grads = delayed(grads, grads_here[0])
         grads_here.append(swap_heads(grads.reshape(group, own_rows, 3 * PAIR), group))
     grads_placed, grad_first = [], 0.0
     for pair in range(pairs):
-        after = (up_half,) if pair == 0 else (in_theirs[0], down_share)
+        after = (up_half,) if pair == 0 else (in_theirs[0],)
         placed = place(me_list, [grads_here[pair]], group, after)
         grads_placed.append(placed)
         in_theirs.append(core_theirs(first_normed, placed, core))
@@ -727,8 +722,10 @@
     wide = up_chunk.shape[1]
     total_out = jnp.concatenate([total_up[:, FF_WIDE:wide], total_up[:, wide + FF_WIDE :]], axis=1)
     total_up = jnp.concatenate([total_up[:, :FF], total_up[:, wide : wide + FF]], axis=1)
-    down_share = spread(down_share, far, (in_share, in_first), 1)
-    total_down = doubled(down_share, "core", 1, 2, 0, in_early).astype(jnp.float32)
+    down_share = delayed(down_share, in_theirs[0])
+    down_share = far_scatter(down_share, far, (in_theirs[-1], in_share), 1)[-1]
+    down_share = spread(down_share, far, (in_first, in_half), 1)
+    total_down = doubled(down_share, "core", 1, 2, 0, in_chunk).astype(jnp.float32)
     _, first_back = jax.vjp(lambda v: layer_norm(v, gain_one), inputs)
     (grad_inputs,) = first_back(grad_first)
     input_grad = (grad_middle + grad_inputs).astype(jnp.bfloat16)

time: 542 us -> 537 us (level)
  other arithmetic: 77.8 us -> 67.9 us
  waiting for transfers between devices: 174 us -> 181 us
    ppermute x55, waiting for transfers between devices: 166 us -> 176 us  [exchange(): return lax.ppermute(array, axis, [(i, i ^ mask) for i in range(size)])]
    convert_element_type x1, other arithmetic: 10.3 us -> 1.02 us  [local(): hidden = (gate * below * upward).astype(jnp.bfloat16)]
    unnamed x152 -> x134, local copies, waits for them, and re-layouts: 11.8 us -> 13.5 us
  transfers between devices with their start and end apart: 58 -> 58, of which waited for: 28 -> 26; matrix products, arithmetic and copies ran while one was open for 22% -> 22% of each run, Pallas kernels for 17% -> 17%
where the time goes in v8:
time: 537 us; the launch traced here: 533 us
  waiting for transfers between devices  181 us (34%)
  Pallas kernels  94.5 us (18%)
  other arithmetic  67.9 us (13%)
  starting transfers between devices  64.6 us (12%)
  matrix products  63.4 us (12%)
  local copies, waits for them, and re-layouts  36.6 us (7%)
  between operations  15.3 us (3%)
  blocking collectives  9.63 us (2%)
    ppermute x55, waiting for transfers between devices, exchange(): return lax.ppermute(array, axis, [(i, i ^ mask) for i in range(size)])  176 us
    ppermute x55, starting transfers between devices, exchange(): return lax.ppermute(array, axis, [(i, i ^ mask) for i in range(size)])  64.5 us
    pallas_call x2, Pallas kernels, attend_back(): pl.pallas_call(skipping(attend_back_kernel, 12, len(after)), grid=(rows /...  34.2 us
    dot_general x9, matrix products, contract(): lax.dot_general(left, right, (((0,), (0,)), ((), ())), preferred_element_...  29.4 us
    sub x5, other arithmetic, adam_update(): return (mean_new, square_new, weight - rate * (step_size + 0.01 * weight))  24.9 us
    pallas_call x2, Pallas kernels, attend(): pl.pallas_call(skipping(attend_kernel, 7, len(after)), grid=(rows // bloc...  20.5 us
    dot_general x4, matrix products, against(): lax.dot_general(left, right, (((1,), (1,)), ((), ())), preferred_element_...  19.9 us
    dot_general x3, matrix products, product(): return jnp.dot(left, right, preferred_element_type=jnp.float32)  14.1 us
  transfers between devices with their start and end apart: 58, of which 26 were waited for; matrix products, arithmetic and copies ran while one was open for 22% of the time, Pallas kernels for 17%

profile of v8, /device:TPU:0, one launch (start us, length us, event | category | flops | bytes accessed | tf_op | source)
XLA Modules:
  0.0 533.3 jit_solution(1800313078495222902)
XLA Ops:
  16.5 3.0 collective-permute-start.6
  21.1 9.6 %all-gather = bf16[4,1,896]{2,1,0:T(2,128)(2,1)S(1)} all-gather(bf16[1,1,896]{2,1,0:T(2,128)(2,1)S(1)} %maximum_bitcast_fusion.1), channel_id=1, replica_groups=mesh['grp'=4,'far'=4,'core'=2] {'grp'}, dimensions={0}, use_global_device_ids=true | all-gather | bytes 8960 | tf_op jit(solution)/shard_map/all_gather | solution.py:611
  33.8 4.6 fusion.57
  52.4 8.4 %collective-permute-done.16 = bf16[4,656,128]{2,1,0:T(8,128)(2,1)S(1)} collective-permute-done((bf16[4,656,128]{2,1,0:T(8,128)(2,1)S(1)}, bf16[4,656,128]{2,1,0:T(8,128)(2,1)S(1)}, u32[]{:S(2)}, u32[]{:S(2)}) %collective-permute-start.16) | collective-permute-done | bytes 671776 | tf_op jit(solution)/shard_map/ppermute | solution.py:202
  61.6 5.8 %project.2.refs_5_ = bf16[4,384,384]{2,1,0:T(8,128)(2,1)} custom-call(s32[1]{0:T(128)} %bitcast.1.refs_0_.me_ref, bf16[384,1024]{1,0:T(8,128)(2,1)} %fusion.42.refs_1_, bf16[1024,3072]{1,0:T(8,128)(2,1)} %all-gather.4.cloned.1.call-done.refs_2_, f32[4,384,128]{2,1,0:T(8,128)} %bitcast.159, f32[4,384,128]{2,1,0:T(8,128)} %bitcast.157), custom_call_target="tpu_custom_call" | custom-call | tf_op jit(solution)/shard_map/project/pallas_call | solution.py:127
  75.0 5.9 %project.3 = bf16[4,384,384]{2,1,0:T(8,128)(2,1)} custom-call(s32[1]{0:T(128)} %bitcast.1.refs_0_.me_ref, bf16[384,1024]{1,0:T(8,128)(2,1)} %fusion.42.refs_1_, bf16[1024,3072]{1,0:T(8,128)(2,1)} %all-gather.4.cloned.1.call-done.refs_2_, f32[4,384,128]{2,1,0:T(8,128)} %bitcast.160, f32[4,384,128]{2,1,0:T(8,128)} %bitcast.158, ...), custom_call_target="tpu_custom_call" | custom-call | tf_op jit(solution)/shard_map/project/pallas_call | solution.py:127
  85.4 6.2 %collective-permute-done.1 = bf16[384,384]{1,0:T(8,128)(2,1)S(1)} collective-permute-done((bf16[384,384]{1,0:T(8,128)(2,1)S(1)}, bf16[384,384]{1,0:T(8,128)(2,1)S(1)}, u32[]{:S(2)}, u32[]{:S(2)}) %collective-permute-start.1) | collective-permute-done | bytes 294944 | tf_op jit(solution)/shard_map/ppermute | solution.py:202
  96.0 10.3 %attend.2 = (bf16[1536,128]{1,0:T(8,128)(2,1)}, f32[1536,128]{1,0:T(8,128)}) custom-call(bf16[1536,384]{1,0:T(8,128)(2,1)} %pad_maximum_fusion.9.refs_0_.refs_1_.refs_2_.refs_5_, bf16[1536,384]{1,0:T(8,128)(2,1)} %pad_maximum_fusion.9.refs_0_.refs_1_.refs_2_.refs_5_, bf16[1536,384]{1,0:T(8,128)(2,1)} %pad_maximum_fusion.9.refs_0_.refs_1_.refs_2_.refs_5_, ...), custom_call_target="tpu_custom_call" | custom-call | tf_op jit(solution)/shard_map/attend/pallas_call | solution.py:328
  110.5 5.1 collective-permute-done.10
  119.4 10.2 %attend.3 = (bf16[1536,128]{1,0:T(8,128)(2,1)}, f32[1536,128]{1,0:T(8,128)}) custom-call(bf16[1536,384]{1,0:T(8,128)(2,1)} %copy-done, bf16[1536,384]{1,0:T(8,128)(2,1)} %copy-done, bf16[1536,384]{1,0:T(8,128)(2,1)} %copy-done, bf16[1536,128]{1,0:T(8,128)(2,1)} %get-tuple-element.191.refs_3_, bf16[1536,128]{1,0:T(8,128)(2,1)} %get-tuple-element.190.refs_4_.refs_6_, ...), custom_call_target="tpu_custom_call" | custom-call | tf_op jit(solution)/shard_map/attend/pallas_call | solution.py:328
  135.0 5.5 %collective-permute-done.15.refs_7_ = bf16[384,128]{1,0:T(8,128)(2,1)} collective-permute-done((bf16[384,128]{1,0:T(8,128)(2,1)}, bf16[384,128]{1,0:T(8,128)(2,1)}, u32[]{:S(2)}, u32[]{:S(2)}) %collective-permute-start.15) | collective-permute-done | bytes 98336 | tf_op jit(solution)/shard_map/ppermute | solution.py:202
  151.8 9.2 %assemble.1 = bf16[2624,1024]{1,0:T(8,128)(2,1)} custom-call(s32[2]{0:T(128)} %pad_add_fusion.me_ref, bf16[4,656,512]{2,1,0:T(8,128)(2,1)} %copy-done.10, bf16[4,656,512]{2,1,0:T(8,128)(2,1)} %collective-permute-done.18.other_ref), custom_call_target="tpu_custom_call" | custom-call | tf_op jit(solution)/shard_map/assemble/pallas_call | solution.py:238
  160.9 5.0 all-gather.6.cloned.1.call-done.refs_2_
  165.9 2.9 fusion.108
  169.1 7.8 %fusion.2 = f32[384,5376]{1,0:T(8,128)S(1)} fusion(bf16[1024,6400]{1,0:T(8,128)(2,1)} %all-gather.6.cloned.1.call-done.refs_2_, f32[384,1024]{1,0:T(8,128)S(1)} %get-tuple-element.197, f32[1024]{0:T(1024)S(1)} %bitcast.178, f32[384]{0:T(512)S(1)} %fusion.85, f32[384]{0:T(512)S(1)} %broadcast_multiply_fusion), kind=kOutput, calls=%fused_computation.5 | convolution fusion | flops 4229431296 | bytes 20847616 | tf_op jit(solution)/shard_map/dot_general | solution.py:451
  181.5 4.7 convolution_convert_fusion.1
  186.2 8.2 %fusion.12 = (bf16[384,2624]{1,0:T(8,128)(2,1)S(1)}, bf16[384,2624]{1,0:T(8,128)(2,1)S(1)}) fusion(f32[384,5376]{1,0:T(8,128)} %copy-done.12, bf16[384,1024]{1,0:T(8,128)(2,1)S(1)} %copy-done.41, bf16[2624,1024]{1,0:T(8,128)(2,1)} %assemble.1), kind=kOutput, calls=%fused_computation.33 | convolution fusion | flops 2077704192 | bytes 18251776 | tf_op jit(solution)/shard_map/dot_general | solution.py:461
  194.8 5.2 convolution_convert_fusion.refs_3_
  200.2 8.6 %multiply_reduce_fusion.1 = (f32[384]{0:T(512)S(1)}, f32[384,1024]{1,0:T(8,128)S(1)}) fusion(f32[384,1024]{1,0:T(8,128)S(1)} %get-tuple-element.197, f32[384]{0:T(512)S(1)} %broadcast_multiply_fusion, f32[1024]{0:T(1024)S(1)} %bitcast.180, bf16[384,5376]{1,0:T(8,128)(2,1)} %copy-done.21, bf16[1024,6400]{1,0:T(8,128)(2,1)} %all-gather.6.cloned.1.call-done.refs_2_), kind=kOutput, calls=%fused_computation.107 | convolution fusion | flops 4229430784 | bytes 18291712 | tf_op jit(solution)/shard_map/dot_general | solution.py:461
  211.8 4.8 row_product.1
  222.9 5.5 %collective-permute-done.21 = bf16[384,256]{1,0:T(8,128)(2,1)} collective-permute-done((bf16[384,256]{1,0:T(8,128)(2,1)}, bf16[384,256]{1,0:T(8,128)(2,1)}, u32[]{:S(2)}, u32[]{:S(2)}) %collective-permute-start.21) | collective-permute-done | bytes 196640 | tf_op jit(solution)/shard_map/ppermute | solution.py:202
  228.3 3.5 collective-permute-done.20
  234.2 3.2 add_convert_fusion.5
  237.4 7.0 %add_convert_fusion = bf16[1024,2688]{1,0:T(8,128)(2,1)} fusion(bf16[1024,2688]{1,0:T(8,128)(2,1)} %collective-permute-done.22, bf16[384,5376]{1,0:T(8,128)(2,1)S(1)} %copy-done.22, s32[]{:T(128)S(6)} %select_n.371, f32[384,1024]{1,0:T(8,128)S(1)} %get-tuple-element.197, f32[1024]{0:T(1024)S(1)} %bitcast.181, f32[384]{0:T(512)S(1)} %copy-done.49, ...), kind=kOutput, calls=%fused_computation.2 | convolution fusion | flops 2123759616 | bytes 14655492 | tf_op jit(solution)/shard_map/dot_general | solution.py:455
  244.5 4.3 pad_maximum_fusion.refs_12_
  253.6 17.0 %attend_back.2.refs_12_ = bf16[1536,384]{1,0:T(8,128)(2,1)} custom-call(bf16[1536,384]{1,0:T(8,128)(2,1)} %pad_maximum_fusion.9.refs_0_.refs_1_.refs_2_.refs_5_, bf16[1536,384]{1,0:T(8,128)(2,1)} %pad_maximum_fusion.9.refs_0_.refs_1_.refs_2_.refs_5_, bf16[1536,384]{1,0:T(8,128)(2,1)} %pad_maximum_fusion.9.refs_0_.refs_1_.refs_2_.refs_5_, ...), custom_call_target="tpu_custom_call" | custom-call | tf_op jit(solution)/shard_map/attend_back/pallas_call | solution.py:429
  276.5 28.8 %collective-permute-done.28 = bf16[2,128,3200]{2,1,0:T(8,128)(2,1)} collective-permute-done((bf16[2,128,3200]{2,1,0:T(8,128)(2,1)S(1)}, bf16[2,128,3200]{2,1,0:T(8,128)(2,1)}, u32[]{:S(2)}, u32[]{:S(2)}) %collective-permute-start.28) | collective-permute-done | bytes 1638432 | tf_op jit(solution)/shard_map/ppermute | solution.py:202
  310.1 13.2 %collective-permute-done.27 = bf16[2,128,3200]{2,1,0:T(8,128)(2,1)S(1)} collective-permute-done((bf16[2,128,3200]{2,1,0:T(8,128)(2,1)S(1)}, bf16[2,128,3200]{2,1,0:T(8,128)(2,1)S(1)}, u32[]{:S(2)}, u32[]{:S(2)}) %collective-permute-start.27) | collective-permute-done | bytes 1638432 | tf_op jit(solution)/shard_map/ppermute | solution.py:202
  326.2 17.2 %attend_back.3 = bf16[1536,384]{1,0:T(8,128)(2,1)} custom-call(bf16[1536,384]{1,0:T(8,128)(2,1)} %copy-done, bf16[1536,384]{1,0:T(8,128)(2,1)} %copy-done, bf16[1536,384]{1,0:T(8,128)(2,1)} %copy-done, bf16[1536,128]{1,0:T(8,128)(2,1)} %get-tuple-element.191.refs_3_, bf16[1536,128]{1,0:T(8,128)(2,1)} %get-tuple-element.190.refs_4_.refs_6_, ...), custom_call_target="tpu_custom_call" | custom-call | tf_op jit(solution)/shard_map/attend_back/pallas_call | solution.py:429
  357.2 2.8 place.4
  360.1 3.4 convolution_convert_fusion.3.refs_4_
  364.2 3.4 fusion.52
  367.6 3.2 place.5
  373.5 6.9 %collective-permute-done.50 = bf16[328,512]{1,0:T(8,128)(2,1)S(1)} collective-permute-done((bf16[328,512]{1,0:T(8,128)(2,1)S(1)}, bf16[328,512]{1,0:T(8,128)(2,1)S(1)}, u32[]{:S(2)}, u32[]{:S(2)}) %collective-permute-start.50) | collective-permute-done | bytes 335904 | tf_op jit(solution)/shard_map/ppermute | solution.py:202
  380.6 3.4 collective-permute-start.51
  387.9 9.5 %collective-permute-done.51 = bf16[328,256]{1,0:T(8,128)(2,1)S(1)} collective-permute-done((bf16[328,256]{1,0:T(8,128)(2,1)S(1)}, bf16[328,256]{1,0:T(8,128)(2,1)S(1)}, u32[]{:S(2)}, u32[]{:S(2)}) %collective-permute-start.51) | collective-permute-done | bytes 167968 | tf_op jit(solution)/shard_map/ppermute | solution.py:202
  403.6 5.9 %collective-permute-done.46 = bf16[64,3200]{1,0:T(8,128)(2,1)S(1)} collective-permute-done((bf16[64,3200]{1,0:T(8,128)(2,1)S(1)}, bf16[64,3200]{1,0:T(8,128)(2,1)S(1)}, u32[]{:S(2)}, u32[]{:S(2)}) %collective-permute-start.46) | collective-permute-done | bytes 409632 | tf_op jit(solution)/shard_map/ppermute | solution.py:202
  413.5 8.6 %collective-permute-start.53 = (bf16[328,512]{1,0:T(8,128)(2,1)S(1)}, bf16[328,512]{1,0:T(8,128)(2,1)S(1)}, u32[]{:S(2)}, u32[]{:S(2)}) collective-permute-start(bf16[328,512]{1,0:T(8,128)(2,1)S(1)} %pad_maximum_fusion.18), channel_id=1, source_target_pairs={{0,2},{2,0},{4,6},{6,4},{1,3},{3,1},{5,7},{7,5},{8,10},{10,8},{12,... | collective-permute-start | bytes 1007624 | tf_op jit(solution)/shard_map/ppermute | solution.py:202
  423.0 6.2 %collective-permute-done.47 = bf16[64,3200]{1,0:T(8,128)(2,1)S(1)} collective-permute-done((bf16[64,3200]{1,0:T(8,128)(2,1)S(1)}, bf16[64,3200]{1,0:T(8,128)(2,1)S(1)}, u32[]{:S(2)}, u32[]{:S(2)}) %collective-permute-start.47) | collective-permute-done | bytes 409632 | tf_op jit(solution)/shard_map/ppermute | solution.py:202
  432.5 3.9 collective-permute-done.53
  436.6 25.6 %collective-permute-done.40 = bf16[128,1536]{1,0:T(8,128)(2,1)S(1)} collective-permute-done((bf16[128,1536]{1,0:T(8,128)(2,1)S(1)}, bf16[128,1536]{1,0:T(8,128)(2,1)S(1)}, u32[]{:S(2)}, u32[]{:S(2)}) %collective-permute-start.40) | collective-permute-done | bytes 393248 | tf_op jit(solution)/shard_map/ppermute | solution.py:202
  463.1 10.8 %collective-permute-done.41 = bf16[64,1536]{1,0:T(8,128)(2,1)S(1)} collective-permute-done((bf16[64,1536]{1,0:T(8,128)(2,1)S(1)}, bf16[64,1536]{1,0:T(8,128)(2,1)S(1)}, u32[]{:S(2)}, u32[]{:S(2)}) %collective-permute-start.41) | collective-permute-done | bytes 196640 | tf_op jit(solution)/shard_map/ppermute | solution.py:202
  474.2 10.8 %collective-permute-done.42 = bf16[64,1536]{1,0:T(8,128)(2,1)S(1)} collective-permute-done((bf16[64,1536]{1,0:T(8,128)(2,1)S(1)}, bf16[64,1536]{1,0:T(8,128)(2,1)S(1)}, u32[]{:S(2)}, u32[]{:S(2)}) %collective-permute-start.42) | collective-permute-done | bytes 196640 | tf_op jit(solution)/shard_map/ppermute | solution.py:202
  485.2 4.2 multiply_subtract_fusion.2
  489.3 6.8 %collective-permute-done.43 = bf16[128,1536]{1,0:T(8,128)(2,1)S(1)} collective-permute-done((bf16[128,1536]{1,0:T(8,128)(2,1)S(1)}, bf16[128,1536]{1,0:T(8,128)(2,1)S(1)}, u32[]{:S(2)}, u32[]{:S(2)}) %collective-permute-start.43) | collective-permute-done | bytes 393248 | tf_op jit(solution)/shard_map/ppermute | solution.py:202
  499.2 11.2 %multiply_subtract_fusion = (f32[256,5248]{1,0:T(8,128)}, f32[256,5248]{1,0:T(8,128)}, f32[256,5248]{1,0:T(8,128)}, f32[256]{0:T(256)S(1)}) fusion(f32[256,5248]{1,0:T(8,128)S(1)} %bitcast.165, f32[256,2624]{1,0:T(8,128)S(1)} %get-tuple-element.107, f32[256,2624]{1,0:T(8,128)S(1)} %get-tuple-element.106, f32[256,5248]{1,0:T(8,128)} %param.28, ...), kind=kLoop, calls=%fused_computation.26 | loop fusion | flops 26869504 | bytes 37618688 | tf_op jit(solution)/shard_map/sub | solution.py:572
  515.4 2.9 merge.1
  519.3 6.6 %multiply_subtract_fusion.1 = (f32[256,3072]{1,0:T(8,128)}, f32[256,3072]{1,0:T(8,128)}, f32[256,3072]{1,0:T(8,128)}, f32[256]{0:T(256)S(1)}) fusion(f32[256,3072]{1,0:T(8,128)S(1)} %copy-done.9, bf16[256,3072]{1,0:T(8,128)(2,1)} %merge.1, f32[256,3072]{1,0:T(8,128)S(1)} %copy-done.28, f32[256,3072]{1,0:T(8,128)} %param.26), kind=kLoop, calls=%fused_computation.55 | loop fusion | flops 15728384 | bytes 20448256 | tf_op jit(solution)/shard_map/sub | solution.py:572
  (371 shorter events, 151.0 us)
Async XLA Ops:
  7.2 54.5 %all-gather.4.cloned.1.call-start = ((), (), s32[]{:S(2)}) async-start(), calls=%async_computation.1 | async-start | bytes 7077888 | tf_op jit(solution)/shard_map/all_gather | solution.py:606
  9.7 156.2 %all-gather.6.cloned.1.call-start = ((), (), s32[]{:S(2)}) async-start(), calls=%async_computation.2 | async-start | bytes 14745600 | tf_op jit(solution)/shard_map/all_gather | solution.py:472
  15.4 310.8 %reduce-scatter.2.cloned.1.call-start = ((), (), s32[]{:S(2)}) async-start(), calls=%async_computation.3 | async-start | bytes 6045696 | tf_op jit(solution)/shard_map/reduce_scatter | solution.py:664
  16.5 24.2 %collective-permute-start.6 = (bf16[656,128]{1,0:T(8,128)(2,1)S(1)}, bf16[656,128]{1,0:T(8,128)(2,1)S(1)}, u32[]{:S(2)}, u32[]{:S(2)}) collective-permute-start(bf16[656,128]{1,0:T(8,128)(2,1)S(1)} %dynamic-slice_convert_fusion), channel_id=1, source_target_pairs={{0,8},{8,0},{16,24},{24,16},{1,9},{9,1},{17,25},{25,17},{2,10},{10... | collective-permute-start | bytes 503816 | tf_op jit(solution)/shard_map/ppermute | solution.py:202
  19.5 22.6 %collective-permute-start.7 = (bf16[656,128]{1,0:T(8,128)(2,1)S(1)}, bf16[656,128]{1,0:T(8,128)(2,1)S(1)}, u32[]{:S(2)}, u32[]{:S(2)}) collective-permute-start(bf16[656,128]{1,0:T(8,128)(2,1)S(1)} %dynamic-slice_convert_fusion), channel_id=1, source_target_pairs={{0,16},{8,24},{16,0},{24,8},{1,17},{9,25},{17,1},{25,9},{2,18},{10... | collective-permute-start | bytes 503816 | tf_op jit(solution)/shard_map/ppermute | solution.py:202
  48.9 11.9 %collective-permute-start.16 = (bf16[4,656,128]{2,1,0:T(8,128)(2,1)S(1)}, bf16[4,656,128]{2,1,0:T(8,128)(2,1)S(1)}, u32[]{:S(2)}, u32[]{:S(2)}) collective-permute-start(bf16[4,656,128]{2,1,0:T(8,128)(2,1)S(1)} %pad_maximum_fusion.15.refs_6_), channel_id=1, source_target_pairs={{0,2},{2,0},{4,6},{6,4},{1,3},{3,1},{5,7},{7,5},{8,10},{10,8},{12,... | collective-permute-start | bytes 2015240 | tf_op jit(solution)/shard_map/ppermute | solution.py:202
  68.8 15.3 %collective-permute-start.2 = (bf16[384,384]{1,0:T(8,128)(2,1)S(1)}, bf16[384,384]{1,0:T(8,128)(2,1)S(1)}, u32[]{:S(2)}, u32[]{:S(2)}) collective-permute-start(bf16[384,384]{1,0:T(8,128)(2,1)S(1)} %get-tuple-element.149), channel_id=1, source_target_pairs={{0,24},{8,16},{16,8},{24,0},{1,25},{9,17},{17,9},{25,1},{2,26},{10... | collective-permute-start | bytes 884744 | tf_op jit(solution)/shard_map/ppermute | solution.py:202
  70.5 21.1 %collective-permute-start.1 = (bf16[384,384]{1,0:T(8,128)(2,1)S(1)}, bf16[384,384]{1,0:T(8,128)(2,1)S(1)}, u32[]{:S(2)}, u32[]{:S(2)}) collective-permute-start(bf16[384,384]{1,0:T(8,128)(2,1)S(1)} %get-tuple-element.150), channel_id=1, source_target_pairs={{0,16},{8,24},{16,0},{24,8},{1,17},{9,25},{17,1},{25,9},{2,18},{10... | collective-permute-start | bytes 884744 | tf_op jit(solution)/shard_map/ppermute | solution.py:202
  71.8 23.1 %collective-permute-start = (bf16[384,384]{1,0:T(8,128)(2,1)S(1)}, bf16[384,384]{1,0:T(8,128)(2,1)S(1)}, u32[]{:S(2)}, u32[]{:S(2)}) collective-permute-start(bf16[384,384]{1,0:T(8,128)(2,1)S(1)} %get-tuple-element.151), channel_id=1, source_target_pairs={{0,8},{8,0},{16,24},{24,16},{1,9},{9,1},{17,25},{25,17},{2,10},{10... | collective-permute-start | bytes 884744 | tf_op jit(solution)/shard_map/ppermute | solution.py:202
  72.5 73.3 %collective-permute-start.17 = (bf16[4,656,256]{2,1,0:T(8,128)(2,1)S(1)}, bf16[4,656,256]{2,1,0:T(8,128)(2,1)S(1)}, u32[]{:S(2)}, u32[]{:S(2)}) collective-permute-start(bf16[4,656,256]{2,1,0:T(8,128)(2,1)S(1)} %pad_maximum_fusion.7), channel_id=1, source_target_pairs={{0,4},{2,6},{4,0},{6,2},{1,5},{3,7},{5,1},{7,3},{8,12},{10,14},{12... | collective-permute-start | bytes 4030472 | tf_op jit(solution)/shard_map/ppermute | solution.py:202
  82.2 36.1 %collective-permute-start.12 = (bf16[384,384]{1,0:T(8,128)(2,1)S(1)}, bf16[384,384]{1,0:T(8,128)(2,1)S(1)}, u32[]{:S(2)}, u32[]{:S(2)}) collective-permute-start(bf16[384,384]{1,0:T(8,128)(2,1)S(1)} %get-tuple-element.144), channel_id=1, source_target_pairs={{0,24},{8,16},{16,8},{24,0},{1,25},{9,17},{17,9},{25,1},{2,26},{10... | collective-permute-start | bytes 884744 | tf_op jit(solution)/shard_map/ppermute | solution.py:202
  84.1 32.7 %collective-permute-start.11 = (bf16[384,384]{1,0:T(8,128)(2,1)S(1)}, bf16[384,384]{1,0:T(8,128)(2,1)S(1)}, u32[]{:S(2)}, u32[]{:S(2)}) collective-permute-start(bf16[384,384]{1,0:T(8,128)(2,1)S(1)} %get-tuple-element.145), channel_id=1, source_target_pairs={{0,16},{8,24},{16,0},{24,8},{1,17},{9,25},{17,1},{25,9},{2,18},{10... | collective-permute-start | bytes 884744 | tf_op jit(solution)/shard_map/ppermute | solution.py:202
  91.6 24.0 %collective-permute-start.10 = (bf16[384,384]{1,0:T(8,128)(2,1)S(1)}, bf16[384,384]{1,0:T(8,128)(2,1)S(1)}, u32[]{:S(2)}, u32[]{:S(2)}) collective-permute-start(bf16[384,384]{1,0:T(8,128)(2,1)S(1)} %get-tuple-element.146), channel_id=1, source_target_pairs={{0,8},{8,0},{16,24},{24,16},{1,9},{9,1},{17,25},{25,17},{2,10},{10... | collective-permute-start | bytes 884744 | tf_op jit(solution)/shard_map/ppermute | solution.py:202
  108.0 21.7 %collective-permute-start.5 = (bf16[384,128]{1,0:T(8,128)(2,1)S(1)}, bf16[384,128]{1,0:T(8,128)(2,1)}, u32[]{:S(2)}, u32[]{:S(2)}) collective-permute-start(bf16[384,128]{1,0:T(8,128)(2,1)S(1)} %get-tuple-element.180), channel_id=1, source_target_pairs={{0,24},{8,16},{16,8},{24,0},{1,25},{9,17},{17,9},{25,1},{2,26},{10... | collective-permute-start | bytes 294920 | tf_op jit(solution)/shard_map/ppermute | solution.py:202
  115.7 14.0 %collective-permute-start.4 = (bf16[384,128]{1,0:T(8,128)(2,1)S(1)}, bf16[384,128]{1,0:T(8,128)(2,1)}, u32[]{:S(2)}, u32[]{:S(2)}) collective-permute-start(bf16[384,128]{1,0:T(8,128)(2,1)S(1)} %get-tuple-element.181), channel_id=1, source_target_pairs={{0,16},{8,24},{16,0},{24,8},{1,17},{9,25},{17,1},{25,9},{2,18},{10... | collective-permute-start | bytes 294920 | tf_op jit(solution)/shard_map/ppermute | solution.py:202
  116.8 12.9 %collective-permute-start.3 = (bf16[384,128]{1,0:T(8,128)(2,1)S(1)}, bf16[384,128]{1,0:T(8,128)(2,1)}, u32[]{:S(2)}, u32[]{:S(2)}) collective-permute-start(bf16[384,128]{1,0:T(8,128)(2,1)S(1)} %get-tuple-element.182), channel_id=1, source_target_pairs={{0,8},{8,0},{16,24},{24,16},{1,9},{9,1},{17,25},{25,17},{2,10},{10... | collective-permute-start | bytes 294920 | tf_op jit(solution)/shard_map/ppermute | solution.py:202
  200.0 37.5 %collective-permute-start.22 = (bf16[1024,2688]{1,0:T(8,128)(2,1)}, bf16[1024,2688]{1,0:T(8,128)(2,1)}, u32[]{:S(2)}, u32[]{:S(2)}) collective-permute-start(bf16[1024,2688]{1,0:T(8,128)(2,1)} %convolution_convert_fusion.refs_3_), channel_id=1, source_target_pairs={{0,1},{1,0},{2,3},{3,2},{4,5},{5,4},{6,7},{7,6},{8,9},{9,8},{10,11... | collective-permute-start | bytes 16515080 | tf_op jit(solution)/shard_map/ppermute | solution.py:202
  218.3 15.9 %collective-permute-start.23 = (bf16[1024,512]{1,0:T(8,128)(2,1)}, bf16[1024,512]{1,0:T(8,128)(2,1)}, u32[]{:S(2)}, u32[]{:S(2)}) collective-permute-start(bf16[1024,512]{1,0:T(8,128)(2,1)} %convolution_convert_fusion.4), channel_id=1, source_target_pairs={{0,1},{1,0},{2,3},{3,2},{4,5},{5,4},{6,7},{7,6},{8,9},{9,8},{10,11... | collective-permute-start | bytes 3145736 | tf_op jit(solution)/shard_map/ppermute | solution.py:202
  220.8 11.1 %collective-permute-start.20 = (bf16[384,256]{1,0:T(8,128)(2,1)}, bf16[384,256]{1,0:T(8,128)(2,1)}, u32[]{:S(2)}, u32[]{:S(2)}) collective-permute-start(bf16[384,256]{1,0:T(8,128)(2,1)} %get-tuple-element.166), channel_id=1, source_target_pairs={{0,16},{8,24},{16,0},{24,8},{1,17},{9,25},{17,1},{25,9},{2,18},{10... | collective-permute-start | bytes 589832 | tf_op jit(solution)/shard_map/ppermute | solution.py:202
  252.7 52.6 %collective-permute-start.28 = (bf16[2,128,3200]{2,1,0:T(8,128)(2,1)S(1)}, bf16[2,128,3200]{2,1,0:T(8,128)(2,1)}, u32[]{:S(2)}, u32[]{:S(2)}) collective-permute-start(bf16[2,128,3200]{2,1,0:T(8,128)(2,1)S(1)} %get-tuple-element.113), channel_id=1, source_target_pairs={{0,8},{8,0},{16,24},{24,16},{1,9},{9,1},{17,25},{25,17},{2,10},{10... | collective-permute-start | bytes 4915208 | tf_op jit(solution)/shard_map/ppermute | solution.py:202
  271.0 52.3 %collective-permute-start.27 = (bf16[2,128,3200]{2,1,0:T(8,128)(2,1)S(1)}, bf16[2,128,3200]{2,1,0:T(8,128)(2,1)S(1)}, u32[]{:S(2)}, u32[]{:S(2)}) collective-permute-start(bf16[2,128,3200]{2,1,0:T(8,128)(2,1)S(1)} %get-tuple-element.115), channel_id=1, source_target_pairs={{0,16},{8,24},{16,0},{24,8},{1,17},{9,25},{17,1},{25,9},{2,18},{10... | collective-permute-start | bytes 4915208 | tf_op jit(solution)/shard_map/ppermute | solution.py:202
  273.0 70.4 %collective-permute-start.26 = (bf16[384,384]{1,0:T(8,128)(2,1)}, bf16[384,384]{1,0:T(8,128)(2,1)}, u32[]{:S(2)}, u32[]{:S(2)}) collective-permute-start(bf16[384,384]{1,0:T(8,128)(2,1)} %get-tuple-element.140), channel_id=1, source_target_pairs={{0,24},{8,16},{16,8},{24,0},{1,25},{9,17},{17,9},{25,1},{2,26},{10... | collective-permute-start | bytes 884744 | tf_op jit(solution)/shard_map/ppermute | solution.py:202
  274.7 68.7 %collective-permute-start.25 = (bf16[384,384]{1,0:T(8,128)(2,1)}, bf16[384,384]{1,0:T(8,128)(2,1)}, u32[]{:S(2)}, u32[]{:S(2)}) collective-permute-start(bf16[384,384]{1,0:T(8,128)(2,1)} %get-tuple-element.141), channel_id=1, source_target_pairs={{0,16},{8,24},{16,0},{24,8},{1,17},{9,25},{17,1},{25,9},{2,18},{10... | collective-permute-start | bytes 884744 | tf_op jit(solution)/shard_map/ppermute | solution.py:202
  275.6 67.8 %collective-permute-start.24 = (bf16[384,384]{1,0:T(8,128)(2,1)}, bf16[384,384]{1,0:T(8,128)(2,1)}, u32[]{:S(2)}, u32[]{:S(2)}) collective-permute-start(bf16[384,384]{1,0:T(8,128)(2,1)} %get-tuple-element.142), channel_id=1, source_target_pairs={{0,8},{8,0},{16,24},{24,16},{1,9},{9,1},{17,25},{25,17},{2,10},{10... | collective-permute-start | bytes 884744 | tf_op jit(solution)/shard_map/ppermute | solution.py:202
  308.6 40.7 %collective-permute-start.30 = (bf16[128,3200]{1,0:T(8,128)(2,1)}, bf16[128,3200]{1,0:T(8,128)(2,1)}, u32[]{:S(2)}, u32[]{:S(2)}) collective-permute-start(bf16[128,3200]{1,0:T(8,128)(2,1)} %get-tuple-element.127), channel_id=1, source_target_pairs={{0,16},{8,24},{16,0},{24,8},{1,17},{9,25},{17,1},{25,9},{2,18},{10... | collective-permute-start | bytes 2457608 | tf_op jit(solution)/shard_map/ppermute | solution.py:202
  325.1 25.8 %collective-permute-start.29 = (bf16[128,3200]{1,0:T(8,128)(2,1)}, bf16[128,3200]{1,0:T(8,128)(2,1)}, u32[]{:S(2)}, u32[]{:S(2)}) collective-permute-start(bf16[128,3200]{1,0:T(8,128)(2,1)} %get-tuple-element.125), channel_id=1, source_target_pairs={{0,8},{8,0},{16,24},{24,16},{1,9},{9,1},{17,25},{25,17},{2,10},{10... | collective-permute-start | bytes 2457608 | tf_op jit(solution)/shard_map/ppermute | solution.py:202
  345.8 21.8 %collective-permute-start.34 = (bf16[384,384]{1,0:T(8,128)(2,1)}, bf16[384,384]{1,0:T(8,128)(2,1)}, u32[]{:S(2)}, u32[]{:S(2)}) collective-permute-start(bf16[384,384]{1,0:T(8,128)(2,1)} %get-tuple-element.136), channel_id=1, source_target_pairs={{0,24},{8,16},{16,8},{24,0},{1,25},{9,17},{17,9},{25,1},{2,26},{10... | collective-permute-start | bytes 884744 | tf_op jit(solution)/shard_map/ppermute | solution.py:202
  346.6 21.0 %collective-permute-start.33 = (bf16[384,384]{1,0:T(8,128)(2,1)}, bf16[384,384]{1,0:T(8,128)(2,1)}, u32[]{:S(2)}, u32[]{:S(2)}) collective-permute-start(bf16[384,384]{1,0:T(8,128)(2,1)} %get-tuple-element.137), channel_id=1, source_target_pairs={{0,16},{8,24},{16,0},{24,8},{1,17},{9,25},{17,1},{25,9},{2,18},{10... | collective-permute-start | bytes 884744 | tf_op jit(solution)/shard_map/ppermute | solution.py:202
  348.2 19.4 %collective-permute-start.32 = (bf16[384,384]{1,0:T(8,128)(2,1)}, bf16[384,384]{1,0:T(8,128)(2,1)}, u32[]{:S(2)}, u32[]{:S(2)}) collective-permute-start(bf16[384,384]{1,0:T(8,128)(2,1)} %get-tuple-element.138), channel_id=1, source_target_pairs={{0,8},{8,0},{16,24},{24,16},{1,9},{9,1},{17,25},{25,17},{2,10},{10... | collective-permute-start | bytes 884744 | tf_op jit(solution)/shard_map/ppermute | solution.py:202
  355.8 28.2 %collective-permute-start.45 = (bf16[128,3200]{1,0:T(8,128)(2,1)}, bf16[128,3200]{1,0:T(8,128)(2,1)}, u32[]{:S(2)}, u32[]{:S(2)}) collective-permute-start(bf16[128,3200]{1,0:T(8,128)(2,1)} %get-tuple-element.123), channel_id=1, source_target_pairs={{0,2},{2,0},{4,6},{6,4},{1,3},{3,1},{5,7},{7,5},{8,10},{10,8},{12,... | collective-permute-start | bytes 2457608 | tf_op jit(solution)/shard_map/ppermute | solution.py:202
  363.5 16.9 %collective-permute-start.50 = (bf16[328,512]{1,0:T(8,128)(2,1)S(1)}, bf16[328,512]{1,0:T(8,128)(2,1)S(1)}, u32[]{:S(2)}, u32[]{:S(2)}) collective-permute-start(bf16[328,512]{1,0:T(8,128)(2,1)S(1)} %get-tuple-element.171), channel_id=1, source_target_pairs={{0,2},{2,0},{4,6},{6,4},{1,3},{3,1},{5,7},{7,5},{8,10},{10,8},{12,... | collective-permute-start | bytes 1007624 | tf_op jit(solution)/shard_map/ppermute | solution.py:202
  367.6 18.0 %collective-permute-start.31 = (bf16[1024,768]{1,0:T(8,128)(2,1)}, bf16[1024,768]{1,0:T(8,128)(2,1)S(1)}, u32[]{:S(2)}, u32[]{:S(2)}) collective-permute-start(bf16[1024,768]{1,0:T(8,128)(2,1)} %convolution_convert_fusion.3.refs_4_), channel_id=1, source_target_pairs={{0,1},{1,0},{2,3},{3,2},{4,5},{5,4},{6,7},{7,6},{8,9},{9,8},{10,11... | collective-permute-start | bytes 4718600 | tf_op jit(solution)/shard_map/ppermute | solution.py:202
  373.0 13.6 %collective-permute-start.35 = (bf16[1024,768]{1,0:T(8,128)(2,1)S(1)}, bf16[1024,768]{1,0:T(8,128)(2,1)S(1)}, u32[]{:S(2)}, u32[]{:S(2)}) collective-permute-start(bf16[1024,768]{1,0:T(8,128)(2,1)S(1)} %convolution_convert_fusion.2), channel_id=1, source_target_pairs={{0,1},{1,0},{2,3},{3,2},{4,5},{5,4},{6,7},{7,6},{8,9},{9,8},{10,11... | collective-permute-start | bytes 4718600 | tf_op jit(solution)/shard_map/ppermute | solution.py:202
  380.6 16.8 %collective-permute-start.51 = (bf16[328,256]{1,0:T(8,128)(2,1)S(1)}, bf16[328,256]{1,0:T(8,128)(2,1)S(1)}, u32[]{:S(2)}, u32[]{:S(2)}) collective-permute-start(bf16[328,256]{1,0:T(8,128)(2,1)S(1)} %get-tuple-element.187), channel_id=1, source_target_pairs={{0,4},{2,6},{4,0},{6,2},{1,5},{3,7},{5,1},{7,3},{8,12},{10,14},{12... | collective-permute-start | bytes 503816 | tf_op jit(solution)/shard_map/ppermute | solution.py:202
  385.4 24.1 %collective-permute-start.46 = (bf16[64,3200]{1,0:T(8,128)(2,1)S(1)}, bf16[64,3200]{1,0:T(8,128)(2,1)S(1)}, u32[]{:S(2)}, u32[]{:S(2)}) collective-permute-start(bf16[64,3200]{1,0:T(8,128)(2,1)S(1)} %get-tuple-element.155), channel_id=1, source_target_pairs={{0,4},{2,6},{4,0},{6,2},{1,5},{3,7},{5,1},{7,3},{8,12},{10,14},{12... | collective-permute-start | bytes 1228808 | tf_op jit(solution)/shard_map/ppermute | solution.py:202
  397.5 16.0 %collective-permute-start.52 = (bf16[328,256]{1,0:T(8,128)(2,1)S(1)}, bf16[328,256]{1,0:T(8,128)(2,1)S(1)}, u32[]{:S(2)}, u32[]{:S(2)}) collective-permute-start(bf16[328,256]{1,0:T(8,128)(2,1)S(1)} %add_convert_fusion.19), channel_id=1, source_target_pairs={{0,4},{2,6},{4,0},{6,2},{1,5},{3,7},{5,1},{7,3},{8,12},{10,14},{12... | collective-permute-start | bytes 503816 | tf_op jit(solution)/shard_map/ppermute | solution.py:202
  398.0 13.8 %collective-permute-start.38 = (bf16[2,128,1536]{2,1,0:T(8,128)(2,1)S(1)}, bf16[2,128,1536]{2,1,0:T(8,128)(2,1)S(1)}, u32[]{:S(2)}, u32[]{:S(2)}) collective-permute-start(bf16[2,128,1536]{2,1,0:T(8,128)(2,1)S(1)} %get-tuple-element.129), channel_id=1, source_target_pairs={{0,8},{8,0},{16,24},{24,16},{1,9},{9,1},{17,25},{25,17},{2,10},{10... | collective-permute-start | bytes 2359304 | tf_op jit(solution)/shard_map/ppermute | solution.py:202
  398.8 14.4 %collective-permute-start.36 = (bf16[2,128,1536]{2,1,0:T(8,128)(2,1)S(1)}, bf16[2,128,1536]{2,1,0:T(8,128)(2,1)S(1)}, u32[]{:S(2)}, u32[]{:S(2)}) collective-permute-start(bf16[2,128,1536]{2,1,0:T(8,128)(2,1)S(1)} %get-tuple-element.131), channel_id=1, source_target_pairs={{0,16},{8,24},{16,0},{24,8},{1,17},{9,25},{17,1},{25,9},{2,18},{10... | collective-permute-start | bytes 2359304 | tf_op jit(solution)/shard_map/ppermute | solution.py:202
  411.8 17.4 %collective-permute-start.47 = (bf16[64,3200]{1,0:T(8,128)(2,1)S(1)}, bf16[64,3200]{1,0:T(8,128)(2,1)S(1)}, u32[]{:S(2)}, u32[]{:S(2)}) collective-permute-start(bf16[64,3200]{1,0:T(8,128)(2,1)S(1)} %add_convert_fusion.13), channel_id=1, source_target_pairs={{0,4},{2,6},{4,0},{6,2},{1,5},{3,7},{5,1},{7,3},{8,12},{10,14},{12... | collective-permute-start | bytes 1228808 | tf_op jit(solution)/shard_map/ppermute | solution.py:202
  412.1 17.4 %collective-permute-start.39 = (bf16[128,1536]{1,0:T(8,128)(2,1)S(1)}, bf16[128,1536]{1,0:T(8,128)(2,1)S(1)}, u32[]{:S(2)}, u32[]{:S(2)}) collective-permute-start(bf16[128,1536]{1,0:T(8,128)(2,1)S(1)} %get-tuple-element.161), channel_id=1, source_target_pairs={{0,16},{8,24},{16,0},{24,8},{1,17},{9,25},{17,1},{25,9},{2,18},{10... | collective-permute-start | bytes 1179656 | tf_op jit(solution)/shard_map/ppermute | solution.py:202
  413.5 22.9 %collective-permute-start.53 = (bf16[328,512]{1,0:T(8,128)(2,1)S(1)}, bf16[328,512]{1,0:T(8,128)(2,1)S(1)}, u32[]{:S(2)}, u32[]{:S(2)}) collective-permute-start(bf16[328,512]{1,0:T(8,128)(2,1)S(1)} %pad_maximum_fusion.18), channel_id=1, source_target_pairs={{0,2},{2,0},{4,6},{6,4},{1,3},{3,1},{5,7},{7,5},{8,10},{10,8},{12,... | collective-permute-start | bytes 1007624 | tf_op jit(solution)/shard_map/ppermute | solution.py:202
  429.4 33.3 %collective-permute-start.48 = (bf16[128,3200]{1,0:T(8,128)(2,1)S(1)}, bf16[128,3200]{1,0:T(8,128)(2,1)S(1)}, u32[]{:S(2)}, u32[]{:S(2)}) collective-permute-start(bf16[128,3200]{1,0:T(8,128)(2,1)S(1)} %pad_maximum_fusion.12), channel_id=1, source_target_pairs={{0,2},{2,0},{4,6},{6,4},{1,3},{3,1},{5,7},{7,5},{8,10},{10,8},{12,... | collective-permute-start | bytes 2457608 | tf_op jit(solution)/shard_map/ppermute | solution.py:202
  431.9 30.3 %collective-permute-start.40 = (bf16[128,1536]{1,0:T(8,128)(2,1)S(1)}, bf16[128,1536]{1,0:T(8,128)(2,1)S(1)}, u32[]{:S(2)}, u32[]{:S(2)}) collective-permute-start(bf16[128,1536]{1,0:T(8,128)(2,1)S(1)} %get-tuple-element.159), channel_id=1, source_target_pairs={{0,2},{2,0},{4,6},{6,4},{1,3},{3,1},{5,7},{7,5},{8,10},{10,8},{12,... | collective-permute-start | bytes 1179656 | tf_op jit(solution)/shard_map/ppermute | solution.py:202
  436.5 37.5 %collective-permute-start.54 = (bf16[328,1024]{1,0:T(8,128)(2,1)S(1)}, bf16[328,1024]{1,0:T(8,128)(2,1)S(1)}, u32[]{:S(2)}, u32[]{:S(2)}) collective-permute-start(bf16[328,1024]{1,0:T(8,128)(2,1)S(1)} %pad_maximum_fusion.16), channel_id=1, source_target_pairs={{0,1},{1,0},{2,3},{3,2},{4,5},{5,4},{6,7},{7,6},{8,9},{9,8},{10,11... | collective-permute-start | bytes 2015240 | tf_op jit(solution)/shard_map/ppermute | solution.py:202
  462.4 11.5 %collective-permute-start.41 = (bf16[64,1536]{1,0:T(8,128)(2,1)S(1)}, bf16[64,1536]{1,0:T(8,128)(2,1)S(1)}, u32[]{:S(2)}, u32[]{:S(2)}) collective-permute-start(bf16[64,1536]{1,0:T(8,128)(2,1)S(1)} %get-tuple-element.175), channel_id=1, source_target_pairs={{0,4},{2,6},{4,0},{6,2},{1,5},{3,7},{5,1},{7,3},{8,12},{10,14},{12... | collective-permute-start | bytes 589832 | tf_op jit(solution)/shard_map/ppermute | solution.py:202
  463.0 33.4 %collective-permute-start.49 = (bf16[256,3200]{1,0:T(8,128)(2,1)S(1)}, bf16[256,3200]{1,0:T(8,128)(2,1)S(1)}, u32[]{:S(2)}, u32[]{:S(2)}) collective-permute-start(bf16[256,3200]{1,0:T(8,128)(2,1)S(1)} %pad_maximum_fusion.5), channel_id=1, source_target_pairs={{0,1},{1,0},{2,3},{3,2},{4,5},{5,4},{6,7},{7,6},{8,9},{9,8},{10,11... | collective-permute-start | bytes 4915208 | tf_op jit(solution)/shard_map/ppermute | solution.py:202
  485.0 11.1 %collective-permute-start.43 = (bf16[128,1536]{1,0:T(8,128)(2,1)S(1)}, bf16[128,1536]{1,0:T(8,128)(2,1)S(1)}, u32[]{:S(2)}, u32[]{:S(2)}) collective-permute-start(bf16[128,1536]{1,0:T(8,128)(2,1)S(1)} %pad_maximum_fusion.17), channel_id=1, source_target_pairs={{0,2},{2,0},{4,6},{6,4},{1,3},{3,1},{5,7},{7,5},{8,10},{10,8},{12,... | collective-permute-start | bytes 1179656 | tf_op jit(solution)/shard_map/ppermute | solution.py:202
  496.3 18.3 %collective-permute-start.44 = (bf16[256,1536]{1,0:T(8,128)(2,1)S(1)}, bf16[256,1536]{1,0:T(8,128)(2,1)S(1)}, u32[]{:S(2)}, u32[]{:S(2)}) collective-permute-start(bf16[256,1536]{1,0:T(8,128)(2,1)S(1)} %pad_maximum_fusion.14.refs_1_), channel_id=1, source_target_pairs={{0,1},{1,0},{2,3},{3,2},{4,5},{5,4},{6,7},{7,6},{8,9},{9,8},{10,11... | collective-permute-start | bytes 2359304 | tf_op jit(solution)/shard_map/ppermute | solution.py:202
  (74 other events, 699.7 us)
Sparse Core Ops, SparseCore 0:
  10.5 51.1 all-gather.3
  64.1 101.7 all-gather.5
  223.0 72.7 reduce-scatter.1

commit v9 on v8

--- a/solution.py
+++ b/solution.py
@@ -338,6 +338,11 @@
         ],
         scratch_shapes=[pltpu.VMEM((rows, 2 * PAIR), jnp.bfloat16)],
         compiler_params=compiler_params(),
+        cost_estimate=pl.CostEstimate(
+            flops=8 * rows * rows * HEAD,
+            transcendentals=2 * rows * rows,
+            bytes_accessed=16 * rows * PAIR,
+        ),
         name="attend",
     )(qkv, qkv, qkv, query_side, key_side, qkv, key_side, *after)
 
@@ -443,6 +448,11 @@
             pltpu.VMEM((rows, PAIR), jnp.float32),
         ],
         compiler_params=compiler_params(),
+        cost_estimate=pl.CostEstimate(
+            flops=20 * rows * rows * HEAD,
+            transcendentals=2 * rows * rows,
+            bytes_accessed=20 * rows * PAIR,
+        ),
         name="attend_back",
     )(qkv, qkv, qkv, query_side, key_side, stat, attended, grad, cos, sin, cos, sin, *after)
 
@@ -689,17 +699,16 @@
             up_halves = group_first(delayed(up_share, grad_near), group, grads)
             grads_near = [grads, down_share, *up_halves]
             result = middle + product(delayed(hidden, grads), w_down)
-        if pair == pairs - 1:
-            up_half = group_second(up_halves, group, grads)
         if pair > 0:
             grads = delayed(grads, grads_here[0])
         grads_here.append(swap_heads(grads.reshape(group, own_rows, 3 * PAIR), group))
     grads_placed, grad_first = [], 0.0
     for pair in range(pairs):
-        after = (up_half,) if pair == 0 else (in_theirs[0],)
+        after = () if pair == 0 else (in_theirs[0],)
         placed = place(me_list, [grads_here[pair]], group, after)
         grads_placed.append(placed)
         in_theirs.append(core_theirs(first_normed, placed, core))
+    up_half = group_second(up_halves, group, in_theirs[-1])
     in_share = jnp.concatenate(
         [
             core_mine(first_normed, grads_placed[pair], core, in_theirs[pair])

time: 537 us -> 559 us (1.041)
  waiting for transfers between devices: 181 us -> 205 us
  starting transfers between devices: 64.6 us -> 59 us
    ppermute x55, waiting for transfers between devices: 176 us -> 198 us  [exchange(): return lax.ppermute(array, axis, [(i, i ^ mask) for i in range(size)])]
    unnamed x134 -> x144, local copies, waits for them, and re-layouts: 13.5 us -> 14.2 us
  transfers between devices with their start and end apart: 58 -> 58, of which waited for: 26 -> 29; matrix products, arithmetic and copies ran while one was open for 22% -> 22% of each run, Pallas kernels for 17% -> 16%
where the time goes in v9:
time: 559 us; the launch traced here: 555 us
  waiting for transfers between devices  205 us (37%)
  Pallas kernels  94.3 us (17%)
  other arithmetic  66.8 us (12%)
  matrix products  64.8 us (12%)
  starting transfers between devices  59 us (11%)
  local copies, waits for them, and re-layouts  40 us (7%)
  between operations  15.4 us (3%)
  blocking collectives  9.63 us (2%)
    ppermute x55, waiting for transfers between devices, exchange(): return lax.ppermute(array, axis, [(i, i ^ mask) for i in range(size)])  198 us
    ppermute x55, starting transfers between devices, exchange(): return lax.ppermute(array, axis, [(i, i ^ mask) for i in range(size)])  58.9 us
    pallas_call x2, Pallas kernels, attend_back(): pl.pallas_call(skipping(attend_back_kernel, 12, len(after)), grid=(rows /...  34.1 us
    dot_general x9, matrix products, contract(): lax.dot_general(left, right, (((0,), (0,)), ((), ())), preferred_element_...  30.9 us
    sub x5, other arithmetic, adam_update(): return (mean_new, square_new, weight - rate * (step_size + 0.01 * weight))  24.7 us
    pallas_call x2, Pallas kernels, attend(): pl.pallas_call(skipping(attend_kernel, 7, len(after)), grid=(rows // bloc...  20.5 us
    dot_general x4, matrix products, against(): lax.dot_general(left, right, (((1,), (1,)), ((), ())), preferred_element_...  19.9 us
    unnamed x144, local copies, waits for them, and re-layouts  14.2 us
  transfers between devices with their start and end apart: 58, of which 29 were waited for; matrix products, arithmetic and copies ran while one was open for 22% of the time, Pallas kernels for 16%

profile of v9, /device:TPU:0, one launch (start us, length us, event | category | flops | bytes accessed | tf_op | source)
XLA Modules:
  0.0 554.8 jit_solution(3871566253568294858)
XLA Ops:
  16.5 3.0 collective-permute-start.6
  21.1 9.6 %all-gather = bf16[4,1,896]{2,1,0:T(2,128)(2,1)S(1)} all-gather(bf16[1,1,896]{2,1,0:T(2,128)(2,1)S(1)} %maximum_bitcast_fusion.1), channel_id=1, replica_groups=mesh['grp'=4,'far'=4,'core'=2] {'grp'}, dimensions={0}, use_global_device_ids=true | all-gather | bytes 8960 | tf_op jit(solution)/shard_map/all_gather | solution.py:621
  33.8 4.5 fusion.57
  52.3 8.0 %collective-permute-done.16 = bf16[4,656,128]{2,1,0:T(8,128)(2,1)S(1)} collective-permute-done((bf16[4,656,128]{2,1,0:T(8,128)(2,1)S(1)}, bf16[4,656,128]{2,1,0:T(8,128)(2,1)S(1)}, u32[]{:S(2)}, u32[]{:S(2)}) %collective-permute-start.16) | collective-permute-done | bytes 671776 | tf_op jit(solution)/shard_map/ppermute | solution.py:202
  61.5 5.8 %project.2.refs_5_ = bf16[4,384,384]{2,1,0:T(8,128)(2,1)} custom-call(s32[1]{0:T(128)} %bitcast.1.refs_0_.me_ref, bf16[384,1024]{1,0:T(8,128)(2,1)} %fusion.42.refs_1_, bf16[1024,3072]{1,0:T(8,128)(2,1)} %all-gather.4.cloned.1.call-done.refs_2_, f32[4,384,128]{2,1,0:T(8,128)} %bitcast.159, f32[4,384,128]{2,1,0:T(8,128)} %bitcast.157), custom_call_target="tpu_custom_call" | custom-call | tf_op jit(solution)/shard_map/project/pallas_call | solution.py:127
  74.8 5.9 %project.3 = bf16[4,384,384]{2,1,0:T(8,128)(2,1)} custom-call(s32[1]{0:T(128)} %bitcast.1.refs_0_.me_ref, bf16[384,1024]{1,0:T(8,128)(2,1)} %fusion.42.refs_1_, bf16[1024,3072]{1,0:T(8,128)(2,1)} %all-gather.4.cloned.1.call-done.refs_2_, f32[4,384,128]{2,1,0:T(8,128)} %bitcast.160, f32[4,384,128]{2,1,0:T(8,128)} %bitcast.158, ...), custom_call_target="tpu_custom_call" | custom-call | tf_op jit(solution)/shard_map/project/pallas_call | solution.py:127
  85.2 6.2 %collective-permute-done.1 = bf16[384,384]{1,0:T(8,128)(2,1)S(1)} collective-permute-done((bf16[384,384]{1,0:T(8,128)(2,1)S(1)}, bf16[384,384]{1,0:T(8,128)(2,1)S(1)}, u32[]{:S(2)}, u32[]{:S(2)}) %collective-permute-start.1) | collective-permute-done | bytes 294944 | tf_op jit(solution)/shard_map/ppermute | solution.py:202
  96.2 10.2 %attend.2 = (bf16[1536,128]{1,0:T(8,128)(2,1)}, f32[1536,128]{1,0:T(8,128)}) custom-call(bf16[1536,384]{1,0:T(8,128)(2,1)} %pad_maximum_fusion.8.refs_0_.refs_1_.refs_2_.refs_5_, bf16[1536,384]{1,0:T(8,128)(2,1)} %pad_maximum_fusion.8.refs_0_.refs_1_.refs_2_.refs_5_, bf16[1536,384]{1,0:T(8,128)(2,1)} %pad_maximum_fusion.8.refs_0_.refs_1_.refs_2_.refs_5_, ...), custom_call_target="tpu_custom_call" | custom-call | flops 1207959552 | bytes 3145728 | tf_op jit(solution)/shard_map/attend/pallas_call | solution.py:328
  110.2 5.5 collective-permute-done.10
  119.2 10.2 %attend.3 = (bf16[1536,128]{1,0:T(8,128)(2,1)}, f32[1536,128]{1,0:T(8,128)}) custom-call(bf16[1536,384]{1,0:T(8,128)(2,1)} %copy-done.9, bf16[1536,384]{1,0:T(8,128)(2,1)} %copy-done.9, bf16[1536,384]{1,0:T(8,128)(2,1)} %copy-done.9, bf16[1536,128]{1,0:T(8,128)(2,1)} %get-tuple-element.191.refs_3_, bf16[1536,128]{1,0:T(8,128)(2,1)} %get-tuple-element.190.refs_4_.refs_6_, ...), custom_call_target="tpu_custom_call" | custom-call | flops 1207959552 | bytes 3145728 | tf_op jit(solution)/shard_map/attend/pallas_call | solution.py:328
  134.8 5.5 collective-permute-done.15.refs_7_
  151.6 8.8 %assemble.1 = bf16[2624,1024]{1,0:T(8,128)(2,1)} custom-call(s32[2]{0:T(128)} %pad_add_fusion.me_ref, bf16[4,656,512]{2,1,0:T(8,128)(2,1)} %copy-done.10, bf16[4,656,512]{2,1,0:T(8,128)(2,1)} %collective-permute-done.18.other_ref), custom_call_target="tpu_custom_call" | custom-call | tf_op jit(solution)/shard_map/assemble/pallas_call | solution.py:238
  160.5 5.3 all-gather.6.cloned.1.call-done.refs_2_
  165.7 2.9 fusion.108
  169.0 7.8 %fusion.2 = f32[384,5376]{1,0:T(8,128)S(1)} fusion(bf16[1024,6400]{1,0:T(8,128)(2,1)} %all-gather.6.cloned.1.call-done.refs_2_, f32[384,1024]{1,0:T(8,128)S(1)} %get-tuple-element.197, f32[1024]{0:T(1024)S(1)} %bitcast.178, f32[384]{0:T(512)S(1)} %fusion.85, f32[384]{0:T(512)S(1)} %broadcast_multiply_fusion), kind=kOutput, calls=%fused_computation.5 | convolution fusion | flops 4229431296 | bytes 20847616 | tf_op jit(solution)/shard_map/dot_general | solution.py:461
  181.2 4.7 convolution_convert_fusion.1
  186.0 8.2 %fusion.12 = (bf16[384,2624]{1,0:T(8,128)(2,1)S(1)}, bf16[384,2624]{1,0:T(8,128)(2,1)S(1)}) fusion(f32[384,5376]{1,0:T(8,128)} %copy-done.11, bf16[384,1024]{1,0:T(8,128)(2,1)S(1)} %copy-done.40, bf16[2624,1024]{1,0:T(8,128)(2,1)} %assemble.1), kind=kOutput, calls=%fused_computation.33 | convolution fusion | flops 2077704192 | bytes 18251776 | tf_op jit(solution)/shard_map/dot_general | solution.py:471
  194.6 5.2 convolution_convert_fusion.refs_3_
  200.0 8.6 %multiply_reduce_fusion.1 = (f32[384]{0:T(512)S(1)}, f32[384,1024]{1,0:T(8,128)S(1)}) fusion(f32[384,1024]{1,0:T(8,128)S(1)} %get-tuple-element.197, f32[384]{0:T(512)S(1)} %broadcast_multiply_fusion, f32[1024]{0:T(1024)S(1)} %bitcast.180, bf16[384,5376]{1,0:T(8,128)(2,1)} %copy-done.22, bf16[1024,6400]{1,0:T(8,128)(2,1)} %all-gather.6.cloned.1.call-done.refs_2_), kind=kOutput, calls=%fused_computation.106 | convolution fusion | flops 4229430784 | bytes 18291712 | tf_op jit(solution)/shard_map/dot_general | solution.py:471
  211.5 5.0 row_product.1
  222.9 5.5 collective-permute-done.21
  228.3 3.5 collective-permute-done.20
  234.2 3.2 add_convert_fusion.5
  237.4 7.0 %add_convert_fusion = bf16[1024,2688]{1,0:T(8,128)(2,1)} fusion(bf16[1024,2688]{1,0:T(8,128)(2,1)} %collective-permute-done.22, bf16[384,5376]{1,0:T(8,128)(2,1)S(1)} %copy-done.23, s32[]{:T(128)S(6)} %select_n.371, f32[384,1024]{1,0:T(8,128)S(1)} %get-tuple-element.197, f32[1024]{0:T(1024)S(1)} %bitcast.181, f32[384]{0:T(512)S(1)} %copy-done.54, ...), kind=kOutput, calls=%fused_computation.2 | convolution fusion | flops 2123759616 | bytes 14655492 | tf_op jit(solution)/shard_map/dot_general | solution.py:465
  244.5 4.3 pad_maximum_fusion.refs_12_
  254.7 17.1 %attend_back.2.refs_12_ = bf16[1536,384]{1,0:T(8,128)(2,1)} custom-call(bf16[1536,384]{1,0:T(8,128)(2,1)} %pad_maximum_fusion.8.refs_0_.refs_1_.refs_2_.refs_5_, bf16[1536,384]{1,0:T(8,128)(2,1)} %pad_maximum_fusion.8.refs_0_.refs_1_.refs_2_.refs_5_, bf16[1536,384]{1,0:T(8,128)(2,1)} %pad_maximum_fusion.8.refs_0_.refs_1_.refs_2_.refs_5_, ...), custom_call_target="tpu_custom_call" | custom-call | flops 3019898880 | bytes 3932160 | tf_op jit(solution)/shard_map/attend_back/pallas_call | solution.py:434
  279.8 32.7 %collective-permute-done.26.refs_3_ = bf16[384,384]{1,0:T(8,128)(2,1)S(1)} collective-permute-done((bf16[384,384]{1,0:T(8,128)(2,1)S(1)}, bf16[384,384]{1,0:T(8,128)(2,1)S(1)}, u32[]{:S(2)}, u32[]{:S(2)}) %collective-permute-start.26) | collective-permute-done | bytes 294944 | tf_op jit(solution)/shard_map/ppermute | solution.py:202
  312.5 5.1 collective-permute-done.24.refs_1_
  318.3 3.0 place.4
  321.4 3.4 convolution_convert_fusion.3.refs_4_
  329.1 3.6 collective-permute-done.28
  334.2 17.0 %attend_back.3 = bf16[1536,384]{1,0:T(8,128)(2,1)} custom-call(bf16[1536,384]{1,0:T(8,128)(2,1)} %copy-done.9, bf16[1536,384]{1,0:T(8,128)(2,1)} %copy-done.9, bf16[1536,384]{1,0:T(8,128)(2,1)} %copy-done.9, bf16[1536,128]{1,0:T(8,128)(2,1)} %get-tuple-element.191.refs_3_, bf16[1536,128]{1,0:T(8,128)(2,1)} %get-tuple-element.190.refs_4_.refs_6_, ...), custom_call_target="tpu_custom_call" | custom-call | flops 3019898880 | bytes 3932160 | tf_op jit(solution)/shard_map/attend_back/pallas_call | solution.py:434
  357.8 6.4 %collective-permute-done.32.refs_3_ = bf16[384,384]{1,0:T(8,128)(2,1)S(1)} collective-permute-done((bf16[384,384]{1,0:T(8,128)(2,1)S(1)}, bf16[384,384]{1,0:T(8,128)(2,1)S(1)}, u32[]{:S(2)}, u32[]{:S(2)}) %collective-permute-start.32) | collective-permute-done | bytes 294944 | tf_op jit(solution)/shard_map/ppermute | solution.py:202
  371.4 3.0 place.5
  378.0 8.1 %collective-permute-done.43 = bf16[128,3200]{1,0:T(8,128)(2,1)} collective-permute-done((bf16[128,3200]{1,0:T(8,128)(2,1)S(1)}, bf16[128,3200]{1,0:T(8,128)(2,1)}, u32[]{:S(2)}, u32[]{:S(2)}) %collective-permute-start.43) | collective-permute-done | bytes 819232 | tf_op jit(solution)/shard_map/ppermute | solution.py:202
  389.8 3.3 fusion.52
  399.2 11.4 %collective-permute-done.45 = bf16[128,3200]{1,0:T(8,128)(2,1)S(1)} collective-permute-done((bf16[128,3200]{1,0:T(8,128)(2,1)S(1)}, bf16[128,3200]{1,0:T(8,128)(2,1)S(1)}, u32[]{:S(2)}, u32[]{:S(2)}) %collective-permute-start.45) | collective-permute-done | bytes 819232 | tf_op jit(solution)/shard_map/ppermute | solution.py:202
  412.5 2.9 collective-permute-start.52
  421.0 11.5 %collective-permute-done.46 = bf16[64,3200]{1,0:T(8,128)(2,1)S(1)} collective-permute-done((bf16[64,3200]{1,0:T(8,128)(2,1)S(1)}, bf16[64,3200]{1,0:T(8,128)(2,1)S(1)}, u32[]{:S(2)}, u32[]{:S(2)}) %collective-permute-start.46) | collective-permute-done | bytes 409632 | tf_op jit(solution)/shard_map/ppermute | solution.py:202
  438.0 16.6 %collective-permute-done.47 = bf16[64,3200]{1,0:T(8,128)(2,1)S(1)} collective-permute-done((bf16[64,3200]{1,0:T(8,128)(2,1)S(1)}, bf16[64,3200]{1,0:T(8,128)(2,1)S(1)}, u32[]{:S(2)}, u32[]{:S(2)}) %collective-permute-start.47) | collective-permute-done | bytes 409632 | tf_op jit(solution)/shard_map/ppermute | solution.py:202
  458.1 25.3 %collective-permute-done.38 = bf16[128,1536]{1,0:T(8,128)(2,1)S(1)} collective-permute-done((bf16[128,1536]{1,0:T(8,128)(2,1)S(1)}, bf16[128,1536]{1,0:T(8,128)(2,1)S(1)}, u32[]{:S(2)}, u32[]{:S(2)}) %collective-permute-start.38) | collective-permute-done | bytes 393248 | tf_op jit(solution)/shard_map/ppermute | solution.py:202
  485.1 9.5 %collective-permute-done.39 = bf16[64,1536]{1,0:T(8,128)(2,1)S(1)} collective-permute-done((bf16[64,1536]{1,0:T(8,128)(2,1)S(1)}, bf16[64,1536]{1,0:T(8,128)(2,1)S(1)}, u32[]{:S(2)}, u32[]{:S(2)}) %collective-permute-start.39) | collective-permute-done | bytes 196640 | tf_op jit(solution)/shard_map/ppermute | solution.py:202
  494.9 11.5 %collective-permute-done.40 = bf16[64,1536]{1,0:T(8,128)(2,1)S(1)} collective-permute-done((bf16[64,1536]{1,0:T(8,128)(2,1)S(1)}, bf16[64,1536]{1,0:T(8,128)(2,1)S(1)}, u32[]{:S(2)}, u32[]{:S(2)}) %collective-permute-start.40) | collective-permute-done | bytes 196640 | tf_op jit(solution)/shard_map/ppermute | solution.py:202
  506.6 4.0 multiply_subtract_fusion.2
  510.6 7.0 %collective-permute-done.41 = bf16[128,1536]{1,0:T(8,128)(2,1)S(1)} collective-permute-done((bf16[128,1536]{1,0:T(8,128)(2,1)S(1)}, bf16[128,1536]{1,0:T(8,128)(2,1)S(1)}, u32[]{:S(2)}, u32[]{:S(2)}) %collective-permute-start.41) | collective-permute-done | bytes 393248 | tf_op jit(solution)/shard_map/ppermute | solution.py:202
  520.7 11.2 %multiply_subtract_fusion = (f32[256,5248]{1,0:T(8,128)}, f32[256,5248]{1,0:T(8,128)}, f32[256,5248]{1,0:T(8,128)}, f32[256]{0:T(256)S(1)}) fusion(f32[256,5248]{1,0:T(8,128)S(1)} %bitcast.165, f32[256,2624]{1,0:T(8,128)S(1)} %get-tuple-element.107, f32[256,2624]{1,0:T(8,128)S(1)} %get-tuple-element.106, f32[256,5248]{1,0:T(8,128)} %param.28, ...), kind=kLoop, calls=%fused_computation.26 | loop fusion | flops 26869504 | bytes 37618688 | tf_op jit(solution)/shard_map/sub | solution.py:582
  536.9 3.0 merge.1
  540.8 6.6 %multiply_subtract_fusion.1 = (f32[256,3072]{1,0:T(8,128)}, f32[256,3072]{1,0:T(8,128)}, f32[256,3072]{1,0:T(8,128)}, f32[256]{0:T(256)S(1)}) fusion(f32[256,3072]{1,0:T(8,128)S(1)} %copy-done.8, bf16[256,3072]{1,0:T(8,128)(2,1)} %merge.1, f32[256,3072]{1,0:T(8,128)S(1)} %copy-done.27, f32[256,3072]{1,0:T(8,128)} %param.26), kind=kLoop, calls=%fused_computation.55 | loop fusion | flops 15728384 | bytes 20448256 | tf_op jit(solution)/shard_map/sub | solution.py:582
  (380 shorter events, 161.8 us)
Async XLA Ops:
  7.2 54.3 %all-gather.4.cloned.1.call-start = ((), (), s32[]{:S(2)}) async-start(), calls=%async_computation.1 | async-start | bytes 7077888 | tf_op jit(solution)/shard_map/all_gather | solution.py:616
  9.7 156.0 %all-gather.6.cloned.1.call-start = ((), (), s32[]{:S(2)}) async-start(), calls=%async_computation.2 | async-start | bytes 14745600 | tf_op jit(solution)/shard_map/all_gather | solution.py:482
  15.4 318.9 %reduce-scatter.2.cloned.1.call-start = ((), (), s32[]{:S(2)}) async-start(), calls=%async_computation.3 | async-start | bytes 6045696 | tf_op jit(solution)/shard_map/reduce_scatter | solution.py:674
  16.5 24.1 %collective-permute-start.6 = (bf16[656,128]{1,0:T(8,128)(2,1)S(1)}, bf16[656,128]{1,0:T(8,128)(2,1)S(1)}, u32[]{:S(2)}, u32[]{:S(2)}) collective-permute-start(bf16[656,128]{1,0:T(8,128)(2,1)S(1)} %dynamic-slice_convert_fusion), channel_id=1, source_target_pairs={{0,8},{8,0},{16,24},{24,16},{1,9},{9,1},{17,25},{25,17},{2,10},{10... | collective-permute-start | bytes 503816 | tf_op jit(solution)/shard_map/ppermute | solution.py:202
  19.5 22.5 %collective-permute-start.7 = (bf16[656,128]{1,0:T(8,128)(2,1)S(1)}, bf16[656,128]{1,0:T(8,128)(2,1)S(1)}, u32[]{:S(2)}, u32[]{:S(2)}) collective-permute-start(bf16[656,128]{1,0:T(8,128)(2,1)S(1)} %dynamic-slice_convert_fusion), channel_id=1, source_target_pairs={{0,16},{8,24},{16,0},{24,8},{1,17},{9,25},{17,1},{25,9},{2,18},{10... | collective-permute-start | bytes 503816 | tf_op jit(solution)/shard_map/ppermute | solution.py:202
  48.8 11.5 %collective-permute-start.16 = (bf16[4,656,128]{2,1,0:T(8,128)(2,1)S(1)}, bf16[4,656,128]{2,1,0:T(8,128)(2,1)S(1)}, u32[]{:S(2)}, u32[]{:S(2)}) collective-permute-start(bf16[4,656,128]{2,1,0:T(8,128)(2,1)S(1)} %pad_maximum_fusion.14.refs_6_), channel_id=1, source_target_pairs={{0,2},{2,0},{4,6},{6,4},{1,3},{3,1},{5,7},{7,5},{8,10},{10,8},{12,... | collective-permute-start | bytes 2015240 | tf_op jit(solution)/shard_map/ppermute | solution.py:202
  68.6 15.3 %collective-permute-start.2 = (bf16[384,384]{1,0:T(8,128)(2,1)S(1)}, bf16[384,384]{1,0:T(8,128)(2,1)S(1)}, u32[]{:S(2)}, u32[]{:S(2)}) collective-permute-start(bf16[384,384]{1,0:T(8,128)(2,1)S(1)} %get-tuple-element.149), channel_id=1, source_target_pairs={{0,24},{8,16},{16,8},{24,0},{1,25},{9,17},{17,9},{25,1},{2,26},{10... | collective-permute-start | bytes 884744 | tf_op jit(solution)/shard_map/ppermute | solution.py:202
  70.3 21.1 %collective-permute-start.1 = (bf16[384,384]{1,0:T(8,128)(2,1)S(1)}, bf16[384,384]{1,0:T(8,128)(2,1)S(1)}, u32[]{:S(2)}, u32[]{:S(2)}) collective-permute-start(bf16[384,384]{1,0:T(8,128)(2,1)S(1)} %get-tuple-element.150), channel_id=1, source_target_pairs={{0,16},{8,24},{16,0},{24,8},{1,17},{9,25},{17,1},{25,9},{2,18},{10... | collective-permute-start | bytes 884744 | tf_op jit(solution)/shard_map/ppermute | solution.py:202
  71.6 23.5 %collective-permute-start = (bf16[384,384]{1,0:T(8,128)(2,1)S(1)}, bf16[384,384]{1,0:T(8,128)(2,1)S(1)}, u32[]{:S(2)}, u32[]{:S(2)}) collective-permute-start(bf16[384,384]{1,0:T(8,128)(2,1)S(1)} %get-tuple-element.151), channel_id=1, source_target_pairs={{0,8},{8,0},{16,24},{24,16},{1,9},{9,1},{17,25},{25,17},{2,10},{10... | collective-permute-start | bytes 884744 | tf_op jit(solution)/shard_map/ppermute | solution.py:202
  72.3 73.3 %collective-permute-start.17 = (bf16[4,656,256]{2,1,0:T(8,128)(2,1)S(1)}, bf16[4,656,256]{2,1,0:T(8,128)(2,1)S(1)}, u32[]{:S(2)}, u32[]{:S(2)}) collective-permute-start(bf16[4,656,256]{2,1,0:T(8,128)(2,1)S(1)} %pad_maximum_fusion.6), channel_id=1, source_target_pairs={{0,4},{2,6},{4,0},{6,2},{1,5},{3,7},{5,1},{7,3},{8,12},{10,14},{12... | collective-permute-start | bytes 4030472 | tf_op jit(solution)/shard_map/ppermute | solution.py:202
  82.0 36.1 %collective-permute-start.12 = (bf16[384,384]{1,0:T(8,128)(2,1)S(1)}, bf16[384,384]{1,0:T(8,128)(2,1)S(1)}, u32[]{:S(2)}, u32[]{:S(2)}) collective-permute-start(bf16[384,384]{1,0:T(8,128)(2,1)S(1)} %get-tuple-element.144), channel_id=1, source_target_pairs={{0,24},{8,16},{16,8},{24,0},{1,25},{9,17},{17,9},{25,1},{2,26},{10... | collective-permute-start | bytes 884744 | tf_op jit(solution)/shard_map/ppermute | solution.py:202
  83.9 32.7 %collective-permute-start.11 = (bf16[384,384]{1,0:T(8,128)(2,1)S(1)}, bf16[384,384]{1,0:T(8,128)(2,1)S(1)}, u32[]{:S(2)}, u32[]{:S(2)}) collective-permute-start(bf16[384,384]{1,0:T(8,128)(2,1)S(1)} %get-tuple-element.145), channel_id=1, source_target_pairs={{0,16},{8,24},{16,0},{24,8},{1,17},{9,25},{17,1},{25,9},{2,18},{10... | collective-permute-start | bytes 884744 | tf_op jit(solution)/shard_map/ppermute | solution.py:202
  91.4 24.2 %collective-permute-start.10 = (bf16[384,384]{1,0:T(8,128)(2,1)S(1)}, bf16[384,384]{1,0:T(8,128)(2,1)S(1)}, u32[]{:S(2)}, u32[]{:S(2)}) collective-permute-start(bf16[384,384]{1,0:T(8,128)(2,1)S(1)} %get-tuple-element.146), channel_id=1, source_target_pairs={{0,8},{8,0},{16,24},{24,16},{1,9},{9,1},{17,25},{25,17},{2,10},{10... | collective-permute-start | bytes 884744 | tf_op jit(solution)/shard_map/ppermute | solution.py:202
  108.1 21.3 %collective-permute-start.5 = (bf16[384,128]{1,0:T(8,128)(2,1)S(1)}, bf16[384,128]{1,0:T(8,128)(2,1)}, u32[]{:S(2)}, u32[]{:S(2)}) collective-permute-start(bf16[384,128]{1,0:T(8,128)(2,1)S(1)} %get-tuple-element.180), channel_id=1, source_target_pairs={{0,24},{8,16},{16,8},{24,0},{1,25},{9,17},{17,9},{25,1},{2,26},{10... | collective-permute-start | bytes 294920 | tf_op jit(solution)/shard_map/ppermute | solution.py:202
  115.6 13.8 %collective-permute-start.4 = (bf16[384,128]{1,0:T(8,128)(2,1)S(1)}, bf16[384,128]{1,0:T(8,128)(2,1)}, u32[]{:S(2)}, u32[]{:S(2)}) collective-permute-start(bf16[384,128]{1,0:T(8,128)(2,1)S(1)} %get-tuple-element.181), channel_id=1, source_target_pairs={{0,16},{8,24},{16,0},{24,8},{1,17},{9,25},{17,1},{25,9},{2,18},{10... | collective-permute-start | bytes 294920 | tf_op jit(solution)/shard_map/ppermute | solution.py:202
  116.6 12.9 %collective-permute-start.3 = (bf16[384,128]{1,0:T(8,128)(2,1)S(1)}, bf16[384,128]{1,0:T(8,128)(2,1)}, u32[]{:S(2)}, u32[]{:S(2)}) collective-permute-start(bf16[384,128]{1,0:T(8,128)(2,1)S(1)} %get-tuple-element.182), channel_id=1, source_target_pairs={{0,8},{8,0},{16,24},{24,16},{1,9},{9,1},{17,25},{25,17},{2,10},{10... | collective-permute-start | bytes 294920 | tf_op jit(solution)/shard_map/ppermute | solution.py:202
  199.7 37.7 %collective-permute-start.22 = (bf16[1024,2688]{1,0:T(8,128)(2,1)}, bf16[1024,2688]{1,0:T(8,128)(2,1)}, u32[]{:S(2)}, u32[]{:S(2)}) collective-permute-start(bf16[1024,2688]{1,0:T(8,128)(2,1)} %convolution_convert_fusion.refs_3_), channel_id=1, source_target_pairs={{0,1},{1,0},{2,3},{3,2},{4,5},{5,4},{6,7},{7,6},{8,9},{9,8},{10,11... | collective-permute-start | bytes 16515080 | tf_op jit(solution)/shard_map/ppermute | solution.py:202
  218.3 15.9 %collective-permute-start.23 = (bf16[1024,512]{1,0:T(8,128)(2,1)}, bf16[1024,512]{1,0:T(8,128)(2,1)}, u32[]{:S(2)}, u32[]{:S(2)}) collective-permute-start(bf16[1024,512]{1,0:T(8,128)(2,1)} %convolution_convert_fusion.4), channel_id=1, source_target_pairs={{0,1},{1,0},{2,3},{3,2},{4,5},{5,4},{6,7},{7,6},{8,9},{9,8},{10,11... | collective-permute-start | bytes 3145736 | tf_op jit(solution)/shard_map/ppermute | solution.py:202
  253.9 70.9 %collective-permute-start.29 = (bf16[2,128,3200]{2,1,0:T(8,128)(2,1)S(1)}, bf16[2,128,3200]{2,1,0:T(8,128)(2,1)}, u32[]{:S(2)}, u32[]{:S(2)}) collective-permute-start(bf16[2,128,3200]{2,1,0:T(8,128)(2,1)S(1)} %get-tuple-element.113), channel_id=1, source_target_pairs={{0,8},{8,0},{16,24},{24,16},{1,9},{9,1},{17,25},{25,17},{2,10},{10... | collective-permute-start | bytes 4915208 | tf_op jit(solution)/shard_map/ppermute | solution.py:202
  273.9 38.6 %collective-permute-start.26 = (bf16[384,384]{1,0:T(8,128)(2,1)S(1)}, bf16[384,384]{1,0:T(8,128)(2,1)S(1)}, u32[]{:S(2)}, u32[]{:S(2)}) collective-permute-start(bf16[384,384]{1,0:T(8,128)(2,1)S(1)} %get-tuple-element.140), channel_id=1, source_target_pairs={{0,24},{8,16},{16,8},{24,0},{1,25},{9,17},{17,9},{25,1},{2,26},{10... | collective-permute-start | bytes 884744 | tf_op jit(solution)/shard_map/ppermute | solution.py:202
  274.8 37.7 %collective-permute-start.25 = (bf16[384,384]{1,0:T(8,128)(2,1)S(1)}, bf16[384,384]{1,0:T(8,128)(2,1)S(1)}, u32[]{:S(2)}, u32[]{:S(2)}) collective-permute-start(bf16[384,384]{1,0:T(8,128)(2,1)S(1)} %get-tuple-element.141), channel_id=1, source_target_pairs={{0,16},{8,24},{16,0},{24,8},{1,17},{9,25},{17,1},{25,9},{2,18},{10... | collective-permute-start | bytes 884744 | tf_op jit(solution)/shard_map/ppermute | solution.py:202
  276.6 41.0 %collective-permute-start.24 = (bf16[384,384]{1,0:T(8,128)(2,1)S(1)}, bf16[384,384]{1,0:T(8,128)(2,1)S(1)}, u32[]{:S(2)}, u32[]{:S(2)}) collective-permute-start(bf16[384,384]{1,0:T(8,128)(2,1)S(1)} %get-tuple-element.142), channel_id=1, source_target_pairs={{0,8},{8,0},{16,24},{24,16},{1,9},{9,1},{17,25},{25,17},{2,10},{10... | collective-permute-start | bytes 884744 | tf_op jit(solution)/shard_map/ppermute | solution.py:202
  279.3 53.4 %collective-permute-start.28 = (bf16[2,128,3200]{2,1,0:T(8,128)(2,1)}, bf16[2,128,3200]{2,1,0:T(8,128)(2,1)S(1)}, u32[]{:S(2)}, u32[]{:S(2)}) collective-permute-start(bf16[2,128,3200]{2,1,0:T(8,128)(2,1)} %get-tuple-element.115), channel_id=1, source_target_pairs={{0,16},{8,24},{16,0},{24,8},{1,17},{9,25},{17,1},{25,9},{2,18},{10... | collective-permute-start | bytes 4915208 | tf_op jit(solution)/shard_map/ppermute | solution.py:202
  324.7 68.4 %collective-permute-start.27 = (bf16[1024,768]{1,0:T(8,128)(2,1)}, bf16[1024,768]{1,0:T(8,128)(2,1)}, u32[]{:S(2)}, u32[]{:S(2)}) collective-permute-start(bf16[1024,768]{1,0:T(8,128)(2,1)} %convolution_convert_fusion.3.refs_4_), channel_id=1, source_target_pairs={{0,1},{1,0},{2,3},{3,2},{4,5},{5,4},{6,7},{7,6},{8,9},{9,8},{10,11... | collective-permute-start | bytes 4718600 | tf_op jit(solution)/shard_map/ppermute | solution.py:202
  327.6 49.1 %collective-permute-start.44 = (bf16[128,3200]{1,0:T(8,128)(2,1)}, bf16[128,3200]{1,0:T(8,128)(2,1)}, u32[]{:S(2)}, u32[]{:S(2)}) collective-permute-start(bf16[128,3200]{1,0:T(8,128)(2,1)} %get-tuple-element.125), channel_id=1, source_target_pairs={{0,16},{8,24},{16,0},{24,8},{1,17},{9,25},{17,1},{25,9},{2,18},{10... | collective-permute-start | bytes 2457608 | tf_op jit(solution)/shard_map/ppermute | solution.py:202
  354.8 12.4 %collective-permute-start.31 = (bf16[384,384]{1,0:T(8,128)(2,1)S(1)}, bf16[384,384]{1,0:T(8,128)(2,1)S(1)}, u32[]{:S(2)}, u32[]{:S(2)}) collective-permute-start(bf16[384,384]{1,0:T(8,128)(2,1)S(1)} %get-tuple-element.137), channel_id=1, source_target_pairs={{0,16},{8,24},{16,0},{24,8},{1,17},{9,25},{17,1},{25,9},{2,18},{10... | collective-permute-start | bytes 884744 | tf_op jit(solution)/shard_map/ppermute | solution.py:202
  356.6 14.1 %collective-permute-start.30 = (bf16[384,384]{1,0:T(8,128)(2,1)S(1)}, bf16[384,384]{1,0:T(8,128)(2,1)S(1)}, u32[]{:S(2)}, u32[]{:S(2)}) collective-permute-start(bf16[384,384]{1,0:T(8,128)(2,1)S(1)} %get-tuple-element.138), channel_id=1, source_target_pairs={{0,8},{8,0},{16,24},{24,16},{1,9},{9,1},{17,25},{25,17},{2,10},{10... | collective-permute-start | bytes 884744 | tf_op jit(solution)/shard_map/ppermute | solution.py:202
  364.3 21.9 %collective-permute-start.43 = (bf16[128,3200]{1,0:T(8,128)(2,1)S(1)}, bf16[128,3200]{1,0:T(8,128)(2,1)}, u32[]{:S(2)}, u32[]{:S(2)}) collective-permute-start(bf16[128,3200]{1,0:T(8,128)(2,1)S(1)} %get-tuple-element.127), channel_id=1, source_target_pairs={{0,8},{8,0},{16,24},{24,16},{1,9},{9,1},{17,25},{25,17},{2,10},{10... | collective-permute-start | bytes 2457608 | tf_op jit(solution)/shard_map/ppermute | solution.py:202
  367.2 28.4 %collective-permute-start.50 = (bf16[328,512]{1,0:T(8,128)(2,1)}, bf16[328,512]{1,0:T(8,128)(2,1)}, u32[]{:S(2)}, u32[]{:S(2)}) collective-permute-start(bf16[328,512]{1,0:T(8,128)(2,1)} %get-tuple-element.171), channel_id=1, source_target_pairs={{0,2},{2,0},{4,6},{6,4},{1,3},{3,1},{5,7},{7,5},{8,10},{10,8},{12,... | collective-permute-start | bytes 1007624 | tf_op jit(solution)/shard_map/ppermute | solution.py:202
  389.0 21.7 %collective-permute-start.45 = (bf16[128,3200]{1,0:T(8,128)(2,1)S(1)}, bf16[128,3200]{1,0:T(8,128)(2,1)S(1)}, u32[]{:S(2)}, u32[]{:S(2)}) collective-permute-start(bf16[128,3200]{1,0:T(8,128)(2,1)S(1)} %get-tuple-element.123), channel_id=1, source_target_pairs={{0,2},{2,0},{4,6},{6,4},{1,3},{3,1},{5,7},{7,5},{8,10},{10,8},{12,... | collective-permute-start | bytes 2457608 | tf_op jit(solution)/shard_map/ppermute | solution.py:202
  395.6 15.6 %collective-permute-start.33 = (bf16[1024,768]{1,0:T(8,128)(2,1)S(1)}, bf16[1024,768]{1,0:T(8,128)(2,1)S(1)}, u32[]{:S(2)}, u32[]{:S(2)}) collective-permute-start(bf16[1024,768]{1,0:T(8,128)(2,1)S(1)} %convolution_convert_fusion.2), channel_id=1, source_target_pairs={{0,1},{1,0},{2,3},{3,2},{4,5},{5,4},{6,7},{7,6},{8,9},{9,8},{10,11... | collective-permute-start | bytes 4718600 | tf_op jit(solution)/shard_map/ppermute | solution.py:202
  396.8 15.7 %collective-permute-start.51 = (bf16[328,256]{1,0:T(8,128)(2,1)S(1)}, bf16[328,256]{1,0:T(8,128)(2,1)S(1)}, u32[]{:S(2)}, u32[]{:S(2)}) collective-permute-start(bf16[328,256]{1,0:T(8,128)(2,1)S(1)} %get-tuple-element.187), channel_id=1, source_target_pairs={{0,4},{2,6},{4,0},{6,2},{1,5},{3,7},{5,1},{7,3},{8,12},{10,14},{12... | collective-permute-start | bytes 503816 | tf_op jit(solution)/shard_map/ppermute | solution.py:202
  411.0 21.5 %collective-permute-start.46 = (bf16[64,3200]{1,0:T(8,128)(2,1)S(1)}, bf16[64,3200]{1,0:T(8,128)(2,1)S(1)}, u32[]{:S(2)}, u32[]{:S(2)}) collective-permute-start(bf16[64,3200]{1,0:T(8,128)(2,1)S(1)} %get-tuple-element.155), channel_id=1, source_target_pairs={{0,4},{2,6},{4,0},{6,2},{1,5},{3,7},{5,1},{7,3},{8,12},{10,14},{12... | collective-permute-start | bytes 1228808 | tf_op jit(solution)/shard_map/ppermute | solution.py:202
  412.5 23.5 %collective-permute-start.52 = (bf16[328,256]{1,0:T(8,128)(2,1)S(1)}, bf16[328,256]{1,0:T(8,128)(2,1)S(1)}, u32[]{:S(2)}, u32[]{:S(2)}) collective-permute-start(bf16[328,256]{1,0:T(8,128)(2,1)S(1)} %add_convert_fusion.19), channel_id=1, source_target_pairs={{0,4},{2,6},{4,0},{6,2},{1,5},{3,7},{5,1},{7,3},{8,12},{10,14},{12... | collective-permute-start | bytes 503816 | tf_op jit(solution)/shard_map/ppermute | solution.py:202
  415.8 19.0 %collective-permute-start.36 = (bf16[2,128,1536]{2,1,0:T(8,128)(2,1)S(1)}, bf16[2,128,1536]{2,1,0:T(8,128)(2,1)S(1)}, u32[]{:S(2)}, u32[]{:S(2)}) collective-permute-start(bf16[2,128,1536]{2,1,0:T(8,128)(2,1)S(1)} %get-tuple-element.129), channel_id=1, source_target_pairs={{0,8},{8,0},{16,24},{24,16},{1,9},{9,1},{17,25},{25,17},{2,10},{10... | collective-permute-start | bytes 2359304 | tf_op jit(solution)/shard_map/ppermute | solution.py:202
  416.0 19.3 %collective-permute-start.34 = (bf16[2,128,1536]{2,1,0:T(8,128)(2,1)S(1)}, bf16[2,128,1536]{2,1,0:T(8,128)(2,1)S(1)}, u32[]{:S(2)}, u32[]{:S(2)}) collective-permute-start(bf16[2,128,1536]{2,1,0:T(8,128)(2,1)S(1)} %get-tuple-element.131), channel_id=1, source_target_pairs={{0,16},{8,24},{16,0},{24,8},{1,17},{9,25},{17,1},{25,9},{2,18},{10... | collective-permute-start | bytes 2359304 | tf_op jit(solution)/shard_map/ppermute | solution.py:202
  434.8 19.9 %collective-permute-start.47 = (bf16[64,3200]{1,0:T(8,128)(2,1)S(1)}, bf16[64,3200]{1,0:T(8,128)(2,1)S(1)}, u32[]{:S(2)}, u32[]{:S(2)}) collective-permute-start(bf16[64,3200]{1,0:T(8,128)(2,1)S(1)} %add_convert_fusion.13), channel_id=1, source_target_pairs={{0,4},{2,6},{4,0},{6,2},{1,5},{3,7},{5,1},{7,3},{8,12},{10,14},{12... | collective-permute-start | bytes 1228808 | tf_op jit(solution)/shard_map/ppermute | solution.py:202
  435.3 19.6 %collective-permute-start.37 = (bf16[128,1536]{1,0:T(8,128)(2,1)S(1)}, bf16[128,1536]{1,0:T(8,128)(2,1)S(1)}, u32[]{:S(2)}, u32[]{:S(2)}) collective-permute-start(bf16[128,1536]{1,0:T(8,128)(2,1)S(1)} %get-tuple-element.161), channel_id=1, source_target_pairs={{0,16},{8,24},{16,0},{24,8},{1,17},{9,25},{17,1},{25,9},{2,18},{10... | collective-permute-start | bytes 1179656 | tf_op jit(solution)/shard_map/ppermute | solution.py:202
  436.0 21.9 %collective-permute-start.53 = (bf16[328,512]{1,0:T(8,128)(2,1)S(1)}, bf16[328,512]{1,0:T(8,128)(2,1)S(1)}, u32[]{:S(2)}, u32[]{:S(2)}) collective-permute-start(bf16[328,512]{1,0:T(8,128)(2,1)S(1)} %pad_maximum_fusion.17), channel_id=1, source_target_pairs={{0,2},{2,0},{4,6},{6,4},{1,3},{3,1},{5,7},{7,5},{8,10},{10,8},{12,... | collective-permute-start | bytes 1007624 | tf_op jit(solution)/shard_map/ppermute | solution.py:202
  437.8 17.1 %collective-permute-start.35 = (bf16[128,1536]{1,0:T(8,128)(2,1)S(1)}, bf16[128,1536]{1,0:T(8,128)(2,1)S(1)}, u32[]{:S(2)}, u32[]{:S(2)}) collective-permute-start(bf16[128,1536]{1,0:T(8,128)(2,1)S(1)} %get-tuple-element.163), channel_id=1, source_target_pairs={{0,8},{8,0},{16,24},{24,16},{1,9},{9,1},{17,25},{25,17},{2,10},{10... | collective-permute-start | bytes 1179656 | tf_op jit(solution)/shard_map/ppermute | solution.py:202
  454.8 30.0 %collective-permute-start.48 = (bf16[128,3200]{1,0:T(8,128)(2,1)S(1)}, bf16[128,3200]{1,0:T(8,128)(2,1)S(1)}, u32[]{:S(2)}, u32[]{:S(2)}) collective-permute-start(bf16[128,3200]{1,0:T(8,128)(2,1)S(1)} %pad_maximum_fusion.11), channel_id=1, source_target_pairs={{0,2},{2,0},{4,6},{6,4},{1,3},{3,1},{5,7},{7,5},{8,10},{10,8},{12,... | collective-permute-start | bytes 2457608 | tf_op jit(solution)/shard_map/ppermute | solution.py:202
  455.8 27.6 %collective-permute-start.38 = (bf16[128,1536]{1,0:T(8,128)(2,1)S(1)}, bf16[128,1536]{1,0:T(8,128)(2,1)S(1)}, u32[]{:S(2)}, u32[]{:S(2)}) collective-permute-start(bf16[128,1536]{1,0:T(8,128)(2,1)S(1)} %get-tuple-element.159), channel_id=1, source_target_pairs={{0,2},{2,0},{4,6},{6,4},{1,3},{3,1},{5,7},{7,5},{8,10},{10,8},{12,... | collective-permute-start | bytes 1179656 | tf_op jit(solution)/shard_map/ppermute | solution.py:202
  458.1 36.7 %collective-permute-start.54 = (bf16[328,1024]{1,0:T(8,128)(2,1)S(1)}, bf16[328,1024]{1,0:T(8,128)(2,1)S(1)}, u32[]{:S(2)}, u32[]{:S(2)}) collective-permute-start(bf16[328,1024]{1,0:T(8,128)(2,1)S(1)} %pad_maximum_fusion.15), channel_id=1, source_target_pairs={{0,1},{1,0},{2,3},{3,2},{4,5},{5,4},{6,7},{7,6},{8,9},{9,8},{10,11... | collective-permute-start | bytes 2015240 | tf_op jit(solution)/shard_map/ppermute | solution.py:202
  483.5 11.1 %collective-permute-start.39 = (bf16[64,1536]{1,0:T(8,128)(2,1)S(1)}, bf16[64,1536]{1,0:T(8,128)(2,1)S(1)}, u32[]{:S(2)}, u32[]{:S(2)}) collective-permute-start(bf16[64,1536]{1,0:T(8,128)(2,1)S(1)} %get-tuple-element.175), channel_id=1, source_target_pairs={{0,4},{2,6},{4,0},{6,2},{1,5},{3,7},{5,1},{7,3},{8,12},{10,14},{12... | collective-permute-start | bytes 589832 | tf_op jit(solution)/shard_map/ppermute | solution.py:202
  485.1 32.7 %collective-permute-start.49 = (bf16[256,3200]{1,0:T(8,128)(2,1)S(1)}, bf16[256,3200]{1,0:T(8,128)(2,1)S(1)}, u32[]{:S(2)}, u32[]{:S(2)}) collective-permute-start(bf16[256,3200]{1,0:T(8,128)(2,1)S(1)} %pad_maximum_fusion.4), channel_id=1, source_target_pairs={{0,1},{1,0},{2,3},{3,2},{4,5},{5,4},{6,7},{7,6},{8,9},{9,8},{10,11... | collective-permute-start | bytes 4915208 | tf_op jit(solution)/shard_map/ppermute | solution.py:202
  494.7 11.7 %collective-permute-start.40 = (bf16[64,1536]{1,0:T(8,128)(2,1)S(1)}, bf16[64,1536]{1,0:T(8,128)(2,1)S(1)}, u32[]{:S(2)}, u32[]{:S(2)}) collective-permute-start(bf16[64,1536]{1,0:T(8,128)(2,1)S(1)} %add_convert_fusion.18), channel_id=1, source_target_pairs={{0,4},{2,6},{4,0},{6,2},{1,5},{3,7},{5,1},{7,3},{8,12},{10,14},{12... | collective-permute-start | bytes 589832 | tf_op jit(solution)/shard_map/ppermute | solution.py:202
  506.5 11.1 %collective-permute-start.41 = (bf16[128,1536]{1,0:T(8,128)(2,1)S(1)}, bf16[128,1536]{1,0:T(8,128)(2,1)S(1)}, u32[]{:S(2)}, u32[]{:S(2)}) collective-permute-start(bf16[128,1536]{1,0:T(8,128)(2,1)S(1)} %pad_maximum_fusion.16), channel_id=1, source_target_pairs={{0,2},{2,0},{4,6},{6,4},{1,3},{3,1},{5,7},{7,5},{8,10},{10,8},{12,... | collective-permute-start | bytes 1179656 | tf_op jit(solution)/shard_map/ppermute | solution.py:202
  517.7 18.3 %collective-permute-start.42 = (bf16[256,1536]{1,0:T(8,128)(2,1)S(1)}, bf16[256,1536]{1,0:T(8,128)(2,1)S(1)}, u32[]{:S(2)}, u32[]{:S(2)}) collective-permute-start(bf16[256,1536]{1,0:T(8,128)(2,1)S(1)} %pad_maximum_fusion.13.refs_1_), channel_id=1, source_target_pairs={{0,1},{1,0},{2,3},{3,2},{4,5},{5,4},{6,7},{7,6},{8,9},{9,8},{10,11... | collective-permute-start | bytes 2359304 | tf_op jit(solution)/shard_map/ppermute | solution.py:202
  (79 other events, 768.9 us)
Sparse Core Ops, SparseCore 0:
  10.5 50.9 all-gather.3
  63.9 101.7 all-gather.5
  223.0 71.6 reduce-scatter.1
